TPU v7x, 32 devices: a whole 2x2x4 slice. The times are simulated.
32 devices in a mesh: section: 2 (over core), dp: 16 (over z, y, x).
Axes of the slice: x: 2, y: 2, z: 4, core: 2. Of those that a mesh axis runs over, the one named last changes fastest.
Arguments:
- inputs: bfloat16 [2, 16, 256, 1024], P(None, 'dp'), may hold values from -6 to 6
- lengths: int32 [2, 16], P(None, 'dp'), may hold values from 1 to 256, 2560 in all within a row
- out_grad: bfloat16 [2, 16, 256, 1024], P(None, 'dp'), may hold values from -6 to 6
- attn_gain: bfloat16 [2, 1024], P('section', 'dp'), may hold values from 0.5 to 1.5
- q_weight: bfloat16 [2, 1024, 512], P('section', 'dp'), may hold values from -1 to 1, as said below
- k_weight: bfloat16 [2, 1024, 512], P('section', 'dp'), may hold values from -1 to 1, as said below
- v_weight: bfloat16 [2, 1024, 1024], P('section', 'dp'), may hold values from -0.1875 to 0.1875
- rank_down: bfloat16 [2, 1024, 16], P('section', 'dp'), may hold values from -0.1875 to 0.1875
- rank_up: bfloat16 [2, 16, 512], P('section', None, 'dp'), may hold values from -1.5 to 1.5
- rank_bias: bfloat16 [2, 512], P('section', 'dp'), may hold values from -1 to 4
- gate_weight: bfloat16 [2, 1024, 1024], P('section', 'dp'), may hold values from -0.1875 to 0.1875
- group_gain: bfloat16 [2, 256], P('section', 'dp'), may hold values from 0.5 to 1.5
- out_weight: bfloat16 [2, 1024, 1024], P('section', 'dp'), may hold values from -0.25 to 0.25
- mlp_gain: bfloat16 [2, 1024], P('section', 'dp'), may hold values from 0.5 to 1.5
- ffn_gate: bfloat16 [2, 1024, 2816], P('section', 'dp'), may hold values from -0.1875 to 0.1875
- ffn_up: bfloat16 [2, 1024, 2816], P('section', 'dp'), may hold values from -0.1875 to 0.1875
- ffn_down: bfloat16 [2, 2816, 1024], P('section', 'dp'), may hold values from -0.15625 to 0.15625
Outputs:
- layer_outputs: bfloat16 [2, 2, 16, 256, 1024], P('section', None, 'dp')
- input_grads: float32 [2, 2, 16, 256, 1024], P('section', None, 'dp')
- grad_attn_gain: float32 [2, 1024], P('section', 'dp')
- grad_q_weight: float32 [2, 1024, 512], P('section', 'dp')
- grad_k_weight: float32 [2, 1024, 512], P('section', 'dp')
- grad_v_weight: float32 [2, 1024, 1024], P('section', 'dp')
- grad_rank_down: float32 [2, 1024, 16], P('section', 'dp')
- grad_rank_up: float32 [2, 16, 512], P('section', None, 'dp')
- grad_rank_bias: float32 [2, 512], P('section', 'dp')
- grad_gate_weight: float32 [2, 1024, 1024], P('section', 'dp')
- grad_group_gain: float32 [2, 256], P('section', 'dp')
- grad_out_weight: float32 [2, 1024, 1024], P('section', 'dp')
- grad_mlp_gain: float32 [2, 1024], P('section', 'dp')
- grad_ffn_gate: float32 [2, 1024, 2816], P('section', 'dp')
- grad_ffn_up: float32 [2, 1024, 2816], P('section', 'dp')
- grad_ffn_down: float32 [2, 2816, 1024], P('section', 'dp')
Inputs may be any that keep to these rules, and one draw needn't show every extreme that they name: `lengths`: each row's valid tokens stand at its first positions; the rest of the row is padding. `q_weight`: entries of deviation about 1024^-0.5. `k_weight`: entries of deviation about 1024^-0.5.
All inputs are finite; a program needn't handle non-finite values. No bound on the sum of `lengths` on one device may be relied on, other than what follows from the above.
Results may differ from a plain program's by a relative error of at most 0.025.
Values may be sent and summed in bfloat16 or wider, within the bound.
No kernel may reach another device: no remote copies, remote signals or barrier semaphores. Data moves between devices by JAX's collectives and lax.ppermute only.
A program may use at most 320 MiB of HBM per device.

v0:
```python
from functools import partial

import jax
import jax.numpy as jnp
from jax import lax
from jax.sharding import PartitionSpec as P

SPAN = 64
MICRO = 2


highest = lax.Precision.HIGHEST
gate_scale = 16.0


def from_behind(shard, axis, by):
    size = lax.axis_size(axis)
    pairs = [(i, i + by) for i in range(size) if 0 <= i + by < size]
    return lax.ppermute(shard, axis, pairs)


def make_tools():

    def value_plain(value):
        return lax.optimization_barrier(value.astype(jnp.bfloat16)).astype(jnp.float32)

    round_value = jax.custom_vjp(value_plain)

    def value_keep(value):
        return (value_plain(value), None)

    def value_pass(saved, grad):
        return (grad,)

    round_value.defvjp(value_keep, value_pass)

    def grad_plain(value):
        return value

    round_grad = jax.custom_vjp(grad_plain)

    def grad_keep(value):
        return (value, None)

    def grad_round(saved, grad):
        return (value_plain(grad),)

    round_grad.defvjp(grad_keep, grad_round)

    def rounded_fn(value):
        return round_grad(round_value(value))

    def product_plain(left, right):
        return jnp.matmul(
            left.astype(jnp.bfloat16),
            right.astype(jnp.bfloat16),
            preferred_element_type=jnp.float32,
        )

    product_fn = jax.custom_vjp(product_plain)

    def product_keep(left, right):
        left_low = left.astype(jnp.bfloat16)
        right_low = right.astype(jnp.bfloat16)
        return (
            jnp.matmul(left_low, right_low, preferred_element_type=jnp.float32),
            (left_low, right_low),
        )

    def product_back(saved, grad):
        left_low, right_low = saved
        upper_part = grad.astype(jnp.bfloat16)
        lower_part = (grad - upper_part.astype(jnp.float32)).astype(jnp.bfloat16)
        right_turned = right_low.T
        grad_left = jnp.matmul(
            upper_part, right_turned, preferred_element_type=jnp.float32
        ) + jnp.matmul(lower_part, right_turned, preferred_element_type=jnp.float32)
        left_flat = left_low.reshape(-1, left_low.shape[-1]).T
        upper_flat = upper_part.reshape(-1, upper_part.shape[-1])
        lower_flat = lower_part.reshape(-1, lower_part.shape[-1])
        grad_right = jnp.dot(left_flat, upper_flat, preferred_element_type=jnp.float32) + jnp.dot(
            left_flat, lower_flat, preferred_element_type=jnp.float32
        )
        return (grad_left, grad_right)

    product_fn.defvjp(product_keep, product_back)
    return (rounded_fn, product_fn)


def matmul(left, right):
    return jnp.matmul(left, right, precision=highest)


def rms_norm(value, gain, eps):
    return value * lax.rsqrt(jnp.mean(value * value, axis=-1, keepdims=True) + eps) * gain


def carry_step(carried, pieces):
    decays, update = pieces
    return (decays[..., None] * carried + update, carried)


def linear_mixer(normed, params, rounded, product):
    row_count, length, _ = normed.shape
    val_head = params[8].shape[0]
    head_count = params[3].shape[1] // val_head
    key_head = params[1].shape[1] // head_count
    blocks = length // SPAN
    queries = rounded(product(normed, params[1])).reshape(
        row_count, blocks, SPAN, head_count, key_head
    )
    key_proj = rounded(product(normed, params[2])).reshape(
        row_count, blocks, SPAN, head_count, key_head
    )
    values = rounded(product(normed, params[3])).reshape(
        row_count, blocks, SPAN, head_count, val_head
    )
    logits = matmul(product(normed, params[4]), params[5]) + params[6]
    log_decay = (jax.nn.log_sigmoid(logits) / gate_scale).reshape(
        row_count, blocks, SPAN, head_count, key_head
    )
    within = jnp.cumsum(log_decay, axis=2)
    span_end = within[:, :, -1:]
    scaled_q = queries * key_head ** (-0.5) * jnp.exp(within)
    scaled_k = key_proj * jnp.exp(-within)
    carried_k = key_proj * jnp.exp(span_end - within)
    scores = jnp.einsum("rnihc,rnjhc->rnhij", scaled_q, scaled_k, precision=highest)
    place = jnp.arange(SPAN)
    causal = place[:, None] >= place[None, :]
    scores = jnp.where(causal, scores, jnp.zeros_like(scores))
    local_out = jnp.einsum("rnhij,rnjhv->rnihv", scores, values, precision=highest)
    updates = jnp.einsum("rnjhc,rnjhv->nrhcv", carried_k, values, precision=highest)
    decays = jnp.exp(jnp.moveaxis(span_end[:, :, 0], 1, 0))
    initial = jnp.zeros((row_count, head_count, key_head, val_head), jnp.float32)
    _, states = lax.scan(jax.checkpoint(carry_step), initial, (decays, updates))
    carried_out = jnp.einsum("rnihc,nrhcv->rnihv", scaled_q, states, precision=highest)
    mixed_out = (local_out + carried_out).reshape(row_count, length, head_count, val_head)
    mixed_out = rms_norm(mixed_out, params[8], 1e-05)
    gate_pre = product(normed, params[7]).reshape(row_count, length, head_count, val_head)
    gated_out = rounded(
        (mixed_out * jax.nn.silu(gate_pre)).reshape(row_count, length, head_count * val_head)
    )
    return product(gated_out, params[9])


def block_forward(inputs, params, token_mask):
    rounded, product = make_tools()
    normed = rounded(rms_norm(inputs, params[0], 1e-06))
    hidden = inputs + linear_mixer(normed, params, rounded, product)
    second = rounded(rms_norm(hidden, params[10], 1e-06))
    activated = rounded(jax.nn.silu(product(second, params[11])) * product(second, params[12]))
    return (hidden + product(activated, params[13])) * token_mask


def fetch_forward(local):
    pulled = (
        lax.all_gather(local[0], "dp", axis=0, tiled=True),
        lax.all_gather(local[1], "dp", axis=0, tiled=True),
        lax.all_gather(local[2], "dp", axis=0, tiled=True),
        lax.all_gather(local[3], "dp", axis=0, tiled=True),
        lax.all_gather(local[4], "dp", axis=0, tiled=True),
        lax.all_gather(local[5], "dp", axis=1, tiled=True),
        lax.all_gather(local[6], "dp", axis=0, tiled=True),
        lax.all_gather(local[7], "dp", axis=0, tiled=True),
        lax.all_gather(local[8], "dp", axis=0, tiled=True),
        lax.all_gather(local[9], "dp", axis=0, tiled=True),
        lax.all_gather(local[10], "dp", axis=0, tiled=True),
        lax.all_gather(local[11], "dp", axis=0, tiled=True),
        lax.all_gather(local[12], "dp", axis=0, tiled=True),
        lax.all_gather(local[13], "dp", axis=0, tiled=True),
    )
    return tuple((piece.astype(jnp.float32) for piece in pulled))


def reduce_end(totals):
    return (
        lax.psum_scatter(totals[0], "dp", scatter_dimension=0, tiled=True),
        lax.psum_scatter(totals[1], "dp", scatter_dimension=0, tiled=True),
        lax.psum_scatter(totals[2], "dp", scatter_dimension=0, tiled=True),
        lax.psum_scatter(totals[3], "dp", scatter_dimension=0, tiled=True),
        lax.psum_scatter(totals[4], "dp", scatter_dimension=0, tiled=True),
        lax.psum_scatter(totals[5], "dp", scatter_dimension=1, tiled=True),
        lax.psum_scatter(totals[6], "dp", scatter_dimension=0, tiled=True),
        lax.psum_scatter(totals[7], "dp", scatter_dimension=0, tiled=True),
        lax.psum_scatter(totals[8], "dp", scatter_dimension=0, tiled=True),
        lax.psum_scatter(totals[9], "dp", scatter_dimension=0, tiled=True),
        lax.psum_scatter(totals[10], "dp", scatter_dimension=0, tiled=True),
        lax.psum_scatter(totals[11], "dp", scatter_dimension=0, tiled=True),
        lax.psum_scatter(totals[12], "dp", scatter_dimension=0, tiled=True),
        lax.psum_scatter(totals[13], "dp", scatter_dimension=0, tiled=True),
    )


def body(
    inputs,
    lengths,
    out_grad,
    attn_gain,
    q_weight,
    k_weight,
    v_weight,
    rank_down,
    rank_up,
    rank_bias,
    gate_weight,
    group_gain,
    out_weight,
    mlp_gain,
    ffn_gate,
    ffn_up,
    ffn_down,
):
    local = (
        attn_gain[0],
        q_weight[0],
        k_weight[0],
        v_weight[0],
        rank_down[0],
        rank_up[0],
        rank_bias[0],
        gate_weight[0],
        group_gain[0],
        out_weight[0],
        mlp_gain[0],
        ffn_gate[0],
        ffn_up[0],
        ffn_down[0],
    )
    section_first = lax.axis_index("section") == 0
    positions = jnp.arange(inputs.shape[2])
    masks = (positions[None, None, :] < lengths[:, :, None]).astype(jnp.float32)[..., None]
    gathered = fetch_forward(local)
    received = jnp.zeros(inputs.shape[1:], jnp.bfloat16)
    kept = []
    outgoing_all = []
    for moment in range(MICRO + 1):
        own_index = min(moment, MICRO - 1)
        prev_index = max(moment - 1, 0)
        active = jnp.where(section_first, moment < MICRO, moment >= 1).astype(jnp.float32)
        source = jnp.where(section_first, inputs[own_index], received).astype(jnp.float32)
        token_mask = jnp.where(section_first, masks[own_index], masks[prev_index])
        forward_fn = partial(block_forward, token_mask=token_mask)
        result, pullback = jax.vjp(forward_fn, source, gathered)
        outgoing = result.astype(jnp.bfloat16)
        outgoing_all.append(outgoing)
        kept.append((source, token_mask, active, pullback))
        if moment < MICRO:
            received = from_behind(outgoing, "section", 1)
    layer_out = jnp.stack(
        [
            jnp.where(section_first, outgoing_all[index], outgoing_all[index + 1])
            for index in range(MICRO)
        ]
    )
    totals = jax.tree.map(jnp.zeros_like, gathered)
    arrived = jnp.zeros(inputs.shape[1:], jnp.bfloat16)
    input_list = []
    for turn in range(MICRO + 1):
        source, token_mask, active, pullback = kept[MICRO - turn]
        top_index = max(MICRO - 1 - turn, 0)
        cotangent = (
            jnp.where(
                section_first, arrived.astype(jnp.float32), out_grad[top_index].astype(jnp.float32)
            )
            * active
        )
        grad_input, grad_weights = pullback(cotangent)
        totals = jax.tree.map(jnp.add, totals, grad_weights)
        input_list.append(grad_input)
        if turn < MICRO:
            arrived = from_behind(grad_input.astype(jnp.bfloat16), "section", -1)
    input_out = jnp.stack(
        [
            jnp.where(section_first, input_list[MICRO - index], input_list[MICRO - 1 - index])
            for index in range(MICRO)
        ]
    )
    reduced = tuple(reduce_end(totals))
    return (
        layer_out[None],
        input_out[None],
        reduced[0][None],
        reduced[1][None],
        reduced[2][None],
        reduced[3][None],
        reduced[4][None],
        reduced[5][None],
        reduced[6][None],
        reduced[7][None],
        reduced[8][None],
        reduced[9][None],
        reduced[10][None],
        reduced[11][None],
        reduced[12][None],
        reduced[13][None],
    )


def solution(mesh):
    return jax.shard_map(
        body,
        mesh=mesh,
        in_specs=(
            P(None, "dp", None, None),
            P(None, "dp"),
            P(None, "dp", None, None),
            P("section", "dp"),
            P("section", "dp", None),
            P("section", "dp", None),
            P("section", "dp", None),
            P("section", "dp", None),
            P("section", None, "dp"),
            P("section", "dp"),
            P("section", "dp", None),
            P("section", "dp"),
            P("section", "dp", None),
            P("section", "dp"),
            P("section", "dp", None),
            P("section", "dp", None),
            P("section", "dp", None),
        ),
        out_specs=(
            P("section", None, "dp", None, None),
            P("section", None, "dp", None, None),
            P("section", "dp"),
            P("section", "dp", None),
            P("section", "dp", None),
            P("section", "dp", None),
            P("section", "dp", None),
            P("section", None, "dp"),
            P("section", "dp"),
            P("section", "dp", None),
            P("section", "dp"),
            P("section", "dp", None),
            P("section", "dp"),
            P("section", "dp", None),
            P("section", "dp", None),
            P("section", "dp", None),
        ),
        check_vma=False,
    )
```

profile of v0, /device:TPU:1, one launch (start us, length us, event | category | flops | bytes accessed | tf_op | source)
XLA Modules:
  0.0 2409.4 jit_solution(9413615801760477699)
XLA Ops:
  19.5 36.3 %all-reduce.12 = (bf16[1024]{0:T(1024)(128)(2,1)S(1)}, bf16[256]{0:T(256)(128)(2,1)S(1)}, bf16[512]{0:T(512)(128)(2,1)S(1)}, bf16[1024]{0:T(1024)(128)(2,1)S(1)}) all-reduce(bf16[1024]{0:T(1024)(128)(2,1)S(1)} %dynamic-update-slice, bf16[256]{0:T(256)(128)(2,1)S(1)} %dynamic-update-slice.2, ...), channel_id=2, replica_groups=mesh['section'=2,'dp'=16] {'dp'}, use_global_device_ids=true, to_apply=%add.3 | all-reduce | flops 2816 | bytes 11264
  59.7 32.7 %all-gather.3 = bf16[1,1024,16]{2,0,1:T(2,128)(2,1)S(1)} all-gather(bf16[1,64,16]{2,0,1:T(2,128)(2,1)S(1)} %copy.548), channel_id=5, replica_groups=mesh['section'=2,'dp'=16] {'dp'}, dimensions={1}, use_global_device_ids=true | all-gather | bytes 34816 | tf_op jit(solution)/shard_map/all_gather | solution.py:161
  93.3 33.3 %all-gather.4 = bf16[1,16,512]{1,0,2:T(2,128)(2,1)S(1)} all-gather(bf16[1,16,32]{1,0,2:T(2,128)(2,1)S(1)} %copy.550), channel_id=6, replica_groups=mesh['section'=2,'dp'=16] {'dp'}, dimensions={2}, use_global_device_ids=true | all-gather | bytes 17408 | tf_op jit(solution)/shard_map/all_gather | solution.py:162
  142.0 47.0 %all-gather.23.cloned.1.call-done = bf16[1,1024,1024]{2,1,0:T(8,128)(2,1)} async-done(((bf16[1,64,1024]{2,1,0:T(8,128)(2,1)}), bf16[1,1024,1024]{2,1,0:T(8,128)(2,1)}) %all-gather.23.cloned.1.call-update) | async-done | bytes 2097168 | tf_op jit(solution)/shard_map/all_gather | solution.py:160
  194.3 3.6 convolution_bitcast_fusion.5
  199.5 8.5 while.96
  215.3 35.7 %all-gather.29.cloned.1.call-done = bf16[1,1024,1024]{2,1,0:T(8,128)(2,1)} async-done(((bf16[1,64,1024]{2,1,0:T(8,128)(2,1)}), bf16[1,1024,1024]{2,1,0:T(8,128)(2,1)}) %all-gather.29.cloned.1.call-update) | async-done | bytes 2097168 | tf_op jit(solution)/shard_map/all_gather | solution.py:164
  256.8 56.3 %all-gather.31.cloned.1.call-done = bf16[1,1024,1024]{2,1,0:T(8,128)(2,1)} async-done(((bf16[1,64,1024]{2,1,0:T(8,128)(2,1)}), bf16[1,1024,1024]{2,1,0:T(8,128)(2,1)}) %all-gather.31.cloned.1.call-update) | async-done | bytes 2097168 | tf_op jit(solution)/shard_map/all_gather | solution.py:166
  316.7 86.5 %all-gather.35.cloned.1.call-done = bf16[1,1024,2816]{2,1,0:T(8,128)(2,1)} async-done(((bf16[1,64,2816]{2,1,0:T(8,128)(2,1)}), bf16[1,1024,2816]{2,1,0:T(8,128)(2,1)}) %all-gather.35.cloned.1.call-update) | async-done | bytes 5767184 | tf_op jit(solution)/shard_map/all_gather | solution.py:169
  403.2 5.9 fusion.34
  409.1 84.7 %all-gather.33.cloned.1.call-done = bf16[1,1024,2816]{2,1,0:T(8,128)(2,1)} async-done(((bf16[1,64,2816]{2,1,0:T(8,128)(2,1)}), bf16[1,1024,2816]{2,1,0:T(8,128)(2,1)}) %all-gather.33.cloned.1.call-update) | async-done | bytes 5767184 | tf_op jit(solution)/shard_map/all_gather | solution.py:168
  493.8 4.4 fusion.52
  501.8 82.6 %all-gather.37.cloned.1.call-done = bf16[1,2816,1024]{2,1,0:T(8,128)(2,1)} async-done(((bf16[1,176,1024]{2,1,0:T(8,128)(2,1)}), bf16[1,2816,1024]{2,1,0:T(8,128)(2,1)}) %all-gather.37.cloned.1.call-update) | async-done | bytes 5767184 | tf_op jit(solution)/shard_map/all_gather | solution.py:170
  584.4 5.1 fusion.446
  589.6 13.9 collective-permute-start
  624.8 3.6 convolution_bitcast_fusion.4
  630.0 8.3 while.97
  698.5 3.8 convolution_bitcast_fusion.3
  703.8 8.5 while.98
  730.7 5.3 fusion.30
  754.4 5.1 convolution_bitcast_fusion.2
  766.7 38.5 %while.99 = (s32[]{:T(128)}, f32[1,4,128,256]{3,2,1,0:T(8,128)}, f32[4,1,4,128]{3,2,1,0:T(4,128)S(1)}, f32[4,1,4,128,256]{4,3,2,1,0:T(8,128)}, f32[4,1,4,128,256...) while((s32[]{:T(128)}, f32[1,4,128,256]{3,2,1,0:T(8,128)}, ...), condition=%wide.region_22.24_spmd.clone, body=%wide.region_20.23_spmd.clone.sunk | while | flops 654852 | bytes 7352471 | solution.py:135
  806.0 4.4 fusion.221
  848.8 4.3 collective-permute-start.2
  865.1 4.3 fusion.40
  869.5 4.5 fusion.436
  882.6 5.2 convolution_bitcast_fusion.1
  894.9 41.9 %while.100 = (s32[]{:T(128)}, f32[1,4,128,256]{3,2,1,0:T(8,128)}, f32[4,1,4,128]{3,2,1,0:T(4,128)S(1)}, f32[4,1,4,128,256]{4,3,2,1,0:T(8,128)}, f32[4,1,4,128,25...) while((s32[]{:T(128)}, f32[1,4,128,256]{3,2,1,0:T(8,128)}, ...), condition=%wide.region_30.32_spmd.clone, body=%wide.region_28.31_spmd.clone.sunk | while | flops 654852 | bytes 7352471 | solution.py:135
  937.7 4.4 fusion.224
  1000.7 4.3 fusion.36
  1016.0 5.1 convolution_bitcast_fusion
  1026.6 17.2 while.101
  1044.7 3.7 fusion.821
  1048.5 4.7 fusion.771
  1063.5 6.1 add_add_fusion.7
  1078.9 5.2 add_add_fusion.6
  1102.2 7.2 add_add_fusion.5
  1126.8 3.6 add_add_fusion.3
  1132.3 6.0 fusion.192
  1138.3 6.0 fusion.598
  1144.3 6.0 fusion.189
  1150.3 5.9 fusion.595
  1156.2 5.9 fusion.186
  1162.1 23.6 add_add_fusion.2
  1187.6 7.7 fusion.652
  1195.3 6.1 fusion.650
  1201.4 6.1 fusion.693
  1207.5 5.9 fusion.691
  1213.4 6.0 fusion.733
  1219.5 24.6 %add_add_fusion.1 = f32[1024,2816]{1,0:T(8,128)} fusion(f32[1024,2816]{1,0:T(8,128)} %fusion.733, f32[1024,2816]{1,0:T(8,128)} %fusion.693, f32[1024,2816]{1,0:T(8,128)} %fusion.691, f32[1024,2816]{1,0:T(8,128)} %fusion.652, f32[1024,2816]{1,0:T(8,128)} %fusion.650, bf16[1,256,1024]{2,1,0:T(8,128)(2,1)S(1)} %copy-done.106, ...), kind=kOutput, calls=%fused_computation.34 | convolution fusion | flops 1498021888 | bytes 74055680 | tf_op jit(solution)/shard_map/transpose(jvp())/dot_general | solution.py:151
  1248.0 6.0 fusion.197
  1254.0 6.1 fusion.195
  1260.0 6.1 fusion.202
  1266.1 5.9 fusion.200
  1272.1 6.0 fusion.206
  1278.1 24.6 %add_add_fusion = f32[2816,1024]{1,0:T(8,128)} fusion(f32[2816,1024]{1,0:T(8,128)} %fusion.206, f32[2816,1024]{1,0:T(8,128)} %fusion.202, f32[2816,1024]{1,0:T(8,128)} %fusion.200, f32[2816,1024]{1,0:T(8,128)} %fusion.197, f32[2816,1024]{1,0:T(8,128)} %fusion.195, bf16[1,256,2816]{2,1,0:T(8,128)(2,1)} %fusion.177, ...), kind=kOutput, calls=%fused_computation.33 | convolution fusion | flops 1493172224 | bytes 71697416 | tf_op jit(solution)/shard_map/transpose(jvp())/dot_general | solution.py:152
  1306.0 4.4 fusion.510
  1321.6 63.4 %all-reduce.11 = (f32[1024]{0:T(1024)S(1)}, f32[512]{0:T(512)S(1)}, f32[256]{0:T(256)S(1)}, f32[1024]{0:T(1024)S(1)}) all-reduce(f32[1024]{0:T(1024)S(1)} %add_add_fusion.18, f32[512]{0:T(512)S(1)} %negate_add_fusion, f32[256]{0:T(256)S(1)} %add_add_fusion.19, ...), channel_id=16, replica_groups=mesh['section'=2,'dp'=16] {'dp'}, use_global_device_ids=true, to_apply=%region_45.47.clone | all-reduce | flops 2816 | bytes 22528
  1393.5 73.2 %reduce-scatter.19.cloned.1.call-done = f32[64,1024]{1,0:T(8,128)} async-done(((f32[1024,1024]{1,0:T(8,128)}), f32[64,1024]{1,0:T(8,128)}) %reduce-scatter.19.cloned.1.call-update) | async-done | bytes 262160 | tf_op jit(solution)/shard_map/reduce_scatter | solution.py:180
  1466.7 97.5 %reduce-scatter.21.cloned.1.call-done = f32[64,1024]{1,0:T(8,128)} async-done(((f32[1024,1024]{1,0:T(8,128)}), f32[64,1024]{1,0:T(8,128)}) %reduce-scatter.21.cloned.1.call-update) | async-done | bytes 262160 | tf_op jit(solution)/shard_map/reduce_scatter | solution.py:184
  1564.1 97.5 %reduce-scatter.23.cloned.1.call-done = f32[64,1024]{1,0:T(8,128)} async-done(((f32[1024,1024]{1,0:T(8,128)}), f32[64,1024]{1,0:T(8,128)}) %reduce-scatter.23.cloned.1.call-update) | async-done | bytes 262160 | tf_op jit(solution)/shard_map/reduce_scatter | solution.py:186
  1661.6 243.9 %reduce-scatter.25.cloned.1.call-done = f32[64,2816]{1,0:T(8,128)} async-done(((f32[1024,2816]{1,0:T(8,128)}), f32[64,2816]{1,0:T(8,128)}) %reduce-scatter.25.cloned.1.call-update) | async-done | bytes 720912 | tf_op jit(solution)/shard_map/reduce_scatter | solution.py:188
  1905.5 248.3 %reduce-scatter.27.cloned.1.call-done = f32[64,2816]{1,0:T(8,128)} async-done(((f32[1024,2816]{1,0:T(8,128)}), f32[64,2816]{1,0:T(8,128)}) %reduce-scatter.27.cloned.1.call-update) | async-done | bytes 720912 | tf_op jit(solution)/shard_map/reduce_scatter | solution.py:189
  2153.8 248.3 %reduce-scatter.29.cloned.1.call-done = f32[176,1024]{1,0:T(8,128)} async-done(((f32[2816,1024]{1,0:T(8,128)}), f32[176,1024]{1,0:T(8,128)}) %reduce-scatter.29.cloned.1.call-update) | async-done | bytes 720912 | tf_op jit(solution)/shard_map/reduce_scatter | solution.py:190
  (1151 shorter events, 530.6 us)
Async XLA Ops:
  7.2 52.4 %copy-start.282 = (bf16[1,64,16]{1,2,0:T(8,128)(2,1)S(1)}, bf16[1,64,16]{1,2,0:T(8,128)(2,1)}, u32[]{:S(2)}) copy-start(bf16[1,64,16]{1,2,0:T(8,128)(2,1)} %param.37) | copy-start | bytes 6148
  7.2 86.1 %copy-start.283 = (bf16[1,16,32]{2,1,0:T(8,128)(2,1)S(1)}, bf16[1,16,32]{2,1,0:T(8,128)(2,1)}, u32[]{:S(2)}) copy-start(bf16[1,16,32]{2,1,0:T(8,128)(2,1)} %param.38) | copy-start | bytes 3076
  7.2 123.1 %all-gather.25.cloned.1.call-start = ((), (), s32[]{:S(2)}) async-start(), calls=%async_computation.19 | async-start | bytes 1114112 | tf_op jit(solution)/shard_map/all_gather | solution.py:158
  7.9 126.2 %all-gather.27.cloned.1.call-start = ((), (), s32[]{:S(2)}) async-start(), calls=%async_computation.20 | async-start | bytes 1114112 | tf_op jit(solution)/shard_map/all_gather | solution.py:159
  8.7 180.3 %all-gather.23.cloned.1.call-start = ((), (), s32[]{:S(2)}) async-start(), calls=%async_computation.18 | async-start | bytes 2228224 | tf_op jit(solution)/shard_map/all_gather | solution.py:160
  9.4 241.6 %all-gather.29.cloned.1.call-start = ((), (), s32[]{:S(2)}) async-start(), calls=%async_computation.21 | async-start | bytes 2228224 | tf_op jit(solution)/shard_map/all_gather | solution.py:164
  10.0 303.0 %all-gather.31.cloned.1.call-start = ((), (), s32[]{:S(2)}) async-start(), calls=%async_computation.22 | async-start | bytes 2228224 | tf_op jit(solution)/shard_map/all_gather | solution.py:166
  10.6 392.6 %all-gather.35.cloned.1.call-start = ((), (), s32[]{:S(2)}) async-start(), calls=%async_computation.24 | async-start | bytes 6127616 | tf_op jit(solution)/shard_map/all_gather | solution.py:169
  11.2 482.6 %all-gather.33.cloned.1.call-start = ((), (), s32[]{:S(2)}) async-start(), calls=%async_computation.23 | async-start | bytes 6127616 | tf_op jit(solution)/shard_map/all_gather | solution.py:168
  11.9 572.5 %all-gather.37.cloned.1.call-start = ((), (), s32[]{:S(2)}) async-start(), calls=%async_computation.25 | async-start | bytes 6127616 | tf_op jit(solution)/shard_map/all_gather | solution.py:170
  12.7 1378.0 %reduce-scatter.33.cloned.1.call-start = ((), (), s32[]{:S(2)}) async-start(), calls=%async_computation.27 | async-start | bytes 278528
  57.6 71.9 %copy-start.291 = (s32[2,1]{0,1:T(1,128)S(1)}, s32[2,1]{0,1:T(1,128)}, u32[]{:S(2)}) copy-start(s32[2,1]{0,1:T(1,128)} %param.31) | copy-start | bytes 28
  58.9 192.1 %copy-start.8 = (bf16[1,256,1024]{2,1,0:T(8,128)(2,1)}, bf16[1,256,1024]{2,1,0:T(8,128)(2,1)S(1)}, u32[]{:S(2)}) copy-start(bf16[1,256,1024]{2,1,0:T(8,128)(2,1)S(1)} %fusion.525) | copy-start | bytes 1572868
  59.5 550.1 %copy-start.289 = (f32[512]{0:T(512)}, f32[512]{0:T(512)S(1)}, u32[]{:S(2)}) copy-start(f32[512]{0:T(512)S(1)} %convert_element_type.1137) | copy-start | bytes 6148
  126.7 482.9 %copy-start.217 = (bf16[1,16,512]{2,1,0:T(8,128)(2,1)}, bf16[1,16,512]{2,1,0:T(8,128)(2,1)S(1)}, u32[]{:S(2)}) copy-start(bf16[1,16,512]{2,1,0:T(8,128)(2,1)S(1)} %copy.551) | copy-start | bytes 49156
  129.6 454.8 %copy-start.232 = (f32[1,1,256]{2,1,0:T(1,128)}, f32[1,1,256]{2,1,0:T(1,128)S(1)}, u32[]{:S(2)}) copy-start(f32[1,1,256]{2,1,0:T(1,128)S(1)} %get-tuple-element.1137) | copy-start | bytes 3076
  129.6 473.9 %copy-start.250 = (f32[1,1,256]{2,1,0:T(1,128)}, f32[1,1,256]{2,1,0:T(1,128)S(1)}, u32[]{:S(2)}) copy-start(f32[1,1,256]{2,1,0:T(1,128)S(1)} %get-tuple-element.1136) | copy-start | bytes 3076
  130.3 64.1 %copy-start.36 = (f32[1,4,64,4,128]{4,3,2,1,0:T(4,128)}, f32[1,4,64,4,128]{4,3,2,1,0:T(4,128)S(1)}, u32[]{:S(2)}) copy-start(f32[1,4,64,4,128]{4,3,2,1,0:T(4,128)S(1)} %fusion.983) | copy-start | bytes 1572868
  130.3 64.0 %copy-start.221 = (f32[4,4,128]{2,1,0:T(4,128)}, f32[4,4,128]{2,1,0:T(4,128)S(1)}, u32[]{:S(2)}) copy-start(f32[4,4,128]{2,1,0:T(4,128)S(1)} %slice_bitcast_fusion.2) | copy-start | bytes 24580
  138.9 69.2 %copy-start.107 = (f32[4,64,4,128]{3,1,2,0:T(8,128)}, f32[4,64,4,128]{3,1,2,0:T(8,128)S(1)}, u32[]{:S(2)}) copy-start(f32[4,64,4,128]{3,1,2,0:T(8,128)S(1)} %fusion.742) | copy-start | bytes 1572868
  213.7 39.6 %copy-start.225 = (f32[4,64,4]{1,2,0:T(4,128)}, f32[4,64,4]{1,2,0:T(4,128)S(1)}, u32[]{:S(2)}) copy-start(f32[4,64,4]{1,2,0:T(4,128)S(1)} %fusion.910) | copy-start | bytes 12292
  256.8 59.9 %copy-start.193 = (bf16[1,256,1024]{2,1,0:T(8,128)(2,1)}, bf16[1,256,1024]{2,1,0:T(8,128)(2,1)S(1)}, u32[]{:S(2)}) copy-start(bf16[1,256,1024]{2,1,0:T(8,128)(2,1)S(1)} %fusion.804) | copy-start | bytes 1572868
  315.5 93.6 %copy-start.284 = (f32[256]{0:T(256)}, f32[256]{0:T(256)S(1)}, u32[]{:S(2)}) copy-start(f32[256]{0:T(256)S(1)} %get-tuple-element.1144) | copy-start | bytes 3076
  315.5 93.5 %copy-start.263 = (f32[256]{0:T(256)}, f32[256]{0:T(256)S(1)}, u32[]{:S(2)}) copy-start(f32[256]{0:T(256)S(1)} %fusion.914) | copy-start | bytes 3076
  316.7 177.1 %copy-start.105 = (bf16[1,256,1024]{2,1,0:T(8,128)(2,1)}, bf16[1,256,1024]{2,1,0:T(8,128)(2,1)S(1)}, u32[]{:S(2)}) copy-start(bf16[1,256,1024]{2,1,0:T(8,128)(2,1)S(1)} %fusion.602) | copy-start | bytes 1572868
  501.8 101.6 %copy-start.48 = (bf16[2,1,256,1024]{3,2,1,0:T(8,128)(2,1)S(1)}, bf16[2,1,256,1024]{3,2,1,0:T(8,128)(2,1)}, u32[]{:S(2)}) copy-start(bf16[2,1,256,1024]{3,2,1,0:T(8,128)(2,1)} %param.32) | copy-start | bytes 3145732
  584.4 19.1 copy-start.74
  589.6 17.3 copy-start.213
  589.6 17.3 copy-start.148
  589.6 17.3 collective-permute-start
  608.6 40.4 %copy-start.2 = (bf16[1,256,1024]{2,1,0:T(8,128)(2,1)}, bf16[1,256,1024]{2,1,0:T(8,128)(2,1)S(1)}, u32[]{:S(2)}) copy-start(bf16[1,256,1024]{2,1,0:T(8,128)(2,1)S(1)} %fusion.524) | copy-start | bytes 1572868
  614.5 10.3 copy-start.40
  614.6 10.2 copy-start.223
  661.6 9.4 collective-permute-start.1
  730.4 16.5 copy-start.87
  818.1 10.4 copy-start.197
  842.7 13.2 slice-start.2
  843.9 12.0 slice-start.3
  845.8 10.1 copy-start.167
  848.8 7.1 collective-permute-start.2
  855.9 19.1 copy-start.169
  894.9 42.8 %copy-start.224 = (f32[4,4,128]{2,1,0:T(4,128)S(1)}, f32[4,4,128]{2,1,0:T(4,128)}, u32[]{:S(2)}) copy-start(f32[4,4,128]{2,1,0:T(4,128)} %copy-done.223) | copy-start | bytes 24580
  978.5 12.8 slice-start.4
  980.9 10.5 slice-start.5
  986.1 5.2 collective-permute-start.3
  991.4 16.5 copy-start.171
  1026.6 18.0 copy-start.222
  1053.5 9.9 copy-start.173
  1062.1 329.9 %reduce-scatter.31.cloned.1.call-start = ((), (), s32[]{:S(2)}) async-start(), calls=%async_computation.26 | async-start | bytes 557056
  1063.4 330.1 %reduce-scatter.15.cloned.1.call-start = ((), (), s32[]{:S(2)}) async-start(), calls=%async_computation.10 | async-start | bytes 2228224 | tf_op jit(solution)/shard_map/reduce_scatter | solution.py:178
  1069.6 323.9 %reduce-scatter.17.cloned.1.call-start = ((), (), s32[]{:S(2)}) async-start(), calls=%async_computation.11 | async-start | bytes 2228224 | tf_op jit(solution)/shard_map/reduce_scatter | solution.py:179
  1084.1 382.5 %reduce-scatter.19.cloned.1.call-start = ((), (), s32[]{:S(2)}) async-start(), calls=%async_computation.12 | async-start | bytes 4456448 | tf_op jit(solution)/shard_map/reduce_scatter | solution.py:180
  1109.5 454.6 %reduce-scatter.21.cloned.1.call-start = ((), (), s32[]{:S(2)}) async-start(), calls=%async_computation.13 | async-start | bytes 4456448 | tf_op jit(solution)/shard_map/reduce_scatter | solution.py:184
  1120.5 541.1 %reduce-scatter.23.cloned.1.call-start = ((), (), s32[]{:S(2)}) async-start(), calls=%async_computation.14 | async-start | bytes 4456448 | tf_op jit(solution)/shard_map/reduce_scatter | solution.py:186
  1130.4 775.1 %reduce-scatter.25.cloned.1.call-start = ((), (), s32[]{:S(2)}) async-start(), calls=%async_computation.15 | async-start | bytes 12255232 | tf_op jit(solution)/shard_map/reduce_scatter | solution.py:188
  1185.8 968.0 %reduce-scatter.27.cloned.1.call-start = ((), (), s32[]{:S(2)}) async-start(), calls=%async_computation.16 | async-start | bytes 12255232 | tf_op jit(solution)/shard_map/reduce_scatter | solution.py:189
  1244.1 1158.0 %reduce-scatter.29.cloned.1.call-start = ((), (), s32[]{:S(2)}) async-start(), calls=%async_computation.17 | async-start | bytes 12255232 | tf_op jit(solution)/shard_map/reduce_scatter | solution.py:190
  1318.8 67.9 %copy-start.272 = (f32[256]{0:T(256)S(1)}, f32[256]{0:T(256)}, u32[]{:S(2)}) copy-start(f32[256]{0:T(256)} %copy-done.271) | copy-start | bytes 3076
  1318.8 67.9 %copy-start.21 = (f32[1,256,1024]{2,1,0:T(8,128)S(1)}, f32[1,256,1024]{2,1,0:T(8,128)}, u32[]{:S(2)}) copy-start(f32[1,256,1024]{2,1,0:T(8,128)} %copy-done.18) | copy-start | bytes 3145732
  1318.8 67.9 %copy-start.32 = (f32[1,256,1024]{2,1,0:T(8,128)S(1)}, f32[1,256,1024]{2,1,0:T(8,128)}, u32[]{:S(2)}) copy-start(f32[1,256,1024]{2,1,0:T(8,128)} %copy-done.30) | copy-start | bytes 3145732
  1318.9 67.9 %copy-start.80 = (bf16[1,256,1024]{2,1,0:T(8,128)(2,1)S(1)}, bf16[1,256,1024]{2,1,0:T(8,128)(2,1)}, u32[]{:S(2)}) copy-start(bf16[1,256,1024]{2,1,0:T(8,128)(2,1)} %copy-done.77) | copy-start | bytes 1572868
  1318.9 67.9 %copy-start.168 = (bf16[1,256,1024]{2,1,0:T(8,128)(2,1)S(1)}, bf16[1,256,1024]{2,1,0:T(8,128)(2,1)}, u32[]{:S(2)}) copy-start(bf16[1,256,1024]{2,1,0:T(8,128)(2,1)} %copy-done.167) | copy-start | bytes 1572868
  1318.9 67.9 %copy-start.255 = (f32[256]{0:T(256)S(1)}, f32[256]{0:T(256)}, u32[]{:S(2)}) copy-start(f32[256]{0:T(256)} %copy-done.253) | copy-start | bytes 3076
  1318.9 67.9 %copy-start.270 = (f32[256]{0:T(256)S(1)}, f32[256]{0:T(256)}, u32[]{:S(2)}) copy-start(f32[256]{0:T(256)} %copy-done.269) | copy-start | bytes 3076
  (271 other events, 981.1 us)
Sparse Core Ops, SparseCore 0:
  10.8 56.9 all-gather.24
  70.5 55.2 all-gather.26
  128.7 60.3 all-gather.22
  191.6 59.3 all-gather.28
  253.7 59.3 all-gather.30
  315.6 87.5 all-gather.34
  405.9 87.8 all-gather.32
  496.5 87.8 all-gather.36
  1062.2 62.5 reduce-scatter.32
  1127.0 73.6 reduce-scatter.30
  1203.6 76.7 reduce-scatter.14
  1283.1 78.8 reduce-scatter.16
  1364.9 101.7 reduce-scatter.18
  1469.4 94.7 reduce-scatter.20
  1566.8 94.7 reduce-scatter.22
  1664.3 241.1 reduce-scatter.24
  1908.3 245.5 reduce-scatter.26
  2156.6 245.5 reduce-scatter.28
where the time goes:
time: 2430 us; the launch traced here: 2410 us
  waiting for transfers between devices  1410 us (58%)
  matrix products  466 us (19%)
  local copies, waits for them, and re-layouts  196 us (8%)
  blocking collectives  166 us (7%)
  other arithmetic  127 us (5%)
    reduce_scatter x1, waiting for transfers between devices, reduce_end(): lax.psum_scatter(totals[13], 'dp', scatter_dimension=0, tiled=True)  248 us
    reduce_scatter x1, waiting for transfers between devices, reduce_end(): lax.psum_scatter(totals[12], 'dp', scatter_dimension=0, tiled=True)  248 us
    reduce_scatter x1, waiting for transfers between devices, reduce_end(): lax.psum_scatter(totals[11], 'dp', scatter_dimension=0, tiled=True)  244 us
    unnamed x2, blocking collectives  99.7 us
    reduce_scatter x1, waiting for transfers between devices, reduce_end(): lax.psum_scatter(totals[7], 'dp', scatter_dimension=0, tiled=True)  97.5 us
    reduce_scatter x1, waiting for transfers between devices, reduce_end(): lax.psum_scatter(totals[9], 'dp', scatter_dimension=0, tiled=True)  97.5 us
    all_gather x1, waiting for transfers between devices, fetch_forward(): lax.all_gather(local[12], 'dp', axis=0, tiled=True)  86.5 us
    all_gather x1, waiting for transfers between devices, fetch_forward(): lax.all_gather(local[11], 'dp', axis=0, tiled=True)  84.7 us
  transfers between devices with their start and end apart: 22, of which 12 were waited for; matrix products, arithmetic and copies ran while one was open for 14% of the time, Pallas kernels for 0%

commit v1 on v0

v1 whole, which is shorter than its diff:
```python
import jax
import jax.numpy as jnp
from jax import lax
from jax.sharding import PartitionSpec as P

SPAN = 64
BF = jnp.bfloat16
F32 = jnp.float32


class Grid:
    def __init__(self, size):
        self.fast = size == 16
        self.size = size

        def pairs(dz, dy, dx):
            return [
                (z * 4 + y * 2 + x, ((z + dz) % 4) * 4 + (y ^ dy) * 2 + (x ^ dx))
                for z in range(4)
                for y in range(2)
                for x in range(2)
            ]

        if self.fast:
            self.px = lambda v: lax.ppermute(v, "dp", pairs(0, 0, 1))
            self.py = lambda v: lax.ppermute(v, "dp", pairs(0, 1, 0))
            self.pz = lambda v: lax.ppermute(v, "dp", pairs(1, 0, 0))

    def place(self):
        i = lax.axis_index("dp")
        return i // 4, (i // 2) % 2, i % 2

    def split(self, v):
        h = (v.shape[-1] // 2 + 127) // 128 * 128
        return v[..., :h], v[..., h:]

    def xy_gather(self, blk):
        X = self.px(blk)
        Y = self.py(blk)
        D1 = self.py(self.split(X)[0])
        D2 = self.px(self.split(Y)[1])
        return (0, 0, blk), (0, 1, X), (1, 0, Y), (1, 1, jnp.concatenate([D1, D2], -1))

    def gather_z_first(self, shard):
        if not self.fast:
            return lax.all_gather(shard, "dp", axis=0, tiled=True)
        z, y, x = self.place()
        R, C = shard.shape
        out = jnp.zeros((4, 2, 2, R, C), shard.dtype)
        cur = shard
        for i in range(4):
            for yy, xx, p in self.xy_gather(cur):
                out = lax.dynamic_update_slice(
                    out, p[None, None, None], ((z - i) % 4, y ^ yy, x ^ xx, 0, 0)
                )
            if i < 3:
                cur = self.pz(cur)
        return out.reshape(16 * R, C)

    def gather_z_last(self, shard):
        if not self.fast:
            return lax.all_gather(shard, "dp", axis=0, tiled=True)
        z, y, x = self.place()
        R, C = shard.shape
        cur = jnp.zeros((2, 2, R, C), shard.dtype)
        for yy, xx, p in self.xy_gather(shard):
            cur = lax.dynamic_update_slice(cur, p[None, None], (y ^ yy, x ^ xx, 0, 0))
        out = jnp.zeros((4, 2, 2, R, C), shard.dtype)
        for i in range(4):
            out = lax.dynamic_update_slice(out, cur[None], ((z - i) % 4, 0, 0, 0, 0))
            if i < 3:
                cur = self.pz(cur)
        return out.reshape(16 * R, C)

    def relative(self, v, axis):
        if not self.fast:
            return v
        z, _, _ = self.place()
        n = v.shape[axis] // 4
        return jnp.concatenate(
            [lax.dynamic_slice_in_dim(v, ((z - 1 - i) % 4) * n, n, axis) for i in range(4)], axis
        )

    def add(self, a, b):
        return (a.astype(F32) + b.astype(F32)).astype(a.dtype)

    def xy_reduce(self, G):
        _, y, x = self.place()
        n, _, _, R, C = G.shape

        def pick(yy, xx):
            return lax.dynamic_slice(G, (0, y ^ yy, x ^ xx, 0, 0), (n, 1, 1, R, C)).reshape(n, R, C)

        d1, d2 = self.split(pick(1, 1))
        r1 = self.px(d1)
        r2 = self.py(d2)
        y1, y2 = self.split(pick(1, 0))
        x1, x2 = self.split(pick(0, 1))
        a = self.py(jnp.concatenate([self.add(y1, r1), y2], -1))
        b = self.px(jnp.concatenate([x1, self.add(x2, r2)], -1))
        return (pick(0, 0).astype(F32) + a.astype(F32) + b.astype(F32)).astype(G.dtype)

    def z_reduce(self, parts):
        v = parts[0]
        for i in range(1, 4):
            v = self.add(self.pz(v), parts[i])
        return v

    def reduce_z_last(self, G):
        if not self.fast:
            return lax.psum_scatter(G, "dp", scatter_dimension=0, tiled=True)
        R, C = G.shape[0] // 16, G.shape[1]
        G = G.reshape(4, 2, 2, R, C)
        return self.z_reduce([self.xy_reduce(G[i : i + 1])[0] for i in range(4)])

    def reduce_z_first(self, G):
        if not self.fast:
            return lax.psum_scatter(G, "dp", scatter_dimension=0, tiled=True)
        R, C = G.shape[0] // 16, G.shape[1]
        G = G.reshape(4, 2, 2, R, C)
        return self.xy_reduce(self.z_reduce([G[i] for i in range(4)])[None])[0]


def over_core(v):
    return lax.ppermute(v, "section", [(0, 1), (1, 0)])


def core_sum(v):
    v = v.astype(BF)
    return v.astype(F32) + over_core(v).astype(F32)


def mm(a, b):
    return lax.dot_general(a, b, (((1,), (0,)), ((), ())), preferred_element_type=F32)


def mm_nt(a, b):
    return lax.dot_general(a, b, (((1,), (1,)), ((), ())), preferred_element_type=F32)


def mm_tn(a, b):
    return lax.dot_general(a, b, (((0,), (0,)), ((), ())), preferred_element_type=F32)


def ein(spec, a, b):
    return jnp.einsum(spec, a.astype(BF), b.astype(BF), preferred_element_type=F32)


def mixer(q, k, v, logits, g, gain, rows):
    heads = v.shape[1] // gain.shape[0]
    blocks = q.shape[0] // rows // SPAN

    def cut(a):
        return a.astype(F32).reshape(rows, blocks, SPAN, heads, a.shape[1] // heads)

    q, k, v = cut(q), cut(k), cut(v)
    b = jnp.cumsum(cut(jax.nn.log_sigmoid(logits) / 16.0), axis=2)
    last = b[:, :, -1:]
    qs = q * q.shape[-1] ** (-0.5) * jnp.exp(b)
    ks = k * jnp.exp(-b)
    kc = k * jnp.exp(last - b)
    sc = ein("rnihc,rnjhc->rnhij", qs, ks)
    i = jnp.arange(SPAN)
    sc = jnp.where(i[:, None] >= i[None, :], sc, 0.0)
    out = ein("rnhij,rnjhv->rnihv", sc, v)
    up = ein("rnjhc,rnjhv->rnhcv", kc, v)
    dec = jnp.exp(last[:, :, 0])[..., None]
    S = jnp.zeros_like(up[:, 0])
    states = []
    for n in range(blocks):
        states.append(S)
        S = dec[:, n] * S + up[:, n]
    out = out + ein("rnihc,rnhcv->rnihv", qs, jnp.stack(states, 1))
    out = out * lax.rsqrt(jnp.mean(out * out, axis=-1, keepdims=True) + 1e-5) * gain
    return (out * jax.nn.silu(cut(g))).reshape(g.shape)


def norm_back(dn, x, r, gain):
    t = dn * gain
    dx = t * r - x * (r * r * r * jnp.mean(t * x, axis=-1, keepdims=True))
    return dx, jnp.sum(dn * x * r, axis=0)


def layer_forward(x, w, mask, rows):
    K = w["ru"].shape[1]
    V = w["WO"].shape[0]
    r1 = lax.rsqrt(jnp.mean(x * x, axis=-1, keepdims=True) + 1e-6)
    n = (x * r1 * w["ag"]).astype(BF)
    pre = mm(n, w["WA"])
    q, k = pre[:, :K].astype(BF), pre[:, K : 2 * K].astype(BF)
    v, g = pre[:, 2 * K : 2 * K + V].astype(BF), pre[:, 2 * K + V :]
    low = mm(n, w["rd"])
    logits = jnp.matmul(low, w["ru"], precision=lax.Precision.HIGHEST) + w["rb"]
    gated, mix_back = jax.vjp(lambda *a: mixer(*a, rows), q, k, v, logits, g, w["gg"])
    gated = gated.astype(BF)
    hidden = x + core_sum(mm(gated, w["WO"]))
    r2 = lax.rsqrt(jnp.mean(hidden * hidden, axis=-1, keepdims=True) + 1e-6)
    second = (hidden * r2 * w["mg"]).astype(BF)
    gu = mm(second, w["WF"])
    F = gu.shape[1] // 2
    act = (jax.nn.silu(gu[:, :F]) * gu[:, F:]).astype(BF)
    y = (hidden + core_sum(mm(act, w["WD"]))) * mask
    saved = (x, r1, n, low, logits, mix_back, gated, hidden, r2, second, gu, act)
    return y, saved


def layer_backward(dy, w, saved, grid):
    x, r1, n, low, logits, mix_back, gated, hidden, r2, second, gu, act = saved
    s = lax.axis_index("section")
    F = gu.shape[1] // 2
    da = mm_nt(dy, w["WD"]).astype(BF).astype(F32)
    gD = back_rows(mm_tn(act, dy).astype(BF), s)
    gate, up = gu[:, :F], gu[:, F:]
    sig = jax.nn.sigmoid(gate)
    dgu = jnp.concatenate([da * up * (sig * (1.0 + gate * (1.0 - sig))), da * (gate * sig)], 1).astype(BF)
    gF = mm_tn(grid.relative(second, 1), dgu).astype(BF)
    dsec = core_sum(mm_nt(dgu, w["WF"])).astype(BF).astype(F32)
    back, d_mg = norm_back(dsec, hidden, r2, w["mg"])
    dhid = dy.astype(F32) + back
    dhid_low = dhid.astype(BF)
    dgated = mm_nt(dhid_low, w["WO"]).astype(BF).astype(F32)
    gO = back_rows(mm_tn(gated, dhid_low).astype(BF), s)
    dq, dk, dv, dlogits, dg, d_gg = mix_back(dgated)
    dpre = jnp.concatenate([dq, dk, dv, dg.astype(BF)], 1)
    dlow = jnp.matmul(dlogits, w["ru"].T, precision=lax.Precision.HIGHEST)
    d_ru = mm_tn(low, dlogits)
    d_rb = jnp.sum(dlogits, axis=0)
    gA = mm_tn(grid.relative(n, 1), dpre).astype(BF)
    dn = mm_nt(dpre, w["WA"]) + mm_nt(dlow.astype(BF), w["rd"])
    dn = core_sum(dn).astype(BF).astype(F32)
    dlow = core_sum(dlow)
    d_rd = mm_tn(n, dlow.astype(BF))
    back, d_ag = norm_back(dn, x, r1, w["ag"])
    dx = dhid + back
    small = (d_ag, d_rd, d_ru, d_rb, d_gg, d_mg)
    gD = grid.relative(gD, 0)
    gAO = jnp.concatenate([gA, grid.relative(gO, 0)], 1)
    return dx, gD, gF, gAO, small


def halves(v, s):
    h = v.shape[1] // 2
    first = s == 0
    return jnp.where(first, v[:, :h], v[:, h:]), jnp.where(first, v[:, h:], v[:, :h])


def in_rows(w, s):
    h = w.shape[0] // 2
    keep = lax.dynamic_slice_in_dim(w, s * h, h, 0)
    got = over_core(lax.dynamic_slice_in_dim(w, (1 - s) * h, h, 0))
    return jnp.where(s == 0, jnp.concatenate([keep, got], 1), jnp.concatenate([got, keep], 1))


def back_rows(w, s):
    keep, give = halves(w, s)
    got = over_core(give)
    return jnp.where(s == 0, jnp.concatenate([keep, got], 0), jnp.concatenate([got, keep], 0))


def body(
    inputs,
    lengths,
    out_grad,
    attn_gain,
    q_weight,
    k_weight,
    v_weight,
    rank_down,
    rank_up,
    rank_bias,
    gate_weight,
    group_gain,
    out_weight,
    mlp_gain,
    ffn_gate,
    ffn_up,
    ffn_down,
):
    size = lax.axis_size("dp")
    grid = Grid(size)
    s = lax.axis_index("section")
    first = s == 0
    shape = inputs.shape
    rows = shape[0] * shape[1]
    length, width = shape[2], shape[3]
    tokens = rows * length
    R = q_weight.shape[1]

    wide = [q_weight[0], k_weight[0], v_weight[0], gate_weight[0], ffn_gate[0], ffn_up[0], out_weight[0]]
    both = [halves(v, s) for v in wide]
    keep = jnp.concatenate([p[0] for p in both], 1)
    give = jnp.concatenate([p[1] for p in both], 1)
    smalls = [attn_gain[0], rank_down[0], rank_up[0], rank_bias[0], group_gain[0], mlp_gain[0]]
    sizes = [v.size for v in smalls]
    small = jnp.concatenate([v.reshape(-1) for v in smalls])
    small = jnp.pad(small, (0, R * 64 - small.size)).reshape(R // 2, 128)
    keep_d, give_d = halves(ffn_down[0], s)
    got, got_d, got_small = over_core(give), over_core(give_d), over_core(small)
    shard0, shard1 = jnp.where(first, keep, got), jnp.where(first, got, keep)
    down0, down1 = jnp.where(first, keep_d, got_d), jnp.where(first, got_d, keep_d)
    both_small = jnp.where(
        first, jnp.concatenate([small, got_small], 0), jnp.concatenate([got_small, small], 0)
    )
    shard0 = jnp.concatenate([shard0, both_small], 1)

    K, V, F = q_weight.shape[2] // 2, v_weight.shape[2] // 2, ffn_gate.shape[2] // 2
    A = 2 * K + 2 * V
    wide0, col0 = grid.gather_z_first(shard0), grid.gather_z_last(down0)
    wide1, col1 = grid.gather_z_first(shard1), grid.gather_z_last(down1)

    table = wide0[:, A + 2 * F + width // 2 :].reshape(size, 2, R * 64)

    def unpack(layer):
        t = table[:, layer].astype(F32)
        parts = []
        at = 0
        for n in sizes:
            parts.append(t[:, at : at + n])
            at += n
        ag, rd, ru, rb, gg, mg = parts
        ru = jnp.moveaxis(ru.reshape(size, rank_up.shape[1], -1), 0, 1).reshape(rank_up.shape[1], -1)
        return dict(
            ag=ag.reshape(1, -1),
            rd=rd.reshape(width, -1).astype(BF),
            ru=lax.dynamic_slice_in_dim(ru, s * K, K, 1),
            rb=lax.dynamic_slice_in_dim(rb.reshape(1, -1), s * K, K, 1),
            gg=gg.reshape(-1),
            mg=mg.reshape(1, -1),
        )

    def weights(w, col, layer):
        return dict(
            unpack(layer),
            WA=w[:, :A],
            WF=w[:, A : A + 2 * F],
            WO=in_rows(w[:, A + 2 * F : A + 2 * F + width // 2], s),
            WD=in_rows(col, s),
        )

    w0, w1 = weights(wide0, col0, 0), weights(wide1, col1, 1)

    spots = jnp.arange(length)
    mask = (spots[None, :] < lengths.reshape(rows, 1)).astype(F32).reshape(tokens, 1)
    x0 = inputs.reshape(tokens, width).astype(F32)
    y0, saved0 = layer_forward(x0, w0, mask, rows)
    x1 = y0.astype(BF)
    y1, saved1 = layer_forward(x1.astype(F32), w1, mask, rows)
    layer_out = jnp.where(first, x1, y1.astype(BF)).reshape((1,) + shape)

    low_mask = mask.astype(BF)
    dx1, gD1, gF1, gAO1, small1 = layer_backward(
        out_grad.reshape(tokens, width) * low_mask, w1, saved1, grid
    )
    rD1 = grid.reduce_z_first(gD1)
    rF1 = grid.reduce_z_last(gF1)
    rAO1 = grid.reduce_z_last(gAO1)
    dx0, gD0, gF0, gAO0, small0 = layer_backward(dx1.astype(BF) * low_mask, w0, saved0, grid)
    input_out = jnp.where(first, dx0, dx1).reshape((1,) + shape)
    rD0 = grid.reduce_z_first(gD0)
    rF0 = grid.reduce_z_last(gF0)

    def flat(pair):
        return jnp.concatenate([pair[2].reshape(-1), pair[3], pair[4]])

    mine = [jnp.where(first, a, b) for a, b in zip(small0, small1)]
    other = over_core(jnp.where(first, flat(small1), flat(small0)))
    n_ru = mine[2].size
    other_ru, other_rb, other_gg = (
        other[:n_ru].reshape(mine[2].shape),
        other[n_ru : n_ru + K],
        other[n_ru + K :],
    )
    full_ru = jnp.where(
        first, jnp.concatenate([mine[2], other_ru], 1), jnp.concatenate([other_ru, mine[2]], 1)
    )
    full_rb = jnp.where(first, jnp.concatenate([mine[3], other_rb]), jnp.concatenate([other_rb, mine[3]]))
    full_gg = mine[4] + other_gg
    pieces = [
        mine[0].reshape(size, -1),
        mine[1].reshape(size, -1),
        jnp.moveaxis(full_ru.reshape(full_ru.shape[0], size, -1), 1, 0).reshape(size, -1),
        full_rb.reshape(size, -1),
        full_gg.reshape(size, -1),
        mine[5].reshape(size, -1),
    ]
    packed = jnp.concatenate(pieces, 1).astype(BF)
    packed = jnp.pad(packed, ((0, 0), (0, R * 128 - packed.shape[1]))).reshape(size * R, 128)
    rAO0 = grid.reduce_z_last(jnp.concatenate([gAO0, grid.relative(packed, 0)], 1))
    small_out = rAO0[:, A + width // 2 :].reshape(-1)
    rAO0 = rAO0[:, : A + width // 2]

    def join(a, b):
        got = over_core(jnp.where(first, b, a))
        keep = jnp.where(first, a, b)
        return jnp.where(first, keep, got), jnp.where(first, got, keep)

    AOs = join(rAO0, rAO1)
    Fs = join(rF0, rF1)
    Ds = join(rD0, rD1)

    def cols(pair, lo, hi):
        return jnp.concatenate([p[:, lo:hi] for p in pair], 1).astype(F32)[None]

    out_small = []
    at = 0
    for v in smalls:
        out_small.append(small_out[at : at + v.size].reshape(v.shape).astype(F32)[None])
        at += v.size
    return (
        layer_out,
        input_out,
        out_small[0],
        cols(AOs, 0, K),
        cols(AOs, K, 2 * K),
        cols(AOs, 2 * K, 2 * K + V),
        out_small[1],
        out_small[2],
        out_small[3],
        cols(AOs, 2 * K + V, A),
        out_small[4],
        cols(AOs, A, A + width // 2),
        out_small[5],
        cols(Fs, 0, F),
        cols(Fs, F, 2 * F),
        cols(Ds, 0, width // 2),
    )


def solution(mesh):
    rows3 = P("section", "dp", None)
    one = P("section", "dp")
    return jax.shard_map(
        body,
        mesh=mesh,
        in_specs=(
            P(None, "dp", None, None),
            P(None, "dp"),
            P(None, "dp", None, None),
            one,
            rows3,
            rows3,
            rows3,
            rows3,
            P("section", None, "dp"),
            one,
            rows3,
            one,
            rows3,
            one,
            rows3,
            rows3,
            rows3,
        ),
        out_specs=(
            P("section", None, "dp", None, None),
            P("section", None, "dp", None, None),
            one,
            rows3,
            rows3,
            rows3,
            rows3,
            P("section", None, "dp"),
            one,
            rows3,
            one,
            rows3,
            one,
            rows3,
            rows3,
            rows3,
        ),
        check_vma=False,
    )
```

time: 2430 us -> 859 us (0.35)
  waiting for transfers between devices: 1410 us -> 269 us
  matrix products: 466 us -> 105 us
  blocking collectives: 166 us -> 0 us
  starting transfers between devices: 23.3 us -> 174 us
  local copies, waits for them, and re-layouts: 196 us -> 154 us
    reduce_scatter x8 -> x0, waiting for transfers between devices: 1010 us -> none  [the longest x1 248 us: reduce_end(): lax.psum_scatter(totals[13], 'dp', scatter_dimension=0, tiled=True)]
    all_gather x8 -> x0, waiting for transfers between devices: 393 us -> none  [the longest x1 86.5 us: fetch_forward(): lax.all_gather(local[12], 'dp', axis=0, tiled=True)]
    dot_general x180 -> x60, matrix products: 466 us -> 105 us  [the longest x10 37.2 us: mm(): lax.dot_general(a, b, (((1,), (0,)), ((), ())), preferred_element_type=F32)]
    ppermute x4 -> x167, waiting for transfers between devices: 0.01 us -> 269 us  [the longest x56 97.3 us: __init__(): self.py = lambda v: lax.ppermute(v, 'dp', pairs(0, 1, 0))]
    ppermute x4 -> x167, starting transfers between devices: 21.4 us -> 174 us  [the longest x25 74.4 us: over_core(): return lax.ppermute(v, 'section', [(0, 1), (1, 0)])]
    unnamed x2 -> x0, blocking collectives: 99.7 us -> none
    all_gather x2 -> x0, blocking collectives: 66 us -> none  [the longest x1 33.3 us: fetch_forward(): lax.all_gather(local[5], 'dp', axis=1, tiled=True)]
    concatenate x0 -> x41, other arithmetic: none -> 28.1 us  [the longest x1 8.13 us: layer_backward(): gAO = jnp.concatenate([gA, grid.relative(gO, 0)], 1)]
  transfers between devices with their start and end apart: 22 -> 167, of which waited for: 12 -> 58; matrix products, arithmetic and copies ran while one was open for 14% -> 42% of each run, Pallas kernels for 0% -> 0%
where the time goes in v1:
time: 859 us; the launch traced here: 849 us
  waiting for transfers between devices  269 us (31%)
  starting transfers between devices  174 us (20%)
  local copies, waits for them, and re-layouts  154 us (18%)
  other arithmetic  140 us (16%)
  matrix products  105 us (12%)
    ppermute x56, waiting for transfers between devices, __init__(): self.py = lambda v: lax.ppermute(v, 'dp', pairs(0, 1, 0))  97.3 us
    ppermute x56, waiting for transfers between devices, __init__(): self.px = lambda v: lax.ppermute(v, 'dp', pairs(0, 0, 1))  87.8 us
    ppermute x30, waiting for transfers between devices, __init__(): self.pz = lambda v: lax.ppermute(v, 'dp', pairs(1, 0, 0))  81.9 us
    ppermute x25, starting transfers between devices, over_core(): return lax.ppermute(v, 'section', [(0, 1), (1, 0)])  74.4 us
    ppermute x56, starting transfers between devices, __init__(): self.px = lambda v: lax.ppermute(v, 'dp', pairs(0, 0, 1))  46.9 us
    dot_general x10, matrix products, mm(): lax.dot_general(a, b, (((1,), (0,)), ((), ())), preferred_element_type=F32)  37.2 us
    ppermute x56, starting transfers between devices, __init__(): self.py = lambda v: lax.ppermute(v, 'dp', pairs(0, 1, 0))  37 us
    dot_general x10, matrix products, mm_nt(): lax.dot_general(a, b, (((1,), (1,)), ((), ())), preferred_element_type=F32)  34.9 us
  transfers between devices with their start and end apart: 167, of which 58 were waited for; matrix products, arithmetic and copies ran while one was open for 42% of the time, Pallas kernels for 0%

profile of v1, /device:TPU:1, one launch (start us, length us, event | category | flops | bytes accessed | tf_op | source)
XLA Modules:
  0.0 848.7 jit_solution(13663376195456136265)
XLA Ops:
  37.9 4.7 broadcast_in_dim.271
  52.5 12.0 %collective-permute-done.58 = bf16[2,2,176,512]{3,2,1,0:T(8,128)(2,1)} collective-permute-done((bf16[2,2,176,512]{3,2,1,0:T(8,128)(2,1)}, bf16[2,2,176,512]{3,2,1,0:T(8,128)(2,1)}, u32[]{:S(2)}, u32[]{:S(2)}) %collective-permute-start.58) | collective-permute-done | bytes 720928 | tf_op jit(solution)/shard_map/ppermute | solution.py:27
  75.1 7.2 collective-permute-done.35
  88.0 6.2 collective-permute-done.5
  95.6 11.5 %collective-permute-done.38 = bf16[64,4864]{1,0:T(8,128)(2,1)S(1)} collective-permute-done((bf16[64,4864]{1,0:T(8,128)(2,1)}, bf16[64,4864]{1,0:T(8,128)(2,1)S(1)}, u32[]{:S(2)}, u32[]{:S(2)}) %collective-permute-start.38) | collective-permute-done | bytes 622624 | tf_op jit(solution)/shard_map/ppermute | solution.py:25
  110.3 13.1 %collective-permute-done.7 = bf16[64,4992]{1,0:T(8,128)(2,1)S(1)} collective-permute-done((bf16[64,4992]{1,0:T(8,128)(2,1)S(1)}, bf16[64,4992]{1,0:T(8,128)(2,1)S(1)}, u32[]{:S(2)}, u32[]{:S(2)}) %collective-permute-start.7) | collective-permute-done | bytes 639008 | tf_op jit(solution)/shard_map/ppermute | solution.py:25
  123.9 11.7 %collective-permute-done.42 = bf16[64,4864]{1,0:T(8,128)(2,1)S(1)} collective-permute-done((bf16[64,4864]{1,0:T(8,128)(2,1)}, bf16[64,4864]{1,0:T(8,128)(2,1)S(1)}, u32[]{:S(2)}, u32[]{:S(2)}) %collective-permute-start.42) | collective-permute-done | bytes 622624 | tf_op jit(solution)/shard_map/ppermute | solution.py:27
  137.8 3.9 collective-permute-done.41
  144.0 14.0 %collective-permute-done.10 = bf16[64,2432]{1,0:T(8,128)(2,1)S(1)} collective-permute-done((bf16[64,2432]{1,0:T(8,128)(2,1)S(1)}, bf16[64,2432]{1,0:T(8,128)(2,1)S(1)}, u32[]{:S(2)}, u32[]{:S(2)}) %collective-permute-start.10) | collective-permute-done | bytes 311328 | tf_op jit(solution)/shard_map/ppermute | solution.py:25
  162.1 5.0 collective-permute-done.44
  168.8 3.0 collective-permute-done.12
  172.8 10.5 %collective-permute-done.13 = bf16[64,4992]{1,0:T(8,128)(2,1)S(1)} collective-permute-done((bf16[64,4992]{1,0:T(8,128)(2,1)S(1)}, bf16[64,4992]{1,0:T(8,128)(2,1)S(1)}, u32[]{:S(2)}, u32[]{:S(2)}) %collective-permute-start.13) | collective-permute-done | bytes 639008 | tf_op jit(solution)/shard_map/ppermute | solution.py:26
  187.1 4.9 collective-permute-done.45
  195.1 17.3 %collective-permute-done.16 = bf16[64,4992]{1,0:T(8,128)(2,1)S(1)} collective-permute-done((bf16[64,4992]{1,0:T(8,128)(2,1)S(1)}, bf16[64,4992]{1,0:T(8,128)(2,1)S(1)}, u32[]{:S(2)}, u32[]{:S(2)}) %collective-permute-start.16) | collective-permute-done | bytes 639008 | tf_op jit(solution)/shard_map/ppermute | solution.py:27
  214.1 10.3 %collective-permute-start.31 = (bf16[1408,512]{1,0:T(8,128)(2,1)}, bf16[1408,512]{1,0:T(8,128)(2,1)}, u32[]{:S(2)}, u32[]{:S(2)}) collective-permute-start(bf16[1408,512]{1,0:T(8,128)(2,1)} %get-tuple-element.175), channel_id=1, source_target_pairs={{0,16},{16,0},{1,17},{17,1},{2,18},{18,2},{3,19},{19,3},{4,20},{20... | collective-permute-start | bytes 4325384 | tf_op jit(solution)/shard_map/ppermute | solution.py:125
  228.5 3.9 collective-permute-done.18
  232.7 5.9 collective-permute-done.20
  238.5 7.5 collective-permute-done.19
  246.2 3.9 copy-done.19
  254.0 5.8 fusion.388
  278.7 10.6 %collective-permute-start.21 = (bf16[512,512]{1,0:T(8,128)(2,1)S(1)}, bf16[512,512]{1,0:T(8,128)(2,1)S(1)}, u32[]{:S(2)}, u32[]{:S(2)}) collective-permute-start(bf16[512,512]{1,0:T(8,128)(2,1)S(1)} %get-tuple-element.272), channel_id=1, source_target_pairs={{0,16},{16,0},{1,17},{17,1},{2,18},{18,2},{3,19},{19,3},{4,20},{20... | collective-permute-start | bytes 1572872 | tf_op jit(solution)/shard_map/ppermute | solution.py:125
  300.5 6.2 fusion.6
  309.1 4.1 convolution_convert_fusion.11
  323.9 5.7 fusion.389
  354.4 3.2 convolution_convert_fusion.14
  368.5 5.9 fusion.2
  374.5 4.9 fusion.9
  379.4 6.0 fusion.75
  389.5 3.7 convolution_convert_fusion
  396.5 4.8 convolution_convert_fusion.10
  404.0 3.0 collective-permute-done.142
  408.4 3.2 collective-permute-done.130
  415.5 13.3 %collective-permute-done.131 = bf16[1,64,2816]{2,1,0:T(8,128)(2,1)S(1)} collective-permute-done((bf16[1,64,2816]{2,1,0:T(8,128)(2,1)S(1)}, bf16[1,64,2816]{2,1,0:T(8,128)(2,1)S(1)}, u32[]{:S(2)}, u32[]{:S(2)}) %collective-permute-start.131) | collective-permute-done | bytes 360480 | tf_op jit(solution)/shard_map/ppermute | solution.py:26
  431.7 4.2 collective-permute-done.138
  443.9 2.9 fusion.101
  467.5 3.8 collective-permute-start.69
  473.5 3.8 add_convert_fusion.4
  488.1 8.1 maximum_maximum_fusion.1
  498.4 3.3 collective-permute-done.101
  503.1 2.9 collective-permute-done.96
  531.2 4.7 fusion.12
  536.0 3.7 convolution_convert_fusion.1
  545.3 5.1 fusion.72
  553.5 4.1 collective-permute-done.95
  570.7 13.5 %collective-permute-start.65 = (bf16[512,1024]{1,0:T(8,128)(2,1)S(1)}, bf16[512,1024]{1,0:T(8,128)(2,1)S(1)}, u32[]{:S(2)}, u32[]{:S(2)}) collective-permute-start(bf16[512,1024]{1,0:T(8,128)(2,1)S(1)} %fusion.72), channel_id=1, source_target_pairs={{0,16},{16,0},{1,17},{17,1},{2,18},{18,2},{3,19},{19,3},{4,20},{20... | collective-permute-start | bytes 3145736 | tf_op jit(solution)/shard_map/ppermute | solution.py:125
  587.8 5.2 collective-permute-done.112
  597.3 18.2 %collective-permute-done.100 = bf16[64,2048]{1,0:T(8,128)(2,1)S(1)} collective-permute-done((bf16[64,2048]{1,0:T(8,128)(2,1)S(1)}, bf16[64,2048]{1,0:T(8,128)(2,1)S(1)}, u32[]{:S(2)}, u32[]{:S(2)}) %collective-permute-start.100) | collective-permute-done | bytes 262176 | tf_op jit(solution)/shard_map/ppermute | solution.py:27
  621.0 3.2 collective-permute-start.150
  630.5 3.0 reshape.1350
  650.6 8.3 collective-permute-start.68
  663.6 4.8 add_convert_fusion.1
  668.4 3.6 convolution_convert_fusion.5
  701.6 7.2 collective-permute-done.127
  713.0 8.5 %collective-permute-done.161 = bf16[2,2,176,512]{3,2,1,0:T(8,128)(2,1)S(1)} collective-permute-done((bf16[2,2,176,512]{3,2,1,0:T(8,128)(2,1)S(1)}, bf16[2,2,176,512]{3,2,1,0:T(8,128)(2,1)S(1)}, u32[]{:S(2)}, u32[]{:S(2)}) %collective-permute-start.161) | collective-permute-done | bytes 720928 | tf_op jit(solution)/shard_map/ppermute | solution.py:27
  721.6 4.3 collective-permute-start.149
  735.6 8.0 maximum_maximum_fusion
  747.9 3.4 fusion.33
  756.5 4.2 collective-permute-done.78
  760.7 3.7 collective-permute-done.73
  770.8 8.1 collective-permute-done.74
  781.3 3.3 collective-permute-done.77
  801.6 2.9 collective-permute-done.85
  810.1 11.1 %collective-permute-start.110 = (bf16[64,2048]{1,0:T(8,128)(2,1)}, bf16[64,2048]{1,0:T(8,128)(2,1)}, u32[]{:S(2)}, u32[]{:S(2)}) collective-permute-start(bf16[64,2048]{1,0:T(8,128)(2,1)} %get-tuple-element.112), channel_id=1, source_target_pairs={{0,16},{16,0},{1,17},{17,1},{2,18},{18,2},{3,19},{19,3},{4,20},{20... | collective-permute-start | bytes 786440 | tf_op jit(solution)/shard_map/ppermute | solution.py:125
  839.4 3.4 collective-permute-done.155
  (1281 shorter events, 430.8 us)
Async XLA Ops:
  20.8 17.1 %collective-permute-start = (bf16[64,4864]{1,0:T(8,128)(2,1)}, bf16[64,4864]{1,0:T(8,128)(2,1)S(1)}, u32[]{:S(2)}, u32[]{:S(2)}) collective-permute-start(bf16[64,4864]{1,0:T(8,128)(2,1)} %copy-done.219), channel_id=1, source_target_pairs={{0,16},{16,0},{1,17},{17,1},{2,18},{18,2},{3,19},{19,3},{4,20},{20... | collective-permute-start | bytes 1867784 | tf_op jit(solution)/shard_map/ppermute | solution.py:125
  31.7 18.9 %collective-permute-start.28 = (bf16[2,2,176,512]{3,2,1,0:T(8,128)(2,1)}, bf16[2,2,176,512]{3,2,1,0:T(8,128)(2,1)}, u32[]{:S(2)}, u32[]{:S(2)}) collective-permute-start(bf16[2,2,176,512]{3,2,1,0:T(8,128)(2,1)} %fusion.304), channel_id=1, source_target_pairs={{0,4},{1,5},{2,6},{3,7},{4,8},{5,9},{6,10},{7,11},{8,12},{9,13},{1... | collective-permute-start | bytes 2162696 | tf_op jit(solution)/shard_map/ppermute | solution.py:27
  33.7 30.8 %collective-permute-start.58 = (bf16[2,2,176,512]{3,2,1,0:T(8,128)(2,1)}, bf16[2,2,176,512]{3,2,1,0:T(8,128)(2,1)}, u32[]{:S(2)}, u32[]{:S(2)}) collective-permute-start(bf16[2,2,176,512]{3,2,1,0:T(8,128)(2,1)} %fusion.305), channel_id=1, source_target_pairs={{0,4},{1,5},{2,6},{3,7},{4,8},{5,9},{6,10},{7,11},{8,12},{9,13},{1... | collective-permute-start | bytes 2162696 | tf_op jit(solution)/shard_map/ppermute | solution.py:27
  43.8 22.3 %collective-permute-start.33 = (bf16[64,4864]{1,0:T(8,128)(2,1)}, bf16[64,4864]{1,0:T(8,128)(2,1)}, u32[]{:S(2)}, u32[]{:S(2)}) collective-permute-start(bf16[64,4864]{1,0:T(8,128)(2,1)} %get-tuple-element.130), channel_id=1, source_target_pairs={{0,1},{1,0},{2,3},{3,2},{4,5},{5,4},{6,7},{7,6},{8,9},{9,8},{10,11... | collective-permute-start | bytes 1867784 | tf_op jit(solution)/shard_map/ppermute | solution.py:25
  44.3 25.1 %collective-permute-start.34 = (bf16[64,4864]{1,0:T(8,128)(2,1)}, bf16[64,4864]{1,0:T(8,128)(2,1)}, u32[]{:S(2)}, u32[]{:S(2)}) collective-permute-start(bf16[64,4864]{1,0:T(8,128)(2,1)} %get-tuple-element.130), channel_id=1, source_target_pairs={{0,2},{1,3},{2,0},{3,1},{4,6},{5,7},{6,4},{7,5},{8,10},{9,11},{10,... | collective-permute-start | bytes 1867784 | tf_op jit(solution)/shard_map/ppermute | solution.py:26
  44.9 40.0 %collective-permute-start.37 = (bf16[64,4864]{1,0:T(8,128)(2,1)}, bf16[64,4864]{1,0:T(8,128)(2,1)}, u32[]{:S(2)}, u32[]{:S(2)}) collective-permute-start(bf16[64,4864]{1,0:T(8,128)(2,1)} %get-tuple-element.130), channel_id=1, source_target_pairs={{0,4},{1,5},{2,6},{3,7},{4,8},{5,9},{6,10},{7,11},{8,12},{9,13},{1... | collective-permute-start | bytes 1867784 | tf_op jit(solution)/shard_map/ppermute | solution.py:27
  50.6 22.2 %collective-permute-start.2 = (bf16[64,4992]{1,0:T(8,128)(2,1)}, bf16[64,4992]{1,0:T(8,128)(2,1)S(1)}, u32[]{:S(2)}, u32[]{:S(2)}) collective-permute-start(bf16[64,4992]{1,0:T(8,128)(2,1)} %pad_maximum_fusion.12), channel_id=1, source_target_pairs={{0,1},{1,0},{2,3},{3,2},{4,5},{5,4},{6,7},{7,6},{8,9},{9,8},{10,11... | collective-permute-start | bytes 1916936 | tf_op jit(solution)/shard_map/ppermute | solution.py:25
  66.1 29.2 %collective-permute-start.6 = (bf16[64,4992]{1,0:T(8,128)(2,1)S(1)}, bf16[64,4992]{1,0:T(8,128)(2,1)S(1)}, u32[]{:S(2)}, u32[]{:S(2)}) collective-permute-start(bf16[64,4992]{1,0:T(8,128)(2,1)S(1)} %copy-done.113), channel_id=1, source_target_pairs={{0,4},{1,5},{2,6},{3,7},{4,8},{5,9},{6,10},{7,11},{8,12},{9,13},{1... | collective-permute-start | bytes 1916936 | tf_op jit(solution)/shard_map/ppermute | solution.py:27
  69.4 40.6 %collective-permute-start.29 = (bf16[2,2,176,512]{3,2,1,0:T(8,128)(2,1)}, bf16[2,2,176,512]{3,2,1,0:T(8,128)(2,1)S(1)}, u32[]{:S(2)}, u32[]{:S(2)}) collective-permute-start(bf16[2,2,176,512]{3,2,1,0:T(8,128)(2,1)} %collective-permute-done.28), channel_id=1, source_target_pairs={{0,4},{1,5},{2,6},{3,7},{4,8},{5,9},{6,10},{7,11},{8,12},{9,13},{1... | collective-permute-start | bytes 2162696 | tf_op jit(solution)/shard_map/ppermute | solution.py:27
  82.3 76.6 %collective-permute-start.59 = (bf16[2,2,176,512]{3,2,1,0:T(8,128)(2,1)}, bf16[2,2,176,512]{3,2,1,0:T(8,128)(2,1)}, u32[]{:S(2)}, u32[]{:S(2)}) collective-permute-start(bf16[2,2,176,512]{3,2,1,0:T(8,128)(2,1)} %collective-permute-done.58), channel_id=1, source_target_pairs={{0,4},{1,5},{2,6},{3,7},{4,8},{5,9},{6,10},{7,11},{8,12},{9,13},{1... | collective-permute-start | bytes 2162696 | tf_op jit(solution)/shard_map/ppermute | solution.py:27
  95.3 40.3 %collective-permute-start.42 = (bf16[64,4864]{1,0:T(8,128)(2,1)}, bf16[64,4864]{1,0:T(8,128)(2,1)S(1)}, u32[]{:S(2)}, u32[]{:S(2)}) collective-permute-start(bf16[64,4864]{1,0:T(8,128)(2,1)} %collective-permute-done.37), channel_id=1, source_target_pairs={{0,4},{1,5},{2,6},{3,7},{4,8},{5,9},{6,10},{7,11},{8,12},{9,13},{1... | collective-permute-start | bytes 1867784 | tf_op jit(solution)/shard_map/ppermute | solution.py:27
  108.8 27.4 %collective-permute-start.8 = (bf16[64,4992]{1,0:T(8,128)(2,1)S(1)}, bf16[64,4992]{1,0:T(8,128)(2,1)S(1)}, u32[]{:S(2)}, u32[]{:S(2)}) collective-permute-start(bf16[64,4992]{1,0:T(8,128)(2,1)S(1)} %collective-permute-done.6), channel_id=1, source_target_pairs={{0,2},{1,3},{2,0},{3,1},{4,6},{5,7},{6,4},{7,5},{8,10},{9,11},{10,... | collective-permute-start | bytes 1916936 | tf_op jit(solution)/shard_map/ppermute | solution.py:26
  110.0 49.6 %collective-permute-start.11 = (bf16[64,4992]{1,0:T(8,128)(2,1)S(1)}, bf16[64,4992]{1,0:T(8,128)(2,1)S(1)}, u32[]{:S(2)}, u32[]{:S(2)}) collective-permute-start(bf16[64,4992]{1,0:T(8,128)(2,1)S(1)} %collective-permute-done.6), channel_id=1, source_target_pairs={{0,4},{1,5},{2,6},{3,7},{4,8},{5,9},{6,10},{7,11},{8,12},{9,13},{1... | collective-permute-start | bytes 1916936 | tf_op jit(solution)/shard_map/ppermute | solution.py:27
  136.3 24.6 %collective-permute-start.43 = (bf16[64,4864]{1,0:T(8,128)(2,1)S(1)}, bf16[64,4864]{1,0:T(8,128)(2,1)S(1)}, u32[]{:S(2)}, u32[]{:S(2)}) collective-permute-start(bf16[64,4864]{1,0:T(8,128)(2,1)S(1)} %collective-permute-done.42), channel_id=1, source_target_pairs={{0,1},{1,0},{2,3},{3,2},{4,5},{5,4},{6,7},{7,6},{8,9},{9,8},{10,11... | collective-permute-start | bytes 1867784 | tf_op jit(solution)/shard_map/ppermute | solution.py:25
  137.2 21.6 %collective-permute-start.9 = (bf16[64,2560]{1,0:T(8,128)(2,1)S(1)}, bf16[64,2560]{1,0:T(8,128)(2,1)S(1)}, u32[]{:S(2)}, u32[]{:S(2)}) collective-permute-start(bf16[64,2560]{1,0:T(8,128)(2,1)S(1)} %slice.1123), channel_id=1, source_target_pairs={{0,2},{1,3},{2,0},{3,1},{4,6},{5,7},{6,4},{7,5},{8,10},{9,11},{10,... | collective-permute-start | bytes 983048 | tf_op jit(solution)/shard_map/ppermute | solution.py:26
  141.7 16.4 %collective-permute-start.10 = (bf16[64,2432]{1,0:T(8,128)(2,1)S(1)}, bf16[64,2432]{1,0:T(8,128)(2,1)S(1)}, u32[]{:S(2)}, u32[]{:S(2)}) collective-permute-start(bf16[64,2432]{1,0:T(8,128)(2,1)S(1)} %slice.1124), channel_id=1, source_target_pairs={{0,1},{1,0},{2,3},{3,2},{4,5},{5,4},{6,7},{7,6},{8,9},{9,8},{10,11... | collective-permute-start | bytes 933896 | tf_op jit(solution)/shard_map/ppermute | solution.py:25
  158.8 24.9 %collective-permute-start.47 = (bf16[64,4864]{1,0:T(8,128)(2,1)S(1)}, bf16[64,4864]{1,0:T(8,128)(2,1)S(1)}, u32[]{:S(2)}, u32[]{:S(2)}) collective-permute-start(bf16[64,4864]{1,0:T(8,128)(2,1)S(1)} %collective-permute-done.42), channel_id=1, source_target_pairs={{0,4},{1,5},{2,6},{3,7},{4,8},{5,9},{6,10},{7,11},{8,12},{9,13},{1... | collective-permute-start | bytes 1867784 | tf_op jit(solution)/shard_map/ppermute | solution.py:27
  158.9 25.6 %collective-permute-start.30 = (bf16[2,2,176,512]{3,2,1,0:T(8,128)(2,1)S(1)}, bf16[2,2,176,512]{3,2,1,0:T(8,128)(2,1)S(1)}, u32[]{:S(2)}, u32[]{:S(2)}) collective-permute-start(bf16[2,2,176,512]{3,2,1,0:T(8,128)(2,1)S(1)} %collective-permute-done.29), channel_id=1, source_target_pairs={{0,4},{1,5},{2,6},{3,7},{4,8},{5,9},{6,10},{7,11},{8,12},{9,13},{1... | collective-permute-start | bytes 2162696 | tf_op jit(solution)/shard_map/ppermute | solution.py:27
  159.5 199.5 %collective-permute-start.60 = (bf16[2,2,176,512]{3,2,1,0:T(8,128)(2,1)}, bf16[2,2,176,512]{3,2,1,0:T(8,128)(2,1)}, u32[]{:S(2)}, u32[]{:S(2)}) collective-permute-start(bf16[2,2,176,512]{3,2,1,0:T(8,128)(2,1)} %collective-permute-done.59), channel_id=1, source_target_pairs={{0,4},{1,5},{2,6},{3,7},{4,8},{5,9},{6,10},{7,11},{8,12},{9,13},{1... | collective-permute-start | bytes 2162696 | tf_op jit(solution)/shard_map/ppermute | solution.py:27
  171.8 40.6 %collective-permute-start.16 = (bf16[64,4992]{1,0:T(8,128)(2,1)S(1)}, bf16[64,4992]{1,0:T(8,128)(2,1)S(1)}, u32[]{:S(2)}, u32[]{:S(2)}) collective-permute-start(bf16[64,4992]{1,0:T(8,128)(2,1)S(1)} %collective-permute-done.11), channel_id=1, source_target_pairs={{0,4},{1,5},{2,6},{3,7},{4,8},{5,9},{6,10},{7,11},{8,12},{9,13},{1... | collective-permute-start | bytes 1916936 | tf_op jit(solution)/shard_map/ppermute | solution.py:27
  184.6 29.6 %collective-permute-start.48 = (bf16[64,4864]{1,0:T(8,128)(2,1)S(1)}, bf16[64,4864]{1,0:T(8,128)(2,1)S(1)}, u32[]{:S(2)}, u32[]{:S(2)}) collective-permute-start(bf16[64,4864]{1,0:T(8,128)(2,1)S(1)} %collective-permute-done.47), channel_id=1, source_target_pairs={{0,1},{1,0},{2,3},{3,2},{4,5},{5,4},{6,7},{7,6},{8,9},{9,8},{10,11... | collective-permute-start | bytes 1867784 | tf_op jit(solution)/shard_map/ppermute | solution.py:25
  192.0 21.6 %collective-permute-start.14 = (bf16[64,2560]{1,0:T(8,128)(2,1)S(1)}, bf16[64,2560]{1,0:T(8,128)(2,1)S(1)}, u32[]{:S(2)}, u32[]{:S(2)}) collective-permute-start(bf16[64,2560]{1,0:T(8,128)(2,1)S(1)} %slice.1125), channel_id=1, source_target_pairs={{0,2},{1,3},{2,0},{3,1},{4,6},{5,7},{6,4},{7,5},{8,10},{9,11},{10,... | collective-permute-start | bytes 983048 | tf_op jit(solution)/shard_map/ppermute | solution.py:26
  192.8 19.8 %collective-permute-start.15 = (bf16[64,2432]{1,0:T(8,128)(2,1)S(1)}, bf16[64,2432]{1,0:T(8,128)(2,1)S(1)}, u32[]{:S(2)}, u32[]{:S(2)}) collective-permute-start(bf16[64,2432]{1,0:T(8,128)(2,1)S(1)} %slice.1126), channel_id=1, source_target_pairs={{0,1},{1,0},{2,3},{3,2},{4,5},{5,4},{6,7},{7,6},{8,9},{9,8},{10,11... | collective-permute-start | bytes 933896 | tf_op jit(solution)/shard_map/ppermute | solution.py:25
  213.6 18.8 %collective-permute-start.18 = (bf16[64,4992]{1,0:T(8,128)(2,1)S(1)}, bf16[64,4992]{1,0:T(8,128)(2,1)S(1)}, u32[]{:S(2)}, u32[]{:S(2)}) collective-permute-start(bf16[64,4992]{1,0:T(8,128)(2,1)S(1)} %collective-permute-done.16), channel_id=1, source_target_pairs={{0,2},{1,3},{2,0},{3,1},{4,6},{5,7},{6,4},{7,5},{8,10},{9,11},{10,... | collective-permute-start | bytes 1916936 | tf_op jit(solution)/shard_map/ppermute | solution.py:26
  214.1 95.0 %collective-permute-start.31 = (bf16[1408,512]{1,0:T(8,128)(2,1)}, bf16[1408,512]{1,0:T(8,128)(2,1)}, u32[]{:S(2)}, u32[]{:S(2)}) collective-permute-start(bf16[1408,512]{1,0:T(8,128)(2,1)} %get-tuple-element.175), channel_id=1, source_target_pairs={{0,16},{16,0},{1,17},{17,1},{2,18},{18,2},{3,19},{19,3},{4,20},{20... | collective-permute-start | bytes 4325384 | tf_op jit(solution)/shard_map/ppermute | solution.py:125
  225.2 88.3 %collective-permute-start.50 = (bf16[64,2432]{1,0:T(8,128)(2,1)}, bf16[64,2432]{1,0:T(8,128)(2,1)}, u32[]{:S(2)}, u32[]{:S(2)}) collective-permute-start(bf16[64,2432]{1,0:T(8,128)(2,1)} %slice.1165), channel_id=1, source_target_pairs={{0,2},{1,3},{2,0},{3,1},{4,6},{5,7},{6,4},{7,5},{8,10},{9,11},{10,... | collective-permute-start | bytes 933896 | tf_op jit(solution)/shard_map/ppermute | solution.py:26
  228.3 17.8 %collective-permute-start.19 = (bf16[64,2560]{1,0:T(8,128)(2,1)S(1)}, bf16[64,2560]{1,0:T(8,128)(2,1)S(1)}, u32[]{:S(2)}, u32[]{:S(2)}) collective-permute-start(bf16[64,2560]{1,0:T(8,128)(2,1)S(1)} %slice.1127), channel_id=1, source_target_pairs={{0,2},{1,3},{2,0},{3,1},{4,6},{5,7},{6,4},{7,5},{8,10},{9,11},{10,... | collective-permute-start | bytes 983048 | tf_op jit(solution)/shard_map/ppermute | solution.py:26
  238.5 75.0 %collective-permute-start.51 = (bf16[64,2432]{1,0:T(8,128)(2,1)}, bf16[64,2432]{1,0:T(8,128)(2,1)}, u32[]{:S(2)}, u32[]{:S(2)}) collective-permute-start(bf16[64,2432]{1,0:T(8,128)(2,1)} %slice.1166), channel_id=1, source_target_pairs={{0,1},{1,0},{2,3},{3,2},{4,5},{5,4},{6,7},{7,6},{8,9},{9,8},{10,11... | collective-permute-start | bytes 933896 | tf_op jit(solution)/shard_map/ppermute | solution.py:25
  318.0 36.4 %collective-permute-start.52 = (bf16[512,512]{1,0:T(8,128)(2,1)}, bf16[512,512]{1,0:T(8,128)(2,1)}, u32[]{:S(2)}, u32[]{:S(2)}) collective-permute-start(bf16[512,512]{1,0:T(8,128)(2,1)} %get-tuple-element.268), channel_id=1, source_target_pairs={{0,16},{16,0},{1,17},{17,1},{2,18},{18,2},{3,19},{19,3},{4,20},{20... | collective-permute-start | bytes 1572872 | tf_op jit(solution)/shard_map/ppermute | solution.py:125
  385.4 55.0 %collective-permute-start.63 = (bf16[512,1024]{1,0:T(8,128)(2,1)S(1)}, bf16[512,1024]{1,0:T(8,128)(2,1)S(1)}, u32[]{:S(2)}, u32[]{:S(2)}) collective-permute-start(bf16[512,1024]{1,0:T(8,128)(2,1)S(1)} %fusion.75), channel_id=1, source_target_pairs={{0,16},{16,0},{1,17},{17,1},{2,18},{18,2},{3,19},{19,3},{4,20},{20... | collective-permute-start | bytes 3145736 | tf_op jit(solution)/shard_map/ppermute | solution.py:125
  389.2 94.5 %collective-permute-start.158 = (bf16[1408,512]{1,0:T(8,128)(2,1)}, bf16[1408,512]{1,0:T(8,128)(2,1)}, u32[]{:S(2)}, u32[]{:S(2)}) collective-permute-start(bf16[1408,512]{1,0:T(8,128)(2,1)} %get-tuple-element.165), channel_id=1, source_target_pairs={{0,16},{16,0},{1,17},{17,1},{2,18},{18,2},{3,19},{19,3},{4,20},{20... | collective-permute-start | bytes 4325384 | tf_op jit(solution)/shard_map/ppermute | solution.py:125
  411.6 20.1 %collective-permute-start.136 = (bf16[1,64,2816]{2,1,0:T(8,128)(2,1)S(1)}, bf16[1,64,2816]{2,1,0:T(8,128)(2,1)S(1)}, u32[]{:S(2)}, u32[]{:S(2)}) collective-permute-start(bf16[1,64,2816]{2,1,0:T(8,128)(2,1)S(1)} %pad_maximum_fusion.23), channel_id=1, source_target_pairs={{0,2},{1,3},{2,0},{3,1},{4,6},{5,7},{6,4},{7,5},{8,10},{9,11},{10,... | collective-permute-start | bytes 1081352 | tf_op jit(solution)/shard_map/ppermute | solution.py:26
  431.7 49.3 %collective-permute-start.141 = (bf16[1,64,2816]{2,1,0:T(8,128)(2,1)}, bf16[1,64,2816]{2,1,0:T(8,128)(2,1)}, u32[]{:S(2)}, u32[]{:S(2)}) collective-permute-start(bf16[1,64,2816]{2,1,0:T(8,128)(2,1)} %pad_maximum_fusion.25), channel_id=1, source_target_pairs={{0,2},{1,3},{2,0},{3,1},{4,6},{5,7},{6,4},{7,5},{8,10},{9,11},{10,... | collective-permute-start | bytes 1081352 | tf_op jit(solution)/shard_map/ppermute | solution.py:26
  435.9 45.3 %collective-permute-start.143 = (bf16[1,64,2816]{2,1,0:T(8,128)(2,1)}, bf16[1,64,2816]{2,1,0:T(8,128)(2,1)}, u32[]{:S(2)}, u32[]{:S(2)}) collective-permute-start(bf16[1,64,2816]{2,1,0:T(8,128)(2,1)} %pad_maximum_fusion.26), channel_id=1, source_target_pairs={{0,1},{1,0},{2,3},{3,2},{4,5},{5,4},{6,7},{7,6},{8,9},{9,8},{10,11... | collective-permute-start | bytes 1081352 | tf_op jit(solution)/shard_map/ppermute | solution.py:25
  440.0 41.5 %collective-permute-start.139 = (bf16[64,2816]{1,0:T(8,128)(2,1)}, bf16[64,2816]{1,0:T(8,128)(2,1)}, u32[]{:S(2)}, u32[]{:S(2)}) collective-permute-start(bf16[64,2816]{1,0:T(8,128)(2,1)} %fusion.177), channel_id=1, source_target_pairs={{0,4},{1,5},{2,6},{3,7},{4,8},{5,9},{6,10},{7,11},{8,12},{9,13},{1... | collective-permute-start | bytes 1081352 | tf_op jit(solution)/shard_map/ppermute | solution.py:27
  480.4 43.7 %collective-permute-start.62 = (bf16[512,1024]{1,0:T(8,128)(2,1)S(1)}, bf16[512,1024]{1,0:T(8,128)(2,1)S(1)}, u32[]{:S(2)}, u32[]{:S(2)}) collective-permute-start(bf16[512,1024]{1,0:T(8,128)(2,1)S(1)} %copy-done.98), channel_id=1, source_target_pairs={{0,16},{16,0},{1,17},{17,1},{2,18},{18,2},{3,19},{19,3},{4,20},{20... | collective-permute-start | bytes 3145736 | tf_op jit(solution)/shard_map/ppermute | solution.py:125
  481.0 41.0 %collective-permute-start.64 = (bf16[512,1024]{1,0:T(8,128)(2,1)S(1)}, bf16[512,1024]{1,0:T(8,128)(2,1)S(1)}, u32[]{:S(2)}, u32[]{:S(2)}) collective-permute-start(bf16[512,1024]{1,0:T(8,128)(2,1)S(1)} %add_convert_fusion.4), channel_id=1, source_target_pairs={{0,16},{16,0},{1,17},{17,1},{2,18},{18,2},{3,19},{19,3},{4,20},{20... | collective-permute-start | bytes 3145736 | tf_op jit(solution)/shard_map/ppermute | solution.py:125
  487.5 62.9 %collective-permute-start.159 = (bf16[2,2,176,512]{3,2,1,0:T(8,128)(2,1)}, bf16[2,2,176,512]{3,2,1,0:T(8,128)(2,1)}, u32[]{:S(2)}, u32[]{:S(2)}) collective-permute-start(bf16[2,2,176,512]{3,2,1,0:T(8,128)(2,1)} %bitcast.254), channel_id=1, source_target_pairs={{0,4},{1,5},{2,6},{3,7},{4,8},{5,9},{6,10},{7,11},{8,12},{9,13},{1... | collective-permute-start | bytes 2162696 | tf_op jit(solution)/shard_map/ppermute | solution.py:27
  520.2 76.1 %collective-permute-start.102 = (bf16[1,64,2048]{2,1,0:T(8,128)(2,1)}, bf16[1,64,2048]{2,1,0:T(8,128)(2,1)}, u32[]{:S(2)}, u32[]{:S(2)}) collective-permute-start(bf16[1,64,2048]{2,1,0:T(8,128)(2,1)} %pad_maximum_fusion.41), channel_id=1, source_target_pairs={{0,2},{1,3},{2,0},{3,1},{4,6},{5,7},{6,4},{7,5},{8,10},{9,11},{10,... | collective-permute-start | bytes 786440 | tf_op jit(solution)/shard_map/ppermute | solution.py:26
  520.8 75.7 %collective-permute-start.104 = (bf16[1,64,2048]{2,1,0:T(8,128)(2,1)}, bf16[1,64,2048]{2,1,0:T(8,128)(2,1)}, u32[]{:S(2)}, u32[]{:S(2)}) collective-permute-start(bf16[1,64,2048]{2,1,0:T(8,128)(2,1)} %pad_maximum_fusion.42), channel_id=1, source_target_pairs={{0,1},{1,0},{2,3},{3,2},{4,5},{5,4},{6,7},{7,6},{8,9},{9,8},{10,11... | collective-permute-start | bytes 786440 | tf_op jit(solution)/shard_map/ppermute | solution.py:25
  522.1 29.7 %collective-permute-start.97 = (bf16[1,64,2048]{2,1,0:T(8,128)(2,1)}, bf16[1,64,2048]{2,1,0:T(8,128)(2,1)}, u32[]{:S(2)}, u32[]{:S(2)}) collective-permute-start(bf16[1,64,2048]{2,1,0:T(8,128)(2,1)} %pad_maximum_fusion.39), channel_id=1, source_target_pairs={{0,2},{1,3},{2,0},{3,1},{4,6},{5,7},{6,4},{7,5},{8,10},{9,11},{10,... | collective-permute-start | bytes 786440 | tf_op jit(solution)/shard_map/ppermute | solution.py:26
  524.1 28.5 %collective-permute-start.99 = (bf16[1,64,2048]{2,1,0:T(8,128)(2,1)}, bf16[1,64,2048]{2,1,0:T(8,128)(2,1)}, u32[]{:S(2)}, u32[]{:S(2)}) collective-permute-start(bf16[1,64,2048]{2,1,0:T(8,128)(2,1)} %pad_maximum_fusion.40), channel_id=1, source_target_pairs={{0,1},{1,0},{2,3},{3,2},{4,5},{5,4},{6,7},{7,6},{8,9},{9,8},{10,11... | collective-permute-start | bytes 786440 | tf_op jit(solution)/shard_map/ppermute | solution.py:25
  570.7 55.2 %collective-permute-start.65 = (bf16[512,1024]{1,0:T(8,128)(2,1)S(1)}, bf16[512,1024]{1,0:T(8,128)(2,1)S(1)}, u32[]{:S(2)}, u32[]{:S(2)}) collective-permute-start(bf16[512,1024]{1,0:T(8,128)(2,1)S(1)} %fusion.72), channel_id=1, source_target_pairs={{0,16},{16,0},{1,17},{17,1},{2,18},{18,2},{3,19},{19,3},{4,20},{20... | collective-permute-start | bytes 3145736 | tf_op jit(solution)/shard_map/ppermute | solution.py:125
  593.0 25.3 %collective-permute-start.160 = (bf16[2,2,176,512]{3,2,1,0:T(8,128)(2,1)S(1)}, bf16[2,2,176,512]{3,2,1,0:T(8,128)(2,1)S(1)}, u32[]{:S(2)}, u32[]{:S(2)}) collective-permute-start(bf16[2,2,176,512]{3,2,1,0:T(8,128)(2,1)S(1)} %fusion.80), channel_id=1, source_target_pairs={{0,4},{1,5},{2,6},{3,7},{4,8},{5,9},{6,10},{7,11},{8,12},{9,13},{1... | collective-permute-start | bytes 2162696 | tf_op jit(solution)/shard_map/ppermute | solution.py:27
  595.0 20.6 %collective-permute-start.100 = (bf16[64,2048]{1,0:T(8,128)(2,1)S(1)}, bf16[64,2048]{1,0:T(8,128)(2,1)S(1)}, u32[]{:S(2)}, u32[]{:S(2)}) collective-permute-start(bf16[64,2048]{1,0:T(8,128)(2,1)S(1)} %fusion.229), channel_id=1, source_target_pairs={{0,4},{1,5},{2,6},{3,7},{4,8},{5,9},{6,10},{7,11},{8,12},{9,13},{1... | collective-permute-start | bytes 786440 | tf_op jit(solution)/shard_map/ppermute | solution.py:27
  596.4 24.6 %collective-permute-start.117 = (bf16[1,64,2816]{2,1,0:T(8,128)(2,1)S(1)}, bf16[1,64,2816]{2,1,0:T(8,128)(2,1)S(1)}, u32[]{:S(2)}, u32[]{:S(2)}) collective-permute-start(bf16[1,64,2816]{2,1,0:T(8,128)(2,1)S(1)} %pad_maximum_fusion.15), channel_id=1, source_target_pairs={{0,2},{1,3},{2,0},{3,1},{4,6},{5,7},{6,4},{7,5},{8,10},{9,11},{10,... | collective-permute-start | bytes 1081352 | tf_op jit(solution)/shard_map/ppermute | solution.py:26
  596.5 27.7 %collective-permute-start.119 = (bf16[1,64,2816]{2,1,0:T(8,128)(2,1)S(1)}, bf16[1,64,2816]{2,1,0:T(8,128)(2,1)S(1)}, u32[]{:S(2)}, u32[]{:S(2)}) collective-permute-start(bf16[1,64,2816]{2,1,0:T(8,128)(2,1)S(1)} %pad_maximum_fusion.16), channel_id=1, source_target_pairs={{0,1},{1,0},{2,3},{3,2},{4,5},{5,4},{6,7},{7,6},{8,9},{9,8},{10,11... | collective-permute-start | bytes 1081352 | tf_op jit(solution)/shard_map/ppermute | solution.py:25
  618.3 76.5 %collective-permute-start.144 = (bf16[64,2816]{1,0:T(8,128)(2,1)}, bf16[64,2816]{1,0:T(8,128)(2,1)}, u32[]{:S(2)}, u32[]{:S(2)}) collective-permute-start(bf16[64,2816]{1,0:T(8,128)(2,1)} %fusion.174), channel_id=1, source_target_pairs={{0,4},{1,5},{2,6},{3,7},{4,8},{5,9},{6,10},{7,11},{8,12},{9,13},{1... | collective-permute-start | bytes 1081352 | tf_op jit(solution)/shard_map/ppermute | solution.py:27
  621.0 74.9 %collective-permute-start.150 = (bf16[1408,512]{1,0:T(8,128)(2,1)}, bf16[1408,512]{1,0:T(8,128)(2,1)}, u32[]{:S(2)}, u32[]{:S(2)}) collective-permute-start(bf16[1408,512]{1,0:T(8,128)(2,1)} %get-tuple-element.171), channel_id=1, source_target_pairs={{0,16},{16,0},{1,17},{17,1},{2,18},{18,2},{3,19},{19,3},{4,20},{20... | collective-permute-start | bytes 4325384 | tf_op jit(solution)/shard_map/ppermute | solution.py:125
  624.1 67.2 %collective-permute-start.122 = (bf16[1,64,2816]{2,1,0:T(8,128)(2,1)}, bf16[1,64,2816]{2,1,0:T(8,128)(2,1)}, u32[]{:S(2)}, u32[]{:S(2)}) collective-permute-start(bf16[1,64,2816]{2,1,0:T(8,128)(2,1)} %pad_maximum_fusion.17), channel_id=1, source_target_pairs={{0,2},{1,3},{2,0},{3,1},{4,6},{5,7},{6,4},{7,5},{8,10},{9,11},{10,... | collective-permute-start | bytes 1081352 | tf_op jit(solution)/shard_map/ppermute | solution.py:26
  624.1 67.7 %collective-permute-start.124 = (bf16[1,64,2816]{2,1,0:T(8,128)(2,1)}, bf16[1,64,2816]{2,1,0:T(8,128)(2,1)}, u32[]{:S(2)}, u32[]{:S(2)}) collective-permute-start(bf16[1,64,2816]{2,1,0:T(8,128)(2,1)} %pad_maximum_fusion.18), channel_id=1, source_target_pairs={{0,1},{1,0},{2,3},{3,2},{4,5},{5,4},{6,7},{7,6},{8,9},{9,8},{10,11... | collective-permute-start | bytes 1081352 | tf_op jit(solution)/shard_map/ppermute | solution.py:25
  650.6 24.1 %collective-permute-start.68 = (bf16[512,16]{0,1:T(8,128)(2,1)S(1)}, bf16[512,16]{0,1:T(8,128)(2,1)S(1)}, u32[]{:S(2)}, u32[]{:S(2)}) collective-permute-start(bf16[512,16]{0,1:T(8,128)(2,1)S(1)} %convolution_convert_fusion.24), channel_id=1, source_target_pairs={{0,16},{16,0},{1,17},{17,1},{2,18},{18,2},{3,19},{19,3},{4,20},{20... | collective-permute-start | bytes 49160 | tf_op jit(solution)/shard_map/ppermute | solution.py:125
  701.1 106.4 %collective-permute-start.107 = (bf16[1,64,2048]{2,1,0:T(8,128)(2,1)}, bf16[1,64,2048]{2,1,0:T(8,128)(2,1)}, u32[]{:S(2)}, u32[]{:S(2)}) collective-permute-start(bf16[1,64,2048]{2,1,0:T(8,128)(2,1)} %pad_maximum_fusion.43), channel_id=1, source_target_pairs={{0,2},{1,3},{2,0},{3,1},{4,6},{5,7},{6,4},{7,5},{8,10},{9,11},{10,... | collective-permute-start | bytes 786440 | tf_op jit(solution)/shard_map/ppermute | solution.py:26
  701.6 20.0 %collective-permute-start.161 = (bf16[2,2,176,512]{3,2,1,0:T(8,128)(2,1)S(1)}, bf16[2,2,176,512]{3,2,1,0:T(8,128)(2,1)S(1)}, u32[]{:S(2)}, u32[]{:S(2)}) collective-permute-start(bf16[2,2,176,512]{3,2,1,0:T(8,128)(2,1)S(1)} %copy-done.112), channel_id=1, source_target_pairs={{0,4},{1,5},{2,6},{3,7},{4,8},{5,9},{6,10},{7,11},{8,12},{9,13},{1... | collective-permute-start | bytes 2162696 | tf_op jit(solution)/shard_map/ppermute | solution.py:27
  708.8 18.2 %collective-permute-start.67 = (bf16[512,512]{1,0:T(8,128)(2,1)S(1)}, bf16[512,512]{1,0:T(8,128)(2,1)S(1)}, u32[]{:S(2)}, u32[]{:S(2)}) collective-permute-start(bf16[512,512]{1,0:T(8,128)(2,1)S(1)} %copy-done.115), channel_id=1, source_target_pairs={{0,16},{16,0},{1,17},{17,1},{2,18},{18,2},{3,19},{19,3},{4,20},{20... | collective-permute-start | bytes 1572872 | tf_op jit(solution)/shard_map/ppermute | solution.py:125
  711.1 19.3 %collective-permute-start.66 = (bf16[512,1024]{1,0:T(8,128)(2,1)S(1)}, bf16[512,1024]{1,0:T(8,128)(2,1)S(1)}, u32[]{:S(2)}, u32[]{:S(2)}) collective-permute-start(bf16[512,1024]{1,0:T(8,128)(2,1)S(1)} %copy-done.61), channel_id=1, source_target_pairs={{0,16},{16,0},{1,17},{17,1},{2,18},{18,2},{3,19},{19,3},{4,20},{20... | collective-permute-start | bytes 3145736 | tf_op jit(solution)/shard_map/ppermute | solution.py:125
  711.2 40.1 %collective-permute-start.151 = (bf16[2,2,176,512]{3,2,1,0:T(8,128)(2,1)}, bf16[2,2,176,512]{3,2,1,0:T(8,128)(2,1)}, u32[]{:S(2)}, u32[]{:S(2)}) collective-permute-start(bf16[2,2,176,512]{3,2,1,0:T(8,128)(2,1)} %bitcast.246), channel_id=1, source_target_pairs={{0,4},{1,5},{2,6},{3,7},{4,8},{5,9},{6,10},{7,11},{8,12},{9,13},{1... | collective-permute-start | bytes 2162696 | tf_op jit(solution)/shard_map/ppermute | solution.py:27
  744.6 20.6 %collective-permute-start.86 = (bf16[1,64,1152]{2,1,0:T(8,128)(2,1)S(1)}, bf16[1,64,1152]{2,1,0:T(8,128)(2,1)S(1)}, u32[]{:S(2)}, u32[]{:S(2)}) collective-permute-start(bf16[1,64,1152]{2,1,0:T(8,128)(2,1)S(1)} %slice.1218), channel_id=1, source_target_pairs={{0,1},{1,0},{2,3},{3,2},{4,5},{5,4},{6,7},{7,6},{8,9},{9,8},{10,11... | collective-permute-start | bytes 442376 | tf_op jit(solution)/shard_map/ppermute | solution.py:25
  746.8 18.5 %collective-permute-start.81 = (bf16[1,64,1152]{2,1,0:T(8,128)(2,1)S(1)}, bf16[1,64,1152]{2,1,0:T(8,128)(2,1)S(1)}, u32[]{:S(2)}, u32[]{:S(2)}) collective-permute-start(bf16[1,64,1152]{2,1,0:T(8,128)(2,1)S(1)} %slice.1211), channel_id=1, source_target_pairs={{0,1},{1,0},{2,3},{3,2},{4,5},{5,4},{6,7},{7,6},{8,9},{9,8},{10,11... | collective-permute-start | bytes 442376 | tf_op jit(solution)/shard_map/ppermute | solution.py:25
  752.7 16.4 %collective-permute-start.76 = (bf16[1,64,1152]{2,1,0:T(8,128)(2,1)S(1)}, bf16[1,64,1152]{2,1,0:T(8,128)(2,1)S(1)}, u32[]{:S(2)}, u32[]{:S(2)}) collective-permute-start(bf16[1,64,1152]{2,1,0:T(8,128)(2,1)S(1)} %slice.1204), channel_id=1, source_target_pairs={{0,1},{1,0},{2,3},{3,2},{4,5},{5,4},{6,7},{7,6},{8,9},{9,8},{10,11... | collective-permute-start | bytes 442376 | tf_op jit(solution)/shard_map/ppermute | solution.py:25
  765.2 32.0 %collective-permute-start.152 = (bf16[2,2,176,512]{3,2,1,0:T(8,128)(2,1)S(1)}, bf16[2,2,176,512]{3,2,1,0:T(8,128)(2,1)S(1)}, u32[]{:S(2)}, u32[]{:S(2)}) collective-permute-start(bf16[2,2,176,512]{3,2,1,0:T(8,128)(2,1)S(1)} %fusion.83), channel_id=1, source_target_pairs={{0,4},{1,5},{2,6},{3,7},{4,8},{5,9},{6,10},{7,11},{8,12},{9,13},{1... | collective-permute-start | bytes 2162696 | tf_op jit(solution)/shard_map/ppermute | solution.py:27
  788.2 19.3 %collective-permute-start.109 = (bf16[1,64,2048]{2,1,0:T(8,128)(2,1)S(1)}, bf16[1,64,2048]{2,1,0:T(8,128)(2,1)}, u32[]{:S(2)}, u32[]{:S(2)}) collective-permute-start(bf16[1,64,2048]{2,1,0:T(8,128)(2,1)S(1)} %copy-done.138), channel_id=1, source_target_pairs={{0,1},{1,0},{2,3},{3,2},{4,5},{5,4},{6,7},{7,6},{8,9},{9,8},{10,11... | collective-permute-start | bytes 786440 | tf_op jit(solution)/shard_map/ppermute | solution.py:25
  801.3 27.1 %collective-permute-start.153 = (bf16[2,2,176,512]{3,2,1,0:T(8,128)(2,1)S(1)}, bf16[2,2,176,512]{3,2,1,0:T(8,128)(2,1)S(1)}, u32[]{:S(2)}, u32[]{:S(2)}) collective-permute-start(bf16[2,2,176,512]{3,2,1,0:T(8,128)(2,1)S(1)} %fusion.82), channel_id=1, source_target_pairs={{0,4},{1,5},{2,6},{3,7},{4,8},{5,9},{6,10},{7,11},{8,12},{9,13},{1... | collective-permute-start | bytes 2162696 | tf_op jit(solution)/shard_map/ppermute | solution.py:27
  810.1 21.7 %collective-permute-start.110 = (bf16[64,2048]{1,0:T(8,128)(2,1)}, bf16[64,2048]{1,0:T(8,128)(2,1)}, u32[]{:S(2)}, u32[]{:S(2)}) collective-permute-start(bf16[64,2048]{1,0:T(8,128)(2,1)} %get-tuple-element.112), channel_id=1, source_target_pairs={{0,16},{16,0},{1,17},{17,1},{2,18},{18,2},{3,19},{19,3},{4,20},{20... | collective-permute-start | bytes 786440 | tf_op jit(solution)/shard_map/ppermute | solution.py:125
  (333 other events, 3048.7 us)

commit v2 on v1

v2 whole, which is shorter than its diff:
```python
from functools import partial

import jax
import jax.numpy as jnp
from jax import lax
from jax.experimental import pallas as pl
from jax.experimental.pallas import tpu as pltpu
from jax.sharding import PartitionSpec as P

SPAN = 64
BF = jnp.bfloat16
F32 = jnp.float32
PARAMS = pltpu.CompilerParams(vmem_limit_bytes=40 << 20)
FULL = pltpu.CompilerParams(vmem_limit_bytes=60 << 20)
COST = pl.CostEstimate(flops=0, bytes_accessed=0, transcendentals=0)


def mm(a, b):
    return lax.dot_general(
        a.astype(BF), b.astype(BF), (((1,), (0,)), ((), ())), preferred_element_type=F32
    )


def mm_nt(a, b):
    return lax.dot_general(
        a.astype(BF), b.astype(BF), (((1,), (1,)), ((), ())), preferred_element_type=F32
    )


def mm_tn(a, b):
    return lax.dot_general(
        a.astype(BF), b.astype(BF), (((0,), (0,)), ((), ())), preferred_element_type=F32
    )


def after(value, *tokens):
    return lax.optimization_barrier((value,) + tokens)[0]


def copy_call(kernel, at, ins, in_specs, outs, out_specs, grid, params=None):
    return pl.pallas_call(
        kernel,
        grid_spec=pltpu.PrefetchScalarGridSpec(
            num_scalar_prefetch=1, grid=grid, in_specs=in_specs, out_specs=out_specs
        ),
        out_shape=[jax.ShapeDtypeStruct(o, BF) for o in outs],
        compiler_params=params or PARAMS,
        cost_estimate=COST,
    )(at, *ins)


def table_block(s, rd, ag, mg, rb, gg, ru):
    R, rank = rd.shape

    def one_hot(n, at):
        i = lax.broadcasted_iota(jnp.int32, (n, 128), 0)
        return jnp.where(i + at + 64 * s == lax.broadcasted_iota(jnp.int32, (n, 128), 1), 1.0, 0.0)

    def upright(row):
        n = row.shape[1]
        i = lax.broadcasted_iota(jnp.int32, (R, n), 0)
        return mm_nt(jnp.where(i == lax.broadcasted_iota(jnp.int32, (R, n), 1), 1.0, 0.0), row)

    out = mm(rd, one_hot(rank, 0)) + mm(upright(ru), one_hot(rank, rank + 4))
    for k, row in enumerate((ag, mg, rb, gg)):
        out = out + mm(upright(jnp.broadcast_to(row, (8, row.shape[1]))), one_hot(8, rank + k)[0:1] * (
            lax.broadcasted_iota(jnp.int32, (8, 1), 0) == 0
        ).astype(F32))
    return out.astype(BF)


def cut_kernel(groups, at_ref, *refs):
    n = sum(len(g) for g in groups)
    ins, smalls, outs = refs[:n], refs[n : n + 6], refs[n + 6 :]
    s = at_ref[3]
    k = 0
    for g, _ in enumerate(groups):
        to = 0
        for _ in groups[g]:
            h = ins[k].shape[2] // 2
            for o, half in ((2 * g, s), (2 * g + 1, 1 - s)):
                outs[o][:, to : to + h] = ins[k][0, :, pl.ds(pl.multiple_of(half * h, h), h)]
            to += h
            k += 1
        if g == 0:
            rd, ag, mg, rb, gg, ru = smalls
            table = table_block(s, rd[0], ag[...], mg[...], rb[...], gg[...], ru[0])
            outs[0][:, to:] = table
            outs[1][:, to:] = table


def cut_columns(groups, smalls, at):
    ins = [v for g in groups for v in g] + list(smalls)
    in_specs = [pl.BlockSpec(v.shape, lambda i, a, d=v.ndim: (0,) * d) for v in ins]
    outs = []
    for g, arrays in enumerate(groups):
        C = sum(v.shape[2] for v in arrays) // 2 + (128 if g == 0 else 0)
        outs += [(arrays[0].shape[1], C)] * 2
    out_specs = [pl.BlockSpec(o, lambda i, a: (0, 0)) for o in outs]
    out = copy_call(partial(cut_kernel, groups), at, ins, in_specs, outs, out_specs, (1,), FULL)
    return [(out[2 * g], out[2 * g + 1]) for g in range(len(groups))]


def join_kernel(at_ref, keep_ref, got_ref, out_ref):
    W = keep_ref.shape[1]
    s = at_ref[3]
    out_ref[:, pl.ds(pl.multiple_of(s * W, W), W)] = keep_ref[...]
    out_ref[:, pl.ds(pl.multiple_of((1 - s) * W, W), W)] = got_ref[...]


def join_columns(keep, got, at):
    H, W = keep.shape
    n = H // 4
    spec = pl.BlockSpec((n, W), lambda i, a: (i, 0))
    out = pl.BlockSpec((n, 2 * W), lambda i, a: (i, 0))
    return copy_call(join_kernel, at, [keep, got], [spec, spec], [(H, 2 * W)], [out], (4,))[0]


def pairs(dz, dy, dx):
    return [
        (z * 4 + y * 2 + x, ((z + dz) % 4) * 4 + (y ^ dy) * 2 + (x ^ dx))
        for z in range(4)
        for y in range(2)
        for x in range(2)
    ]


class Link:
    def __init__(self, step, depth=1):
        self.pairs = pairs(*step)
        self.depth = depth
        self.sent = []

    def __call__(self, v, step=None):
        if len(self.sent) >= self.depth:
            v = after(v, self.sent[-self.depth])
        self.sent.append(lax.ppermute(v, "dp", pairs(*step) if step else self.pairs))
        return self.sent[-1]


def over_core(v):
    return lax.ppermute(v, "section", [(0, 1), (1, 0)])


def core_sum(v):
    v = v.astype(BF)
    return v.astype(F32) + over_core(v).astype(F32)


def add(a, b):
    return (a.astype(F32) + b.astype(F32)).astype(BF)


def ring(pz, v):
    slabs = [v]
    for _ in range(3):
        slabs.append(pz(slabs[-1]))
    return slabs


BLOCKS = ((0, 0), (0, 1), (1, 0), (1, 1))


class Idle:
    def __getattr__(self, name):
        return lambda: None


class GatherWide:
    def __init__(self, links, shard, half):
        self.px, self.py, self.pz = links
        self.slabs, self.half = [shard], half

    def ring(self):
        self.slabs.append(self.pz(self.slabs[-1]))

    def first(self):
        h = self.half
        self.a = jnp.stack([v[:, :h] for v in self.slabs])
        self.b = jnp.stack([v[:, h:] for v in self.slabs])
        self.X1, self.Y2 = self.px(self.a), self.py(self.b)

    def second(self):
        self.X2, self.Y1 = self.px(self.b), self.py(self.a)

    def third(self):
        self.D2, self.D1 = self.px(self.Y2), self.py(self.X1)

    def parts(self):
        return [self.a, self.X1, self.Y1, self.D1], [self.b, self.X2, self.Y2, self.D2]


def plane_of(j, a):
    return (2 * a[3] + j) % 4


def slab_of(j, a):
    return (a[0] + 4 - plane_of(j, a)) % 4


def place_kernel(columns, split, n_out, at_ref, *refs):
    ins, outs = refs[:-n_out], refs[-n_out:]
    j = pl.program_id(0)
    y, x = at_ref[1], at_ref[2]

    def write(h, lo, hi, o, to):
        for b, (yy, xx) in enumerate(BLOCKS):
            outs[o][0, y ^ yy, x ^ xx, :, to : to + hi - lo] = ins[4 * h + b][0, :, lo:hi]

    for h, half in enumerate(columns):
        for lo, hi, o, to in half:
            if o == split:
                pl.when(j < 2)(partial(write, h, lo, hi, o, to))
                pl.when(j >= 2)(partial(write, h, lo, hi, o + 1, to))
            else:
                write(h, lo, hi, o, to)


def place_blocks(halves_, columns, at, split=None):
    _, R, _ = halves_[0][0].shape
    width = {}
    for half in columns:
        for lo, hi, o, to in half:
            width[o] = max(width.get(o, 0), to + hi - lo)
    if split is not None:
        width[split + 1] = width[split]
    shapes, specs = [], []
    for o in sorted(width):
        block = (1, 2, 2, R, width[o])
        if split is not None and o == split:
            shapes.append((2,) + block[1:])
            specs.append(pl.BlockSpec(block, lambda j, a: (jnp.minimum(j, 1), 0, 0, 0, 0)))
        elif split is not None and o == split + 1:
            shapes.append((2,) + block[1:])
            specs.append(pl.BlockSpec(block, lambda j, a: (jnp.maximum(j, 2) - 2, 0, 0, 0, 0)))
        else:
            shapes.append((4,) + block[1:])
            specs.append(pl.BlockSpec(block, lambda j, a: (plane_of(j, a), 0, 0, 0, 0)))
    ins = list(halves_[0]) + list(halves_[1])
    in_specs = [pl.BlockSpec((1,) + v.shape[1:], lambda j, a: (slab_of(j, a), 0, 0)) for v in ins]
    return copy_call(
        partial(place_kernel, columns, split, len(shapes)), at, ins, in_specs, shapes, specs, (4,)
    )


class GatherDown:
    def __init__(self, links, shard, at):
        self.px, self.py, self.pz = links
        self.shard, self.at = shard, at

    def sides(self):
        self.X, self.Y = self.px(self.shard), self.py(self.shard)

    def diag(self):
        R, C = self.shard.shape
        h = C // 2
        y, x = self.at[1], self.at[2]
        D2, D1 = self.px(self.Y[:, h:]), self.py(self.X[:, :h])
        out = jnp.zeros((2, 2, R, C), BF)
        for b, p, c in ((0, self.shard, 0), (1, self.X, 0), (2, self.Y, 0), (3, D1, 0), (3, D2, h)):
            yy, xx = BLOCKS[b]
            out = lax.dynamic_update_slice(out, p[None, None], (y ^ yy, x ^ xx, 0, c))
        self.slabs = [out.reshape(4 * R, C)]

    def ring(self):
        self.slabs.append(self.pz(self.slabs[-1]))


def split_kernel(at_ref, *refs):
    ins, keep, give = refs[:4], refs[4], refs[5]
    j = pl.program_id(0)
    slab = slab_of(j, at_ref)
    for i in range(4):

        @pl.when((slab == i) & (j < 2))
        def _(i=i):
            keep[0] = ins[i][...]

        @pl.when((slab == i) & (j >= 2))
        def _(i=i):
            give[0] = ins[i][...]


def split_planes(slabs, at):
    n, C = slabs[0].shape
    specs = [
        pl.BlockSpec((1, n, C), lambda j, a: (jnp.minimum(j, 1), 0, 0)),
        pl.BlockSpec((1, n, C), lambda j, a: (jnp.maximum(j, 2) - 2, 0, 0)),
    ]
    whole = pl.BlockSpec((n, C), lambda j, a: (0, 0))
    out = copy_call(split_kernel, at, slabs, [whole] * 4, [(2, n, C)] * 2, specs, (4,))
    return out[0].reshape(2 * n, C), out[1].reshape(2 * n, C)


def grad_kernel(half, R, at_ref, lhs_ref, rhs_ref, *refs):
    acc = refs[-1]
    extras, outs = refs[:-9], refs[-9:-1]
    C = rhs_ref.shape[1]
    acc[:, :C] = mm_tn(lhs_ref[...], rhs_ref[...])
    i = pl.program_id(0)
    z, y, x, s = at_ref[0], at_ref[1], at_ref[2], at_ref[3]
    if extras:
        d = (z + 3 - i) % 4
        keep, got = extras[0][...].astype(F32), extras[1][...].astype(F32)
        W = keep.shape[1]
        acc[:, C : C + W] = jnp.where((d // 2) == s, keep, got)
        if len(extras) > 2:
            acc[:, C + W :] = extras[2][...].astype(F32)
    for b, (yy, xx) in enumerate(BLOCKS):
        rows = pl.ds(pl.multiple_of(((y ^ yy) * 2 + (x ^ xx)) * R, R), R)
        outs[2 * b][0] = acc[rows, :half].astype(BF)
        outs[2 * b + 1][0] = acc[rows, half:].astype(BF)


def grad_blocks(lhs, rhs, half, at, extras=()):
    tokens, D = lhs.shape
    C = rhs.shape[1]
    E = sum(e.shape[1] for e in extras[:1] + extras[2:])
    n = D // 4
    R = n // 4

    def plane(i, a):
        return (a[0] + 3 - i) % 4

    in_specs = [
        pl.BlockSpec((tokens, n), lambda i, a: (0, plane(i, a))),
        pl.BlockSpec((tokens, C), lambda i, a: (0, 0)),
    ]
    for k, e in enumerate(extras):
        if k < 2:
            in_specs.append(pl.BlockSpec((n, e.shape[1]), lambda i, a: (plane(i, a) % 2, 0)))
        else:
            in_specs.append(pl.BlockSpec((n, e.shape[1]), lambda i, a: (plane(i, a), 0)))
    widths = (half, C + E - half)
    return pl.pallas_call(
        partial(grad_kernel, half, R),
        grid_spec=pltpu.PrefetchScalarGridSpec(
            num_scalar_prefetch=1,
            grid=(4,),
            in_specs=in_specs,
            out_specs=[pl.BlockSpec((1, R, widths[k % 2]), lambda i, a: (i, 0, 0)) for k in range(8)],
            scratch_shapes=[pltpu.VMEM((n, C + E), F32)],
        ),
        out_shape=[jax.ShapeDtypeStruct((4, R, widths[k % 2]), BF) for k in range(8)],
        compiler_params=PARAMS,
        cost_estimate=COST,
    )(at, lhs, rhs, *extras)


def slab_kernel(o1, o2, x1, x2, y1, y2, out):
    h = o1.shape[2]
    out[0, :, :h] = (o1[0].astype(F32) + x1[0].astype(F32) + y1[0].astype(F32)).astype(BF)
    out[0, :, h:] = (o2[0].astype(F32) + x2[0].astype(F32) + y2[0].astype(F32)).astype(BF)


def slabs_kernel(n, *refs):
    ins, outs = refs[:-4], refs[-4:]
    i = pl.program_id(0)
    for k in range(4):

        @pl.when(i == k)
        def _(k=k):
            to = 0
            for p in range(0, len(ins), n):
                w = ins[p].shape[2]
                total = ins[p][0].astype(F32)
                for v in ins[p + 1 : p + n]:
                    total = total + v[0].astype(F32)
                outs[k][:, to : to + w] = total.astype(BF)
                to += w


def sum_slabs(*groups):
    n = len(groups[0])
    ins = [v for g in groups for v in g]
    R = ins[0].shape[1]
    C = sum(g[0].shape[2] for g in groups)
    return pl.pallas_call(
        partial(slabs_kernel, n),
        grid=(4,),
        in_specs=[pl.BlockSpec((1,) + v.shape[1:], lambda i: (i, 0, 0)) for v in ins],
        out_specs=[pl.BlockSpec((R, C), lambda i: (0, 0))] * 4,
        out_shape=[jax.ShapeDtypeStruct((R, C), BF)] * 4,
        compiler_params=PARAMS,
    )(*ins)


def total(*parts):
    t = parts[0].astype(F32)
    for v in parts[1:]:
        t = t + v.astype(F32)
    return t.astype(BF)


class ReduceWide:
    def __init__(self, links, blocks):
        self.px, self.py, self.pz = links
        self.o1, self.o2, self.X1, self.X2, self.Y1, self.Y2, self.D1, self.D2 = blocks

    def diag(self):
        self.r1, self.r2 = self.px(self.D1), self.py(self.D2)

    def sides(self):
        self.a1, self.b2 = self.px(self.X1), self.py(self.Y2)

    def rest(self):
        self.a2, self.b1 = self.px(add(self.X2, self.r2)), self.py(add(self.Y1, self.r1))

    def ring(self):
        if not hasattr(self, "slabs"):
            _, R, h = self.o1.shape
            C = h + self.o2.shape[2]
            spec1 = pl.BlockSpec((1, R, h), lambda i: (i, 0, 0))
            spec2 = pl.BlockSpec((1, R, C - h), lambda i: (i, 0, 0))
            self.slabs = pl.pallas_call(
                slab_kernel,
                grid=(4,),
                in_specs=[spec1, spec2] * 3,
                out_specs=pl.BlockSpec((1, R, C), lambda i: (i, 0, 0)),
                out_shape=jax.ShapeDtypeStruct((4, R, C), BF),
            )(self.o1, self.o2, self.a1, self.a2, self.b1, self.b2)
            self.sum, self.at = self.slabs[0], 0
        self.at += 1
        self.sum = add(self.pz(self.sum), self.slabs[self.at])

    def along(self):
        a, b, c, d = sum_slabs((self.o1, self.a1, self.b1), (self.o2, self.a2, self.b2))
        self.sum = total(d, *[self.pz(v, (up, 0, 0)) for v, up in ((a, 3), (b, 2), (c, 1))])


class ReduceDown:
    def __init__(self, links, keep, got, at):
        self.px, self.py, self.pz = links
        self.keep, self.got, self.at, self.step = keep, got, at, 0

    def plane(self):
        n = self.keep.shape[0] // 2
        d = (self.at[0] + 3 - self.step) % 4
        self.step += 1
        a = lax.dynamic_slice_in_dim(self.keep, (d % 2) * n, n, 0)
        b = lax.dynamic_slice_in_dim(self.got, (d % 2) * n, n, 0)
        return jnp.where((d // 2) == self.at[3], a, b)

    def ring(self):
        if self.step == 0:
            self.sum = self.plane()
        self.sum = add(self.pz(self.sum), self.plane())

    def pick(self, b, lo, hi):
        yy, xx = BLOCKS[b]
        R = self.sum.shape[0] // 4
        v = self.sum.reshape(2, 2, R, -1)
        y, x = self.at[1], self.at[2]
        return lax.dynamic_slice(v, (y ^ yy, x ^ xx, 0, lo), (1, 1, R, hi - lo)).reshape(R, hi - lo)

    def diag(self):
        C = self.sum.shape[1]
        h = C // 2
        self.r1, self.r2 = self.px(self.pick(3, 0, h)), self.py(self.pick(3, h, C))

    def sides(self):
        C = self.sum.shape[1]
        h = C // 2
        self.a1, self.b2 = self.px(self.pick(1, 0, h)), self.py(self.pick(2, h, C))

    def rest(self):
        C = self.sum.shape[1]
        h = C // 2
        a2 = self.px(add(self.pick(1, h, C), self.r2))
        b1 = self.py(add(self.pick(2, 0, h), self.r1))
        first = add(add(self.pick(0, 0, h), self.a1), b1)
        second = add(add(self.pick(0, h, C), a2), self.b2)
        self.sum = jnp.concatenate([first, second], 1)


def finish_kernel(widths, at_ref, keep_ref, got_ref, *outs):
    s = at_ref[3]
    to = 0
    for w, out in zip(widths, outs):
        out[0, :, pl.ds(pl.multiple_of(s * w, w), w)] = keep_ref[:, to : to + w].astype(F32)
        out[0, :, pl.ds(pl.multiple_of((1 - s) * w, w), w)] = got_ref[:, to : to + w].astype(F32)
        to += w


def finish(keep, got, widths, at):
    R = keep.shape[0]
    return pl.pallas_call(
        partial(finish_kernel, widths),
        grid_spec=pltpu.PrefetchScalarGridSpec(
            num_scalar_prefetch=1,
            grid=(1,),
            in_specs=[pl.BlockSpec(keep.shape, lambda i, a: (0, 0))] * 2,
            out_specs=[pl.BlockSpec((1, R, 2 * w), lambda i, a: (0, 0, 0)) for w in widths],
        ),
        out_shape=[jax.ShapeDtypeStruct((1, R, 2 * w), F32) for w in widths],
        compiler_params=PARAMS,
    )(at, keep, got)


def causal(length):
    i = lax.broadcasted_iota(jnp.int32, (length, length), 0)
    j = lax.broadcasted_iota(jnp.int32, (length, length), 1)
    return (i >= j) & (i // SPAN == j // SPAN)

def head_state(pre, logits, h, K, V, heads, keep):
    kh, vh = K // heads, V // heads
    length = pre.shape[0]
    q = pre[:, h * kh : (h + 1) * kh].astype(F32)
    k = pre[:, K + h * kh : K + (h + 1) * kh].astype(F32)
    v = pre[:, 2 * K + h * vh : 2 * K + (h + 1) * vh]
    x = logits[:, h * kh : (h + 1) * kh]
    a = (jnp.minimum(x, 0.0) - jnp.log1p(jnp.exp(-jnp.abs(x)))) * (1.0 / 16.0)
    tri = jnp.where(keep, 1.0, 0.0)
    b = lax.dot_general(tri, a, (((1,), (0,)), ((), ())), precision=lax.Precision.HIGHEST, preferred_element_type=F32)
    n = length // SPAN
    lasts = [b[(i + 1) * SPAN - 1 : (i + 1) * SPAN] for i in range(n)]
    last = jnp.concatenate([jnp.broadcast_to(t, (SPAN, kh)) for t in lasts], 0)
    eb = jnp.exp(b)
    enb = jnp.exp(-b)
    elb = jnp.exp(last - b)
    qs = q * (kh ** -0.5) * eb
    ks = k * enb
    kc = k * elb
    qs_l, ks_l, kc_l = qs.astype(BF), ks.astype(BF), kc.astype(BF)
    sc = jnp.where(keep, mm_nt(qs_l, ks_l), 0.0).astype(BF)
    local = mm(sc, v)
    states, decs, outs = [], [], []
    S = jnp.zeros((vh, kh), F32)
    for i in range(n):
        at = slice(i * SPAN, (i + 1) * SPAN)
        states.append(S)
        decs.append(jnp.exp(lasts[i]))
        o = local[at]
        if i:
            o = o + mm_nt(qs_l[at], S)
        outs.append(o)
        if i < n - 1:
            S = S * decs[i] + mm_tn(v[at], kc_l[at])
    return dict(q=q, k=k, v=v, x=x, eb=eb, enb=enb, elb=elb, qs=qs, ks=ks, kc=kc, qs_l=qs_l, ks_l=ks_l,
                kc_l=kc_l, sc=sc, states=states, decs=decs, out=jnp.concatenate(outs, 0))

def mixer_fwd_kernel(K, V, heads, pre_ref, logits_ref, gain_ref, out_ref):
    pre, logits, gain = pre_ref[...], logits_ref[...], gain_ref[...]
    keep = causal(pre.shape[0])
    vh = V // heads
    for h in range(heads):
        o = head_state(pre, logits, h, K, V, heads, keep)["out"]
        g = pre[:, 2 * K + V + h * vh : 2 * K + V + (h + 1) * vh].astype(F32)
        o = o * lax.rsqrt(jnp.mean(o * o, axis=-1, keepdims=True) + 1e-5) * gain
        out_ref[:, h * vh : (h + 1) * vh] = (o * (g * jax.nn.sigmoid(g))).astype(BF)

def mixer_bwd_kernel(K, V, heads, pre_ref, logits_ref, gain_ref, dg_ref, dpre_ref, dlog_ref, dgain_ref):
    pre, logits, gain = pre_ref[...], logits_ref[...], gain_ref[...]
    keep = causal(pre.shape[0])
    length = pre.shape[0]
    kh, vh = K // heads, V // heads
    n = length // SPAN
    dgain = jnp.zeros((1, vh), F32)
    for h in range(heads):
        st = head_state(pre, logits, h, K, V, heads, keep)
        out, v = st["out"], st["v"]
        g = pre[:, 2 * K + V + h * vh : 2 * K + V + (h + 1) * vh].astype(F32)
        dgated = dg_ref[:, h * vh : (h + 1) * vh].astype(F32)
        r = lax.rsqrt(jnp.mean(out * out, axis=-1, keepdims=True) + 1e-5)
        sg = jax.nn.sigmoid(g)
        on = out * r
        dgate = dgated * (on * gain) * (sg * (1.0 + g * (1.0 - sg)))
        dm = dgated * (g * sg)
        dgain = dgain + jnp.sum(dm * on, axis=0, keepdims=True)
        t = dm * gain
        dO = (t * r - on * (r * r * jnp.mean(t * out, axis=-1, keepdims=True))).astype(BF)
        dsc = jnp.where(keep, mm_nt(dO, v), 0.0).astype(BF)
        dv = mm_tn(st["sc"], dO)
        dqs = mm(dsc, st["ks_l"])
        dks = mm_tn(dsc, st["qs_l"])
        dqs_c, dkc, dv_c, dlast = [None] * n, [None] * n, [None] * n, [None] * n
        T = None
        for i in range(n - 1, -1, -1):
            at = slice(i * SPAN, (i + 1) * SPAN)
            if i:
                dqs_c[i] = mm(dO[at], st["states"][i])
            else:
                dqs_c[i] = jnp.zeros((SPAN, kh), F32)
            if T is None:
                dkc[i] = jnp.zeros((SPAN, kh), F32)
                dv_c[i] = jnp.zeros((SPAN, vh), F32)
                dlast[i] = jnp.zeros((SPAN, kh), F32)
            else:
                T_l = T.astype(BF)
                dkc[i] = mm(v[at], T_l)
                dv_c[i] = mm_nt(st["kc_l"][at], T_l)
                dl = jnp.sum(dkc[i] * st["kc"][at], axis=0, keepdims=True)
                if i:
                    dl = dl + jnp.sum(T * st["states"][i], axis=0, keepdims=True) * st["decs"][i]
                dlast[i] = jnp.broadcast_to(dl, (SPAN, kh))
            if i:
                new = mm_tn(dO[at], st["qs_l"][at])
                T = new if T is None else T * st["decs"][i] + new
        dqs = dqs + jnp.concatenate(dqs_c, 0)
        dkc = jnp.concatenate(dkc, 0)
        dv = dv + jnp.concatenate(dv_c, 0)
        db = dqs * st["qs"] - dks * st["ks"] - dkc * st["kc"]
        tri = jnp.where(keep, 1.0, 0.0)
        da = lax.dot_general(tri, db, (((0,), (0,)), ((), ())), precision=lax.Precision.HIGHEST, preferred_element_type=F32)
        da = da + jnp.concatenate(dlast, 0)
        x = st["x"]
        dlog_ref[:, h * kh : (h + 1) * kh] = da * (1.0 / 16.0) * (1.0 - jax.nn.sigmoid(x))
        dpre_ref[:, h * kh : (h + 1) * kh] = (dqs * (kh ** -0.5) * st["eb"]).astype(BF)
        dpre_ref[:, K + h * kh : K + (h + 1) * kh] = (dks * st["enb"] + dkc * st["elb"]).astype(BF)
        dpre_ref[:, 2 * K + h * vh : 2 * K + (h + 1) * vh] = dv.astype(BF)
        dpre_ref[:, 2 * K + V + h * vh : 2 * K + V + (h + 1) * vh] = dgate.astype(BF)
    @pl.when(pl.program_id(0) == 0)
    def _():
        dgain_ref[...] = jnp.zeros_like(dgain_ref)
    dgain_ref[...] += dgain

def row_spec(length, cols):
    return pl.BlockSpec((length, cols), lambda r: (r, 0))
def mixer_fwd(pre, logits, gain, rows, V):
    tokens, K = logits.shape
    length = tokens // rows
    heads = V // gain.shape[1]
    return pl.pallas_call(
        partial(mixer_fwd_kernel, K, V, heads),
        grid=(rows,),
        in_specs=[row_spec(length, pre.shape[1]), row_spec(length, K), pl.BlockSpec(gain.shape, lambda r: (0, 0))],
        out_specs=row_spec(length, V),
        out_shape=jax.ShapeDtypeStruct((tokens, V), BF),
        compiler_params=PARAMS,
        cost_estimate=COST,
    )(pre, logits, gain)
def mixer_bwd(pre, logits, gain, dgated, rows):
    tokens, K = logits.shape
    V = dgated.shape[1]
    length = tokens // rows
    heads = V // gain.shape[1]
    return pl.pallas_call(
        partial(mixer_bwd_kernel, K, V, heads),
        grid=(rows,),
        in_specs=[row_spec(length, pre.shape[1]), row_spec(length, K), pl.BlockSpec(gain.shape, lambda r: (0, 0)), row_spec(length, V)],
        out_specs=[row_spec(length, pre.shape[1]), row_spec(length, K), pl.BlockSpec(gain.shape, lambda r: (0, 0))],
        out_shape=[jax.ShapeDtypeStruct(pre.shape, BF), jax.ShapeDtypeStruct(logits.shape, F32), jax.ShapeDtypeStruct(gain.shape, F32)],
        compiler_params=PARAMS,
        cost_estimate=COST,
    )(pre, logits, gain, dgated)


def norm_back(dn, x, r, gain):
    t = dn * gain
    dx = t * r - x * (r * r * r * jnp.mean(t * x, axis=-1, keepdims=True))
    return dx, jnp.sum(dn * x * r, axis=0)


def exact_nt(a, b):
    return lax.dot_general(a, b, (((1,), (1,)), ((), ())), precision=lax.Precision.HIGHEST)


def project(x, w):
    r = lax.rsqrt(jnp.mean(x * x, axis=-1, keepdims=True) + 1e-6)
    n = (x * r * w["ag"]).astype(BF)
    pre = mm(n, w["WA"]).astype(BF)
    low = mm(n, w["rd"])
    logits = exact_nt(low, w["ru"]) + w["rb"]
    return dict(x=x, r=r, n=n, pre=pre, low=low, logits=logits)


def mix(m, w, rows):
    gated = mixer_fwd(m["pre"], m["logits"], w["gg"], rows, w["WO"].shape[0])
    return m["x"] + core_sum(mm(gated, w["WO"])), dict(m, gated=gated)


def expand(hidden, w):
    r = lax.rsqrt(jnp.mean(hidden * hidden, axis=-1, keepdims=True) + 1e-6)
    second = (hidden * r * w["mg"]).astype(BF)
    gu = mm(second, w["WF"]).astype(BF)
    return dict(hidden=hidden, r=r, second=second, gu=gu)


def contract(f, w, mask):
    gu = f["gu"]
    F = gu.shape[1] // 2
    gate, up = gu[:, :F].astype(F32), gu[:, F:].astype(F32)
    act = (gate * jax.nn.sigmoid(gate) * up).astype(BF)
    return (f["hidden"] + core_sum(mm(act, w["WD"]))) * mask, dict(f, act=act)


def column_halves(v, s):
    h = v.shape[1] // 2
    return lax.dynamic_slice_in_dim(v, s * h, h, 1), lax.dynamic_slice_in_dim(v, (1 - s) * h, h, 1)


def row_grads(rows_, cols, s):
    keep, give = column_halves(cols, s)
    got = over_core(mm_tn(rows_, give).astype(BF))
    return mm_tn(rows_, keep).astype(BF), got


def contract_back(dy, f, w):
    gu = f["gu"]
    F = gu.shape[1] // 2
    da = mm_nt(dy, w["WD"]).astype(BF).astype(F32)
    gate, up = gu[:, :F].astype(F32), gu[:, F:].astype(F32)
    sig = jax.nn.sigmoid(gate)
    return jnp.concatenate([da * up * (sig * (1.0 + gate * (1.0 - sig))), da * (gate * sig)], 1).astype(BF)


def expand_back(dy, dgu, f, w):
    dsec = core_sum(mm_nt(dgu, w["WF"])).astype(BF).astype(F32)
    back, d_mg = norm_back(dsec, f["hidden"], f["r"], w["mg"])
    return dy.astype(F32) + back, d_mg


def project_back(dhid, dpre, dlogits, d_gg, d_mg, m, w):
    dlow = jnp.matmul(dlogits, w["ru"], precision=lax.Precision.HIGHEST)
    dn = mm_nt(dpre, w["WA"]) + mm_nt(dlow, w["rd"])
    dn = core_sum(dn).astype(BF).astype(F32)
    dlow = core_sum(dlow)
    back, d_ag = norm_back(dn, m["x"], m["r"], w["ag"])
    small = dict(
        rd=mm_tn(m["n"], dlow),
        ru=mm_tn(dlogits, m["low"]),
        rb=jnp.sum(dlogits, axis=0),
        gg=d_gg[0],
        ag=d_ag,
        mg=d_mg,
    )
    return dhid + back, small


def body(
    inputs,
    lengths,
    out_grad,
    attn_gain,
    q_weight,
    k_weight,
    v_weight,
    rank_down,
    rank_up,
    rank_bias,
    gate_weight,
    group_gain,
    out_weight,
    mlp_gain,
    ffn_gate,
    ffn_up,
    ffn_down,
):
    size = lax.axis_size("dp")
    meshed = size == 16
    s = lax.axis_index("section")
    me = lax.axis_index("dp")
    at = jnp.stack([me // 4 % 4, (me // 2) % 2, me % 2, s]).astype(jnp.int32)
    first = s == 0
    shape = inputs.shape
    rows = shape[0] * shape[1]
    length, width = shape[2], shape[3]
    tokens = rows * length
    R = q_weight.shape[1]
    K, V, F, W = q_weight.shape[2] // 2, v_weight.shape[2] // 2, ffn_gate.shape[2] // 2, width // 2
    A = 2 * K + 2 * V
    half = (A + W) // 2
    rank = rank_down.shape[2]
    kc, gc = rank_bias.shape[1], group_gain.shape[1]
    ru_at = rank + 4
    links = [Link((0, 0, 1)), Link((0, 1, 0)), Link((1, 0, 0))]

    def paced(*values):
        if meshed:
            tokens = [link.sent[-1] for link in links]
            values = lax.optimization_barrier((values, tokens))[0]
        return values if len(values) > 1 else values[0]

    cuts = cut_columns(
        [
            (q_weight, k_weight, v_weight, gate_weight, out_weight),
            (ffn_gate, ffn_up),
            (ffn_down,),
        ],
        (rank_down, attn_gain, mlp_gain, rank_bias, group_gain, rank_up),
        at,
    )

    def by_layer(pair):
        keep, give = pair
        got = over_core(give)
        return jnp.where(first, keep, got), jnp.where(first, got, keep)

    (keep, give), ff, down = cuts[0], by_layer(cuts[1]), by_layer(cuts[2])
    got = over_core(give)
    table = keep[:, A + W :] + got[:, A + W :]
    keep, got = keep[:, : A + W], got[:, : A + W]
    ao = (jnp.concatenate([jnp.where(first, keep, got), table], 1), jnp.where(first, got, keep))

    def whole(v):
        return lax.all_gather(v, "dp", axis=0, tiled=True)

    def own_rows(v):
        h = v.shape[0] // 2
        keep = lax.dynamic_slice_in_dim(v, s * h, h, 0)
        got = over_core(lax.dynamic_slice_in_dim(v, (1 - s) * h, h, 0))
        return jnp.where(first, jnp.concatenate([keep, got], 1), jnp.concatenate([got, keep], 1))

    if meshed:
        gA = [GatherWide(links, v, half) for v in ao]
        gF = [GatherWide(links, v, F) for v in ff]
        gD = [GatherDown(links, v, at) for v in down]
    else:
        gA = gF = gD = [Idle(), Idle()]

    def place_ao(layer):
        if not meshed:
            v = whole(ao[layer])
            return v[:, :A], own_rows(v[:, A : A + W]), v[:, A + W :]
        columns = [
            [(0, half, 0, 0)],
            [(0, A - half, 0, half), (A - half, A - half + W, 1, 0)],
        ]
        C = ao[layer].shape[1]
        if C > A + W:
            columns[1].append((A - half + W, C - half, 3, 0))
        out = place_blocks(gA[layer].parts(), columns, at, split=1)
        keep, give = out[1].reshape(width // 2, W), out[2].reshape(width // 2, W)
        WO = join_columns(keep, over_core(give), at)
        return out[0].reshape(width, A), WO, (out[3].reshape(width, -1) if len(out) > 3 else None)

    def place_ff(layer):
        if not meshed:
            return whole(ff[layer])
        return place_blocks(gF[layer].parts(), [[(0, F, 0, 0)], [(0, F, 0, F)]], at)[0].reshape(width, 2 * F)

    def place_down(layer):
        if not meshed:
            return own_rows(whole(down[layer]))
        keep, give = split_planes(gD[layer].slabs, at)
        return join_columns(keep, over_core(give), at)

    def unpack(table, layer):
        t = table[:, 64 * layer : 64 * layer + ru_at + rank]
        flat = t[:, rank:ru_at].astype(F32).T
        ru = t.reshape(size, R, -1)[:, :kc, ru_at:].reshape(size * kc, rank).astype(F32)
        rb = flat[2].reshape(size, R)[:, :kc].reshape(1, size * kc)
        return dict(
            rd=t[:, :rank],
            ag=flat[0:1],
            mg=flat[1:2],
            ru=lax.dynamic_slice_in_dim(ru, s * K, K, 0),
            rb=lax.dynamic_slice_in_dim(rb, s * K, K, 1),
            gg=flat[3].reshape(size, R)[:, :gc].reshape(1, size * gc),
        )

    spots = jnp.arange(length)
    mask = (spots[None, :] < lengths.reshape(rows, 1)).astype(F32).reshape(tokens, 1)
    low_mask = mask.astype(BF)
    x0 = inputs.reshape(tokens, width).astype(F32)

    gD[0].sides(), gD[1].sides()
    gA[0].ring(), gA[0].ring(), gA[0].ring()
    gD[0].diag(), gD[1].diag()
    gA[0].first(), gA[0].second(), gA[0].third()
    gF[0].ring(), gF[0].ring(), gF[0].ring(), gD[0].ring()
    WA0, WO0, table = place_ao(0)
    p0, p1 = unpack(table, 0), unpack(table, 1)
    w0 = dict(p0, WA=WA0, WO=WO0)
    gF[0].first(), gD[0].ring()
    x0, w0 = paced(x0, w0)
    m0 = project(x0, w0)
    m0, p1 = paced(m0, p1)
    gF[0].second(), gD[0].ring(), gA[1].ring()
    h0, m0 = paced(*mix(m0, w0, rows))
    gF[0].third(), gA[1].ring(), gA[1].ring()
    w0["WF"] = place_ff(0)
    w0["WD"] = place_down(0)
    gA[1].first(), gF[1].ring()
    f0 = paced(expand(h0, w0))
    gA[1].second(), gF[1].ring()
    y0, f0 = paced(*contract(f0, w0, mask))
    x1 = y0.astype(BF)
    gA[1].third(), gF[1].ring()
    WA1, WO1, _ = place_ao(1)
    w1 = dict(p1, WA=WA1, WO=WO1)
    gF[1].first(), gD[1].ring()
    m1 = paced(project(x1.astype(F32), w1))
    gF[1].second(), gD[1].ring()
    h1, m1 = paced(*mix(m1, w1, rows))
    gF[1].third(), gD[1].ring()
    w1["WF"] = place_ff(1)
    w1["WD"] = place_down(1)
    f1 = expand(h1, w1)
    y1, f1 = contract(f1, w1, mask)
    layer_out = jnp.where(first, x1, y1.astype(BF)).reshape((1,) + shape)

    def all_rows(keep, got):
        return jnp.where(first, jnp.concatenate([keep, got], 0), jnp.concatenate([got, keep], 0))

    def scatter(v):
        return lax.psum_scatter(v, "dp", scatter_dimension=0, tiled=True)

    class Sum:
        def __init__(self, v):
            self.sum = scatter(v)

        def ring(self):
            pass

        along = diag = sides = rest = ring

    def sum_down(g):
        return ReduceDown(links, *g, at) if meshed else Sum(all_rows(*g))

    def sum_ff(second, dgu):
        if meshed:
            return ReduceWide(links, grad_blocks(second, dgu, F, at))
        return Sum(mm_tn(second, dgu).astype(BF))

    def sum_ao(n, dpre, gO, packed=()):
        extras = gO + packed
        if meshed:
            return ReduceWide(links, grad_blocks(n, dpre, half, at, extras))
        return Sum(jnp.concatenate((mm_tn(n, dpre).astype(BF), all_rows(*gO)) + packed, 1))

    dy1 = out_grad.reshape(tokens, width) * low_mask
    gD1 = row_grads(f1["act"], dy1, s)
    rD1 = sum_down(gD1)
    dgu = contract_back(dy1, f1, w1)
    rF1 = sum_ff(after(f1["second"], *gD1), dgu)
    rF1.diag(), rD1.ring()
    dh1, d_mg1 = expand_back(dy1, dgu, f1, w1)
    low = dh1.astype(BF)
    dgated = mm_nt(low, w1["WO"]).astype(BF)
    gO1 = row_grads(m1["gated"], low, s)
    dh1, d_mg1, dgated, gO1 = paced(dh1, d_mg1, dgated, gO1)
    rF1.sides(), rD1.ring()
    back = paced(mixer_bwd(m1["pre"], m1["logits"], w1["gg"], dgated, rows))
    rF1.rest(), rD1.ring()
    rA1 = sum_ao(m1["n"], back[0], gO1)
    dx1, small1 = paced(*project_back(dh1, *back, d_mg1, m1, w1))
    rA1.diag(), rF1.ring()
    dy0 = dx1.astype(BF) * low_mask
    gD0 = row_grads(f0["act"], dy0, s)
    dgu, gD0, dy0 = paced(contract_back(dy0, f0, w0), gD0, dy0)
    rD0 = sum_down(gD0)
    rA1.sides(), rF1.ring()
    rF0 = sum_ff(f0["second"], dgu)
    dh0, d_mg0 = paced(*expand_back(dy0, dgu, f0, w0))
    rA1.rest(), rF1.ring()
    low = dh0.astype(BF)
    dgated = mm_nt(low, w0["WO"]).astype(BF)
    dgated, gO0 = paced(dgated, row_grads(m0["gated"], low, s))
    rF0.diag(), rA1.ring()
    back = paced(mixer_bwd(m0["pre"], m0["logits"], w0["gg"], dgated, rows))
    rF0.sides(), rA1.ring()
    dx0, small0 = project_back(dh0, *back, d_mg0, m0, w0)
    dpre = back[0]
    input_out = jnp.where(first, dx0, dx1).reshape((1,) + shape)

    mine = {k: jnp.where(first, small0[k], small1[k]) for k in small0}
    other = {k: over_core(jnp.where(first, small1[k], small0[k])) for k in ("ru", "rb", "gg")}
    ru = all_rows(mine["ru"], other["ru"])
    rb = all_rows(mine["rb"], other["rb"])

    def tall_blocks(v):
        v = v.reshape(size, v.shape[0] // size, -1)
        return jnp.pad(v, ((0, 0), (0, R - v.shape[1]), (0, 0))).reshape(size * R, -1)

    def long_blocks(v):
        v = v.reshape(size, -1)
        return jnp.pad(v, ((0, 0), (0, R - v.shape[1]))).reshape(size * R)

    flat = jnp.stack([mine["ag"], mine["mg"], long_blocks(rb), long_blocks(mine["gg"] + other["gg"])]).T
    packed = jnp.concatenate([mine["rd"], flat, tall_blocks(ru)], 1)
    packed = jnp.pad(packed, ((0, 0), (0, 128 - packed.shape[1]))).astype(BF)

    rA0 = sum_ao(m0["n"], dpre, gO0, (packed,))
    rF0.rest(), rA1.ring(), rD0.ring(), rD0.ring(), rD0.ring()
    rA0.diag()
    rF0.along()
    rA0.sides()
    rA0.rest()
    rA0.along()
    for r in (rD1, rD0):
        r.diag()
    for r in (rD1, rD0):
        r.sides()
    for r in (rD1, rD0):
        r.rest()

    def join(a, b, widths):
        keep = jnp.where(first, a, b)
        got = over_core(jnp.where(first, b, a))
        return finish(keep, got, widths, at)

    dD = join(rD0.sum, rD1.sum, (W,))[0]
    dFg, dFu = join(rF0.sum, rF1.sum, (F, F))
    dq, dk, dv, dg, dO = join(rA0.sum[:, : A + W], rA1.sum, (K, K, V, V, W))
    t = rA0.sum[:, A + W :].astype(F32)
    return (
        layer_out,
        input_out,
        t[:, rank][None],
        dq,
        dk,
        dv,
        t[:, :rank][None],
        t[:kc, ru_at : ru_at + rank].T[None],
        t[:kc, rank + 2][None],
        dg,
        t[:gc, rank + 3][None],
        dO,
        t[:, rank + 1][None],
        dFg,
        dFu,
        dD,
    )


def solution(mesh):
    rows3 = P("section", "dp", None)
    one = P("section", "dp")
    return jax.shard_map(
        body,
        mesh=mesh,
        in_specs=(
            P(None, "dp", None, None),
            P(None, "dp"),
            P(None, "dp", None, None),
            one,
            rows3,
            rows3,
            rows3,
            rows3,
            P("section", None, "dp"),
            one,
            rows3,
            one,
            rows3,
            one,
            rows3,
            rows3,
            rows3,
        ),
        out_specs=(
            P("section", None, "dp", None, None),
            P("section", None, "dp", None, None),
            one,
            rows3,
            rows3,
            rows3,
            rows3,
            P("section", None, "dp"),
            one,
            rows3,
            one,
            rows3,
            one,
            rows3,
            rows3,
            rows3,
        ),
        check_vma=False,
    )
```

time: 859 us -> 648 us (0.75)
  local copies, waits for them, and re-layouts: 154 us -> 48.2 us
  Pallas kernels: 0 us -> 96.9 us
  other arithmetic: 140 us -> 64.3 us
  waiting for transfers between devices: 269 us -> 219 us
  matrix products: 105 us -> 57.9 us
  starting transfers between devices: 174 us -> 149 us
    pallas_call x0 -> x26, Pallas kernels: none -> 96.9 us  [the longest x11 30.1 us: copy_call(): pl.pallas_call(kernel, grid_spec=pltpu.PrefetchScalarGridSpec(num_scalar_...]
    ppermute x142 -> x104, waiting for transfers between devices: 267 us -> 215 us  [__call__(): lax.ppermute(v, 'dp', pairs(*step) if step else self.pairs)]
    dot_general x60 -> x36, matrix products: 105 us -> 57.9 us  [the longest x10 23.5 us: mm_nt(): lax.dot_general(a.astype(BF), b.astype(BF), (((1,), (1,)), ((), ())), pre...]
    concatenate x41 -> x4, other arithmetic: 28.1 us -> 2.39 us  [the longest x2 2.35 us: contract_back(): jnp.concatenate([da * up * (sig * (1.0 + gate * (1.0 - sig))), da * (gate...]
    dynamic_update_slice x34 -> x8, local copies, waits for them, and re-layouts: 23.6 us -> 2.73 us  [diag(): out = lax.dynamic_update_slice(out, p[None, None], (y ^ yy, x ^ xx, 0, c))]
    reshape x37 -> x8, local copies, waits for them, and re-layouts: 20.4 us -> 0.58 us  [the longest x2 0.16 us: unpack(): flat[3].reshape(size, R)[:, :gc].reshape(1, size * gc)]
    slice x105 -> x13, local copies, waits for them, and re-layouts: 27.5 us -> 7.87 us  [the longest x2 2.83 us: unpack(): t.reshape(size, R, -1)[:, :kc, ru_at:].reshape(size * kc, rank).astype(F32)]
    ppermute x142 -> x104, starting transfers between devices: 99.7 us -> 81.7 us  [__call__(): lax.ppermute(v, 'dp', pairs(*step) if step else self.pairs)]
  transfers between devices with their start and end apart: 167 -> 131, of which waited for: 58 -> 55; matrix products, arithmetic and copies ran while one was open for 42% -> 21% of each run, Pallas kernels for 0% -> 14%
where the time goes in v2:
time: 648 us; the launch traced here: 639 us
  waiting for transfers between devices  219 us (34%)
  starting transfers between devices  149 us (23%)
  Pallas kernels  96.9 us (15%)
  other arithmetic  64.3 us (10%)
  matrix products  57.9 us (9%)
  local copies, waits for them, and re-layouts  48.2 us (7%)
    ppermute x104, waiting for transfers between devices, __call__(): lax.ppermute(v, 'dp', pairs(*step) if step else self.pairs)  215 us
    ppermute x104, starting transfers between devices, __call__(): lax.ppermute(v, 'dp', pairs(*step) if step else self.pairs)  81.7 us
    ppermute x27, starting transfers between devices, over_core(): return lax.ppermute(v, 'section', [(0, 1), (1, 0)])  67.1 us
    pallas_call x11, Pallas kernels, copy_call(): pl.pallas_call(kernel, grid_spec=pltpu.PrefetchScalarGridSpec(num_scalar_...  30.1 us
    unnamed x332, local copies, waits for them, and re-layouts  29.4 us
    dot_general x10, matrix products, mm_nt(): lax.dot_general(a.astype(BF), b.astype(BF), (((1,), (1,)), ((), ())), pre...  23.5 us
    pallas_call x2, Pallas kernels, mixer_bwd(): pl.pallas_call(partial(mixer_bwd_kernel, K, V, heads), grid=(rows,), in_s...  19.9 us
    dot_general x10, matrix products, mm(): lax.dot_general(a.astype(BF), b.astype(BF), (((1,), (0,)), ((), ())), pre...  19.3 us
  transfers between devices with their start and end apart: 131, of which 55 were waited for; matrix products, arithmetic and copies ran while one was open for 21% of the time, Pallas kernels for 14%

profile of v2, /device:TPU:1, one launch (start us, length us, event | category | flops | bytes accessed | tf_op | source)
XLA Modules:
  0.0 639.1 jit_solution(10887525068806838427)
XLA Ops:
  2.8 3.5 shard_map.288
  30.1 4.8 collective-permute-done.2
  34.9 7.2 %collective-permute-done.3 = bf16[64,2176]{1,0:T(8,128)(2,1)S(1)} collective-permute-done((bf16[64,2176]{1,0:T(8,128)(2,1)S(1)}, bf16[64,2176]{1,0:T(8,128)(2,1)S(1)}, u32[]{:S(2)}, u32[]{:S(2)}) %collective-permute-start.3) | collective-permute-done | bytes 278560 | tf_op jit(solution)/shard_map/ppermute | solution.py:137
  45.4 6.8 %collective-permute-done.21 = bf16[64,2816]{1,0:T(8,128)(2,1)S(1)} collective-permute-done((bf16[64,2816]{1,0:T(8,128)(2,1)S(1)}, bf16[64,2816]{1,0:T(8,128)(2,1)S(1)}, u32[]{:S(2)}, u32[]{:S(2)}) %collective-permute-start.21) | collective-permute-done | bytes 360480 | tf_op jit(solution)/shard_map/ppermute | solution.py:137
  54.2 7.4 %collective-permute-done.22 = bf16[64,2816]{1,0:T(8,128)(2,1)S(1)} collective-permute-done((bf16[64,2816]{1,0:T(8,128)(2,1)S(1)}, bf16[64,2816]{1,0:T(8,128)(2,1)S(1)}, u32[]{:S(2)}, u32[]{:S(2)}) %collective-permute-start.22) | collective-permute-done | bytes 360480 | tf_op jit(solution)/shard_map/ppermute | solution.py:137
  61.7 10.5 %collective-permute-done.23 = bf16[64,2816]{1,0:T(8,128)(2,1)S(1)} collective-permute-done((bf16[64,2816]{1,0:T(8,128)(2,1)S(1)}, bf16[64,2816]{1,0:T(8,128)(2,1)S(1)}, u32[]{:S(2)}, u32[]{:S(2)}) %collective-permute-start.23) | collective-permute-done | bytes 360480 | tf_op jit(solution)/shard_map/ppermute | solution.py:137
  74.0 6.5 %collective-permute-done.16.refs_3_ = bf16[4,64,1024]{2,1,0:T(8,128)(2,1)S(1)} collective-permute-done((bf16[4,64,1024]{2,1,0:T(8,128)(2,1)S(1)}, bf16[4,64,1024]{2,1,0:T(8,128)(2,1)S(1)}, u32[]{:S(2)}, u32[]{:S(2)}) %collective-permute-start.16) | collective-permute-done | bytes 524320 | tf_op jit(solution)/shard_map/ppermute | solution.py:137
  84.0 16.0 %collective-permute-start.19 = (bf16[512,512]{1,0:T(8,128)(2,1)S(1)}, bf16[512,512]{1,0:T(8,128)(2,1)}, u32[]{:S(2)}, u32[]{:S(2)}) collective-permute-start(bf16[512,512]{1,0:T(8,128)(2,1)S(1)} %bitcast.334), channel_id=1, source_target_pairs={{0,16},{16,0},{1,17},{17,1},{2,18},{18,2},{3,19},{19,3},{4,20},{20... | collective-permute-start | bytes 1572872 | tf_op jit(solution)/shard_map/ppermute | solution.py:142
  120.5 4.4 collective-permute-done.27.refs_2_
  129.6 5.8 shard_map.291
  137.5 10.6 %collective-permute-done.31.refs_3_ = bf16[704,512]{1,0:T(8,128)(2,1)S(1)} collective-permute-done((bf16[704,512]{1,0:T(8,128)(2,1)}, bf16[704,512]{1,0:T(8,128)(2,1)S(1)}, u32[]{:S(2)}, u32[]{:S(2)}) %collective-permute-start.31) | collective-permute-done | bytes 720928 | tf_op jit(solution)/shard_map/ppermute | solution.py:137
  156.9 6.1 collective-permute-done.35
  165.3 2.8 shard_map.292
  172.2 3.4 convolution_convert_fusion.1
  175.6 4.6 collective-permute-done.39
  185.7 8.9 %collective-permute-start.41 = (bf16[512,1024]{1,0:T(8,128)(2,1)S(1)}, bf16[512,1024]{1,0:T(8,128)(2,1)S(1)}, u32[]{:S(2)}, u32[]{:S(2)}) collective-permute-start(bf16[512,1024]{1,0:T(8,128)(2,1)S(1)} %convolution_convert_fusion.13), channel_id=1, source_target_pairs={{0,16},{16,0},{1,17},{17,1},{2,18},{18,2},{3,19},{19,3},{4,20},{20... | collective-permute-start | bytes 3145736 | tf_op jit(solution)/shard_map/ppermute | solution.py:142
  196.4 7.3 %collective-permute-done.47 = bf16[64,2816]{1,0:T(8,128)(2,1)S(1)} collective-permute-done((bf16[64,2816]{1,0:T(8,128)(2,1)S(1)}, bf16[64,2816]{1,0:T(8,128)(2,1)S(1)}, u32[]{:S(2)}, u32[]{:S(2)}) %collective-permute-start.47) | collective-permute-done | bytes 360480 | tf_op jit(solution)/shard_map/ppermute | solution.py:137
  205.7 4.4 collective-permute-start.49
  211.1 2.8 collective-permute-start.51
  217.2 4.4 collective-permute-done.50.refs_1_
  224.6 5.8 shard_map.296
  232.2 3.6 collective-permute-start.52
  235.9 3.2 collective-permute-start.54
  241.9 13.9 %collective-permute-done.54.refs_2_ = bf16[4,64,1408]{2,1,0:T(8,128)(2,1)} collective-permute-done((bf16[4,64,1408]{2,1,0:T(8,128)(2,1)}, bf16[4,64,1408]{2,1,0:T(8,128)(2,1)}, u32[]{:S(2)}, u32[]{:S(2)}) %collective-permute-start.54) | collective-permute-done | bytes 720928 | tf_op jit(solution)/shard_map/ppermute | solution.py:137
  257.1 11.0 %shard_map.299 = (bf16[2,704,512]{2,1,0:T(8,128)(2,1)S(1)}, bf16[2,704,512]{2,1,0:T(8,128)(2,1)S(1)}) custom-call(s32[4]{0:T(128)S(1)} %copy-done.55, bf16[704,512]{1,0:T(8,128)(2,1)S(1)} %bitcast.319, bf16[704,512]{1,0:T(8,128)(2,1)S(1)} %copy-done.24, bf16[704,512]{1,0:T(8,128)(2,1)} %collective-permute-done.55.refs_2_, ...), custom_call_target="tpu_custom_call" | custom-call | tf_op jit(solution)/shard_map/pallas_call | solution.py:41
  268.1 3.0 collective-permute-start.59
  275.4 3.5 shard_map.298
  278.9 4.5 convolution_convert_fusion
  285.6 3.2 fusion.6
  288.7 3.2 convolution_convert_fusion.11
  292.4 2.8 convolution_convert_fusion.12
  301.6 5.4 shard_map.301
  308.1 2.9 collective-permute-start.65
  314.6 10.2 %collective-permute-done.64 = bf16[4,64,1408]{2,1,0:T(8,128)(2,1)S(1)} collective-permute-done((bf16[4,64,1408]{2,1,0:T(8,128)(2,1)S(1)}, bf16[4,64,1408]{2,1,0:T(8,128)(2,1)S(1)}, u32[]{:S(2)}, u32[]{:S(2)}) %collective-permute-start.64) | collective-permute-done | bytes 720928 | tf_op jit(solution)/shard_map/ppermute | solution.py:137
  331.5 10.0 %shard_map.302 = (bf16[512,1536]{1,0:T(8,128)(2,1)S(1)}, f32[512,256]{1,0:T(8,128)S(1)}, f32[1,256]{1,0:T(1,128)S(1)}) custom-call(bf16[512,1536]{1,0:T(8,128)(2,1)S(1)} %copy-done.3, f32[512,256]{1,0:T(8,128)S(1)} %convolution_add_fusion.logits_ref, f32[1,256]{1,0:T(1,128)S(1)} %reshape.362.gain_ref, bf16[512,512]{1,0:T(8,128)(2,1)S(1)} %convolution_convert_fusion.21.dg_ref), custom_call_target="tpu_custom_call" | custom-call | tf_op jit(solution)/shard_map/pallas_call | solution.py:637
  343.8 4.4 collective-permute-done.69
  364.5 4.4 shard_map.303
  375.1 4.3 shard_map.304
  380.4 9.7 %collective-permute-done.74 = bf16[704,512]{1,0:T(8,128)(2,1)} collective-permute-done((bf16[704,512]{1,0:T(8,128)(2,1)}, bf16[704,512]{1,0:T(8,128)(2,1)}, u32[]{:S(2)}, u32[]{:S(2)}) %collective-permute-start.74) | collective-permute-done | bytes 720928 | tf_op jit(solution)/shard_map/ppermute | solution.py:137
  390.6 3.6 fusion.46
  399.2 4.3 fusion.9
  411.7 9.6 %collective-permute-done.80.x1 = bf16[4,64,1024]{2,1,0:T(8,128)(2,1)S(1)} collective-permute-done((bf16[4,64,1024]{2,1,0:T(8,128)(2,1)S(1)}, bf16[4,64,1024]{2,1,0:T(8,128)(2,1)S(1)}, u32[]{:S(2)}, u32[]{:S(2)}) %collective-permute-start.80) | collective-permute-done | bytes 524320 | tf_op jit(solution)/shard_map/ppermute | solution.py:137
  423.7 10.3 %collective-permute-done.84.x2 = bf16[4,64,1024]{2,1,0:T(8,128)(2,1)S(1)} collective-permute-done((bf16[4,64,1024]{2,1,0:T(8,128)(2,1)S(1)}, bf16[4,64,1024]{2,1,0:T(8,128)(2,1)S(1)}, u32[]{:S(2)}, u32[]{:S(2)}) %collective-permute-start.84) | collective-permute-done | bytes 524320 | tf_op jit(solution)/shard_map/ppermute | solution.py:137
  435.0 4.0 shard_map.307
  442.2 6.0 collective-permute-done.89
  450.8 5.2 shard_map.306
  458.6 3.2 convolution_convert_fusion.10
  461.8 4.9 collective-permute-start.79
  478.7 4.6 collective-permute-start.83
  492.8 9.9 %shard_map.305 = (bf16[512,1536]{1,0:T(8,128)(2,1)S(1)}, f32[512,256]{1,0:T(8,128)S(1)}, f32[1,256]{1,0:T(1,128)S(1)}) custom-call(bf16[512,1536]{1,0:T(8,128)(2,1)S(1)} %copy-done.1, f32[512,256]{1,0:T(8,128)S(1)} %convolution_add_fusion.1.logits_ref, f32[1,256]{1,0:T(1,128)S(1)} %reshape.358.gain_ref, bf16[512,512]{1,0:T(8,128)(2,1)S(1)} %convolution_convert_fusion.20.dg_ref), custom_call_target="tpu_custom_call" | custom-call | tf_op jit(solution)/shard_map/pallas_call | solution.py:637
  505.9 3.7 add_convert_fusion.1
  526.0 3.8 shard_map.308
  529.8 4.6 collective-permute-done.100.refs_2_
  535.6 3.2 fusion.52
  542.5 3.4 collective-permute-start.110
  555.0 6.2 collective-permute-done.102.refs_5_
  567.9 4.0 collective-permute-done.103.refs_2_
  572.9 3.2 collective-permute-done.122
  581.5 3.3 fusion.32
  585.4 3.1 collective-permute-start.113
  598.2 8.5 %collective-permute-start.117 = (bf16[64,2816]{1,0:T(8,128)(2,1)S(1)}, bf16[64,2816]{1,0:T(8,128)(2,1)S(1)}, u32[]{:S(2)}, u32[]{:S(2)}) collective-permute-start(bf16[64,2816]{1,0:T(8,128)(2,1)S(1)} %get-tuple-element.582), channel_id=1, source_target_pairs={{0,16},{16,0},{1,17},{17,1},{2,18},{18,2},{3,19},{19,3},{4,20},{20... | collective-permute-start | bytes 1081352 | tf_op jit(solution)/shard_map/ppermute | solution.py:142
  607.1 3.0 collective-permute-done.128
  610.5 11.1 %collective-permute-done.114 = bf16[64,2176]{1,0:T(8,128)(2,1)S(1)} collective-permute-done((bf16[64,2176]{1,0:T(8,128)(2,1)S(1)}, bf16[64,2176]{1,0:T(8,128)(2,1)S(1)}, u32[]{:S(2)}, u32[]{:S(2)}) %collective-permute-start.114) | collective-permute-done | bytes 278560 | tf_op jit(solution)/shard_map/ppermute | solution.py:137
  625.6 5.6 collective-permute-done.115
  (767 shorter events, 265.4 us)
Async XLA Ops:
  6.9 14.7 %collective-permute-start.20 = (bf16[64,2816]{1,0:T(8,128)(2,1)}, bf16[64,2816]{1,0:T(8,128)(2,1)S(1)}, u32[]{:S(2)}, u32[]{:S(2)}) collective-permute-start(bf16[64,2816]{1,0:T(8,128)(2,1)} %get-tuple-element.291), channel_id=1, source_target_pairs={{0,16},{16,0},{1,17},{17,1},{2,18},{18,2},{3,19},{19,3},{4,20},{20... | collective-permute-start | bytes 1081352 | tf_op jit(solution)/shard_map/ppermute | solution.py:142
  52.2 20.0 %collective-permute-start.17 = (bf16[4,64,1152]{2,1,0:T(8,128)(2,1)S(1)}, bf16[4,64,1152]{2,1,0:T(8,128)(2,1)S(1)}, u32[]{:S(2)}, u32[]{:S(2)}) collective-permute-start(bf16[4,64,1152]{2,1,0:T(8,128)(2,1)S(1)} %pad_maximum_fusion.6.refs_4_), channel_id=1, source_target_pairs={{0,1},{1,0},{2,3},{3,2},{4,5},{5,4},{6,7},{7,6},{8,9},{9,8},{10,11... | collective-permute-start | bytes 1769480 | tf_op jit(solution)/shard_map/ppermute | solution.py:137
  53.5 18.7 %collective-permute-start.15 = (bf16[4,64,1024]{2,1,0:T(8,128)(2,1)S(1)}, bf16[4,64,1024]{2,1,0:T(8,128)(2,1)S(1)}, u32[]{:S(2)}, u32[]{:S(2)}) collective-permute-start(bf16[4,64,1024]{2,1,0:T(8,128)(2,1)S(1)} %pad_maximum_fusion.7.refs_0_), channel_id=1, source_target_pairs={{0,2},{1,3},{2,0},{3,1},{4,6},{5,7},{6,4},{7,5},{8,10},{9,11},{10,... | collective-permute-start | bytes 1572872 | tf_op jit(solution)/shard_map/ppermute | solution.py:137
  72.2 33.2 %collective-permute-start.26 = (bf16[704,512]{1,0:T(8,128)(2,1)}, bf16[704,512]{1,0:T(8,128)(2,1)}, u32[]{:S(2)}, u32[]{:S(2)}) collective-permute-start(bf16[704,512]{1,0:T(8,128)(2,1)} %bitcast.33.refs_0_), channel_id=1, source_target_pairs={{0,4},{1,5},{2,6},{3,7},{4,8},{5,9},{6,10},{7,11},{8,12},{9,13},{1... | collective-permute-start | bytes 2162696 | tf_op jit(solution)/shard_map/ppermute | solution.py:137
  80.5 35.0 %collective-permute-start.25 = (bf16[4,64,1408]{2,1,0:T(8,128)(2,1)S(1)}, bf16[4,64,1408]{2,1,0:T(8,128)(2,1)}, u32[]{:S(2)}, u32[]{:S(2)}) collective-permute-start(bf16[4,64,1408]{2,1,0:T(8,128)(2,1)S(1)} %pad_maximum_fusion.3.refs_4_), channel_id=1, source_target_pairs={{0,2},{1,3},{2,0},{3,1},{4,6},{5,7},{6,4},{7,5},{8,10},{9,11},{10,... | collective-permute-start | bytes 2162696 | tf_op jit(solution)/shard_map/ppermute | solution.py:137
  84.0 29.0 %collective-permute-start.19 = (bf16[512,512]{1,0:T(8,128)(2,1)S(1)}, bf16[512,512]{1,0:T(8,128)(2,1)}, u32[]{:S(2)}, u32[]{:S(2)}) collective-permute-start(bf16[512,512]{1,0:T(8,128)(2,1)S(1)} %bitcast.334), channel_id=1, source_target_pairs={{0,16},{16,0},{1,17},{17,1},{2,18},{18,2},{3,19},{19,3},{4,20},{20... | collective-permute-start | bytes 1572872 | tf_op jit(solution)/shard_map/ppermute | solution.py:142
  101.2 17.9 %collective-permute-start.24 = (bf16[4,64,1408]{2,1,0:T(8,128)(2,1)S(1)}, bf16[4,64,1408]{2,1,0:T(8,128)(2,1)S(1)}, u32[]{:S(2)}, u32[]{:S(2)}) collective-permute-start(bf16[4,64,1408]{2,1,0:T(8,128)(2,1)S(1)} %pad_maximum_fusion.2.refs_0_), channel_id=1, source_target_pairs={{0,1},{1,0},{2,3},{3,2},{4,5},{5,4},{6,7},{7,6},{8,9},{9,8},{10,11... | collective-permute-start | bytes 2162696 | tf_op jit(solution)/shard_map/ppermute | solution.py:137
  105.4 19.6 %collective-permute-start.27 = (bf16[704,512]{1,0:T(8,128)(2,1)}, bf16[704,512]{1,0:T(8,128)(2,1)}, u32[]{:S(2)}, u32[]{:S(2)}) collective-permute-start(bf16[704,512]{1,0:T(8,128)(2,1)} %collective-permute-done.26.refs_1_), channel_id=1, source_target_pairs={{0,4},{1,5},{2,6},{3,7},{4,8},{5,9},{6,10},{7,11},{8,12},{9,13},{1... | collective-permute-start | bytes 2162696 | tf_op jit(solution)/shard_map/ppermute | solution.py:137
  115.5 32.7 %collective-permute-start.30 = (bf16[4,64,1408]{2,1,0:T(8,128)(2,1)S(1)}, bf16[4,64,1408]{2,1,0:T(8,128)(2,1)S(1)}, u32[]{:S(2)}, u32[]{:S(2)}) collective-permute-start(bf16[4,64,1408]{2,1,0:T(8,128)(2,1)S(1)} %pad_maximum_fusion.2.refs_0_), channel_id=1, source_target_pairs={{0,2},{1,3},{2,0},{3,1},{4,6},{5,7},{6,4},{7,5},{8,10},{9,11},{10,... | collective-permute-start | bytes 2162696 | tf_op jit(solution)/shard_map/ppermute | solution.py:137
  119.1 30.7 %collective-permute-start.29 = (bf16[4,64,1408]{2,1,0:T(8,128)(2,1)S(1)}, bf16[4,64,1408]{2,1,0:T(8,128)(2,1)S(1)}, u32[]{:S(2)}, u32[]{:S(2)}) collective-permute-start(bf16[4,64,1408]{2,1,0:T(8,128)(2,1)S(1)} %pad_maximum_fusion.3.refs_4_), channel_id=1, source_target_pairs={{0,1},{1,0},{2,3},{3,2},{4,5},{5,4},{6,7},{7,6},{8,9},{9,8},{10,11... | collective-permute-start | bytes 2162696 | tf_op jit(solution)/shard_map/ppermute | solution.py:137
  129.6 18.6 %collective-permute-start.31 = (bf16[704,512]{1,0:T(8,128)(2,1)}, bf16[704,512]{1,0:T(8,128)(2,1)S(1)}, u32[]{:S(2)}, u32[]{:S(2)}) collective-permute-start(bf16[704,512]{1,0:T(8,128)(2,1)} %collective-permute-done.27.refs_2_), channel_id=1, source_target_pairs={{0,4},{1,5},{2,6},{3,7},{4,8},{5,9},{6,10},{7,11},{8,12},{9,13},{1... | collective-permute-start | bytes 2162696 | tf_op jit(solution)/shard_map/ppermute | solution.py:137
  136.3 19.7 %collective-permute-start.28 = (bf16[512,1024]{1,0:T(8,128)(2,1)S(1)}, bf16[512,1024]{1,0:T(8,128)(2,1)S(1)}, u32[]{:S(2)}, u32[]{:S(2)}) collective-permute-start(bf16[512,1024]{1,0:T(8,128)(2,1)S(1)} %convolution_convert_fusion.15), channel_id=1, source_target_pairs={{0,16},{16,0},{1,17},{17,1},{2,18},{18,2},{3,19},{19,3},{4,20},{20... | collective-permute-start | bytes 3145736 | tf_op jit(solution)/shard_map/ppermute | solution.py:142
  148.3 15.7 %collective-permute-start.33 = (bf16[4,64,1408]{2,1,0:T(8,128)(2,1)S(1)}, bf16[4,64,1408]{2,1,0:T(8,128)(2,1)S(1)}, u32[]{:S(2)}, u32[]{:S(2)}) collective-permute-start(bf16[4,64,1408]{2,1,0:T(8,128)(2,1)S(1)} %copy-done.38), channel_id=1, source_target_pairs={{0,2},{1,3},{2,0},{3,1},{4,6},{5,7},{6,4},{7,5},{8,10},{9,11},{10,... | collective-permute-start | bytes 2162696 | tf_op jit(solution)/shard_map/ppermute | solution.py:137
  149.8 15.5 %collective-permute-start.34 = (bf16[4,64,1408]{2,1,0:T(8,128)(2,1)}, bf16[4,64,1408]{2,1,0:T(8,128)(2,1)S(1)}, u32[]{:S(2)}, u32[]{:S(2)}) collective-permute-start(bf16[4,64,1408]{2,1,0:T(8,128)(2,1)} %collective-permute-done.25.refs_6_), channel_id=1, source_target_pairs={{0,1},{1,0},{2,3},{3,2},{4,5},{5,4},{6,7},{7,6},{8,9},{9,8},{10,11... | collective-permute-start | bytes 2162696 | tf_op jit(solution)/shard_map/ppermute | solution.py:137
  152.3 30.4 %collective-permute-start.40 = (bf16[1408,512]{1,0:T(8,128)(2,1)S(1)}, bf16[1408,512]{1,0:T(8,128)(2,1)S(1)}, u32[]{:S(2)}, u32[]{:S(2)}) collective-permute-start(bf16[1408,512]{1,0:T(8,128)(2,1)S(1)} %bitcast.332), channel_id=1, source_target_pairs={{0,16},{16,0},{1,17},{17,1},{2,18},{18,2},{3,19},{19,3},{4,20},{20... | collective-permute-start | bytes 4325384 | tf_op jit(solution)/shard_map/ppermute | solution.py:142
  180.2 14.3 %collective-permute-start.44 = (bf16[64,2816]{1,0:T(8,128)(2,1)S(1)}, bf16[64,2816]{1,0:T(8,128)(2,1)S(1)}, u32[]{:S(2)}, u32[]{:S(2)}) collective-permute-start(bf16[64,2816]{1,0:T(8,128)(2,1)S(1)} %collective-permute-done.39), channel_id=1, source_target_pairs={{0,4},{1,5},{2,6},{3,7},{4,8},{5,9},{6,10},{7,11},{8,12},{9,13},{1... | collective-permute-start | bytes 1081352 | tf_op jit(solution)/shard_map/ppermute | solution.py:137
  181.4 15.0 %collective-permute-start.42 = (bf16[4,64,1024]{2,1,0:T(8,128)(2,1)S(1)}, bf16[4,64,1024]{2,1,0:T(8,128)(2,1)S(1)}, u32[]{:S(2)}, u32[]{:S(2)}) collective-permute-start(bf16[4,64,1024]{2,1,0:T(8,128)(2,1)S(1)} %pad_maximum_fusion.9.refs_4_), channel_id=1, source_target_pairs={{0,1},{1,0},{2,3},{3,2},{4,5},{5,4},{6,7},{7,6},{8,9},{9,8},{10,11... | collective-permute-start | bytes 1572872 | tf_op jit(solution)/shard_map/ppermute | solution.py:137
  185.7 28.2 %collective-permute-start.41 = (bf16[512,1024]{1,0:T(8,128)(2,1)S(1)}, bf16[512,1024]{1,0:T(8,128)(2,1)S(1)}, u32[]{:S(2)}, u32[]{:S(2)}) collective-permute-start(bf16[512,1024]{1,0:T(8,128)(2,1)S(1)} %convolution_convert_fusion.13), channel_id=1, source_target_pairs={{0,16},{16,0},{1,17},{17,1},{2,18},{18,2},{3,19},{19,3},{4,20},{20... | collective-permute-start | bytes 3145736 | tf_op jit(solution)/shard_map/ppermute | solution.py:142
  203.7 17.9 %collective-permute-start.50 = (bf16[704,512]{1,0:T(8,128)(2,1)S(1)}, bf16[704,512]{1,0:T(8,128)(2,1)S(1)}, u32[]{:S(2)}, u32[]{:S(2)}) collective-permute-start(bf16[704,512]{1,0:T(8,128)(2,1)S(1)} %bitcast.318), channel_id=1, source_target_pairs={{0,4},{1,5},{2,6},{3,7},{4,8},{5,9},{6,10},{7,11},{8,12},{9,13},{1... | collective-permute-start | bytes 2162696 | tf_op jit(solution)/shard_map/ppermute | solution.py:137
  205.7 18.9 %collective-permute-start.48 = (bf16[4,64,1408]{2,1,0:T(8,128)(2,1)}, bf16[4,64,1408]{2,1,0:T(8,128)(2,1)S(1)}, u32[]{:S(2)}, u32[]{:S(2)}) collective-permute-start(bf16[4,64,1408]{2,1,0:T(8,128)(2,1)} %pad_maximum_fusion.4.refs_0_), channel_id=1, source_target_pairs={{0,1},{1,0},{2,3},{3,2},{4,5},{5,4},{6,7},{7,6},{8,9},{9,8},{10,11... | collective-permute-start | bytes 2162696 | tf_op jit(solution)/shard_map/ppermute | solution.py:137
  205.7 18.9 %collective-permute-start.49 = (bf16[4,64,1408]{2,1,0:T(8,128)(2,1)}, bf16[4,64,1408]{2,1,0:T(8,128)(2,1)S(1)}, u32[]{:S(2)}, u32[]{:S(2)}) collective-permute-start(bf16[4,64,1408]{2,1,0:T(8,128)(2,1)} %pad_maximum_fusion.5.refs_4_), channel_id=1, source_target_pairs={{0,2},{1,3},{2,0},{3,1},{4,6},{5,7},{6,4},{7,5},{8,10},{9,11},{10,... | collective-permute-start | bytes 2162696 | tf_op jit(solution)/shard_map/ppermute | solution.py:137
  221.6 17.5 %collective-permute-start.55 = (bf16[704,512]{1,0:T(8,128)(2,1)S(1)}, bf16[704,512]{1,0:T(8,128)(2,1)}, u32[]{:S(2)}, u32[]{:S(2)}) collective-permute-start(bf16[704,512]{1,0:T(8,128)(2,1)S(1)} %collective-permute-done.50.refs_1_), channel_id=1, source_target_pairs={{0,4},{1,5},{2,6},{3,7},{4,8},{5,9},{6,10},{7,11},{8,12},{9,13},{1... | collective-permute-start | bytes 2162696 | tf_op jit(solution)/shard_map/ppermute | solution.py:137
  232.2 39.0 %collective-permute-start.52 = (bf16[512,1024]{1,0:T(8,128)(2,1)}, bf16[512,1024]{1,0:T(8,128)(2,1)}, u32[]{:S(2)}, u32[]{:S(2)}) collective-permute-start(bf16[512,1024]{1,0:T(8,128)(2,1)} %convolution_convert_fusion.14), channel_id=1, source_target_pairs={{0,16},{16,0},{1,17},{17,1},{2,18},{18,2},{3,19},{19,3},{4,20},{20... | collective-permute-start | bytes 3145736 | tf_op jit(solution)/shard_map/ppermute | solution.py:142
  235.9 20.0 %collective-permute-start.54 = (bf16[4,64,1408]{2,1,0:T(8,128)(2,1)}, bf16[4,64,1408]{2,1,0:T(8,128)(2,1)}, u32[]{:S(2)}, u32[]{:S(2)}) collective-permute-start(bf16[4,64,1408]{2,1,0:T(8,128)(2,1)} %pad_maximum_fusion.4.refs_0_), channel_id=1, source_target_pairs={{0,2},{1,3},{2,0},{3,1},{4,6},{5,7},{6,4},{7,5},{8,10},{9,11},{10,... | collective-permute-start | bytes 2162696 | tf_op jit(solution)/shard_map/ppermute | solution.py:137
  239.1 18.0 %collective-permute-start.53 = (bf16[4,64,1408]{2,1,0:T(8,128)(2,1)}, bf16[4,64,1408]{2,1,0:T(8,128)(2,1)}, u32[]{:S(2)}, u32[]{:S(2)}) collective-permute-start(bf16[4,64,1408]{2,1,0:T(8,128)(2,1)} %pad_maximum_fusion.5.refs_4_), channel_id=1, source_target_pairs={{0,1},{1,0},{2,3},{3,2},{4,5},{5,4},{6,7},{7,6},{8,9},{9,8},{10,11... | collective-permute-start | bytes 2162696 | tf_op jit(solution)/shard_map/ppermute | solution.py:137
  239.1 18.0 %collective-permute-start.58 = (bf16[704,512]{1,0:T(8,128)(2,1)}, bf16[704,512]{1,0:T(8,128)(2,1)}, u32[]{:S(2)}, u32[]{:S(2)}) collective-permute-start(bf16[704,512]{1,0:T(8,128)(2,1)} %collective-permute-done.55.refs_2_), channel_id=1, source_target_pairs={{0,4},{1,5},{2,6},{3,7},{4,8},{5,9},{6,10},{7,11},{8,12},{9,13},{1... | collective-permute-start | bytes 2162696 | tf_op jit(solution)/shard_map/ppermute | solution.py:137
  255.8 18.5 %collective-permute-start.56 = (bf16[4,64,1408]{2,1,0:T(8,128)(2,1)}, bf16[4,64,1408]{2,1,0:T(8,128)(2,1)S(1)}, u32[]{:S(2)}, u32[]{:S(2)}) collective-permute-start(bf16[4,64,1408]{2,1,0:T(8,128)(2,1)} %copy-done.25), channel_id=1, source_target_pairs={{0,2},{1,3},{2,0},{3,1},{4,6},{5,7},{6,4},{7,5},{8,10},{9,11},{10,... | collective-permute-start | bytes 2162696 | tf_op jit(solution)/shard_map/ppermute | solution.py:137
  257.1 17.2 %collective-permute-start.57 = (bf16[4,64,1408]{2,1,0:T(8,128)(2,1)}, bf16[4,64,1408]{2,1,0:T(8,128)(2,1)S(1)}, u32[]{:S(2)}, u32[]{:S(2)}) collective-permute-start(bf16[4,64,1408]{2,1,0:T(8,128)(2,1)} %copy-done.27), channel_id=1, source_target_pairs={{0,1},{1,0},{2,3},{3,2},{4,5},{5,4},{6,7},{7,6},{8,9},{9,8},{10,11... | collective-permute-start | bytes 2162696 | tf_op jit(solution)/shard_map/ppermute | solution.py:137
  268.1 15.3 %collective-permute-start.59 = (bf16[1408,512]{1,0:T(8,128)(2,1)S(1)}, bf16[1408,512]{1,0:T(8,128)(2,1)S(1)}, u32[]{:S(2)}, u32[]{:S(2)}) collective-permute-start(bf16[1408,512]{1,0:T(8,128)(2,1)S(1)} %bitcast.333), channel_id=1, source_target_pairs={{0,16},{16,0},{1,17},{17,1},{2,18},{18,2},{3,19},{19,3},{4,20},{20... | collective-permute-start | bytes 4325384 | tf_op jit(solution)/shard_map/ppermute | solution.py:142
  295.3 240.3 %collective-permute-start.60 = (bf16[512,1024]{1,0:T(8,128)(2,1)}, bf16[512,1024]{1,0:T(8,128)(2,1)}, u32[]{:S(2)}, u32[]{:S(2)}) collective-permute-start(bf16[512,1024]{1,0:T(8,128)(2,1)} %convolution_convert_fusion.12), channel_id=1, source_target_pairs={{0,16},{16,0},{1,17},{17,1},{2,18},{18,2},{3,19},{19,3},{4,20},{20... | collective-permute-start | bytes 3145736 | tf_op jit(solution)/shard_map/ppermute | solution.py:142
  307.1 17.8 %collective-permute-start.64 = (bf16[4,64,1408]{2,1,0:T(8,128)(2,1)S(1)}, bf16[4,64,1408]{2,1,0:T(8,128)(2,1)S(1)}, u32[]{:S(2)}, u32[]{:S(2)}) collective-permute-start(bf16[4,64,1408]{2,1,0:T(8,128)(2,1)S(1)} %get-tuple-element.369), channel_id=1, source_target_pairs={{0,1},{1,0},{2,3},{3,2},{4,5},{5,4},{6,7},{7,6},{8,9},{9,8},{10,11... | collective-permute-start | bytes 2162696 | tf_op jit(solution)/shard_map/ppermute | solution.py:137
  308.1 19.0 %collective-permute-start.65 = (bf16[4,64,1408]{2,1,0:T(8,128)(2,1)S(1)}, bf16[4,64,1408]{2,1,0:T(8,128)(2,1)S(1)}, u32[]{:S(2)}, u32[]{:S(2)}) collective-permute-start(bf16[4,64,1408]{2,1,0:T(8,128)(2,1)S(1)} %get-tuple-element.371), channel_id=1, source_target_pairs={{0,2},{1,3},{2,0},{3,1},{4,6},{5,7},{6,4},{7,5},{8,10},{9,11},{10,... | collective-permute-start | bytes 2162696 | tf_op jit(solution)/shard_map/ppermute | solution.py:137
  311.3 18.8 %collective-permute-start.66 = (bf16[704,512]{1,0:T(8,128)(2,1)S(1)}, bf16[704,512]{1,0:T(8,128)(2,1)S(1)}, u32[]{:S(2)}, u32[]{:S(2)}) collective-permute-start(bf16[704,512]{1,0:T(8,128)(2,1)S(1)} %dynamic-slice_select_fusion.1), channel_id=1, source_target_pairs={{0,4},{1,5},{2,6},{3,7},{4,8},{5,9},{6,10},{7,11},{8,12},{9,13},{1... | collective-permute-start | bytes 2162696 | tf_op jit(solution)/shard_map/ppermute | solution.py:137
  311.8 19.6 %collective-permute-start.62 = (bf16[512,512]{1,0:T(8,128)(2,1)S(1)}, bf16[512,512]{1,0:T(8,128)(2,1)S(1)}, u32[]{:S(2)}, u32[]{:S(2)}) collective-permute-start(bf16[512,512]{1,0:T(8,128)(2,1)S(1)} %convolution_convert_fusion.18), channel_id=1, source_target_pairs={{0,16},{16,0},{1,17},{17,1},{2,18},{18,2},{3,19},{19,3},{4,20},{20... | collective-permute-start | bytes 1572872 | tf_op jit(solution)/shard_map/ppermute | solution.py:142
  324.9 17.6 %collective-permute-start.67 = (bf16[4,64,1408]{2,1,0:T(8,128)(2,1)S(1)}, bf16[4,64,1408]{2,1,0:T(8,128)(2,1)S(1)}, u32[]{:S(2)}, u32[]{:S(2)}) collective-permute-start(bf16[4,64,1408]{2,1,0:T(8,128)(2,1)S(1)} %get-tuple-element.381), channel_id=1, source_target_pairs={{0,1},{1,0},{2,3},{3,2},{4,5},{5,4},{6,7},{7,6},{8,9},{9,8},{10,11... | collective-permute-start | bytes 2162696 | tf_op jit(solution)/shard_map/ppermute | solution.py:137
  327.2 16.6 %collective-permute-start.68 = (bf16[4,64,1408]{2,1,0:T(8,128)(2,1)S(1)}, bf16[4,64,1408]{2,1,0:T(8,128)(2,1)S(1)}, u32[]{:S(2)}, u32[]{:S(2)}) collective-permute-start(bf16[4,64,1408]{2,1,0:T(8,128)(2,1)S(1)} %get-tuple-element.383), channel_id=1, source_target_pairs={{0,2},{1,3},{2,0},{3,1},{4,6},{5,7},{6,4},{7,5},{8,10},{9,11},{10,... | collective-permute-start | bytes 2162696 | tf_op jit(solution)/shard_map/ppermute | solution.py:137
  330.3 17.9 %collective-permute-start.69 = (bf16[704,512]{1,0:T(8,128)(2,1)S(1)}, bf16[704,512]{1,0:T(8,128)(2,1)S(1)}, u32[]{:S(2)}, u32[]{:S(2)}) collective-permute-start(bf16[704,512]{1,0:T(8,128)(2,1)S(1)} %add_convert_fusion.15), channel_id=1, source_target_pairs={{0,4},{1,5},{2,6},{3,7},{4,8},{5,9},{6,10},{7,11},{8,12},{9,13},{1... | collective-permute-start | bytes 2162696 | tf_op jit(solution)/shard_map/ppermute | solution.py:137
  350.6 20.8 %collective-permute-start.71 = (bf16[512,16]{0,1:T(8,128)(2,1)}, bf16[512,16]{0,1:T(8,128)(2,1)S(1)}, u32[]{:S(2)}, u32[]{:S(2)}) collective-permute-start(bf16[512,16]{0,1:T(8,128)(2,1)} %convolution_convert_fusion.23), channel_id=1, source_target_pairs={{0,16},{16,0},{1,17},{17,1},{2,18},{18,2},{3,19},{19,3},{4,20},{20... | collective-permute-start | bytes 49160 | tf_op jit(solution)/shard_map/ppermute | solution.py:142
  356.0 34.5 %collective-permute-start.70 = (bf16[512,1024]{1,0:T(8,128)(2,1)}, bf16[512,1024]{1,0:T(8,128)(2,1)}, u32[]{:S(2)}, u32[]{:S(2)}) collective-permute-start(bf16[512,1024]{1,0:T(8,128)(2,1)} %add_convert_fusion.4), channel_id=1, source_target_pairs={{0,16},{16,0},{1,17},{17,1},{2,18},{18,2},{3,19},{19,3},{4,20},{20... | collective-permute-start | bytes 3145736 | tf_op jit(solution)/shard_map/ppermute | solution.py:142
  356.0 17.6 %collective-permute-start.72 = (bf16[4,64,1408]{2,1,0:T(8,128)(2,1)}, bf16[4,64,1408]{2,1,0:T(8,128)(2,1)}, u32[]{:S(2)}, u32[]{:S(2)}) collective-permute-start(bf16[4,64,1408]{2,1,0:T(8,128)(2,1)} %add_convert_fusion.14), channel_id=1, source_target_pairs={{0,1},{1,0},{2,3},{3,2},{4,5},{5,4},{6,7},{7,6},{8,9},{9,8},{10,11... | collective-permute-start | bytes 2162696 | tf_op jit(solution)/shard_map/ppermute | solution.py:137
  357.1 17.6 %collective-permute-start.73 = (bf16[4,64,1408]{2,1,0:T(8,128)(2,1)}, bf16[4,64,1408]{2,1,0:T(8,128)(2,1)}, u32[]{:S(2)}, u32[]{:S(2)}) collective-permute-start(bf16[4,64,1408]{2,1,0:T(8,128)(2,1)} %add_convert_fusion.13), channel_id=1, source_target_pairs={{0,2},{1,3},{2,0},{3,1},{4,6},{5,7},{6,4},{7,5},{8,10},{9,11},{10,... | collective-permute-start | bytes 2162696 | tf_op jit(solution)/shard_map/ppermute | solution.py:137
  371.4 18.8 %collective-permute-start.74 = (bf16[704,512]{1,0:T(8,128)(2,1)}, bf16[704,512]{1,0:T(8,128)(2,1)}, u32[]{:S(2)}, u32[]{:S(2)}) collective-permute-start(bf16[704,512]{1,0:T(8,128)(2,1)} %add_convert_fusion.12), channel_id=1, source_target_pairs={{0,4},{1,5},{2,6},{3,7},{4,8},{5,9},{6,10},{7,11},{8,12},{9,13},{1... | collective-permute-start | bytes 2162696 | tf_op jit(solution)/shard_map/ppermute | solution.py:137
  373.7 34.0 %collective-permute-start.76 = (bf16[4,64,1024]{2,1,0:T(8,128)(2,1)}, bf16[4,64,1024]{2,1,0:T(8,128)(2,1)}, u32[]{:S(2)}, u32[]{:S(2)}) collective-permute-start(bf16[4,64,1024]{2,1,0:T(8,128)(2,1)} %get-tuple-element.404), channel_id=1, source_target_pairs={{0,1},{1,0},{2,3},{3,2},{4,5},{5,4},{6,7},{7,6},{8,9},{9,8},{10,11... | collective-permute-start | bytes 1572872 | tf_op jit(solution)/shard_map/ppermute | solution.py:137
  374.7 33.5 %collective-permute-start.77 = (bf16[4,64,1024]{2,1,0:T(8,128)(2,1)}, bf16[4,64,1024]{2,1,0:T(8,128)(2,1)}, u32[]{:S(2)}, u32[]{:S(2)}) collective-permute-start(bf16[4,64,1024]{2,1,0:T(8,128)(2,1)} %get-tuple-element.406), channel_id=1, source_target_pairs={{0,2},{1,3},{2,0},{3,1},{4,6},{5,7},{6,4},{7,5},{8,10},{9,11},{10,... | collective-permute-start | bytes 1572872 | tf_op jit(solution)/shard_map/ppermute | solution.py:137
  390.1 17.4 %collective-permute-start.78 = (bf16[64,2816]{1,0:T(8,128)(2,1)S(1)}, bf16[64,2816]{1,0:T(8,128)(2,1)S(1)}, u32[]{:S(2)}, u32[]{:S(2)}) collective-permute-start(bf16[64,2816]{1,0:T(8,128)(2,1)S(1)} %slice_bitcast_fusion.3), channel_id=1, source_target_pairs={{0,4},{1,5},{2,6},{3,7},{4,8},{5,9},{6,10},{7,11},{8,12},{9,13},{1... | collective-permute-start | bytes 1081352 | tf_op jit(solution)/shard_map/ppermute | solution.py:137
  405.6 45.2 %collective-permute-start.75 = (bf16[1408,512]{1,0:T(8,128)(2,1)}, bf16[1408,512]{1,0:T(8,128)(2,1)}, u32[]{:S(2)}, u32[]{:S(2)}) collective-permute-start(bf16[1408,512]{1,0:T(8,128)(2,1)} %convolution_convert_fusion.2), channel_id=1, source_target_pairs={{0,16},{16,0},{1,17},{17,1},{2,18},{18,2},{3,19},{19,3},{4,20},{20... | collective-permute-start | bytes 4325384 | tf_op jit(solution)/shard_map/ppermute | solution.py:142
  407.6 15.3 %collective-permute-start.82 = (bf16[64,2816]{1,0:T(8,128)(2,1)S(1)}, bf16[64,2816]{1,0:T(8,128)(2,1)S(1)}, u32[]{:S(2)}, u32[]{:S(2)}) collective-permute-start(bf16[64,2816]{1,0:T(8,128)(2,1)S(1)} %fusion.55), channel_id=1, source_target_pairs={{0,4},{1,5},{2,6},{3,7},{4,8},{5,9},{6,10},{7,11},{8,12},{9,13},{1... | collective-permute-start | bytes 1081352 | tf_op jit(solution)/shard_map/ppermute | solution.py:137
  407.7 13.6 %collective-permute-start.80 = (bf16[4,64,1024]{2,1,0:T(8,128)(2,1)S(1)}, bf16[4,64,1024]{2,1,0:T(8,128)(2,1)S(1)}, u32[]{:S(2)}, u32[]{:S(2)}) collective-permute-start(bf16[4,64,1024]{2,1,0:T(8,128)(2,1)S(1)} %copy-done.63), channel_id=1, source_target_pairs={{0,1},{1,0},{2,3},{3,2},{4,5},{5,4},{6,7},{7,6},{8,9},{9,8},{10,11... | collective-permute-start | bytes 1572872 | tf_op jit(solution)/shard_map/ppermute | solution.py:137
  408.2 13.6 %collective-permute-start.81 = (bf16[4,64,1024]{2,1,0:T(8,128)(2,1)S(1)}, bf16[4,64,1024]{2,1,0:T(8,128)(2,1)S(1)}, u32[]{:S(2)}, u32[]{:S(2)}) collective-permute-start(bf16[4,64,1024]{2,1,0:T(8,128)(2,1)S(1)} %copy-done.61), channel_id=1, source_target_pairs={{0,2},{1,3},{2,0},{3,1},{4,6},{5,7},{6,4},{7,5},{8,10},{9,11},{10,... | collective-permute-start | bytes 1572872 | tf_op jit(solution)/shard_map/ppermute | solution.py:137
  423.7 16.2 %collective-permute-start.86 = (bf16[64,2816]{1,0:T(8,128)(2,1)}, bf16[64,2816]{1,0:T(8,128)(2,1)S(1)}, u32[]{:S(2)}, u32[]{:S(2)}) collective-permute-start(bf16[64,2816]{1,0:T(8,128)(2,1)} %fusion.54), channel_id=1, source_target_pairs={{0,4},{1,5},{2,6},{3,7},{4,8},{5,9},{6,10},{7,11},{8,12},{9,13},{1... | collective-permute-start | bytes 1081352 | tf_op jit(solution)/shard_map/ppermute | solution.py:137
  456.1 15.1 %collective-permute-start.87 = (bf16[4,64,1408]{2,1,0:T(8,128)(2,1)S(1)}, bf16[4,64,1408]{2,1,0:T(8,128)(2,1)S(1)}, u32[]{:S(2)}, u32[]{:S(2)}) collective-permute-start(bf16[4,64,1408]{2,1,0:T(8,128)(2,1)S(1)} %get-tuple-element.434), channel_id=1, source_target_pairs={{0,1},{1,0},{2,3},{3,2},{4,5},{5,4},{6,7},{7,6},{8,9},{9,8},{10,11... | collective-permute-start | bytes 2162696 | tf_op jit(solution)/shard_map/ppermute | solution.py:137
  457.1 15.0 %collective-permute-start.88 = (bf16[4,64,1408]{2,1,0:T(8,128)(2,1)S(1)}, bf16[4,64,1408]{2,1,0:T(8,128)(2,1)S(1)}, u32[]{:S(2)}, u32[]{:S(2)}) collective-permute-start(bf16[4,64,1408]{2,1,0:T(8,128)(2,1)S(1)} %get-tuple-element.436), channel_id=1, source_target_pairs={{0,2},{1,3},{2,0},{3,1},{4,6},{5,7},{6,4},{7,5},{8,10},{9,11},{10,... | collective-permute-start | bytes 2162696 | tf_op jit(solution)/shard_map/ppermute | solution.py:137
  468.0 18.0 %collective-permute-start.107 = (bf16[704,512]{1,0:T(8,128)(2,1)S(1)}, bf16[704,512]{1,0:T(8,128)(2,1)S(1)}, u32[]{:S(2)}, u32[]{:S(2)}) collective-permute-start(bf16[704,512]{1,0:T(8,128)(2,1)S(1)} %dynamic-slice_select_fusion), channel_id=1, source_target_pairs={{0,4},{1,5},{2,6},{3,7},{4,8},{5,9},{6,10},{7,11},{8,12},{9,13},{1... | collective-permute-start | bytes 2162696 | tf_op jit(solution)/shard_map/ppermute | solution.py:137
  471.2 18.8 %collective-permute-start.95 = (bf16[4,64,1408]{2,1,0:T(8,128)(2,1)S(1)}, bf16[4,64,1408]{2,1,0:T(8,128)(2,1)S(1)}, u32[]{:S(2)}, u32[]{:S(2)}) collective-permute-start(bf16[4,64,1408]{2,1,0:T(8,128)(2,1)S(1)} %get-tuple-element.461), channel_id=1, source_target_pairs={{0,1},{1,0},{2,3},{3,2},{4,5},{5,4},{6,7},{7,6},{8,9},{9,8},{10,11... | collective-permute-start | bytes 2162696 | tf_op jit(solution)/shard_map/ppermute | solution.py:137
  472.1 19.0 %collective-permute-start.99 = (bf16[4,64,1408]{2,1,0:T(8,128)(2,1)S(1)}, bf16[4,64,1408]{2,1,0:T(8,128)(2,1)S(1)}, u32[]{:S(2)}, u32[]{:S(2)}) collective-permute-start(bf16[4,64,1408]{2,1,0:T(8,128)(2,1)S(1)} %get-tuple-element.470), channel_id=1, source_target_pairs={{0,2},{1,3},{2,0},{3,1},{4,6},{5,7},{6,4},{7,5},{8,10},{9,11},{10,... | collective-permute-start | bytes 2162696 | tf_op jit(solution)/shard_map/ppermute | solution.py:137
  488.3 29.6 %collective-permute-start.108 = (bf16[704,512]{1,0:T(8,128)(2,1)}, bf16[704,512]{1,0:T(8,128)(2,1)}, u32[]{:S(2)}, u32[]{:S(2)}) collective-permute-start(bf16[704,512]{1,0:T(8,128)(2,1)} %add_convert_fusion.9), channel_id=1, source_target_pairs={{0,4},{1,5},{2,6},{3,7},{4,8},{5,9},{6,10},{7,11},{8,12},{9,13},{1... | collective-permute-start | bytes 2162696 | tf_op jit(solution)/shard_map/ppermute | solution.py:137
  490.8 48.0 %collective-permute-start.96 = (bf16[4,64,1408]{2,1,0:T(8,128)(2,1)}, bf16[4,64,1408]{2,1,0:T(8,128)(2,1)}, u32[]{:S(2)}, u32[]{:S(2)}) collective-permute-start(bf16[4,64,1408]{2,1,0:T(8,128)(2,1)} %add_convert_fusion.11), channel_id=1, source_target_pairs={{0,1},{1,0},{2,3},{3,2},{4,5},{5,4},{6,7},{7,6},{8,9},{9,8},{10,11... | collective-permute-start | bytes 2162696 | tf_op jit(solution)/shard_map/ppermute | solution.py:137
  516.6 17.9 %collective-permute-start.100 = (bf16[4,64,1408]{2,1,0:T(8,128)(2,1)}, bf16[4,64,1408]{2,1,0:T(8,128)(2,1)}, u32[]{:S(2)}, u32[]{:S(2)}) collective-permute-start(bf16[4,64,1408]{2,1,0:T(8,128)(2,1)} %add_convert_fusion.10), channel_id=1, source_target_pairs={{0,2},{1,3},{2,0},{3,1},{4,6},{5,7},{6,4},{7,5},{8,10},{9,11},{10,... | collective-permute-start | bytes 2162696 | tf_op jit(solution)/shard_map/ppermute | solution.py:137
  520.6 21.9 %collective-permute-start.109 = (bf16[704,512]{1,0:T(8,128)(2,1)}, bf16[704,512]{1,0:T(8,128)(2,1)}, u32[]{:S(2)}, u32[]{:S(2)}) collective-permute-start(bf16[704,512]{1,0:T(8,128)(2,1)} %add_convert_fusion.8), channel_id=1, source_target_pairs={{0,4},{1,5},{2,6},{3,7},{4,8},{5,9},{6,10},{7,11},{8,12},{9,13},{1... | collective-permute-start | bytes 2162696 | tf_op jit(solution)/shard_map/ppermute | solution.py:137
  534.5 13.9 %collective-permute-start.101 = (bf16[4,64,1152]{2,1,0:T(8,128)(2,1)S(1)}, bf16[4,64,1152]{2,1,0:T(8,128)(2,1)S(1)}, u32[]{:S(2)}, u32[]{:S(2)}) collective-permute-start(bf16[4,64,1152]{2,1,0:T(8,128)(2,1)S(1)} %get-tuple-element.472), channel_id=1, source_target_pairs={{0,2},{1,3},{2,0},{3,1},{4,6},{5,7},{6,4},{7,5},{8,10},{9,11},{10,... | collective-permute-start | bytes 1769480 | tf_op jit(solution)/shard_map/ppermute | solution.py:137
  552.1 25.2 %collective-permute-start.111 = (bf16[64,2816]{1,0:T(8,128)(2,1)S(1)}, bf16[64,2816]{1,0:T(8,128)(2,1)S(1)}, u32[]{:S(2)}, u32[]{:S(2)}) collective-permute-start(bf16[64,2816]{1,0:T(8,128)(2,1)S(1)} %get-tuple-element.493), channel_id=1, source_target_pairs={{0,8},{1,9},{2,10},{3,11},{4,12},{5,13},{6,14},{7,15},{8,0},{9,1},... | collective-permute-start | bytes 1081352 | tf_op jit(solution)/shard_map/ppermute | solution.py:137
  585.4 21.3 %collective-permute-start.113 = (bf16[64,2176]{1,0:T(8,128)(2,1)S(1)}, bf16[64,2176]{1,0:T(8,128)(2,1)S(1)}, u32[]{:S(2)}, u32[]{:S(2)}) collective-permute-start(bf16[64,2176]{1,0:T(8,128)(2,1)S(1)} %get-tuple-element.495), channel_id=1, source_target_pairs={{0,12},{1,13},{2,14},{3,15},{4,0},{5,1},{6,2},{7,3},{8,4},{9,5},{1... | collective-permute-start | bytes 835592 | tf_op jit(solution)/shard_map/ppermute | solution.py:137
  598.2 24.2 %collective-permute-start.117 = (bf16[64,2816]{1,0:T(8,128)(2,1)S(1)}, bf16[64,2816]{1,0:T(8,128)(2,1)S(1)}, u32[]{:S(2)}, u32[]{:S(2)}) collective-permute-start(bf16[64,2816]{1,0:T(8,128)(2,1)S(1)} %get-tuple-element.582), channel_id=1, source_target_pairs={{0,16},{16,0},{1,17},{17,1},{2,18},{18,2},{3,19},{19,3},{4,20},{20... | collective-permute-start | bytes 1081352 | tf_op jit(solution)/shard_map/ppermute | solution.py:142
  606.7 14.9 %collective-permute-start.114 = (bf16[64,2176]{1,0:T(8,128)(2,1)S(1)}, bf16[64,2176]{1,0:T(8,128)(2,1)S(1)}, u32[]{:S(2)}, u32[]{:S(2)}) collective-permute-start(bf16[64,2176]{1,0:T(8,128)(2,1)S(1)} %get-tuple-element.497), channel_id=1, source_target_pairs={{0,8},{1,9},{2,10},{3,11},{4,12},{5,13},{6,14},{7,15},{8,0},{9,1},... | collective-permute-start | bytes 835592 | tf_op jit(solution)/shard_map/ppermute | solution.py:137
  (230 other events, 2120.7 us)

commit v3 on v2

--- a/solution.py
+++ b/solution.py
@@ -10,7 +10,7 @@
 SPAN = 64
 BF = jnp.bfloat16
 F32 = jnp.float32
-PARAMS = pltpu.CompilerParams(vmem_limit_bytes=40 << 20)
+PARAMS = pltpu.CompilerParams(vmem_limit_bytes=20 << 20)
 FULL = pltpu.CompilerParams(vmem_limit_bytes=60 << 20)
 COST = pl.CostEstimate(flops=0, bytes_accessed=0, transcendentals=0)
 
@@ -125,17 +125,45 @@
     ]
 
 
-class Link:
-    def __init__(self, step, depth=1):
-        self.pairs = pairs(*step)
-        self.depth = depth
-        self.sent = []
-
-    def __call__(self, v, step=None):
-        if len(self.sent) >= self.depth:
-            v = after(v, self.sent[-self.depth])
-        self.sent.append(lax.ppermute(v, "dp", pairs(*step) if step else self.pairs))
-        return self.sent[-1]
+LINES = [[z * 4 + y * 2 + x for z in range(4)] for y in range(2) for x in range(2)]
+
+
+class Links:
+    def __init__(self):
+        self.sent = {"x": [], "y": []}
+        self.open, self.before = [], []
+
+    def hop(self, name, v, step):
+        sent = self.sent[name]
+        if sent:
+            v = after(v, sent[-1], *self.before)
+        sent.append(lax.ppermute(v, "dp", pairs(*step)))
+        return sent[-1]
+
+    def x(self, v):
+        return self.hop("x", v, (0, 0, 1))
+
+    def y(self, v):
+        return self.hop("y", v, (0, 1, 0))
+
+    def gather(self, v, due):
+        v = lax.all_gather(v, "dp", axis=0, tiled=True, axis_index_groups=LINES)
+        self.open.append([due, v])
+        return v
+
+    def scatter(self, v, due):
+        self.before.append(v)
+        v = lax.psum_scatter(v, "dp", scatter_dimension=0, tiled=True, axis_index_groups=LINES)
+        self.open.append([due, v])
+        return v
+
+    def meeting(self):
+        tokens = self.sent["x"][-1:] + self.sent["y"][-1:]
+        for entry in self.open:
+            entry[0] -= 1
+            if entry[0] == 0:
+                tokens.append(entry[1])
+        return tokens
 
 
 def over_core(v):
@@ -163,39 +191,37 @@
 
 class Idle:
     def __getattr__(self, name):
-        return lambda: None
+        return lambda *a: None
 
 
 class GatherWide:
-    def __init__(self, links, shard, half):
-        self.px, self.py, self.pz = links
-        self.slabs, self.half = [shard], half
-
-    def ring(self):
-        self.slabs.append(self.pz(self.slabs[-1]))
-
-    def first(self):
-        h = self.half
-        self.a = jnp.stack([v[:, :h] for v in self.slabs])
-        self.b = jnp.stack([v[:, h:] for v in self.slabs])
-        self.X1, self.Y2 = self.px(self.a), self.py(self.b)
-
-    def second(self):
-        self.X2, self.Y1 = self.px(self.b), self.py(self.a)
-
-    def third(self):
-        self.D2, self.D1 = self.px(self.Y2), self.py(self.X1)
+    def __init__(self, links, shard):
+        self.links, self.shard = links, shard
+
+    def along(self, due, *tokens):
+        v = after(self.shard, *tokens) if tokens else self.shard
+        self.line = self.links.gather(v, due).reshape((4,) + self.shard.shape)
+
+    def along_with(self, other, due, *tokens):
+        R, C = self.shard.shape
+        v = after(jnp.concatenate([self.shard, other.shard.reshape(R, -1)], 1), *tokens)
+        v = self.links.gather(v, due)
+        v = v.reshape(4, R, -1)
+        self.line = v[:, :, :C]
+        other.line = v[:, :, C:].reshape((4,) + other.shard.shape)
+
+    def sides(self):
+        self.X, self.Y = self.links.x(self.line), self.links.y(self.line)
+
+    def diag(self):
+        self.hi, self.lo = self.links.x(self.Y[2:]), self.links.y(self.X[:2])
 
     def parts(self):
-        return [self.a, self.X1, self.Y1, self.D1], [self.b, self.X2, self.Y2, self.D2]
+        return [self.line, self.X, self.Y, self.lo, self.hi]
 
 
 def plane_of(j, a):
     return (2 * a[3] + j) % 4
-
-
-def slab_of(j, a):
-    return (a[0] + 4 - plane_of(j, a)) % 4
 
 
 def place_kernel(columns, split, n_out, at_ref, *refs):
@@ -203,25 +229,31 @@
     j = pl.program_id(0)
     y, x = at_ref[1], at_ref[2]
 
-    def write(h, lo, hi, o, to):
-        for b, (yy, xx) in enumerate(BLOCKS):
-            outs[o][0, y ^ yy, x ^ xx, :, to : to + hi - lo] = ins[4 * h + b][0, :, lo:hi]
-
-    for h, half in enumerate(columns):
-        for lo, hi, o, to in half:
-            if o == split:
-                pl.when(j < 2)(partial(write, h, lo, hi, o, to))
-                pl.when(j >= 2)(partial(write, h, lo, hi, o + 1, to))
-            else:
-                write(h, lo, hi, o, to)
-
-
-def place_blocks(halves_, columns, at, split=None):
-    _, R, _ = halves_[0][0].shape
+    def write(lo, hi, o, to):
+        for (yy, xx), v in zip(BLOCKS, ins[:3]):
+            outs[o][0, y ^ yy, x ^ xx, :, to : to + hi - lo] = v[0, :, lo:hi]
+
+        @pl.when(plane_of(j, at_ref) < 2)
+        def _():
+            outs[o][0, 1 - y, 1 - x, :, to : to + hi - lo] = ins[3][0, :, lo:hi]
+
+        @pl.when(plane_of(j, at_ref) >= 2)
+        def _():
+            outs[o][0, 1 - y, 1 - x, :, to : to + hi - lo] = ins[4][0, :, lo:hi]
+
+    for lo, hi, o, to in columns:
+        if o == split:
+            pl.when(j < 2)(partial(write, lo, hi, o, to))
+            pl.when(j >= 2)(partial(write, lo, hi, o + 1, to))
+        else:
+            write(lo, hi, o, to)
+
+
+def place_blocks(ins, columns, at, split=None):
+    _, R, _ = ins[0].shape
     width = {}
-    for half in columns:
-        for lo, hi, o, to in half:
-            width[o] = max(width.get(o, 0), to + hi - lo)
+    for lo, hi, o, to in columns:
+        width[o] = max(width.get(o, 0), to + hi - lo)
     if split is not None:
         width[split + 1] = width[split]
     shapes, specs = [], []
@@ -236,8 +268,8 @@
         else:
             shapes.append((4,) + block[1:])
             specs.append(pl.BlockSpec(block, lambda j, a: (plane_of(j, a), 0, 0, 0, 0)))
-    ins = list(halves_[0]) + list(halves_[1])
-    in_specs = [pl.BlockSpec((1,) + v.shape[1:], lambda j, a: (slab_of(j, a), 0, 0)) for v in ins]
+    in_specs = [pl.BlockSpec((1,) + v.shape[1:], lambda j, a: (plane_of(j, a), 0, 0)) for v in ins[:3]]
+    in_specs += [pl.BlockSpec((1,) + v.shape[1:], lambda j, a: (plane_of(j, a) % 2, 0, 0)) for v in ins[3:]]
     return copy_call(
         partial(place_kernel, columns, split, len(shapes)), at, ins, in_specs, shapes, specs, (4,)
     )
@@ -245,144 +277,126 @@
 
 class GatherDown:
     def __init__(self, links, shard, at):
-        self.px, self.py, self.pz = links
-        self.shard, self.at = shard, at
-
-    def sides(self):
-        self.X, self.Y = self.px(self.shard), self.py(self.shard)
-
-    def diag(self):
-        R, C = self.shard.shape
+        self.links, self.shard, self.at = links, shard, at
+
+    def around(self):
+        v, links = self.shard, self.links
+        R, C = v.shape
         h = C // 2
         y, x = self.at[1], self.at[2]
-        D2, D1 = self.px(self.Y[:, h:]), self.py(self.X[:, :h])
+        X, Y = links.x(v), links.y(v)
+        D2, D1 = links.x(Y[:, h:]), links.y(X[:, :h])
         out = jnp.zeros((2, 2, R, C), BF)
-        for b, p, c in ((0, self.shard, 0), (1, self.X, 0), (2, self.Y, 0), (3, D1, 0), (3, D2, h)):
+        for b, p, c in ((0, v, 0), (1, X, 0), (2, Y, 0), (3, D1, 0), (3, D2, h)):
             yy, xx = BLOCKS[b]
             out = lax.dynamic_update_slice(out, p[None, None], (y ^ yy, x ^ xx, 0, c))
-        self.slabs = [out.reshape(4 * R, C)]
-
-    def ring(self):
-        self.slabs.append(self.pz(self.slabs[-1]))
-
-
-def split_kernel(at_ref, *refs):
-    ins, keep, give = refs[:4], refs[4], refs[5]
-    j = pl.program_id(0)
-    slab = slab_of(j, at_ref)
-    for i in range(4):
-
-        @pl.when((slab == i) & (j < 2))
-        def _(i=i):
-            keep[0] = ins[i][...]
-
-        @pl.when((slab == i) & (j >= 2))
-        def _(i=i):
-            give[0] = ins[i][...]
-
-
-def split_planes(slabs, at):
-    n, C = slabs[0].shape
-    specs = [
-        pl.BlockSpec((1, n, C), lambda j, a: (jnp.minimum(j, 1), 0, 0)),
-        pl.BlockSpec((1, n, C), lambda j, a: (jnp.maximum(j, 2) - 2, 0, 0)),
-    ]
-    whole = pl.BlockSpec((n, C), lambda j, a: (0, 0))
-    out = copy_call(split_kernel, at, slabs, [whole] * 4, [(2, n, C)] * 2, specs, (4,))
-    return out[0].reshape(2 * n, C), out[1].reshape(2 * n, C)
-
-
-def grad_kernel(half, R, at_ref, lhs_ref, rhs_ref, *refs):
+        self.block = out.reshape(4 * R, C)
+
+    def along(self, due, *tokens):
+        self.all = self.links.gather(after(self.block, *tokens), due)
+
+
+def grad_kernel(R, at_ref, lhs_ref, rhs_ref, *refs):
     acc = refs[-1]
-    extras, outs = refs[:-9], refs[-9:-1]
+    extras, (own, Sx, Sy, Rx, Ry) = refs[:-6], refs[-6:-1]
     C = rhs_ref.shape[1]
     acc[:, :C] = mm_tn(lhs_ref[...], rhs_ref[...])
     i = pl.program_id(0)
-    z, y, x, s = at_ref[0], at_ref[1], at_ref[2], at_ref[3]
+    y, x, s = at_ref[1], at_ref[2], at_ref[3]
     if extras:
-        d = (z + 3 - i) % 4
         keep, got = extras[0][...].astype(F32), extras[1][...].astype(F32)
         W = keep.shape[1]
-        acc[:, C : C + W] = jnp.where((d // 2) == s, keep, got)
+        acc[:, C : C + W] = jnp.where((i // 2) == s, keep, got)
         if len(extras) > 2:
             acc[:, C + W :] = extras[2][...].astype(F32)
-    for b, (yy, xx) in enumerate(BLOCKS):
-        rows = pl.ds(pl.multiple_of(((y ^ yy) * 2 + (x ^ xx)) * R, R), R)
-        outs[2 * b][0] = acc[rows, :half].astype(BF)
-        outs[2 * b + 1][0] = acc[rows, half:].astype(BF)
-
-
-def grad_blocks(lhs, rhs, half, at, extras=()):
+
+    def block(b):
+        yy, xx = BLOCKS[b]
+        return acc[pl.ds(pl.multiple_of(((y ^ yy) * 2 + (x ^ xx)) * R, R), R), :].astype(BF)
+
+    own[0] = block(0)
+
+    @pl.when(i < 2)
+    def _():
+        Sx[0, 0] = block(3)
+        Sx[1, 0] = block(1)
+        Ry[0] = block(2)
+
+    @pl.when(i >= 2)
+    def _():
+        Sy[0, 0] = block(3)
+        Sy[1, 0] = block(2)
+        Rx[0] = block(1)
+
+
+def grad_blocks(lhs, rhs, at, extras=()):
     tokens, D = lhs.shape
-    C = rhs.shape[1]
-    E = sum(e.shape[1] for e in extras[:1] + extras[2:])
+    C = rhs.shape[1] + sum(e.shape[1] for e in extras[:1] + extras[2:])
     n = D // 4
     R = n // 4
-
-    def plane(i, a):
-        return (a[0] + 3 - i) % 4
-
     in_specs = [
-        pl.BlockSpec((tokens, n), lambda i, a: (0, plane(i, a))),
-        pl.BlockSpec((tokens, C), lambda i, a: (0, 0)),
+        pl.BlockSpec((tokens, n), lambda i, a: (0, i)),
+        pl.BlockSpec(rhs.shape, lambda i, a: (0, 0)),
     ]
     for k, e in enumerate(extras):
         if k < 2:
-            in_specs.append(pl.BlockSpec((n, e.shape[1]), lambda i, a: (plane(i, a) % 2, 0)))
+            in_specs.append(pl.BlockSpec((n, e.shape[1]), lambda i, a: (i % 2, 0)))
         else:
-            in_specs.append(pl.BlockSpec((n, e.shape[1]), lambda i, a: (plane(i, a), 0)))
-    widths = (half, C + E - half)
+            in_specs.append(pl.BlockSpec((n, e.shape[1]), lambda i, a: (i, 0)))
+    pair = (2, 1, R, C)
     return pl.pallas_call(
-        partial(grad_kernel, half, R),
+        partial(grad_kernel, R),
         grid_spec=pltpu.PrefetchScalarGridSpec(
             num_scalar_prefetch=1,
             grid=(4,),
             in_specs=in_specs,
-            out_specs=[pl.BlockSpec((1, R, widths[k % 2]), lambda i, a: (i, 0, 0)) for k in range(8)],
-            scratch_shapes=[pltpu.VMEM((n, C + E), F32)],
+            out_specs=[
+                pl.BlockSpec((1, R, C), lambda i, a: (i, 0, 0)),
+                pl.BlockSpec(pair, lambda i, a: (0, jnp.minimum(i, 1), 0, 0)),
+                pl.BlockSpec(pair, lambda i, a: (0, jnp.maximum(i, 2) - 2, 0, 0)),
+                pl.BlockSpec((1, R, C), lambda i, a: (jnp.maximum(i, 2) - 2, 0, 0)),
+                pl.BlockSpec((1, R, C), lambda i, a: (jnp.minimum(i, 1), 0, 0)),
+            ],
+            scratch_shapes=[pltpu.VMEM((n, C), F32)],
         ),
-        out_shape=[jax.ShapeDtypeStruct((4, R, widths[k % 2]), BF) for k in range(8)],
+        out_shape=[
+            jax.ShapeDtypeStruct(v, BF)
+            for v in ((4, R, C), (2, 2, R, C), (2, 2, R, C), (2, R, C), (2, R, C))
+        ],
         compiler_params=PARAMS,
-        cost_estimate=COST,
     )(at, lhs, rhs, *extras)
 
 
-def slab_kernel(o1, o2, x1, x2, y1, y2, out):
-    h = o1.shape[2]
-    out[0, :, :h] = (o1[0].astype(F32) + x1[0].astype(F32) + y1[0].astype(F32)).astype(BF)
-    out[0, :, h:] = (o2[0].astype(F32) + x2[0].astype(F32) + y2[0].astype(F32)).astype(BF)
-
-
-def slabs_kernel(n, *refs):
-    ins, outs = refs[:-4], refs[-4:]
+def slab_kernel(own, gx, gy, tx, ty, out):
     i = pl.program_id(0)
-    for k in range(4):
-
-        @pl.when(i == k)
-        def _(k=k):
-            to = 0
-            for p in range(0, len(ins), n):
-                w = ins[p].shape[2]
-                total = ins[p][0].astype(F32)
-                for v in ins[p + 1 : p + n]:
-                    total = total + v[0].astype(F32)
-                outs[k][:, to : to + w] = total.astype(BF)
-                to += w
-
-
-def sum_slabs(*groups):
-    n = len(groups[0])
-    ins = [v for g in groups for v in g]
-    R = ins[0].shape[1]
-    C = sum(g[0].shape[2] for g in groups)
+
+    @pl.when(i < 2)
+    def _():
+        out[...] = (own[0].astype(F32) + gx[0, 0].astype(F32) + ty[0].astype(F32)).astype(BF)
+
+    @pl.when(i >= 2)
+    def _():
+        out[...] = (own[0].astype(F32) + gy[0, 0].astype(F32) + tx[0].astype(F32)).astype(BF)
+
+
+def sum_slabs(own, gx, gy, tx, ty):
+    _, R, C = own.shape
+    low = lambda i: jnp.minimum(i, 1)
+    high = lambda i: jnp.maximum(i, 2) - 2
     return pl.pallas_call(
-        partial(slabs_kernel, n),
+        slab_kernel,
         grid=(4,),
-        in_specs=[pl.BlockSpec((1,) + v.shape[1:], lambda i: (i, 0, 0)) for v in ins],
-        out_specs=[pl.BlockSpec((R, C), lambda i: (0, 0))] * 4,
-        out_shape=[jax.ShapeDtypeStruct((R, C), BF)] * 4,
+        in_specs=[
+            pl.BlockSpec((1, R, C), lambda i: (i, 0, 0)),
+            pl.BlockSpec((1, 1, R, C), lambda i: (1, low(i), 0, 0)),
+            pl.BlockSpec((1, 1, R, C), lambda i: (1, high(i), 0, 0)),
+            pl.BlockSpec((1, R, C), lambda i: (high(i), 0, 0)),
+            pl.BlockSpec((1, R, C), lambda i: (low(i), 0, 0)),
+        ],
+        out_specs=pl.BlockSpec((R, C), lambda i: (i, 0)),
+        out_shape=jax.ShapeDtypeStruct((4 * R, C), BF),
         compiler_params=PARAMS,
-    )(*ins)
+    )(own, gx, gy, tx, ty)
 
 
 def total(*parts):
@@ -394,57 +408,26 @@
 
 class ReduceWide:
     def __init__(self, links, blocks):
-        self.px, self.py, self.pz = links
-        self.o1, self.o2, self.X1, self.X2, self.Y1, self.Y2, self.D1, self.D2 = blocks
-
-    def diag(self):
-        self.r1, self.r2 = self.px(self.D1), self.py(self.D2)
+        self.links = links
+        self.own, self.Sx, self.Sy, self.Rx, self.Ry = blocks
 
     def sides(self):
-        self.a1, self.b2 = self.px(self.X1), self.py(self.Y2)
+        self.gx, self.gy = self.links.x(self.Sx), self.links.y(self.Sy)
 
     def rest(self):
-        self.a2, self.b1 = self.px(add(self.X2, self.r2)), self.py(add(self.Y1, self.r1))
-
-    def ring(self):
-        if not hasattr(self, "slabs"):
-            _, R, h = self.o1.shape
-            C = h + self.o2.shape[2]
-            spec1 = pl.BlockSpec((1, R, h), lambda i: (i, 0, 0))
-            spec2 = pl.BlockSpec((1, R, C - h), lambda i: (i, 0, 0))
-            self.slabs = pl.pallas_call(
-                slab_kernel,
-                grid=(4,),
-                in_specs=[spec1, spec2] * 3,
-                out_specs=pl.BlockSpec((1, R, C), lambda i: (i, 0, 0)),
-                out_shape=jax.ShapeDtypeStruct((4, R, C), BF),
-            )(self.o1, self.o2, self.a1, self.a2, self.b1, self.b2)
-            self.sum, self.at = self.slabs[0], 0
-        self.at += 1
-        self.sum = add(self.pz(self.sum), self.slabs[self.at])
-
-    def along(self):
-        a, b, c, d = sum_slabs((self.o1, self.a1, self.b1), (self.o2, self.a2, self.b2))
-        self.sum = total(d, *[self.pz(v, (up, 0, 0)) for v, up in ((a, 3), (b, 2), (c, 1))])
+        self.tx = self.links.x(add(self.Rx, self.gy[0]))
+        self.ty = self.links.y(add(self.Ry, self.gx[0]))
+
+    def along(self, due):
+        self.sum = self.links.scatter(sum_slabs(self.own, self.gx, self.gy, self.tx, self.ty), due)
 
 
 class ReduceDown:
-    def __init__(self, links, keep, got, at):
-        self.px, self.py, self.pz = links
-        self.keep, self.got, self.at, self.step = keep, got, at, 0
-
-    def plane(self):
-        n = self.keep.shape[0] // 2
-        d = (self.at[0] + 3 - self.step) % 4
-        self.step += 1
-        a = lax.dynamic_slice_in_dim(self.keep, (d % 2) * n, n, 0)
-        b = lax.dynamic_slice_in_dim(self.got, (d % 2) * n, n, 0)
-        return jnp.where((d // 2) == self.at[3], a, b)
-
-    def ring(self):
-        if self.step == 0:
-            self.sum = self.plane()
-        self.sum = add(self.pz(self.sum), self.plane())
+    def __init__(self, links, v, at):
+        self.links, self.v, self.at = links, v, at
+
+    def along(self, due):
+        self.sum = self.links.scatter(self.v, due)
 
     def pick(self, b, lo, hi):
         yy, xx = BLOCKS[b]
@@ -453,24 +436,22 @@
         y, x = self.at[1], self.at[2]
         return lax.dynamic_slice(v, (y ^ yy, x ^ xx, 0, lo), (1, 1, R, hi - lo)).reshape(R, hi - lo)
 
-    def diag(self):
-        C = self.sum.shape[1]
-        h = C // 2
-        self.r1, self.r2 = self.px(self.pick(3, 0, h)), self.py(self.pick(3, h, C))
-
-    def sides(self):
-        C = self.sum.shape[1]
-        h = C // 2
-        self.a1, self.b2 = self.px(self.pick(1, 0, h)), self.py(self.pick(2, h, C))
-
-    def rest(self):
-        C = self.sum.shape[1]
-        h = C // 2
-        a2 = self.px(add(self.pick(1, h, C), self.r2))
-        b1 = self.py(add(self.pick(2, 0, h), self.r1))
-        first = add(add(self.pick(0, 0, h), self.a1), b1)
-        second = add(add(self.pick(0, h, C), a2), self.b2)
-        self.sum = jnp.concatenate([first, second], 1)
+
+def around(links, parts):
+    C = parts[0].sum.shape[1]
+    h = C // 2
+
+    def pick(b, lo, hi):
+        return jnp.concatenate([p.pick(b, lo, hi) for p in parts], 0)
+
+    r1, r2 = links.x(pick(3, 0, h)), links.y(pick(3, h, C))
+    a1, b2 = links.x(pick(1, 0, h)), links.y(pick(2, h, C))
+    a2 = links.x(add(pick(1, h, C), r2))
+    b1 = links.y(add(pick(2, 0, h), r1))
+    v = jnp.concatenate([total(pick(0, 0, h), a1, b1), total(pick(0, h, C), a2, b2)], 1)
+    R = v.shape[0] // len(parts)
+    for n, p in enumerate(parts):
+        p.sum = v[n * R : (n + 1) * R]
 
 
 def finish_kernel(widths, at_ref, keep_ref, got_ref, *outs):
@@ -759,16 +740,14 @@
     R = q_weight.shape[1]
     K, V, F, W = q_weight.shape[2] // 2, v_weight.shape[2] // 2, ffn_gate.shape[2] // 2, width // 2
     A = 2 * K + 2 * V
-    half = (A + W) // 2
     rank = rank_down.shape[2]
     kc, gc = rank_bias.shape[1], group_gain.shape[1]
     ru_at = rank + 4
-    links = [Link((0, 0, 1)), Link((0, 1, 0)), Link((1, 0, 0))]
+    links = Links()
 
     def paced(*values):
         if meshed:
-            tokens = [link.sent[-1] for link in links]
-            values = lax.optimization_barrier((values, tokens))[0]
+            values = lax.optimization_barrier((values, links.meeting()))[0]
         return values if len(values) > 1 else values[0]
 
     cuts = cut_columns(
@@ -802,9 +781,9 @@
         return jnp.where(first, jnp.concatenate([keep, got], 1), jnp.concatenate([got, keep], 1))
 
     if meshed:
-        gA = [GatherWide(links, v, half) for v in ao]
-        gF = [GatherWide(links, v, F) for v in ff]
-        gD = [GatherDown(links, v, at) for v in down]
+        gA = [GatherWide(links, v) for v in ao]
+        gF = [GatherWide(links, v) for v in ff]
+        gD = [GatherWide(links, down[0]), GatherDown(links, down[1], at)]
     else:
         gA = gF = gD = [Idle(), Idle()]
 
@@ -812,13 +791,9 @@
         if not meshed:
             v = whole(ao[layer])
             return v[:, :A], own_rows(v[:, A : A + W]), v[:, A + W :]
-        columns = [
-            [(0, half, 0, 0)],
-            [(0, A - half, 0, half), (A - half, A - half + W, 1, 0)],
-        ]
-        C = ao[layer].shape[1]
-        if C > A + W:
-            columns[1].append((A - half + W, C - half, 3, 0))
+        columns = [(0, A, 0, 0), (A, A + W, 1, 0)]
+        if ao[layer].shape[1] > A + W:
+            columns.append((A + W, ao[layer].shape[1], 3, 0))
         out = place_blocks(gA[layer].parts(), columns, at, split=1)
         keep, give = out[1].reshape(width // 2, W), out[2].reshape(width // 2, W)
         WO = join_columns(keep, over_core(give), at)
@@ -827,12 +802,19 @@
     def place_ff(layer):
         if not meshed:
             return whole(ff[layer])
-        return place_blocks(gF[layer].parts(), [[(0, F, 0, 0)], [(0, F, 0, F)]], at)[0].reshape(width, 2 * F)
+        return place_blocks(gF[layer].parts(), [(0, 2 * F, 0, 0)], at)[0].reshape(width, 2 * F)
 
     def place_down(layer):
         if not meshed:
             return own_rows(whole(down[layer]))
-        keep, give = split_planes(gD[layer].slabs, at)
+        if layer == 0:
+            keep, give = place_blocks(gD[0].parts(), [(0, W, 0, 0)], at, split=0)
+            keep, give = keep.reshape(-1, W), give.reshape(-1, W)
+        else:
+            v = gD[1].all
+            h = v.shape[0] // 2
+            keep = lax.dynamic_slice_in_dim(v, s * h, h, 0)
+            give = lax.dynamic_slice_in_dim(v, (1 - s) * h, h, 0)
         return join_columns(keep, over_core(give), at)
 
     def unpack(table, layer):
@@ -854,38 +836,38 @@
     low_mask = mask.astype(BF)
     x0 = inputs.reshape(tokens, width).astype(F32)
 
-    gD[0].sides(), gD[1].sides()
-    gA[0].ring(), gA[0].ring(), gA[0].ring()
-    gD[0].diag(), gD[1].diag()
-    gA[0].first(), gA[0].second(), gA[0].third()
-    gF[0].ring(), gF[0].ring(), gF[0].ring(), gD[0].ring()
+    gA[0].along(9), gD[1].around(), gF[0].along(9)
+    if meshed:
+        gA[1].along_with(gD[0], 3, gA[0].line)
+    gA[0].sides(), gA[0].diag()
     WA0, WO0, table = place_ao(0)
     p0, p1 = unpack(table, 0), unpack(table, 1)
     w0 = dict(p0, WA=WA0, WO=WO0)
-    gF[0].first(), gD[0].ring()
-    x0, w0 = paced(x0, w0)
-    m0 = project(x0, w0)
-    m0, p1 = paced(m0, p1)
-    gF[0].second(), gD[0].ring(), gA[1].ring()
-    h0, m0 = paced(*mix(m0, w0, rows))
-    gF[0].third(), gA[1].ring(), gA[1].ring()
+    gF[0].sides()
+    if meshed:
+        gF[1].along(2, gA[1].line)
+    h0, m0 = mix(project(x0, w0), w0, rows)
+    h0, m0, p1 = paced(h0, m0, p1)
+    gF[0].diag()
     w0["WF"] = place_ff(0)
+    gD[0].sides()
+    f0 = paced(expand(h0, w0))
+    gD[0].diag()
+    if meshed:
+        gD[1].along(3, gF[1].line)
     w0["WD"] = place_down(0)
-    gA[1].first(), gF[1].ring()
-    f0 = paced(expand(h0, w0))
-    gA[1].second(), gF[1].ring()
+    gA[1].sides()
     y0, f0 = paced(*contract(f0, w0, mask))
     x1 = y0.astype(BF)
-    gA[1].third(), gF[1].ring()
+    gA[1].diag()
     WA1, WO1, _ = place_ao(1)
     w1 = dict(p1, WA=WA1, WO=WO1)
-    gF[1].first(), gD[1].ring()
-    m1 = paced(project(x1.astype(F32), w1))
-    gF[1].second(), gD[1].ring()
-    h1, m1 = paced(*mix(m1, w1, rows))
-    gF[1].third(), gD[1].ring()
+    gF[1].sides()
+    h1, m1 = mix(project(x1.astype(F32), w1), w1, rows)
+    h1, m1 = paced(h1, m1)
+    gF[1].diag()
+    w1["WD"] = place_down(1)
     w1["WF"] = place_ff(1)
-    w1["WD"] = place_down(1)
     f1 = expand(h1, w1)
     y1, f1 = contract(f1, w1, mask)
     layer_out = jnp.where(first, x1, y1.astype(BF)).reshape((1,) + shape)
@@ -900,60 +882,62 @@
         def __init__(self, v):
             self.sum = scatter(v)
 
-        def ring(self):
+        def along(self, *a):
             pass
 
-        along = diag = sides = rest = ring
+        sides = rest = along
 
     def sum_down(g):
-        return ReduceDown(links, *g, at) if meshed else Sum(all_rows(*g))
+        return ReduceDown(links, all_rows(*g), at) if meshed else Sum(all_rows(*g))
 
     def sum_ff(second, dgu):
         if meshed:
-            return ReduceWide(links, grad_blocks(second, dgu, F, at))
+            return ReduceWide(links, grad_blocks(second, dgu, at))
         return Sum(mm_tn(second, dgu).astype(BF))
 
     def sum_ao(n, dpre, gO, packed=()):
         extras = gO + packed
         if meshed:
-            return ReduceWide(links, grad_blocks(n, dpre, half, at, extras))
+            return ReduceWide(links, grad_blocks(n, dpre, at, extras))
         return Sum(jnp.concatenate((mm_tn(n, dpre).astype(BF), all_rows(*gO)) + packed, 1))
 
     dy1 = out_grad.reshape(tokens, width) * low_mask
     gD1 = row_grads(f1["act"], dy1, s)
     rD1 = sum_down(gD1)
     dgu = contract_back(dy1, f1, w1)
-    rF1 = sum_ff(after(f1["second"], *gD1), dgu)
-    rF1.diag(), rD1.ring()
+    rF1 = sum_ff(f1["second"], dgu)
+    rF1.sides(), rD1.along(3)
+    if meshed:
+        dgu = after(dgu, rF1.own)
     dh1, d_mg1 = expand_back(dy1, dgu, f1, w1)
     low = dh1.astype(BF)
-    dgated = mm_nt(low, w1["WO"]).astype(BF)
     gO1 = row_grads(m1["gated"], low, s)
-    dh1, d_mg1, dgated, gO1 = paced(dh1, d_mg1, dgated, gO1)
-    rF1.sides(), rD1.ring()
-    back = paced(mixer_bwd(m1["pre"], m1["logits"], w1["gg"], dgated, rows))
-    rF1.rest(), rD1.ring()
+    back = mixer_bwd(m1["pre"], m1["logits"], w1["gg"], mm_nt(low, w1["WO"]).astype(BF), rows)
+    dh1, d_mg1, gO1, back = paced(dh1, d_mg1, gO1, back)
+    rF1.rest()
     rA1 = sum_ao(m1["n"], back[0], gO1)
     dx1, small1 = paced(*project_back(dh1, *back, d_mg1, m1, w1))
-    rA1.diag(), rF1.ring()
+    rA1.sides(), rF1.along(3)
     dy0 = dx1.astype(BF) * low_mask
     gD0 = row_grads(f0["act"], dy0, s)
-    dgu, gD0, dy0 = paced(contract_back(dy0, f0, w0), gD0, dy0)
+    dgu = contract_back(dy0, f0, w0)
+    rF0 = sum_ff(f0["second"], dgu)
     rD0 = sum_down(gD0)
-    rA1.sides(), rF1.ring()
-    rF0 = sum_ff(f0["second"], dgu)
-    dh0, d_mg0 = paced(*expand_back(dy0, dgu, f0, w0))
-    rA1.rest(), rF1.ring()
+    rD0.along(9)
+    dh0, d_mg0 = expand_back(dy0, dgu, f0, w0)
+    if meshed:
+        (rF0.own, rF0.Sx, rF0.Sy, rF0.Rx, rF0.Ry), dh0, d_mg0 = paced(
+            (rF0.own, rF0.Sx, rF0.Sy, rF0.Rx, rF0.Ry), dh0, d_mg0
+        )
+    rA1.rest()
     low = dh0.astype(BF)
-    dgated = mm_nt(low, w0["WO"]).astype(BF)
-    dgated, gO0 = paced(dgated, row_grads(m0["gated"], low, s))
-    rF0.diag(), rA1.ring()
+    gO0 = row_grads(m0["gated"], low, s)
+    dgated, gO0, dh0 = paced(mm_nt(low, w0["WO"]).astype(BF), gO0, dh0)
+    rF0.sides(), rA1.along(9)
     back = paced(mixer_bwd(m0["pre"], m0["logits"], w0["gg"], dgated, rows))
-    rF0.sides(), rA1.ring()
+    rF0.rest()
     dx0, small0 = project_back(dh0, *back, d_mg0, m0, w0)
     dpre = back[0]
-    input_out = jnp.where(first, dx0, dx1).reshape((1,) + shape)
-
     mine = {k: jnp.where(first, small0[k], small1[k]) for k in small0}
     other = {k: over_core(jnp.where(first, small1[k], small0[k])) for k in ("ru", "rb", "gg")}
     ru = all_rows(mine["ru"], other["ru"])
@@ -972,18 +956,16 @@
     packed = jnp.pad(packed, ((0, 0), (0, 128 - packed.shape[1]))).astype(BF)
 
     rA0 = sum_ao(m0["n"], dpre, gO0, (packed,))
-    rF0.rest(), rA1.ring(), rD0.ring(), rD0.ring(), rD0.ring()
-    rA0.diag()
-    rF0.along()
-    rA0.sides()
+    rA0.sides(), rF0.along(9)
+    if meshed:
+        links.before += [rA1.sum]
     rA0.rest()
-    rA0.along()
-    for r in (rD1, rD0):
-        r.diag()
-    for r in (rD1, rD0):
-        r.sides()
-    for r in (rD1, rD0):
-        r.rest()
+    rA0.along(9)
+    if meshed:
+        links.before += [rF0.sum]
+        around(links, (rD1, rD0))
+
+    input_out = jnp.where(first, dx0, dx1).reshape((1,) + shape)
 
     def join(a, b, widths):
         keep = jnp.where(first, a, b)

time: 648 us -> 610 us (0.941)
  starting transfers between devices: 149 us -> 84.9 us
  waiting for transfers between devices: 219 us -> 172 us
  other arithmetic: 64.3 us -> 93.1 us
  local copies, waits for them, and re-layouts: 48.2 us -> 75.1 us
  between operations: 3.7 us -> 16 us
    ppermute x104 -> x46, waiting for transfers between devices: 215 us -> 144 us  [hop(): sent.append(lax.ppermute(v, 'dp', pairs(*step)))]
    ppermute x104 -> x46, starting transfers between devices: 81.7 us -> 40.7 us  [hop(): sent.append(lax.ppermute(v, 'dp', pairs(*step)))]
    ppermute x27, starting transfers between devices: 67.1 us -> 42.3 us  [over_core(): return lax.ppermute(v, 'section', [(0, 1), (1, 0)])]
    all_gather x0 -> x5, waiting for transfers between devices: none -> 23.1 us  [gather(): v = lax.all_gather(v, 'dp', axis=0, tiled=True, axis_index_groups=LINES)]
    slice x4 -> x15, local copies, waits for them, and re-layouts: 0.03 us -> 15.9 us  [the longest x10 12.5 us: diag(): self.hi, self.lo = (self.links.x(self.Y[2:]), self.links.y(self.X[:2]))]
    dot_general x10, matrix products: 19.3 us -> 25.9 us  [mm(): lax.dot_general(a.astype(BF), b.astype(BF), (((1,), (0,)), ((), ())), pre...]
    unnamed x332 -> x282, local copies, waits for them, and re-layouts: 29.4 us -> 35.4 us
    convert_element_type x23 -> x10, other arithmetic: 17.8 us -> 12.3 us  [add(): return (a.astype(F32) + b.astype(F32)).astype(BF)]
  transfers between devices with their start and end apart: 131 -> 84, of which waited for: 55 -> 33; matrix products, arithmetic and copies ran while one was open for 21% -> 31% of each run, Pallas kernels for 14% -> 16%
where the time goes in v3:
time: 610 us; the launch traced here: 601 us
  waiting for transfers between devices  172 us (28%)
  Pallas kernels  99.4 us (16%)
  other arithmetic  93.1 us (15%)
  starting transfers between devices  84.9 us (14%)
  local copies, waits for them, and re-layouts  75.1 us (12%)
  matrix products  61 us (10%)
  between operations  16 us (3%)
    ppermute x46, waiting for transfers between devices, hop(): sent.append(lax.ppermute(v, 'dp', pairs(*step)))  144 us
    ppermute x27, starting transfers between devices, over_core(): return lax.ppermute(v, 'section', [(0, 1), (1, 0)])  42.3 us
    ppermute x46, starting transfers between devices, hop(): sent.append(lax.ppermute(v, 'dp', pairs(*step)))  40.7 us
    unnamed x282, local copies, waits for them, and re-layouts  35.4 us
    dot_general x10, matrix products, mm(): lax.dot_general(a.astype(BF), b.astype(BF), (((1,), (0,)), ((), ())), pre...  25.9 us
    pallas_call x10, Pallas kernels, copy_call(): pl.pallas_call(kernel, grid_spec=pltpu.PrefetchScalarGridSpec(num_scalar_...  25.9 us
    dot_general x10, matrix products, mm_nt(): lax.dot_general(a.astype(BF), b.astype(BF), (((1,), (1,)), ((), ())), pre...  24.2 us
    all_gather x5, waiting for transfers between devices, gather(): v = lax.all_gather(v, 'dp', axis=0, tiled=True, axis_index_groups=LINES)  23.1 us
  transfers between devices with their start and end apart: 84, of which 33 were waited for; matrix products, arithmetic and copies ran while one was open for 31% of the time, Pallas kernels for 16%

profile of v3, /device:TPU:1, one launch (start us, length us, event | category | flops | bytes accessed | tf_op | source)
XLA Modules:
  0.0 601.2 jit_solution(13483223686363233748)
XLA Ops:
  9.2 3.5 shard_map.288
  26.1 3.4 collective-permute-done.2
  34.1 14.8 %all-gather.6.cloned.1.call-done = bf16[256,2176]{1,0:T(8,128)(2,1)} async-done(((bf16[64,2176]{1,0:T(8,128)(2,1)}), bf16[256,2176]{1,0:T(8,128)(2,1)}) %all-gather.6.cloned.1.call-update) | async-done | bytes 1114128 | tf_op jit(solution)/shard_map/all_gather | solution.py:150
  52.8 21.7 %collective-permute-done.5.refs_1_ = bf16[4,64,2176]{2,1,0:T(8,128)(2,1)S(1)} collective-permute-done((bf16[4,64,2176]{2,1,0:T(8,128)(2,1)}, bf16[4,64,2176]{2,1,0:T(8,128)(2,1)S(1)}, u32[]{:S(2)}, u32[]{:S(2)}) %collective-permute-start.5) | collective-permute-done | bytes 1114144 | tf_op jit(solution)/shard_map/ppermute | solution.py:140
  82.2 5.5 collective-permute-done.8.refs_3_
  103.7 3.5 collective-permute-start.10
  110.3 4.0 convolution_convert_fusion.9.pre_ref
  114.4 5.8 shard_map.290
  125.6 2.9 collective-permute-done.13.refs_1_
  145.0 2.6 reshape.409.refs_0_
  152.2 9.2 %collective-permute-done.17.refs_1_ = bf16[4,176,512]{2,1,0:T(8,128)(2,1)S(1)} collective-permute-done((bf16[4,176,512]{2,1,0:T(8,128)(2,1)}, bf16[4,176,512]{2,1,0:T(8,128)(2,1)S(1)}, u32[]{:S(2)}, u32[]{:S(2)}) %collective-permute-start.17) | collective-permute-done | bytes 720928 | tf_op jit(solution)/shard_map/ppermute | solution.py:140
  164.0 3.7 shard_map.292
  173.3 7.2 %collective-permute-start.21 = (bf16[1408,512]{1,0:T(8,128)(2,1)}, bf16[1408,512]{1,0:T(8,128)(2,1)}, u32[]{:S(2)}, u32[]{:S(2)}) collective-permute-start(bf16[1408,512]{1,0:T(8,128)(2,1)} %bitcast.25), channel_id=1, source_target_pairs={{0,16},{16,0},{1,17},{17,1},{2,18},{18,2},{3,19},{19,3},{4,20},{20... | collective-permute-start | bytes 4325384 | tf_op jit(solution)/shard_map/ppermute | solution.py:170
  182.5 4.5 convolution_convert_fusion.1
  187.0 2.7 fusion.21
  189.7 16.2 %collective-permute-done.23.refs_1_ = bf16[4,64,2048]{2,1,0:T(8,128)(2,1)} collective-permute-done((bf16[4,64,2048]{2,1,0:T(8,128)(2,1)S(1)}, bf16[4,64,2048]{2,1,0:T(8,128)(2,1)}, u32[]{:S(2)}, u32[]{:S(2)}) %collective-permute-start.23) | collective-permute-done | bytes 1048608 | tf_op jit(solution)/shard_map/ppermute | solution.py:140
  211.2 2.8 shard_map.294
  214.0 2.8 convolution_convert_fusion.13
  222.7 3.4 shard_map.295
  237.6 5.8 shard_map.296
  249.8 11.7 %collective-permute-done.29.refs_1_ = bf16[4,64,2816]{2,1,0:T(8,128)(2,1)} collective-permute-done((bf16[4,64,2816]{2,1,0:T(8,128)(2,1)}, bf16[4,64,2816]{2,1,0:T(8,128)(2,1)}, u32[]{:S(2)}, u32[]{:S(2)}) %collective-permute-start.29) | collective-permute-done | bytes 1441824 | tf_op jit(solution)/shard_map/ppermute | solution.py:140
  268.1 3.5 add_add_fusion
  271.6 8.3 %all-gather.14.cloned.1.call-done = bf16[2816,512]{1,0:T(8,128)(2,1)} async-done(((bf16[704,512]{1,0:T(8,128)(2,1)}), bf16[2816,512]{1,0:T(8,128)(2,1)}) %all-gather.14.cloned.1.call-update) | async-done | bytes 2883600 | tf_op jit(solution)/shard_map/all_gather | solution.py:150
  283.7 4.4 shard_map.298
  288.1 3.4 convolution_convert_fusion
  292.8 3.2 fusion.6
  299.3 5.7 shard_map.300
  310.1 4.1 convolution_convert_fusion.11
  319.0 3.1 fusion.44
  322.1 3.8 fusion.102
  328.6 10.3 %shard_map.301 = (bf16[512,1536]{1,0:T(8,128)(2,1)S(1)}, f32[512,256]{1,0:T(8,128)S(1)}, f32[1,256]{1,0:T(1,128)S(1)}) custom-call(bf16[512,1536]{1,0:T(8,128)(2,1)S(1)} %copy-done.3, f32[512,256]{1,0:T(8,128)S(1)} %convolution_add_fusion.logits_ref, f32[1,256]{1,0:T(1,128)S(1)} %reshape.402.gain_ref, bf16[512,512]{1,0:T(8,128)(2,1)S(1)} %convolution_convert_fusion.21.dg_ref), custom_call_target="tpu_custom_call" | custom-call | tf_op jit(solution)/shard_map/pallas_call | solution.py:618
  340.4 10.9 %collective-permute-done.38.gy = bf16[2,2,64,2816]{3,2,1,0:T(8,128)(2,1)S(1)} collective-permute-done((bf16[2,2,64,2816]{3,2,1,0:T(8,128)(2,1)}, bf16[2,2,64,2816]{3,2,1,0:T(8,128)(2,1)S(1)}, u32[]{:S(2)}, u32[]{:S(2)}) %collective-permute-start.38) | collective-permute-done | bytes 1441824 | tf_op jit(solution)/shard_map/ppermute | solution.py:140
  354.8 2.8 add_convert_fusion.4
  365.5 4.8 shard_map.303
  373.4 4.9 collective-permute-done.43.ty
  378.5 3.8 shard_map.304
  382.6 3.6 fusion.46
  388.9 2.5 copy-done.15
  391.4 2.7 fusion.9
  396.1 4.2 convolution_convert_fusion.10
  409.2 10.0 %collective-permute-done.49.tx = bf16[2,64,2048]{2,1,0:T(8,128)(2,1)S(1)} collective-permute-done((bf16[2,64,2048]{2,1,0:T(8,128)(2,1)S(1)}, bf16[2,64,2048]{2,1,0:T(8,128)(2,1)S(1)}, u32[]{:S(2)}, u32[]{:S(2)}) %collective-permute-start.49) | collective-permute-done | bytes 524320 | tf_op jit(solution)/shard_map/ppermute | solution.py:140
  421.6 3.5 shard_map.307
  427.3 6.4 %shard_map.302 = (bf16[4,64,2816]{2,1,0:T(8,128)(2,1)S(1)}, bf16[2,2,64,2816]{3,2,1,0:T(8,128)(2,1)}, bf16[2,2,64,2816]{3,2,1,0:T(8,128)(2,1)}, bf16[2,64,2816]{2,1,0:T(8,128)(2,1)S(1)}, bf16[2,64,2816]{2,1,0:T(8,128)(2,1)S(1)}) custom-call(s32[4]{0:T(128)S(1)} %copy-done.64, bf16[512,1024]{1,0:T(8,128)(2,1)S(1)} %copy-done.7, ...), custom_call_target="tpu_custom_call" | custom-call | tf_op jit(solution)/shard_map/pallas_call | solution.py:347
  433.8 3.4 fusion.48
  437.3 3.7 fusion.35
  441.9 4.6 convolution_convert_fusion.12
  446.6 3.2 collective-permute-start.34
  455.7 9.9 %shard_map.305 = (bf16[512,1536]{1,0:T(8,128)(2,1)S(1)}, f32[512,256]{1,0:T(8,128)S(1)}, f32[1,256]{1,0:T(1,128)S(1)}) custom-call(bf16[512,1536]{1,0:T(8,128)(2,1)S(1)} %copy-done.1, f32[512,256]{1,0:T(8,128)S(1)} %convolution_add_fusion.1.logits_ref, f32[1,256]{1,0:T(1,128)S(1)} %reshape.399.gain_ref, bf16[512,512]{1,0:T(8,128)(2,1)S(1)} %convolution_convert_fusion.20.dg_ref), custom_call_target="tpu_custom_call" | custom-call | tf_op jit(solution)/shard_map/pallas_call | solution.py:618
  466.8 4.7 collective-permute-done.51.gx
  471.9 4.0 collective-permute-start.54
  476.4 4.8 add_convert_fusion.1
  490.7 3.6 fusion.50
  497.3 4.8 shard_map.306
  507.7 4.3 shard_map.308
  512.7 3.7 fusion.58
  517.3 14.7 %collective-permute-done.61.gy = bf16[2,2,64,2176]{3,2,1,0:T(8,128)(2,1)S(1)} collective-permute-done((bf16[2,2,64,2176]{3,2,1,0:T(8,128)(2,1)}, bf16[2,2,64,2176]{3,2,1,0:T(8,128)(2,1)S(1)}, u32[]{:S(2)}, u32[]{:S(2)}) %collective-permute-start.61) | collective-permute-done | bytes 1114144 | tf_op jit(solution)/shard_map/ppermute | solution.py:140
  532.9 4.3 collective-permute-done.59.gx
  546.1 3.1 collective-permute-done.62.tx
  551.3 3.6 shard_map.309
  558.2 4.1 collective-permute-start.65
  563.8 4.1 collective-permute-done.67
  568.9 3.8 collective-permute-done.71
  573.1 6.0 collective-permute-start.72
  579.1 4.2 fusion.32
  (602 shorter events, 234.9 us)
Async XLA Ops:
  7.2 41.7 %all-gather.6.cloned.1.call-start = ((), (), s32[]{:S(2)}) async-start(), calls=%async_computation.6 | async-start | bytes 1392640 | tf_op jit(solution)/shard_map/all_gather | solution.py:150
  17.8 80.4 %all-gather.8.cloned.1.call-start = ((), (), s32[]{:S(2)}) async-start(), calls=%async_computation.7 | async-start | bytes 1802240 | tf_op jit(solution)/shard_map/all_gather | solution.py:150
  20.8 119.0 %all-gather.10.cloned.1.call-start = ((), (), s32[]{:S(2)}) async-start(), calls=%async_computation.8 | async-start | bytes 2211840 | tf_op jit(solution)/shard_map/all_gather | solution.py:150
  31.6 18.5 %collective-permute-start.6 = (bf16[176,256]{1,0:T(8,128)(2,1)S(1)}, bf16[176,256]{1,0:T(8,128)(2,1)}, u32[]{:S(2)}, u32[]{:S(2)}) collective-permute-start(bf16[176,256]{1,0:T(8,128)(2,1)S(1)} %slice.257), channel_id=1, source_target_pairs={{0,2},{1,3},{2,0},{3,1},{4,6},{5,7},{6,4},{7,5},{8,10},{9,11},{10,... | collective-permute-start | bytes 270344 | tf_op jit(solution)/shard_map/ppermute | solution.py:140
  48.9 25.5 %collective-permute-start.5 = (bf16[4,64,2176]{2,1,0:T(8,128)(2,1)}, bf16[4,64,2176]{2,1,0:T(8,128)(2,1)S(1)}, u32[]{:S(2)}, u32[]{:S(2)}) collective-permute-start(bf16[4,64,2176]{2,1,0:T(8,128)(2,1)} %bitcast.246), channel_id=1, source_target_pairs={{0,1},{1,0},{2,3},{3,2},{4,5},{5,4},{6,7},{7,6},{8,9},{9,8},{10,11... | collective-permute-start | bytes 3342344 | tf_op jit(solution)/shard_map/ppermute | solution.py:140
  50.1 25.2 %collective-permute-start.7 = (bf16[4,64,2176]{2,1,0:T(8,128)(2,1)}, bf16[4,64,2176]{2,1,0:T(8,128)(2,1)S(1)}, u32[]{:S(2)}, u32[]{:S(2)}) collective-permute-start(bf16[4,64,2176]{2,1,0:T(8,128)(2,1)} %bitcast.247), channel_id=1, source_target_pairs={{0,2},{1,3},{2,0},{3,1},{4,6},{5,7},{6,4},{7,5},{8,10},{9,11},{10,... | collective-permute-start | bytes 3342344 | tf_op jit(solution)/shard_map/ppermute | solution.py:140
  75.3 12.4 %collective-permute-start.8 = (bf16[2,64,2176]{2,1,0:T(8,128)(2,1)}, bf16[2,64,2176]{2,1,0:T(8,128)(2,1)S(1)}, u32[]{:S(2)}, u32[]{:S(2)}) collective-permute-start(bf16[2,64,2176]{2,1,0:T(8,128)(2,1)} %slice.258), channel_id=1, source_target_pairs={{0,2},{1,3},{2,0},{3,1},{4,6},{5,7},{6,4},{7,5},{8,10},{9,11},{10,... | collective-permute-start | bytes 1671176 | tf_op jit(solution)/shard_map/ppermute | solution.py:140
  77.4 12.1 %collective-permute-start.9 = (bf16[2,64,2176]{2,1,0:T(8,128)(2,1)}, bf16[2,64,2176]{2,1,0:T(8,128)(2,1)S(1)}, u32[]{:S(2)}, u32[]{:S(2)}) collective-permute-start(bf16[2,64,2176]{2,1,0:T(8,128)(2,1)} %slice.259), channel_id=1, source_target_pairs={{0,1},{1,0},{2,3},{3,2},{4,5},{5,4},{6,7},{7,6},{8,9},{9,8},{10,11... | collective-permute-start | bytes 1671176 | tf_op jit(solution)/shard_map/ppermute | solution.py:140
  82.1 104.8 %all-gather.12.cloned.1.call-start = ((), (), s32[]{:S(2)}) async-start(), calls=%async_computation.9 | async-start | bytes 1802240 | tf_op jit(solution)/shard_map/all_gather | solution.py:150
  98.3 30.2 %collective-permute-start.13 = (bf16[4,64,2816]{2,1,0:T(8,128)(2,1)}, bf16[4,64,2816]{2,1,0:T(8,128)(2,1)S(1)}, u32[]{:S(2)}, u32[]{:S(2)}) collective-permute-start(bf16[4,64,2816]{2,1,0:T(8,128)(2,1)} %bitcast.242), channel_id=1, source_target_pairs={{0,1},{1,0},{2,3},{3,2},{4,5},{5,4},{6,7},{7,6},{8,9},{9,8},{10,11... | collective-permute-start | bytes 4325384 | tf_op jit(solution)/shard_map/ppermute | solution.py:140
  99.8 30.2 %collective-permute-start.14 = (bf16[4,64,2816]{2,1,0:T(8,128)(2,1)}, bf16[4,64,2816]{2,1,0:T(8,128)(2,1)}, u32[]{:S(2)}, u32[]{:S(2)}) collective-permute-start(bf16[4,64,2816]{2,1,0:T(8,128)(2,1)} %bitcast.243), channel_id=1, source_target_pairs={{0,2},{1,3},{2,0},{3,1},{4,6},{5,7},{6,4},{7,5},{8,10},{9,11},{10,... | collective-permute-start | bytes 4325384 | tf_op jit(solution)/shard_map/ppermute | solution.py:140
  103.7 17.7 %collective-permute-start.10 = (bf16[512,512]{1,0:T(8,128)(2,1)}, bf16[512,512]{1,0:T(8,128)(2,1)}, u32[]{:S(2)}, u32[]{:S(2)}) collective-permute-start(bf16[512,512]{1,0:T(8,128)(2,1)} %bitcast.15), channel_id=1, source_target_pairs={{0,16},{16,0},{1,17},{17,1},{2,18},{18,2},{3,19},{19,3},{4,20},{20... | collective-permute-start | bytes 1572872 | tf_op jit(solution)/shard_map/ppermute | solution.py:170
  125.6 23.9 %collective-permute-start.11 = (bf16[512,1024]{1,0:T(8,128)(2,1)}, bf16[512,1024]{1,0:T(8,128)(2,1)}, u32[]{:S(2)}, u32[]{:S(2)}) collective-permute-start(bf16[512,1024]{1,0:T(8,128)(2,1)} %convolution_convert_fusion.15), channel_id=1, source_target_pairs={{0,16},{16,0},{1,17},{17,1},{2,18},{18,2},{3,19},{19,3},{4,20},{20... | collective-permute-start | bytes 3145736 | tf_op jit(solution)/shard_map/ppermute | solution.py:170
  129.9 17.8 %collective-permute-start.15 = (bf16[2,64,2816]{2,1,0:T(8,128)(2,1)}, bf16[2,64,2816]{2,1,0:T(8,128)(2,1)}, u32[]{:S(2)}, u32[]{:S(2)}) collective-permute-start(bf16[2,64,2816]{2,1,0:T(8,128)(2,1)} %slice.280), channel_id=1, source_target_pairs={{0,2},{1,3},{2,0},{3,1},{4,6},{5,7},{6,4},{7,5},{8,10},{9,11},{10,... | collective-permute-start | bytes 2162696 | tf_op jit(solution)/shard_map/ppermute | solution.py:140
  132.3 15.3 %collective-permute-start.16 = (bf16[2,64,2816]{2,1,0:T(8,128)(2,1)}, bf16[2,64,2816]{2,1,0:T(8,128)(2,1)}, u32[]{:S(2)}, u32[]{:S(2)}) collective-permute-start(bf16[2,64,2816]{2,1,0:T(8,128)(2,1)} %slice.281), channel_id=1, source_target_pairs={{0,1},{1,0},{2,3},{3,2},{4,5},{5,4},{6,7},{7,6},{8,9},{9,8},{10,11... | collective-permute-start | bytes 2162696 | tf_op jit(solution)/shard_map/ppermute | solution.py:140
  141.1 138.8 %all-gather.14.cloned.1.call-start = ((), (), s32[]{:S(2)}) async-start(), calls=%async_computation.10 | async-start | bytes 3604480 | tf_op jit(solution)/shard_map/all_gather | solution.py:150
  147.6 13.8 %collective-permute-start.17 = (bf16[4,176,512]{2,1,0:T(8,128)(2,1)}, bf16[4,176,512]{2,1,0:T(8,128)(2,1)S(1)}, u32[]{:S(2)}, u32[]{:S(2)}) collective-permute-start(bf16[4,176,512]{2,1,0:T(8,128)(2,1)} %reshape.409.refs_0_), channel_id=1, source_target_pairs={{0,1},{1,0},{2,3},{3,2},{4,5},{5,4},{6,7},{7,6},{8,9},{9,8},{10,11... | collective-permute-start | bytes 2162696 | tf_op jit(solution)/shard_map/ppermute | solution.py:140
  147.8 13.7 %collective-permute-start.18 = (bf16[4,176,512]{2,1,0:T(8,128)(2,1)}, bf16[4,176,512]{2,1,0:T(8,128)(2,1)S(1)}, u32[]{:S(2)}, u32[]{:S(2)}) collective-permute-start(bf16[4,176,512]{2,1,0:T(8,128)(2,1)} %reshape.409.refs_0_), channel_id=1, source_target_pairs={{0,2},{1,3},{2,0},{3,1},{4,6},{5,7},{6,4},{7,5},{8,10},{9,11},{10,... | collective-permute-start | bytes 2162696 | tf_op jit(solution)/shard_map/ppermute | solution.py:140
  161.5 8.6 %collective-permute-start.19 = (bf16[2,176,512]{2,1,0:T(8,128)(2,1)S(1)}, bf16[2,176,512]{2,1,0:T(8,128)(2,1)S(1)}, u32[]{:S(2)}, u32[]{:S(2)}) collective-permute-start(bf16[2,176,512]{2,1,0:T(8,128)(2,1)S(1)} %slice.284), channel_id=1, source_target_pairs={{0,2},{1,3},{2,0},{3,1},{4,6},{5,7},{6,4},{7,5},{8,10},{9,11},{10,... | collective-permute-start | bytes 1081352 | tf_op jit(solution)/shard_map/ppermute | solution.py:140
  173.3 37.9 %collective-permute-start.21 = (bf16[1408,512]{1,0:T(8,128)(2,1)}, bf16[1408,512]{1,0:T(8,128)(2,1)}, u32[]{:S(2)}, u32[]{:S(2)}) collective-permute-start(bf16[1408,512]{1,0:T(8,128)(2,1)} %bitcast.25), channel_id=1, source_target_pairs={{0,16},{16,0},{1,17},{17,1},{2,18},{18,2},{3,19},{19,3},{4,20},{20... | collective-permute-start | bytes 4325384 | tf_op jit(solution)/shard_map/ppermute | solution.py:170
  180.5 25.4 %collective-permute-start.23 = (bf16[4,64,2048]{2,1,0:T(8,128)(2,1)S(1)}, bf16[4,64,2048]{2,1,0:T(8,128)(2,1)}, u32[]{:S(2)}, u32[]{:S(2)}) collective-permute-start(bf16[4,64,2048]{2,1,0:T(8,128)(2,1)S(1)} %slice.283.refs_0_), channel_id=1, source_target_pairs={{0,1},{1,0},{2,3},{3,2},{4,5},{5,4},{6,7},{7,6},{8,9},{9,8},{10,11... | collective-permute-start | bytes 3145736 | tf_op jit(solution)/shard_map/ppermute | solution.py:140
  182.2 25.5 %collective-permute-start.24 = (bf16[4,64,2048]{2,1,0:T(8,128)(2,1)S(1)}, bf16[4,64,2048]{2,1,0:T(8,128)(2,1)}, u32[]{:S(2)}, u32[]{:S(2)}) collective-permute-start(bf16[4,64,2048]{2,1,0:T(8,128)(2,1)S(1)} %slice.283.refs_0_), channel_id=1, source_target_pairs={{0,2},{1,3},{2,0},{3,1},{4,6},{5,7},{6,4},{7,5},{8,10},{9,11},{10,... | collective-permute-start | bytes 3145736 | tf_op jit(solution)/shard_map/ppermute | solution.py:140
  207.7 13.7 %collective-permute-start.25 = (bf16[2,64,2048]{2,1,0:T(8,128)(2,1)}, bf16[2,64,2048]{2,1,0:T(8,128)(2,1)S(1)}, u32[]{:S(2)}, u32[]{:S(2)}) collective-permute-start(bf16[2,64,2048]{2,1,0:T(8,128)(2,1)} %slice.286), channel_id=1, source_target_pairs={{0,2},{1,3},{2,0},{3,1},{4,6},{5,7},{6,4},{7,5},{8,10},{9,11},{10,... | collective-permute-start | bytes 1572872 | tf_op jit(solution)/shard_map/ppermute | solution.py:140
  209.9 12.9 %collective-permute-start.26 = (bf16[2,64,2048]{2,1,0:T(8,128)(2,1)}, bf16[2,64,2048]{2,1,0:T(8,128)(2,1)}, u32[]{:S(2)}, u32[]{:S(2)}) collective-permute-start(bf16[2,64,2048]{2,1,0:T(8,128)(2,1)} %slice.287), channel_id=1, source_target_pairs={{0,1},{1,0},{2,3},{3,2},{4,5},{5,4},{6,7},{7,6},{8,9},{9,8},{10,11... | collective-permute-start | bytes 1572872 | tf_op jit(solution)/shard_map/ppermute | solution.py:140
  216.7 14.5 %collective-permute-start.22 = (bf16[512,1024]{1,0:T(8,128)(2,1)}, bf16[512,1024]{1,0:T(8,128)(2,1)}, u32[]{:S(2)}, u32[]{:S(2)}) collective-permute-start(bf16[512,1024]{1,0:T(8,128)(2,1)} %convolution_convert_fusion.13), channel_id=1, source_target_pairs={{0,16},{16,0},{1,17},{17,1},{2,18},{18,2},{3,19},{19,3},{4,20},{20... | collective-permute-start | bytes 3145736 | tf_op jit(solution)/shard_map/ppermute | solution.py:170
  221.2 219.7 %reduce-scatter.7.cloned.1.call-start = ((), (), s32[]{:S(2)}) async-start(), calls=%async_computation.11 | async-start | bytes 3604480 | tf_op jit(solution)/shard_map/reduce_scatter | solution.py:156
  228.1 33.5 %collective-permute-start.29 = (bf16[4,64,2816]{2,1,0:T(8,128)(2,1)}, bf16[4,64,2816]{2,1,0:T(8,128)(2,1)}, u32[]{:S(2)}, u32[]{:S(2)}) collective-permute-start(bf16[4,64,2816]{2,1,0:T(8,128)(2,1)} %bitcast.33.refs_0_), channel_id=1, source_target_pairs={{0,1},{1,0},{2,3},{3,2},{4,5},{5,4},{6,7},{7,6},{8,9},{9,8},{10,11... | collective-permute-start | bytes 4325384 | tf_op jit(solution)/shard_map/ppermute | solution.py:140
  229.4 34.2 %collective-permute-start.30 = (bf16[4,64,2816]{2,1,0:T(8,128)(2,1)}, bf16[4,64,2816]{2,1,0:T(8,128)(2,1)}, u32[]{:S(2)}, u32[]{:S(2)}) collective-permute-start(bf16[4,64,2816]{2,1,0:T(8,128)(2,1)} %bitcast.33.refs_0_), channel_id=1, source_target_pairs={{0,2},{1,3},{2,0},{3,1},{4,6},{5,7},{6,4},{7,5},{8,10},{9,11},{10,... | collective-permute-start | bytes 4325384 | tf_op jit(solution)/shard_map/ppermute | solution.py:140
  245.2 22.9 %collective-permute-start.28 = (bf16[512,1024]{1,0:T(8,128)(2,1)}, bf16[512,1024]{1,0:T(8,128)(2,1)}, u32[]{:S(2)}, u32[]{:S(2)}) collective-permute-start(bf16[512,1024]{1,0:T(8,128)(2,1)} %convolution_convert_fusion.14), channel_id=1, source_target_pairs={{0,16},{16,0},{1,17},{17,1},{2,18},{18,2},{3,19},{19,3},{4,20},{20... | collective-permute-start | bytes 3145736 | tf_op jit(solution)/shard_map/ppermute | solution.py:170
  263.6 19.7 %collective-permute-start.31 = (bf16[2,64,2816]{2,1,0:T(8,128)(2,1)}, bf16[2,64,2816]{2,1,0:T(8,128)(2,1)}, u32[]{:S(2)}, u32[]{:S(2)}) collective-permute-start(bf16[2,64,2816]{2,1,0:T(8,128)(2,1)} %slice.288), channel_id=1, source_target_pairs={{0,2},{1,3},{2,0},{3,1},{4,6},{5,7},{6,4},{7,5},{8,10},{9,11},{10,... | collective-permute-start | bytes 2162696 | tf_op jit(solution)/shard_map/ppermute | solution.py:140
  266.8 16.8 %collective-permute-start.32 = (bf16[2,64,2816]{2,1,0:T(8,128)(2,1)}, bf16[2,64,2816]{2,1,0:T(8,128)(2,1)}, u32[]{:S(2)}, u32[]{:S(2)}) collective-permute-start(bf16[2,64,2816]{2,1,0:T(8,128)(2,1)} %slice.289), channel_id=1, source_target_pairs={{0,1},{1,0},{2,3},{3,2},{4,5},{5,4},{6,7},{7,6},{8,9},{9,8},{10,11... | collective-permute-start | bytes 2162696 | tf_op jit(solution)/shard_map/ppermute | solution.py:140
  282.0 9.5 %collective-permute-start.33 = (bf16[1408,512]{1,0:T(8,128)(2,1)S(1)}, bf16[1408,512]{1,0:T(8,128)(2,1)S(1)}, u32[]{:S(2)}, u32[]{:S(2)}) collective-permute-start(bf16[1408,512]{1,0:T(8,128)(2,1)S(1)} %get-tuple-element.399), channel_id=1, source_target_pairs={{0,16},{16,0},{1,17},{17,1},{2,18},{18,2},{3,19},{19,3},{4,20},{20... | collective-permute-start | bytes 4325384 | tf_op jit(solution)/shard_map/ppermute | solution.py:170
  297.0 18.2 %collective-permute-start.41 = (bf16[1408,512]{1,0:T(8,128)(2,1)S(1)}, bf16[1408,512]{1,0:T(8,128)(2,1)S(1)}, u32[]{:S(2)}, u32[]{:S(2)}) collective-permute-start(bf16[1408,512]{1,0:T(8,128)(2,1)S(1)} %convolution_convert_fusion.4), channel_id=1, source_target_pairs={{0,16},{16,0},{1,17},{17,1},{2,18},{18,2},{3,19},{19,3},{4,20},{20... | collective-permute-start | bytes 4325384 | tf_op jit(solution)/shard_map/ppermute | solution.py:170
  317.3 149.5 %reduce-scatter.9.cloned.1.call-start = ((), (), s32[]{:S(2)}) async-start(), calls=%async_computation.12 | async-start | bytes 1802240 | tf_op jit(solution)/shard_map/reduce_scatter | solution.py:156
  317.4 35.0 %collective-permute-start.37 = (bf16[2,2,64,2816]{3,2,1,0:T(8,128)(2,1)}, bf16[2,2,64,2816]{3,2,1,0:T(8,128)(2,1)S(1)}, u32[]{:S(2)}, u32[]{:S(2)}) collective-permute-start(bf16[2,2,64,2816]{3,2,1,0:T(8,128)(2,1)} %copy-done.68), channel_id=1, source_target_pairs={{0,1},{1,0},{2,3},{3,2},{4,5},{5,4},{6,7},{7,6},{8,9},{9,8},{10,11... | collective-permute-start | bytes 4325384 | tf_op jit(solution)/shard_map/ppermute | solution.py:140
  318.7 32.7 %collective-permute-start.38 = (bf16[2,2,64,2816]{3,2,1,0:T(8,128)(2,1)}, bf16[2,2,64,2816]{3,2,1,0:T(8,128)(2,1)S(1)}, u32[]{:S(2)}, u32[]{:S(2)}) collective-permute-start(bf16[2,2,64,2816]{3,2,1,0:T(8,128)(2,1)} %copy-done.69), channel_id=1, source_target_pairs={{0,2},{1,3},{2,0},{3,1},{4,6},{5,7},{6,4},{7,5},{8,10},{9,11},{10,... | collective-permute-start | bytes 4325384 | tf_op jit(solution)/shard_map/ppermute | solution.py:140
  326.4 26.3 %collective-permute-start.36 = (bf16[512,512]{1,0:T(8,128)(2,1)S(1)}, bf16[512,512]{1,0:T(8,128)(2,1)S(1)}, u32[]{:S(2)}, u32[]{:S(2)}) collective-permute-start(bf16[512,512]{1,0:T(8,128)(2,1)S(1)} %convolution_convert_fusion.18), channel_id=1, source_target_pairs={{0,16},{16,0},{1,17},{17,1},{2,18},{18,2},{3,19},{19,3},{4,20},{20... | collective-permute-start | bytes 1572872 | tf_op jit(solution)/shard_map/ppermute | solution.py:170
  352.4 19.7 %collective-permute-start.42 = (bf16[2,64,2816]{2,1,0:T(8,128)(2,1)}, bf16[2,64,2816]{2,1,0:T(8,128)(2,1)}, u32[]{:S(2)}, u32[]{:S(2)}) collective-permute-start(bf16[2,64,2816]{2,1,0:T(8,128)(2,1)} %fusion.54), channel_id=1, source_target_pairs={{0,1},{1,0},{2,3},{3,2},{4,5},{5,4},{6,7},{7,6},{8,9},{9,8},{10,11... | collective-permute-start | bytes 2162696 | tf_op jit(solution)/shard_map/ppermute | solution.py:140
  357.6 25.0 %collective-permute-start.39 = (bf16[512,1024]{1,0:T(8,128)(2,1)}, bf16[512,1024]{1,0:T(8,128)(2,1)}, u32[]{:S(2)}, u32[]{:S(2)}) collective-permute-start(bf16[512,1024]{1,0:T(8,128)(2,1)} %add_convert_fusion.4), channel_id=1, source_target_pairs={{0,16},{16,0},{1,17},{17,1},{2,18},{18,2},{3,19},{19,3},{4,20},{20... | collective-permute-start | bytes 3145736 | tf_op jit(solution)/shard_map/ppermute | solution.py:170
  360.2 18.1 %collective-permute-start.43 = (bf16[2,64,2816]{2,1,0:T(8,128)(2,1)}, bf16[2,64,2816]{2,1,0:T(8,128)(2,1)}, u32[]{:S(2)}, u32[]{:S(2)}) collective-permute-start(bf16[2,64,2816]{2,1,0:T(8,128)(2,1)} %fusion.53), channel_id=1, source_target_pairs={{0,2},{1,3},{2,0},{3,1},{4,6},{5,7},{6,4},{7,5},{8,10},{9,11},{10,... | collective-permute-start | bytes 2162696 | tf_op jit(solution)/shard_map/ppermute | solution.py:140
  360.4 10.7 %collective-permute-start.40 = (bf16[512,16]{0,1:T(8,128)(2,1)S(1)}, bf16[512,16]{0,1:T(8,128)(2,1)S(1)}, u32[]{:S(2)}, u32[]{:S(2)}) collective-permute-start(bf16[512,16]{0,1:T(8,128)(2,1)S(1)} %convolution_convert_fusion.22), channel_id=1, source_target_pairs={{0,16},{16,0},{1,17},{17,1},{2,18},{18,2},{3,19},{19,3},{4,20},{20... | collective-permute-start | bytes 49160 | tf_op jit(solution)/shard_map/ppermute | solution.py:170
  372.1 32.4 %collective-permute-start.45 = (bf16[2,2,64,2048]{3,2,1,0:T(8,128)(2,1)}, bf16[2,2,64,2048]{3,2,1,0:T(8,128)(2,1)S(1)}, u32[]{:S(2)}, u32[]{:S(2)}) collective-permute-start(bf16[2,2,64,2048]{3,2,1,0:T(8,128)(2,1)} %get-tuple-element.263), channel_id=1, source_target_pairs={{0,1},{1,0},{2,3},{3,2},{4,5},{5,4},{6,7},{7,6},{8,9},{9,8},{10,11... | collective-permute-start | bytes 3145736 | tf_op jit(solution)/shard_map/ppermute | solution.py:140
  378.3 24.2 %collective-permute-start.46 = (bf16[2,2,64,2048]{3,2,1,0:T(8,128)(2,1)}, bf16[2,2,64,2048]{3,2,1,0:T(8,128)(2,1)}, u32[]{:S(2)}, u32[]{:S(2)}) collective-permute-start(bf16[2,2,64,2048]{3,2,1,0:T(8,128)(2,1)} %get-tuple-element.265), channel_id=1, source_target_pairs={{0,2},{1,3},{2,0},{3,1},{4,6},{5,7},{6,4},{7,5},{8,10},{9,11},{10,... | collective-permute-start | bytes 3145736 | tf_op jit(solution)/shard_map/ppermute | solution.py:140
  382.4 150.5 %reduce-scatter.11.cloned.1.call-start = ((), (), s32[]{:S(2)}) async-start(), calls=%async_computation.13 | async-start | bytes 1310720 | tf_op jit(solution)/shard_map/reduce_scatter | solution.py:156
  395.1 10.3 %collective-permute-start.48 = (bf16[1408,512]{1,0:T(8,128)(2,1)S(1)}, bf16[1408,512]{1,0:T(8,128)(2,1)S(1)}, u32[]{:S(2)}, u32[]{:S(2)}) collective-permute-start(bf16[1408,512]{1,0:T(8,128)(2,1)S(1)} %convolution_convert_fusion.2), channel_id=1, source_target_pairs={{0,16},{16,0},{1,17},{17,1},{2,18},{18,2},{3,19},{19,3},{4,20},{20... | collective-permute-start | bytes 4325384 | tf_op jit(solution)/shard_map/ppermute | solution.py:170
  400.3 33.4 %collective-permute-start.44 = (bf16[512,1024]{1,0:T(8,128)(2,1)}, bf16[512,1024]{1,0:T(8,128)(2,1)}, u32[]{:S(2)}, u32[]{:S(2)}) collective-permute-start(bf16[512,1024]{1,0:T(8,128)(2,1)} %convolution_convert_fusion.10), channel_id=1, source_target_pairs={{0,16},{16,0},{1,17},{17,1},{2,18},{18,2},{3,19},{19,3},{4,20},{20... | collective-permute-start | bytes 3145736 | tf_op jit(solution)/shard_map/ppermute | solution.py:170
  407.5 11.7 %collective-permute-start.49 = (bf16[2,64,2048]{2,1,0:T(8,128)(2,1)S(1)}, bf16[2,64,2048]{2,1,0:T(8,128)(2,1)S(1)}, u32[]{:S(2)}, u32[]{:S(2)}) collective-permute-start(bf16[2,64,2048]{2,1,0:T(8,128)(2,1)S(1)} %copy-done.102), channel_id=1, source_target_pairs={{0,1},{1,0},{2,3},{3,2},{4,5},{5,4},{6,7},{7,6},{8,9},{9,8},{10,11... | collective-permute-start | bytes 1572872 | tf_op jit(solution)/shard_map/ppermute | solution.py:140
  408.7 11.7 %collective-permute-start.50 = (bf16[2,64,2048]{2,1,0:T(8,128)(2,1)}, bf16[2,64,2048]{2,1,0:T(8,128)(2,1)S(1)}, u32[]{:S(2)}, u32[]{:S(2)}) collective-permute-start(bf16[2,64,2048]{2,1,0:T(8,128)(2,1)} %fusion.59), channel_id=1, source_target_pairs={{0,2},{1,3},{2,0},{3,1},{4,6},{5,7},{6,4},{7,5},{8,10},{9,11},{10,... | collective-permute-start | bytes 1572872 | tf_op jit(solution)/shard_map/ppermute | solution.py:140
  425.2 115.1 %reduce-scatter.17.cloned.1.call-start = ((), (), s32[]{:S(2)}) async-start(), calls=%async_computation.16 | async-start | bytes 3604480 | tf_op jit(solution)/shard_map/reduce_scatter | solution.py:156
  440.9 30.5 %collective-permute-start.51 = (bf16[2,2,64,2816]{3,2,1,0:T(8,128)(2,1)}, bf16[2,2,64,2816]{3,2,1,0:T(8,128)(2,1)}, u32[]{:S(2)}, u32[]{:S(2)}) collective-permute-start(bf16[2,2,64,2816]{3,2,1,0:T(8,128)(2,1)} %get-tuple-element.281), channel_id=1, source_target_pairs={{0,1},{1,0},{2,3},{3,2},{4,5},{5,4},{6,7},{7,6},{8,9},{9,8},{10,11... | collective-permute-start | bytes 4325384 | tf_op jit(solution)/shard_map/ppermute | solution.py:140
  441.1 30.3 %collective-permute-start.52 = (bf16[2,2,64,2816]{3,2,1,0:T(8,128)(2,1)}, bf16[2,2,64,2816]{3,2,1,0:T(8,128)(2,1)}, u32[]{:S(2)}, u32[]{:S(2)}) collective-permute-start(bf16[2,2,64,2816]{3,2,1,0:T(8,128)(2,1)} %get-tuple-element.283), channel_id=1, source_target_pairs={{0,2},{1,3},{2,0},{3,1},{4,6},{5,7},{6,4},{7,5},{8,10},{9,11},{10,... | collective-permute-start | bytes 4325384 | tf_op jit(solution)/shard_map/ppermute | solution.py:140
  446.6 66.1 %collective-permute-start.34 = (bf16[512,1024]{1,0:T(8,128)(2,1)}, bf16[512,1024]{1,0:T(8,128)(2,1)}, u32[]{:S(2)}, u32[]{:S(2)}) collective-permute-start(bf16[512,1024]{1,0:T(8,128)(2,1)} %convolution_convert_fusion.12), channel_id=1, source_target_pairs={{0,16},{16,0},{1,17},{17,1},{2,18},{18,2},{3,19},{19,3},{4,20},{20... | collective-permute-start | bytes 3145736 | tf_op jit(solution)/shard_map/ppermute | solution.py:170
  449.8 105.3 %reduce-scatter.15.cloned.1.call-start = ((), (), s32[]{:S(2)}) async-start(), calls=%async_computation.15 | async-start | bytes 1802240 | tf_op jit(solution)/shard_map/reduce_scatter | solution.py:156
  471.9 18.5 %collective-permute-start.54 = (bf16[512,16]{0,1:T(8,128)(2,1)S(1)}, bf16[512,16]{0,1:T(8,128)(2,1)S(1)}, u32[]{:S(2)}, u32[]{:S(2)}) collective-permute-start(bf16[512,16]{0,1:T(8,128)(2,1)S(1)} %convolution_convert_fusion.23), channel_id=1, source_target_pairs={{0,16},{16,0},{1,17},{17,1},{2,18},{18,2},{3,19},{19,3},{4,20},{20... | collective-permute-start | bytes 49160 | tf_op jit(solution)/shard_map/ppermute | solution.py:170
  481.2 9.5 %collective-permute-start.53 = (bf16[512,1024]{1,0:T(8,128)(2,1)}, bf16[512,1024]{1,0:T(8,128)(2,1)}, u32[]{:S(2)}, u32[]{:S(2)}) collective-permute-start(bf16[512,1024]{1,0:T(8,128)(2,1)} %add_convert_fusion.1), channel_id=1, source_target_pairs={{0,16},{16,0},{1,17},{17,1},{2,18},{18,2},{3,19},{19,3},{4,20},{20... | collective-permute-start | bytes 3145736 | tf_op jit(solution)/shard_map/ppermute | solution.py:170
  487.9 19.8 %collective-permute-start.58 = (bf16[2,64,2816]{2,1,0:T(8,128)(2,1)}, bf16[2,64,2816]{2,1,0:T(8,128)(2,1)}, u32[]{:S(2)}, u32[]{:S(2)}) collective-permute-start(bf16[2,64,2816]{2,1,0:T(8,128)(2,1)} %fusion.52), channel_id=1, source_target_pairs={{0,1},{1,0},{2,3},{3,2},{4,5},{5,4},{6,7},{7,6},{8,9},{9,8},{10,11... | collective-permute-start | bytes 2162696 | tf_op jit(solution)/shard_map/ppermute | solution.py:140
  489.4 17.6 %collective-permute-start.60 = (bf16[2,64,2816]{2,1,0:T(8,128)(2,1)}, bf16[2,64,2816]{2,1,0:T(8,128)(2,1)}, u32[]{:S(2)}, u32[]{:S(2)}) collective-permute-start(bf16[2,64,2816]{2,1,0:T(8,128)(2,1)} %fusion.51), channel_id=1, source_target_pairs={{0,2},{1,3},{2,0},{3,1},{4,6},{5,7},{6,4},{7,5},{8,10},{9,11},{10,... | collective-permute-start | bytes 2162696 | tf_op jit(solution)/shard_map/ppermute | solution.py:140
  506.9 25.1 %collective-permute-start.61 = (bf16[2,2,64,2176]{3,2,1,0:T(8,128)(2,1)}, bf16[2,2,64,2176]{3,2,1,0:T(8,128)(2,1)S(1)}, u32[]{:S(2)}, u32[]{:S(2)}) collective-permute-start(bf16[2,2,64,2176]{3,2,1,0:T(8,128)(2,1)} %get-tuple-element.309), channel_id=1, source_target_pairs={{0,2},{1,3},{2,0},{3,1},{4,6},{5,7},{6,4},{7,5},{8,10},{9,11},{10,... | collective-permute-start | bytes 3342344 | tf_op jit(solution)/shard_map/ppermute | solution.py:140
  512.0 74.5 %reduce-scatter.13.cloned.1.call-start = ((), (), s32[]{:S(2)}) async-start(), calls=%async_computation.14 | async-start | bytes 1392640 | tf_op jit(solution)/shard_map/reduce_scatter | solution.py:156
  512.4 24.8 %collective-permute-start.59 = (bf16[2,2,64,2176]{3,2,1,0:T(8,128)(2,1)}, bf16[2,2,64,2176]{3,2,1,0:T(8,128)(2,1)S(1)}, u32[]{:S(2)}, u32[]{:S(2)}) collective-permute-start(bf16[2,2,64,2176]{3,2,1,0:T(8,128)(2,1)} %copy-done.70), channel_id=1, source_target_pairs={{0,1},{1,0},{2,3},{3,2},{4,5},{5,4},{6,7},{7,6},{8,9},{9,8},{10,11... | collective-permute-start | bytes 3342344 | tf_op jit(solution)/shard_map/ppermute | solution.py:140
  537.2 12.0 %collective-permute-start.62 = (bf16[2,64,2176]{2,1,0:T(8,128)(2,1)}, bf16[2,64,2176]{2,1,0:T(8,128)(2,1)}, u32[]{:S(2)}, u32[]{:S(2)}) collective-permute-start(bf16[2,64,2176]{2,1,0:T(8,128)(2,1)} %fusion.57), channel_id=1, source_target_pairs={{0,1},{1,0},{2,3},{3,2},{4,5},{5,4},{6,7},{7,6},{8,9},{9,8},{10,11... | collective-permute-start | bytes 1671176 | tf_op jit(solution)/shard_map/ppermute | solution.py:140
  539.6 11.8 %collective-permute-start.63 = (bf16[2,64,2176]{2,1,0:T(8,128)(2,1)}, bf16[2,64,2176]{2,1,0:T(8,128)(2,1)}, u32[]{:S(2)}, u32[]{:S(2)}) collective-permute-start(bf16[2,64,2176]{2,1,0:T(8,128)(2,1)} %fusion.56), channel_id=1, source_target_pairs={{0,2},{1,3},{2,0},{3,1},{4,6},{5,7},{6,4},{7,5},{8,10},{9,11},{10,... | collective-permute-start | bytes 1671176 | tf_op jit(solution)/shard_map/ppermute | solution.py:140
  558.2 25.1 %collective-permute-start.65 = (bf16[64,2816]{1,0:T(8,128)(2,1)S(1)}, bf16[64,2816]{1,0:T(8,128)(2,1)S(1)}, u32[]{:S(2)}, u32[]{:S(2)}) collective-permute-start(bf16[64,2816]{1,0:T(8,128)(2,1)S(1)} %get-tuple-element.417), channel_id=1, source_target_pairs={{0,16},{16,0},{1,17},{17,1},{2,18},{18,2},{3,19},{19,3},{4,20},{20... | collective-permute-start | bytes 1081352 | tf_op jit(solution)/shard_map/ppermute | solution.py:170
  573.1 12.0 %collective-permute-start.72 = (bf16[176,512]{1,0:T(8,128)(2,1)S(1)}, bf16[176,512]{1,0:T(8,128)(2,1)S(1)}, u32[]{:S(2)}, u32[]{:S(2)}) collective-permute-start(bf16[176,512]{1,0:T(8,128)(2,1)S(1)} %get-tuple-element.425), channel_id=1, source_target_pairs={{0,16},{16,0},{1,17},{17,1},{2,18},{18,2},{3,19},{19,3},{4,20},{20... | collective-permute-start | bytes 540680 | tf_op jit(solution)/shard_map/ppermute | solution.py:170
  (157 other events, 1088.5 us)
Sparse Core Ops, SparseCore 0:
  18.0 30.8 all-gather.5
  51.0 33.8 all-gather.7
  87.1 39.9 all-gather.9
  141.2 37.9 all-gather.11
  221.3 58.5 all-gather.13
  317.4 55.8 reduce-scatter.6
  382.5 34.3 reduce-scatter.8
  425.3 28.4 reduce-scatter.10
  456.2 54.7 reduce-scatter.16
  513.3 33.0 reduce-scatter.14
  555.2 31.3 reduce-scatter.12

commit v4 on v3

--- a/solution.py
+++ b/solution.py
@@ -415,8 +415,8 @@
         self.gx, self.gy = self.links.x(self.Sx), self.links.y(self.Sy)
 
     def rest(self):
-        self.tx = self.links.x(add(self.Rx, self.gy[0]))
-        self.ty = self.links.y(add(self.Ry, self.gx[0]))
+        self.last = add(self.Rx, self.gy[0]), add(self.Ry, self.gx[0])
+        self.tx, self.ty = self.links.x(self.last[0]), self.links.y(self.last[1])
 
     def along(self, due):
         self.sum = self.links.scatter(sum_slabs(self.own, self.gx, self.gy, self.tx, self.ty), due)
@@ -483,6 +483,16 @@
     j = lax.broadcasted_iota(jnp.int32, (length, length), 1)
     return (i >= j) & (i // SPAN == j // SPAN)
 
+def sum_parts(ones, v, axis):
+    high = v.astype(BF)
+    rest = v - high.astype(F32)
+    middle = rest.astype(BF)
+    low = (rest - middle.astype(F32)).astype(BF)
+    dims = (((axis,), (0,)), ((), ()))
+    dot = partial(lax.dot_general, dimension_numbers=dims, preferred_element_type=F32)
+    return dot(ones, high) + (dot(ones, middle) + dot(ones, low))
+
+
 def head_state(pre, logits, h, K, V, heads, keep):
     kh, vh = K // heads, V // heads
     length = pre.shape[0]
@@ -491,8 +501,8 @@
     v = pre[:, 2 * K + h * vh : 2 * K + (h + 1) * vh]
     x = logits[:, h * kh : (h + 1) * kh]
     a = (jnp.minimum(x, 0.0) - jnp.log1p(jnp.exp(-jnp.abs(x)))) * (1.0 / 16.0)
-    tri = jnp.where(keep, 1.0, 0.0)
-    b = lax.dot_general(tri, a, (((1,), (0,)), ((), ())), precision=lax.Precision.HIGHEST, preferred_element_type=F32)
+    tri = jnp.where(keep, 1.0, 0.0).astype(BF)
+    b = sum_parts(tri, a, 1)
     n = length // SPAN
     lasts = [b[(i + 1) * SPAN - 1 : (i + 1) * SPAN] for i in range(n)]
     last = jnp.concatenate([jnp.broadcast_to(t, (SPAN, kh)) for t in lasts], 0)
@@ -581,8 +591,8 @@
         dkc = jnp.concatenate(dkc, 0)
         dv = dv + jnp.concatenate(dv_c, 0)
         db = dqs * st["qs"] - dks * st["ks"] - dkc * st["kc"]
-        tri = jnp.where(keep, 1.0, 0.0)
-        da = lax.dot_general(tri, db, (((0,), (0,)), ((), ())), precision=lax.Precision.HIGHEST, preferred_element_type=F32)
+        tri = jnp.where(keep, 1.0, 0.0).astype(BF)
+        da = sum_parts(tri, db, 0)
         da = da + jnp.concatenate(dlast, 0)
         x = st["x"]
         dlog_ref[:, h * kh : (h + 1) * kh] = da * (1.0 / 16.0) * (1.0 - jax.nn.sigmoid(x))
@@ -657,12 +667,16 @@
     return dict(hidden=hidden, r=r, second=second, gu=gu)
 
 
-def contract(f, w, mask):
+def activate(f):
     gu = f["gu"]
     F = gu.shape[1] // 2
     gate, up = gu[:, :F].astype(F32), gu[:, F:].astype(F32)
-    act = (gate * jax.nn.sigmoid(gate) * up).astype(BF)
-    return (f["hidden"] + core_sum(mm(act, w["WD"]))) * mask, dict(f, act=act)
+    return dict(f, act=(gate * jax.nn.sigmoid(gate) * up).astype(BF))
+
+
+def contract(f, w, mask):
+    f = activate(f)
+    return (f["hidden"] + core_sum(mm(f["act"], w["WD"]))) * mask, f
 
 
 def column_halves(v, s):
@@ -869,8 +883,7 @@
     w1["WD"] = place_down(1)
     w1["WF"] = place_ff(1)
     f1 = expand(h1, w1)
-    y1, f1 = contract(f1, w1, mask)
-    layer_out = jnp.where(first, x1, y1.astype(BF)).reshape((1,) + shape)
+    f1 = activate(f1)
 
     def all_rows(keep, got):
         return jnp.where(first, jnp.concatenate([keep, got], 0), jnp.concatenate([got, keep], 0))
@@ -913,7 +926,11 @@
     low = dh1.astype(BF)
     gO1 = row_grads(m1["gated"], low, s)
     back = mixer_bwd(m1["pre"], m1["logits"], w1["gg"], mm_nt(low, w1["WO"]).astype(BF), rows)
-    dh1, d_mg1, gO1, back = paced(dh1, d_mg1, gO1, back)
+    act = after(f1["act"], dh1) if meshed else f1["act"]
+    y1 = (f1["hidden"] + core_sum(mm(act, w1["WD"]))) * mask
+    y1, dh1, d_mg1, gO1, back = paced(y1, dh1, d_mg1, gO1, back)
+    if meshed:
+        links.before += [y1]
     rF1.rest()
     rA1 = sum_ao(m1["n"], back[0], gO1)
     dx1, small1 = paced(*project_back(dh1, *back, d_mg1, m1, w1))
@@ -933,6 +950,8 @@
     low = dh0.astype(BF)
     gO0 = row_grads(m0["gated"], low, s)
     dgated, gO0, dh0 = paced(mm_nt(low, w0["WO"]).astype(BF), gO0, dh0)
+    if meshed:
+        rA1.own = after(rA1.own, rF0.own)
     rF0.sides(), rA1.along(9)
     back = paced(mixer_bwd(m0["pre"], m0["logits"], w0["gg"], dgated, rows))
     rF0.rest()
@@ -966,6 +985,7 @@
         around(links, (rD1, rD0))
 
     input_out = jnp.where(first, dx0, dx1).reshape((1,) + shape)
+    layer_out = jnp.where(first, x1, y1.astype(BF)).reshape((1,) + shape)
 
     def join(a, b, widths):
         keep = jnp.where(first, a, b)

time: 610 us -> 605 us (level)
  waiting for transfers between devices: 172 us -> 185 us
  Pallas kernels: 99.4 us -> 89.6 us
    reduce_scatter x6, waiting for transfers between devices: 0.06 us -> 8.29 us  [scatter(): lax.psum_scatter(v, 'dp', scatter_dimension=0, tiled=True, axis_index_gro...]
    ppermute x27, starting transfers between devices: 42.3 us -> 35.5 us  [over_core(): return lax.ppermute(v, 'section', [(0, 1), (1, 0)])]
    unnamed x282 -> x260, local copies, waits for them, and re-layouts: 35.4 us -> 31 us
  transfers between devices with their start and end apart: 84 -> 84, of which waited for: 33 -> 36; matrix products, arithmetic and copies ran while one was open for 31% -> 31% of each run, Pallas kernels for 16% -> 13%
where the time goes in v4:
time: 605 us; the launch traced here: 596 us
  waiting for transfers between devices  185 us (31%)
  other arithmetic  94.9 us (16%)
  Pallas kernels  89.6 us (15%)
  starting transfers between devices  80.5 us (13%)
  local copies, waits for them, and re-layouts  70.2 us (12%)
  matrix products  59.4 us (10%)
  between operations  16.1 us (3%)
    ppermute x46, waiting for transfers between devices, hop(): sent.append(lax.ppermute(v, 'dp', pairs(*step)))  150 us
    ppermute x46, starting transfers between devices, hop(): sent.append(lax.ppermute(v, 'dp', pairs(*step)))  43.3 us
    ppermute x27, starting transfers between devices, over_core(): return lax.ppermute(v, 'section', [(0, 1), (1, 0)])  35.5 us
    unnamed x260, local copies, waits for them, and re-layouts  31 us
    pallas_call x10, Pallas kernels, copy_call(): pl.pallas_call(kernel, grid_spec=pltpu.PrefetchScalarGridSpec(num_scalar_...  25.9 us
    all_gather x5, waiting for transfers between devices, gather(): v = lax.all_gather(v, 'dp', axis=0, tiled=True, axis_index_groups=LINES)  23.2 us
    dot_general x10, matrix products, mm(): lax.dot_general(a.astype(BF), b.astype(BF), (((1,), (0,)), ((), ())), pre...  23 us
    dot_general x10, matrix products, mm_nt(): lax.dot_general(a.astype(BF), b.astype(BF), (((1,), (1,)), ((), ())), pre...  22.4 us
  transfers between devices with their start and end apart: 84, of which 36 were waited for; matrix products, arithmetic and copies ran while one was open for 31% of the time, Pallas kernels for 13%

profile of v4, /device:TPU:1, one launch (start us, length us, event | category | flops | bytes accessed | tf_op | source)
XLA Modules:
  0.0 595.8 jit_solution(398532638862323767)
XLA Ops:
  9.2 3.5 shard_map.288
  26.1 3.4 collective-permute-done.2
  34.1 14.8 %all-gather.6.cloned.1.call-done = bf16[256,2176]{1,0:T(8,128)(2,1)} async-done(((bf16[64,2176]{1,0:T(8,128)(2,1)}), bf16[256,2176]{1,0:T(8,128)(2,1)}) %all-gather.6.cloned.1.call-update) | async-done | bytes 1114128 | tf_op jit(solution)/shard_map/all_gather | solution.py:150
  52.8 21.7 %collective-permute-done.5.refs_1_ = bf16[4,64,2176]{2,1,0:T(8,128)(2,1)S(1)} collective-permute-done((bf16[4,64,2176]{2,1,0:T(8,128)(2,1)}, bf16[4,64,2176]{2,1,0:T(8,128)(2,1)S(1)}, u32[]{:S(2)}, u32[]{:S(2)}) %collective-permute-start.5) | collective-permute-done | bytes 1114144 | tf_op jit(solution)/shard_map/ppermute | solution.py:140
  82.2 5.5 collective-permute-done.8.refs_3_
  103.8 3.5 collective-permute-start.10
  107.3 2.5 multiply_convert_fusion.4
  110.4 4.0 convolution_convert_fusion.9.pre_ref
  114.4 3.0 shard_map.290
  118.6 2.5 shard_map.291
  122.9 5.7 collective-permute-done.13.refs_1_
  144.7 2.6 reshape.409.refs_0_
  152.0 9.3 %collective-permute-done.17.refs_1_ = bf16[4,176,512]{2,1,0:T(8,128)(2,1)S(1)} collective-permute-done((bf16[4,176,512]{2,1,0:T(8,128)(2,1)}, bf16[4,176,512]{2,1,0:T(8,128)(2,1)S(1)}, u32[]{:S(2)}, u32[]{:S(2)}) %collective-permute-start.17) | collective-permute-done | bytes 720928 | tf_op jit(solution)/shard_map/ppermute | solution.py:140
  163.8 3.7 shard_map.292
  173.3 7.0 %collective-permute-start.21 = (bf16[1408,512]{1,0:T(8,128)(2,1)}, bf16[1408,512]{1,0:T(8,128)(2,1)}, u32[]{:S(2)}, u32[]{:S(2)}) collective-permute-start(bf16[1408,512]{1,0:T(8,128)(2,1)} %bitcast.25), channel_id=1, source_target_pairs={{0,16},{16,0},{1,17},{17,1},{2,18},{18,2},{3,19},{19,3},{4,20},{20... | collective-permute-start | bytes 4325384 | tf_op jit(solution)/shard_map/ppermute | solution.py:170
  182.0 4.5 convolution_convert_fusion.1
  186.5 2.7 fusion.21
  189.2 16.5 %collective-permute-done.23.refs_1_ = bf16[4,64,2048]{2,1,0:T(8,128)(2,1)} collective-permute-done((bf16[4,64,2048]{2,1,0:T(8,128)(2,1)S(1)}, bf16[4,64,2048]{2,1,0:T(8,128)(2,1)}, u32[]{:S(2)}, u32[]{:S(2)}) %collective-permute-start.23) | collective-permute-done | bytes 1048608 | tf_op jit(solution)/shard_map/ppermute | solution.py:140
  210.7 2.8 shard_map.294
  213.5 2.8 convolution_convert_fusion.13
  222.3 3.4 shard_map.295
  237.4 3.0 shard_map.296
  242.7 2.5 bitcast_multiply_fusion
  246.9 14.2 %collective-permute-done.29.refs_1_ = bf16[4,64,2816]{2,1,0:T(8,128)(2,1)} collective-permute-done((bf16[4,64,2816]{2,1,0:T(8,128)(2,1)}, bf16[4,64,2816]{2,1,0:T(8,128)(2,1)}, u32[]{:S(2)}, u32[]{:S(2)}) %collective-permute-start.29) | collective-permute-done | bytes 1441824 | tf_op jit(solution)/shard_map/ppermute | solution.py:140
  267.9 3.5 add_add_fusion
  271.3 8.4 %all-gather.14.cloned.1.call-done = bf16[2816,512]{1,0:T(8,128)(2,1)} async-done(((bf16[704,512]{1,0:T(8,128)(2,1)}), bf16[2816,512]{1,0:T(8,128)(2,1)}) %all-gather.14.cloned.1.call-update) | async-done | bytes 2883600 | tf_op jit(solution)/shard_map/all_gather | solution.py:150
  283.5 4.4 shard_map.298
  287.9 3.4 convolution_convert_fusion
  292.6 3.2 fusion.6
  296.0 5.9 shard_map.300
  302.0 2.6 convolution_convert_fusion.4
  307.0 4.1 convolution_convert_fusion.11
  314.8 3.4 maximum_select_fusion
  318.3 3.1 fusion.44
  321.4 3.8 fusion.101
  329.7 8.1 %shard_map.301 = (bf16[512,1536]{1,0:T(8,128)(2,1)S(1)}, f32[512,256]{1,0:T(8,128)S(1)}, f32[1,256]{1,0:T(1,128)S(1)}) custom-call(bf16[512,1536]{1,0:T(8,128)(2,1)S(1)} %copy-done.3, f32[512,256]{1,0:T(8,128)S(1)} %convolution_add_fusion.logits_ref, f32[1,256]{1,0:T(1,128)S(1)} %reshape.402.gain_ref, bf16[512,512]{1,0:T(8,128)(2,1)S(1)} %convolution_convert_fusion.21.dg_ref), custom_call_target="tpu_custom_call" | custom-call | tf_op jit(solution)/shard_map/pallas_call | solution.py:628
  339.3 5.7 collective-permute-done.38.gy
  350.1 2.8 add_convert_fusion.4
  362.2 4.8 shard_map.303
  368.8 3.9 collective-permute-done.42.tx
  374.7 4.3 shard_map.304
  379.3 3.6 fusion.46
  385.5 3.0 copy-done.11
  388.4 2.7 fusion.9
  391.2 3.2 convolution_convert_fusion.10
  399.3 5.5 shard_map.302
  404.8 2.5 fusion.59
  414.2 4.8 fusion.35
  419.0 6.1 %collective-permute-done.49.tx = bf16[2,64,2048]{2,1,0:T(8,128)(2,1)S(1)} collective-permute-done((bf16[2,64,2048]{2,1,0:T(8,128)(2,1)}, bf16[2,64,2048]{2,1,0:T(8,128)(2,1)S(1)}, u32[]{:S(2)}, u32[]{:S(2)}) %collective-permute-start.49) | collective-permute-done | bytes 524320 | tf_op jit(solution)/shard_map/ppermute | solution.py:140
  427.3 3.6 shard_map.307
  440.6 8.0 %shard_map.305 = (bf16[512,1536]{1,0:T(8,128)(2,1)S(1)}, f32[512,256]{1,0:T(8,128)S(1)}, f32[1,256]{1,0:T(1,128)S(1)}) custom-call(bf16[512,1536]{1,0:T(8,128)(2,1)S(1)} %copy-done.1, f32[512,256]{1,0:T(8,128)S(1)} %convolution_add_fusion.1.logits_ref, f32[1,256]{1,0:T(1,128)S(1)} %reshape.399.gain_ref, bf16[512,512]{1,0:T(8,128)(2,1)S(1)} %convolution_convert_fusion.20.dg_ref), custom_call_target="tpu_custom_call" | custom-call | tf_op jit(solution)/shard_map/pallas_call | solution.py:628
  449.8 13.3 %collective-permute-done.51.gx = bf16[2,2,64,2816]{3,2,1,0:T(8,128)(2,1)} collective-permute-done((bf16[2,2,64,2816]{3,2,1,0:T(8,128)(2,1)}, bf16[2,2,64,2816]{3,2,1,0:T(8,128)(2,1)}, u32[]{:S(2)}, u32[]{:S(2)}) %collective-permute-start.51) | collective-permute-done | bytes 1441824 | tf_op jit(solution)/shard_map/ppermute | solution.py:140
  466.6 3.9 add_convert_fusion.1
  479.9 3.1 fusion.50
  485.5 4.8 shard_map.306
  496.5 4.3 shard_map.308
  505.9 13.9 %collective-permute-done.61.gy = bf16[2,2,64,2176]{3,2,1,0:T(8,128)(2,1)S(1)} collective-permute-done((bf16[2,2,64,2176]{3,2,1,0:T(8,128)(2,1)}, bf16[2,2,64,2176]{3,2,1,0:T(8,128)(2,1)S(1)}, u32[]{:S(2)}, u32[]{:S(2)}) %collective-permute-start.61) | collective-permute-done | bytes 1114144 | tf_op jit(solution)/shard_map/ppermute | solution.py:140
  520.7 4.9 collective-permute-done.59.gx
  534.0 3.2 collective-permute-done.62.tx
  539.6 3.7 shard_map.309
  543.3 8.3 %reduce-scatter.15.cloned.1.call-done = bf16[64,2816]{1,0:T(8,128)(2,1)} async-done(((bf16[256,2816]{1,0:T(8,128)(2,1)}), bf16[64,2816]{1,0:T(8,128)(2,1)}) %reduce-scatter.15.cloned.1.call-update) | async-done | bytes 360464 | tf_op jit(solution)/shard_map/reduce_scatter | solution.py:156
  560.4 2.8 collective-permute-done.67
  570.3 3.9 collective-permute-start.72
  574.2 3.9 fusion.32
  (581 shorter events, 242.3 us)
Async XLA Ops:
  7.2 41.7 %all-gather.6.cloned.1.call-start = ((), (), s32[]{:S(2)}) async-start(), calls=%async_computation.6 | async-start | bytes 1392640 | tf_op jit(solution)/shard_map/all_gather | solution.py:150
  17.8 80.4 %all-gather.8.cloned.1.call-start = ((), (), s32[]{:S(2)}) async-start(), calls=%async_computation.7 | async-start | bytes 1802240 | tf_op jit(solution)/shard_map/all_gather | solution.py:150
  20.8 119.0 %all-gather.10.cloned.1.call-start = ((), (), s32[]{:S(2)}) async-start(), calls=%async_computation.8 | async-start | bytes 2211840 | tf_op jit(solution)/shard_map/all_gather | solution.py:150
  31.5 18.6 %collective-permute-start.6 = (bf16[176,256]{1,0:T(8,128)(2,1)S(1)}, bf16[176,256]{1,0:T(8,128)(2,1)}, u32[]{:S(2)}, u32[]{:S(2)}) collective-permute-start(bf16[176,256]{1,0:T(8,128)(2,1)S(1)} %slice.257), channel_id=1, source_target_pairs={{0,2},{1,3},{2,0},{3,1},{4,6},{5,7},{6,4},{7,5},{8,10},{9,11},{10,... | collective-permute-start | bytes 270344 | tf_op jit(solution)/shard_map/ppermute | solution.py:140
  48.9 25.5 %collective-permute-start.5 = (bf16[4,64,2176]{2,1,0:T(8,128)(2,1)}, bf16[4,64,2176]{2,1,0:T(8,128)(2,1)S(1)}, u32[]{:S(2)}, u32[]{:S(2)}) collective-permute-start(bf16[4,64,2176]{2,1,0:T(8,128)(2,1)} %bitcast.246), channel_id=1, source_target_pairs={{0,1},{1,0},{2,3},{3,2},{4,5},{5,4},{6,7},{7,6},{8,9},{9,8},{10,11... | collective-permute-start | bytes 3342344 | tf_op jit(solution)/shard_map/ppermute | solution.py:140
  50.1 25.2 %collective-permute-start.7 = (bf16[4,64,2176]{2,1,0:T(8,128)(2,1)}, bf16[4,64,2176]{2,1,0:T(8,128)(2,1)S(1)}, u32[]{:S(2)}, u32[]{:S(2)}) collective-permute-start(bf16[4,64,2176]{2,1,0:T(8,128)(2,1)} %bitcast.247), channel_id=1, source_target_pairs={{0,2},{1,3},{2,0},{3,1},{4,6},{5,7},{6,4},{7,5},{8,10},{9,11},{10,... | collective-permute-start | bytes 3342344 | tf_op jit(solution)/shard_map/ppermute | solution.py:140
  75.3 12.4 %collective-permute-start.8 = (bf16[2,64,2176]{2,1,0:T(8,128)(2,1)}, bf16[2,64,2176]{2,1,0:T(8,128)(2,1)S(1)}, u32[]{:S(2)}, u32[]{:S(2)}) collective-permute-start(bf16[2,64,2176]{2,1,0:T(8,128)(2,1)} %slice.258), channel_id=1, source_target_pairs={{0,2},{1,3},{2,0},{3,1},{4,6},{5,7},{6,4},{7,5},{8,10},{9,11},{10,... | collective-permute-start | bytes 1671176 | tf_op jit(solution)/shard_map/ppermute | solution.py:140
  77.4 12.1 %collective-permute-start.9 = (bf16[2,64,2176]{2,1,0:T(8,128)(2,1)}, bf16[2,64,2176]{2,1,0:T(8,128)(2,1)S(1)}, u32[]{:S(2)}, u32[]{:S(2)}) collective-permute-start(bf16[2,64,2176]{2,1,0:T(8,128)(2,1)} %slice.259), channel_id=1, source_target_pairs={{0,1},{1,0},{2,3},{3,2},{4,5},{5,4},{6,7},{7,6},{8,9},{9,8},{10,11... | collective-permute-start | bytes 1671176 | tf_op jit(solution)/shard_map/ppermute | solution.py:140
  82.1 104.3 %all-gather.12.cloned.1.call-start = ((), (), s32[]{:S(2)}) async-start(), calls=%async_computation.9 | async-start | bytes 1802240 | tf_op jit(solution)/shard_map/all_gather | solution.py:150
  98.3 30.2 %collective-permute-start.13 = (bf16[4,64,2816]{2,1,0:T(8,128)(2,1)}, bf16[4,64,2816]{2,1,0:T(8,128)(2,1)S(1)}, u32[]{:S(2)}, u32[]{:S(2)}) collective-permute-start(bf16[4,64,2816]{2,1,0:T(8,128)(2,1)} %bitcast.242), channel_id=1, source_target_pairs={{0,1},{1,0},{2,3},{3,2},{4,5},{5,4},{6,7},{7,6},{8,9},{9,8},{10,11... | collective-permute-start | bytes 4325384 | tf_op jit(solution)/shard_map/ppermute | solution.py:140
  99.8 30.2 %collective-permute-start.14 = (bf16[4,64,2816]{2,1,0:T(8,128)(2,1)}, bf16[4,64,2816]{2,1,0:T(8,128)(2,1)}, u32[]{:S(2)}, u32[]{:S(2)}) collective-permute-start(bf16[4,64,2816]{2,1,0:T(8,128)(2,1)} %bitcast.243), channel_id=1, source_target_pairs={{0,2},{1,3},{2,0},{3,1},{4,6},{5,7},{6,4},{7,5},{8,10},{9,11},{10,... | collective-permute-start | bytes 4325384 | tf_op jit(solution)/shard_map/ppermute | solution.py:140
  103.8 14.9 %collective-permute-start.10 = (bf16[512,512]{1,0:T(8,128)(2,1)}, bf16[512,512]{1,0:T(8,128)(2,1)}, u32[]{:S(2)}, u32[]{:S(2)}) collective-permute-start(bf16[512,512]{1,0:T(8,128)(2,1)} %bitcast.15), channel_id=1, source_target_pairs={{0,16},{16,0},{1,17},{17,1},{2,18},{18,2},{3,19},{19,3},{4,20},{20... | collective-permute-start | bytes 1572872 | tf_op jit(solution)/shard_map/ppermute | solution.py:170
  122.9 26.5 %collective-permute-start.11 = (bf16[512,1024]{1,0:T(8,128)(2,1)}, bf16[512,1024]{1,0:T(8,128)(2,1)}, u32[]{:S(2)}, u32[]{:S(2)}) collective-permute-start(bf16[512,1024]{1,0:T(8,128)(2,1)} %convolution_convert_fusion.15), channel_id=1, source_target_pairs={{0,16},{16,0},{1,17},{17,1},{2,18},{18,2},{3,19},{19,3},{4,20},{20... | collective-permute-start | bytes 3145736 | tf_op jit(solution)/shard_map/ppermute | solution.py:170
  130.0 17.6 %collective-permute-start.15 = (bf16[2,64,2816]{2,1,0:T(8,128)(2,1)}, bf16[2,64,2816]{2,1,0:T(8,128)(2,1)}, u32[]{:S(2)}, u32[]{:S(2)}) collective-permute-start(bf16[2,64,2816]{2,1,0:T(8,128)(2,1)} %slice.280), channel_id=1, source_target_pairs={{0,2},{1,3},{2,0},{3,1},{4,6},{5,7},{6,4},{7,5},{8,10},{9,11},{10,... | collective-permute-start | bytes 2162696 | tf_op jit(solution)/shard_map/ppermute | solution.py:140
  132.3 15.0 %collective-permute-start.16 = (bf16[2,64,2816]{2,1,0:T(8,128)(2,1)}, bf16[2,64,2816]{2,1,0:T(8,128)(2,1)}, u32[]{:S(2)}, u32[]{:S(2)}) collective-permute-start(bf16[2,64,2816]{2,1,0:T(8,128)(2,1)} %slice.281), channel_id=1, source_target_pairs={{0,1},{1,0},{2,3},{3,2},{4,5},{5,4},{6,7},{7,6},{8,9},{9,8},{10,11... | collective-permute-start | bytes 2162696 | tf_op jit(solution)/shard_map/ppermute | solution.py:140
  141.1 138.6 %all-gather.14.cloned.1.call-start = ((), (), s32[]{:S(2)}) async-start(), calls=%async_computation.10 | async-start | bytes 3604480 | tf_op jit(solution)/shard_map/all_gather | solution.py:150
  147.3 14.0 %collective-permute-start.17 = (bf16[4,176,512]{2,1,0:T(8,128)(2,1)}, bf16[4,176,512]{2,1,0:T(8,128)(2,1)S(1)}, u32[]{:S(2)}, u32[]{:S(2)}) collective-permute-start(bf16[4,176,512]{2,1,0:T(8,128)(2,1)} %reshape.409.refs_0_), channel_id=1, source_target_pairs={{0,1},{1,0},{2,3},{3,2},{4,5},{5,4},{6,7},{7,6},{8,9},{9,8},{10,11... | collective-permute-start | bytes 2162696 | tf_op jit(solution)/shard_map/ppermute | solution.py:140
  147.6 13.8 %collective-permute-start.18 = (bf16[4,176,512]{2,1,0:T(8,128)(2,1)}, bf16[4,176,512]{2,1,0:T(8,128)(2,1)S(1)}, u32[]{:S(2)}, u32[]{:S(2)}) collective-permute-start(bf16[4,176,512]{2,1,0:T(8,128)(2,1)} %reshape.409.refs_0_), channel_id=1, source_target_pairs={{0,2},{1,3},{2,0},{3,1},{4,6},{5,7},{6,4},{7,5},{8,10},{9,11},{10,... | collective-permute-start | bytes 2162696 | tf_op jit(solution)/shard_map/ppermute | solution.py:140
  161.4 8.6 %collective-permute-start.19 = (bf16[2,176,512]{2,1,0:T(8,128)(2,1)S(1)}, bf16[2,176,512]{2,1,0:T(8,128)(2,1)S(1)}, u32[]{:S(2)}, u32[]{:S(2)}) collective-permute-start(bf16[2,176,512]{2,1,0:T(8,128)(2,1)S(1)} %slice.284), channel_id=1, source_target_pairs={{0,2},{1,3},{2,0},{3,1},{4,6},{5,7},{6,4},{7,5},{8,10},{9,11},{10,... | collective-permute-start | bytes 1081352 | tf_op jit(solution)/shard_map/ppermute | solution.py:140
  173.3 37.4 %collective-permute-start.21 = (bf16[1408,512]{1,0:T(8,128)(2,1)}, bf16[1408,512]{1,0:T(8,128)(2,1)}, u32[]{:S(2)}, u32[]{:S(2)}) collective-permute-start(bf16[1408,512]{1,0:T(8,128)(2,1)} %bitcast.25), channel_id=1, source_target_pairs={{0,16},{16,0},{1,17},{17,1},{2,18},{18,2},{3,19},{19,3},{4,20},{20... | collective-permute-start | bytes 4325384 | tf_op jit(solution)/shard_map/ppermute | solution.py:170
  180.3 25.4 %collective-permute-start.23 = (bf16[4,64,2048]{2,1,0:T(8,128)(2,1)S(1)}, bf16[4,64,2048]{2,1,0:T(8,128)(2,1)}, u32[]{:S(2)}, u32[]{:S(2)}) collective-permute-start(bf16[4,64,2048]{2,1,0:T(8,128)(2,1)S(1)} %slice.283.refs_0_), channel_id=1, source_target_pairs={{0,1},{1,0},{2,3},{3,2},{4,5},{5,4},{6,7},{7,6},{8,9},{9,8},{10,11... | collective-permute-start | bytes 3145736 | tf_op jit(solution)/shard_map/ppermute | solution.py:140
  182.0 25.5 %collective-permute-start.24 = (bf16[4,64,2048]{2,1,0:T(8,128)(2,1)S(1)}, bf16[4,64,2048]{2,1,0:T(8,128)(2,1)}, u32[]{:S(2)}, u32[]{:S(2)}) collective-permute-start(bf16[4,64,2048]{2,1,0:T(8,128)(2,1)S(1)} %slice.283.refs_0_), channel_id=1, source_target_pairs={{0,2},{1,3},{2,0},{3,1},{4,6},{5,7},{6,4},{7,5},{8,10},{9,11},{10,... | collective-permute-start | bytes 3145736 | tf_op jit(solution)/shard_map/ppermute | solution.py:140
  207.5 13.5 %collective-permute-start.25 = (bf16[2,64,2048]{2,1,0:T(8,128)(2,1)}, bf16[2,64,2048]{2,1,0:T(8,128)(2,1)S(1)}, u32[]{:S(2)}, u32[]{:S(2)}) collective-permute-start(bf16[2,64,2048]{2,1,0:T(8,128)(2,1)} %slice.286), channel_id=1, source_target_pairs={{0,2},{1,3},{2,0},{3,1},{4,6},{5,7},{6,4},{7,5},{8,10},{9,11},{10,... | collective-permute-start | bytes 1572872 | tf_op jit(solution)/shard_map/ppermute | solution.py:140
  209.4 12.9 %collective-permute-start.26 = (bf16[2,64,2048]{2,1,0:T(8,128)(2,1)}, bf16[2,64,2048]{2,1,0:T(8,128)(2,1)}, u32[]{:S(2)}, u32[]{:S(2)}) collective-permute-start(bf16[2,64,2048]{2,1,0:T(8,128)(2,1)} %slice.287), channel_id=1, source_target_pairs={{0,1},{1,0},{2,3},{3,2},{4,5},{5,4},{6,7},{7,6},{8,9},{9,8},{10,11... | collective-permute-start | bytes 1572872 | tf_op jit(solution)/shard_map/ppermute | solution.py:140
  216.3 14.8 %collective-permute-start.22 = (bf16[512,1024]{1,0:T(8,128)(2,1)}, bf16[512,1024]{1,0:T(8,128)(2,1)}, u32[]{:S(2)}, u32[]{:S(2)}) collective-permute-start(bf16[512,1024]{1,0:T(8,128)(2,1)} %convolution_convert_fusion.13), channel_id=1, source_target_pairs={{0,16},{16,0},{1,17},{17,1},{2,18},{18,2},{3,19},{19,3},{4,20},{20... | collective-permute-start | bytes 3145736 | tf_op jit(solution)/shard_map/ppermute | solution.py:170
  220.7 198.3 %reduce-scatter.7.cloned.1.call-start = ((), (), s32[]{:S(2)}) async-start(), calls=%async_computation.11 | async-start | bytes 3604480 | tf_op jit(solution)/shard_map/reduce_scatter | solution.py:156
  227.6 33.5 %collective-permute-start.29 = (bf16[4,64,2816]{2,1,0:T(8,128)(2,1)}, bf16[4,64,2816]{2,1,0:T(8,128)(2,1)}, u32[]{:S(2)}, u32[]{:S(2)}) collective-permute-start(bf16[4,64,2816]{2,1,0:T(8,128)(2,1)} %bitcast.33.refs_0_), channel_id=1, source_target_pairs={{0,1},{1,0},{2,3},{3,2},{4,5},{5,4},{6,7},{7,6},{8,9},{9,8},{10,11... | collective-permute-start | bytes 4325384 | tf_op jit(solution)/shard_map/ppermute | solution.py:140
  228.9 34.3 %collective-permute-start.30 = (bf16[4,64,2816]{2,1,0:T(8,128)(2,1)}, bf16[4,64,2816]{2,1,0:T(8,128)(2,1)}, u32[]{:S(2)}, u32[]{:S(2)}) collective-permute-start(bf16[4,64,2816]{2,1,0:T(8,128)(2,1)} %bitcast.33.refs_0_), channel_id=1, source_target_pairs={{0,2},{1,3},{2,0},{3,1},{4,6},{5,7},{6,4},{7,5},{8,10},{9,11},{10,... | collective-permute-start | bytes 4325384 | tf_op jit(solution)/shard_map/ppermute | solution.py:140
  242.1 25.7 %collective-permute-start.28 = (bf16[512,1024]{1,0:T(8,128)(2,1)}, bf16[512,1024]{1,0:T(8,128)(2,1)}, u32[]{:S(2)}, u32[]{:S(2)}) collective-permute-start(bf16[512,1024]{1,0:T(8,128)(2,1)} %convolution_convert_fusion.14), channel_id=1, source_target_pairs={{0,16},{16,0},{1,17},{17,1},{2,18},{18,2},{3,19},{19,3},{4,20},{20... | collective-permute-start | bytes 3145736 | tf_op jit(solution)/shard_map/ppermute | solution.py:170
  263.1 20.0 %collective-permute-start.31 = (bf16[2,64,2816]{2,1,0:T(8,128)(2,1)}, bf16[2,64,2816]{2,1,0:T(8,128)(2,1)}, u32[]{:S(2)}, u32[]{:S(2)}) collective-permute-start(bf16[2,64,2816]{2,1,0:T(8,128)(2,1)} %slice.288), channel_id=1, source_target_pairs={{0,2},{1,3},{2,0},{3,1},{4,6},{5,7},{6,4},{7,5},{8,10},{9,11},{10,... | collective-permute-start | bytes 2162696 | tf_op jit(solution)/shard_map/ppermute | solution.py:140
  266.6 16.8 %collective-permute-start.32 = (bf16[2,64,2816]{2,1,0:T(8,128)(2,1)}, bf16[2,64,2816]{2,1,0:T(8,128)(2,1)}, u32[]{:S(2)}, u32[]{:S(2)}) collective-permute-start(bf16[2,64,2816]{2,1,0:T(8,128)(2,1)} %slice.289), channel_id=1, source_target_pairs={{0,1},{1,0},{2,3},{3,2},{4,5},{5,4},{6,7},{7,6},{8,9},{9,8},{10,11... | collective-permute-start | bytes 2162696 | tf_op jit(solution)/shard_map/ppermute | solution.py:140
  281.9 9.5 %collective-permute-start.33 = (bf16[1408,512]{1,0:T(8,128)(2,1)S(1)}, bf16[1408,512]{1,0:T(8,128)(2,1)S(1)}, u32[]{:S(2)}, u32[]{:S(2)}) collective-permute-start(bf16[1408,512]{1,0:T(8,128)(2,1)S(1)} %get-tuple-element.405), channel_id=1, source_target_pairs={{0,16},{16,0},{1,17},{17,1},{2,18},{18,2},{3,19},{19,3},{4,20},{20... | collective-permute-start | bytes 4325384 | tf_op jit(solution)/shard_map/ppermute | solution.py:170
  304.9 9.9 %collective-permute-start.41 = (bf16[1408,512]{1,0:T(8,128)(2,1)}, bf16[1408,512]{1,0:T(8,128)(2,1)}, u32[]{:S(2)}, u32[]{:S(2)}) collective-permute-start(bf16[1408,512]{1,0:T(8,128)(2,1)} %convolution_convert_fusion.4), channel_id=1, source_target_pairs={{0,16},{16,0},{1,17},{17,1},{2,18},{18,2},{3,19},{19,3},{4,20},{20... | collective-permute-start | bytes 4325384 | tf_op jit(solution)/shard_map/ppermute | solution.py:170
  311.1 37.6 %collective-permute-start.37 = (bf16[2,2,64,2816]{3,2,1,0:T(8,128)(2,1)}, bf16[2,2,64,2816]{3,2,1,0:T(8,128)(2,1)}, u32[]{:S(2)}, u32[]{:S(2)}) collective-permute-start(bf16[2,2,64,2816]{3,2,1,0:T(8,128)(2,1)} %copy-done.67), channel_id=1, source_target_pairs={{0,1},{1,0},{2,3},{3,2},{4,5},{5,4},{6,7},{7,6},{8,9},{9,8},{10,11... | collective-permute-start | bytes 4325384 | tf_op jit(solution)/shard_map/ppermute | solution.py:140
  312.4 32.6 %collective-permute-start.38 = (bf16[2,2,64,2816]{3,2,1,0:T(8,128)(2,1)}, bf16[2,2,64,2816]{3,2,1,0:T(8,128)(2,1)}, u32[]{:S(2)}, u32[]{:S(2)}) collective-permute-start(bf16[2,2,64,2816]{3,2,1,0:T(8,128)(2,1)} %copy-done.68), channel_id=1, source_target_pairs={{0,2},{1,3},{2,0},{3,1},{4,6},{5,7},{6,4},{7,5},{8,10},{9,11},{10,... | collective-permute-start | bytes 4325384 | tf_op jit(solution)/shard_map/ppermute | solution.py:140
  318.2 131.5 %reduce-scatter.9.cloned.1.call-start = ((), (), s32[]{:S(2)}) async-start(), calls=%async_computation.12 | async-start | bytes 1802240 | tf_op jit(solution)/shard_map/reduce_scatter | solution.py:156
  327.0 20.2 %collective-permute-start.35 = (bf16[512,1024]{1,0:T(8,128)(2,1)S(1)}, bf16[512,1024]{1,0:T(8,128)(2,1)S(1)}, u32[]{:S(2)}, u32[]{:S(2)}) collective-permute-start(bf16[512,1024]{1,0:T(8,128)(2,1)S(1)} %convolution_convert_fusion.12), channel_id=1, source_target_pairs={{0,16},{16,0},{1,17},{17,1},{2,18},{18,2},{3,19},{19,3},{4,20},{20... | collective-permute-start | bytes 3145736 | tf_op jit(solution)/shard_map/ppermute | solution.py:170
  329.4 19.3 %collective-permute-start.36 = (bf16[512,512]{1,0:T(8,128)(2,1)S(1)}, bf16[512,512]{1,0:T(8,128)(2,1)S(1)}, u32[]{:S(2)}, u32[]{:S(2)}) collective-permute-start(bf16[512,512]{1,0:T(8,128)(2,1)S(1)} %convolution_convert_fusion.18), channel_id=1, source_target_pairs={{0,16},{16,0},{1,17},{17,1},{2,18},{18,2},{3,19},{19,3},{4,20},{20... | collective-permute-start | bytes 1572872 | tf_op jit(solution)/shard_map/ppermute | solution.py:170
  352.9 26.4 %collective-permute-start.39 = (bf16[512,1024]{1,0:T(8,128)(2,1)}, bf16[512,1024]{1,0:T(8,128)(2,1)}, u32[]{:S(2)}, u32[]{:S(2)}) collective-permute-start(bf16[512,1024]{1,0:T(8,128)(2,1)} %add_convert_fusion.4), channel_id=1, source_target_pairs={{0,16},{16,0},{1,17},{17,1},{2,18},{18,2},{3,19},{19,3},{4,20},{20... | collective-permute-start | bytes 3145736 | tf_op jit(solution)/shard_map/ppermute | solution.py:170
  354.5 18.1 %collective-permute-start.42 = (bf16[2,64,2816]{2,1,0:T(8,128)(2,1)}, bf16[2,64,2816]{2,1,0:T(8,128)(2,1)}, u32[]{:S(2)}, u32[]{:S(2)}) collective-permute-start(bf16[2,64,2816]{2,1,0:T(8,128)(2,1)} %fusion.54), channel_id=1, source_target_pairs={{0,1},{1,0},{2,3},{3,2},{4,5},{5,4},{6,7},{7,6},{8,9},{9,8},{10,11... | collective-permute-start | bytes 2162696 | tf_op jit(solution)/shard_map/ppermute | solution.py:140
  356.9 17.8 %collective-permute-start.43 = (bf16[2,64,2816]{2,1,0:T(8,128)(2,1)}, bf16[2,64,2816]{2,1,0:T(8,128)(2,1)}, u32[]{:S(2)}, u32[]{:S(2)}) collective-permute-start(bf16[2,64,2816]{2,1,0:T(8,128)(2,1)} %fusion.53), channel_id=1, source_target_pairs={{0,2},{1,3},{2,0},{3,1},{4,6},{5,7},{6,4},{7,5},{8,10},{9,11},{10,... | collective-permute-start | bytes 2162696 | tf_op jit(solution)/shard_map/ppermute | solution.py:140
  356.9 10.9 %collective-permute-start.40 = (bf16[512,16]{0,1:T(8,128)(2,1)S(1)}, bf16[512,16]{0,1:T(8,128)(2,1)S(1)}, u32[]{:S(2)}, u32[]{:S(2)}) collective-permute-start(bf16[512,16]{0,1:T(8,128)(2,1)S(1)} %convolution_convert_fusion.22), channel_id=1, source_target_pairs={{0,16},{16,0},{1,17},{17,1},{2,18},{18,2},{3,19},{19,3},{4,20},{20... | collective-permute-start | bytes 49160 | tf_op jit(solution)/shard_map/ppermute | solution.py:170
  372.6 34.7 %collective-permute-start.45 = (bf16[2,2,64,2048]{3,2,1,0:T(8,128)(2,1)}, bf16[2,2,64,2048]{3,2,1,0:T(8,128)(2,1)S(1)}, u32[]{:S(2)}, u32[]{:S(2)}) collective-permute-start(bf16[2,2,64,2048]{3,2,1,0:T(8,128)(2,1)} %get-tuple-element.268), channel_id=1, source_target_pairs={{0,1},{1,0},{2,3},{3,2},{4,5},{5,4},{6,7},{7,6},{8,9},{9,8},{10,11... | collective-permute-start | bytes 3145736 | tf_op jit(solution)/shard_map/ppermute | solution.py:140
  374.7 30.2 %collective-permute-start.46 = (bf16[2,2,64,2048]{3,2,1,0:T(8,128)(2,1)}, bf16[2,2,64,2048]{3,2,1,0:T(8,128)(2,1)}, u32[]{:S(2)}, u32[]{:S(2)}) collective-permute-start(bf16[2,2,64,2048]{3,2,1,0:T(8,128)(2,1)} %get-tuple-element.270), channel_id=1, source_target_pairs={{0,2},{1,3},{2,0},{3,1},{4,6},{5,7},{6,4},{7,5},{8,10},{9,11},{10,... | collective-permute-start | bytes 3145736 | tf_op jit(solution)/shard_map/ppermute | solution.py:140
  379.0 141.8 %reduce-scatter.11.cloned.1.call-start = ((), (), s32[]{:S(2)}) async-start(), calls=%async_computation.13 | async-start | bytes 1310720 | tf_op jit(solution)/shard_map/reduce_scatter | solution.py:156
  394.4 13.9 %collective-permute-start.44 = (bf16[512,1024]{1,0:T(8,128)(2,1)S(1)}, bf16[512,1024]{1,0:T(8,128)(2,1)S(1)}, u32[]{:S(2)}, u32[]{:S(2)}) collective-permute-start(bf16[512,1024]{1,0:T(8,128)(2,1)S(1)} %convolution_convert_fusion.10), channel_id=1, source_target_pairs={{0,16},{16,0},{1,17},{17,1},{2,18},{18,2},{3,19},{19,3},{4,20},{20... | collective-permute-start | bytes 3145736 | tf_op jit(solution)/shard_map/ppermute | solution.py:170
  398.0 11.3 %collective-permute-start.48 = (bf16[1408,512]{1,0:T(8,128)(2,1)S(1)}, bf16[1408,512]{1,0:T(8,128)(2,1)S(1)}, u32[]{:S(2)}, u32[]{:S(2)}) collective-permute-start(bf16[1408,512]{1,0:T(8,128)(2,1)S(1)} %convolution_convert_fusion.2), channel_id=1, source_target_pairs={{0,16},{16,0},{1,17},{17,1},{2,18},{18,2},{3,19},{19,3},{4,20},{20... | collective-permute-start | bytes 4325384 | tf_op jit(solution)/shard_map/ppermute | solution.py:170
  411.5 13.7 %collective-permute-start.49 = (bf16[2,64,2048]{2,1,0:T(8,128)(2,1)}, bf16[2,64,2048]{2,1,0:T(8,128)(2,1)S(1)}, u32[]{:S(2)}, u32[]{:S(2)}) collective-permute-start(bf16[2,64,2048]{2,1,0:T(8,128)(2,1)} %fusion.59), channel_id=1, source_target_pairs={{0,1},{1,0},{2,3},{3,2},{4,5},{5,4},{6,7},{7,6},{8,9},{9,8},{10,11... | collective-permute-start | bytes 1572872 | tf_op jit(solution)/shard_map/ppermute | solution.py:140
  412.7 13.3 %collective-permute-start.50 = (bf16[2,64,2048]{2,1,0:T(8,128)(2,1)}, bf16[2,64,2048]{2,1,0:T(8,128)(2,1)}, u32[]{:S(2)}, u32[]{:S(2)}) collective-permute-start(bf16[2,64,2048]{2,1,0:T(8,128)(2,1)} %fusion.58), channel_id=1, source_target_pairs={{0,2},{1,3},{2,0},{3,1},{4,6},{5,7},{6,4},{7,5},{8,10},{9,11},{10,... | collective-permute-start | bytes 1572872 | tf_op jit(solution)/shard_map/ppermute | solution.py:140
  430.9 97.3 %reduce-scatter.17.cloned.1.call-start = ((), (), s32[]{:S(2)}) async-start(), calls=%async_computation.16 | async-start | bytes 3604480 | tf_op jit(solution)/shard_map/reduce_scatter | solution.py:156
  430.9 32.1 %collective-permute-start.51 = (bf16[2,2,64,2816]{3,2,1,0:T(8,128)(2,1)}, bf16[2,2,64,2816]{3,2,1,0:T(8,128)(2,1)}, u32[]{:S(2)}, u32[]{:S(2)}) collective-permute-start(bf16[2,2,64,2816]{3,2,1,0:T(8,128)(2,1)} %copy-done.66), channel_id=1, source_target_pairs={{0,1},{1,0},{2,3},{3,2},{4,5},{5,4},{6,7},{7,6},{8,9},{9,8},{10,11... | collective-permute-start | bytes 4325384 | tf_op jit(solution)/shard_map/ppermute | solution.py:140
  431.3 31.9 %collective-permute-start.52 = (bf16[2,2,64,2816]{3,2,1,0:T(8,128)(2,1)}, bf16[2,2,64,2816]{3,2,1,0:T(8,128)(2,1)}, u32[]{:S(2)}, u32[]{:S(2)}) collective-permute-start(bf16[2,2,64,2816]{3,2,1,0:T(8,128)(2,1)} %copy-done.65), channel_id=1, source_target_pairs={{0,2},{1,3},{2,0},{3,1},{4,6},{5,7},{6,4},{7,5},{8,10},{9,11},{10,... | collective-permute-start | bytes 4325384 | tf_op jit(solution)/shard_map/ppermute | solution.py:140
  432.8 118.8 %reduce-scatter.15.cloned.1.call-start = ((), (), s32[]{:S(2)}) async-start(), calls=%async_computation.15 | async-start | bytes 1802240 | tf_op jit(solution)/shard_map/reduce_scatter | solution.py:156
  463.7 15.9 %collective-permute-start.54 = (bf16[512,16]{0,1:T(8,128)(2,1)S(1)}, bf16[512,16]{0,1:T(8,128)(2,1)S(1)}, u32[]{:S(2)}, u32[]{:S(2)}) collective-permute-start(bf16[512,16]{0,1:T(8,128)(2,1)S(1)} %convolution_convert_fusion.23), channel_id=1, source_target_pairs={{0,16},{16,0},{1,17},{17,1},{2,18},{18,2},{3,19},{19,3},{4,20},{20... | collective-permute-start | bytes 49160 | tf_op jit(solution)/shard_map/ppermute | solution.py:170
  470.5 9.3 %collective-permute-start.53 = (bf16[512,1024]{1,0:T(8,128)(2,1)S(1)}, bf16[512,1024]{1,0:T(8,128)(2,1)}, u32[]{:S(2)}, u32[]{:S(2)}) collective-permute-start(bf16[512,1024]{1,0:T(8,128)(2,1)S(1)} %add_convert_fusion.1), channel_id=1, source_target_pairs={{0,16},{16,0},{1,17},{17,1},{2,18},{18,2},{3,19},{19,3},{4,20},{20... | collective-permute-start | bytes 3145736 | tf_op jit(solution)/shard_map/ppermute | solution.py:170
  476.5 20.0 %collective-permute-start.58 = (bf16[2,64,2816]{2,1,0:T(8,128)(2,1)}, bf16[2,64,2816]{2,1,0:T(8,128)(2,1)}, u32[]{:S(2)}, u32[]{:S(2)}) collective-permute-start(bf16[2,64,2816]{2,1,0:T(8,128)(2,1)} %fusion.52), channel_id=1, source_target_pairs={{0,1},{1,0},{2,3},{3,2},{4,5},{5,4},{6,7},{7,6},{8,9},{9,8},{10,11... | collective-permute-start | bytes 2162696 | tf_op jit(solution)/shard_map/ppermute | solution.py:140
  477.6 17.4 %collective-permute-start.60 = (bf16[2,64,2816]{2,1,0:T(8,128)(2,1)}, bf16[2,64,2816]{2,1,0:T(8,128)(2,1)}, u32[]{:S(2)}, u32[]{:S(2)}) collective-permute-start(bf16[2,64,2816]{2,1,0:T(8,128)(2,1)} %fusion.51), channel_id=1, source_target_pairs={{0,2},{1,3},{2,0},{3,1},{4,6},{5,7},{6,4},{7,5},{8,10},{9,11},{10,... | collective-permute-start | bytes 2162696 | tf_op jit(solution)/shard_map/ppermute | solution.py:140
  495.0 24.8 %collective-permute-start.61 = (bf16[2,2,64,2176]{3,2,1,0:T(8,128)(2,1)}, bf16[2,2,64,2176]{3,2,1,0:T(8,128)(2,1)S(1)}, u32[]{:S(2)}, u32[]{:S(2)}) collective-permute-start(bf16[2,2,64,2176]{3,2,1,0:T(8,128)(2,1)} %get-tuple-element.316), channel_id=1, source_target_pairs={{0,2},{1,3},{2,0},{3,1},{4,6},{5,7},{6,4},{7,5},{8,10},{9,11},{10,... | collective-permute-start | bytes 3342344 | tf_op jit(solution)/shard_map/ppermute | solution.py:140
  500.8 80.5 %reduce-scatter.13.cloned.1.call-start = ((), (), s32[]{:S(2)}) async-start(), calls=%async_computation.14 | async-start | bytes 1392640 | tf_op jit(solution)/shard_map/reduce_scatter | solution.py:156
  501.2 24.5 %collective-permute-start.59 = (bf16[2,2,64,2176]{3,2,1,0:T(8,128)(2,1)}, bf16[2,2,64,2176]{3,2,1,0:T(8,128)(2,1)S(1)}, u32[]{:S(2)}, u32[]{:S(2)}) collective-permute-start(bf16[2,2,64,2176]{3,2,1,0:T(8,128)(2,1)} %copy-done.69), channel_id=1, source_target_pairs={{0,1},{1,0},{2,3},{3,2},{4,5},{5,4},{6,7},{7,6},{8,9},{9,8},{10,11... | collective-permute-start | bytes 3342344 | tf_op jit(solution)/shard_map/ppermute | solution.py:140
  525.6 11.6 %collective-permute-start.62 = (bf16[2,64,2176]{2,1,0:T(8,128)(2,1)}, bf16[2,64,2176]{2,1,0:T(8,128)(2,1)}, u32[]{:S(2)}, u32[]{:S(2)}) collective-permute-start(bf16[2,64,2176]{2,1,0:T(8,128)(2,1)} %fusion.57), channel_id=1, source_target_pairs={{0,1},{1,0},{2,3},{3,2},{4,5},{5,4},{6,7},{7,6},{8,9},{9,8},{10,11... | collective-permute-start | bytes 1671176 | tf_op jit(solution)/shard_map/ppermute | solution.py:140
  528.1 11.4 %collective-permute-start.63 = (bf16[2,64,2176]{2,1,0:T(8,128)(2,1)}, bf16[2,64,2176]{2,1,0:T(8,128)(2,1)}, u32[]{:S(2)}, u32[]{:S(2)}) collective-permute-start(bf16[2,64,2176]{2,1,0:T(8,128)(2,1)} %fusion.56), channel_id=1, source_target_pairs={{0,2},{1,3},{2,0},{3,1},{4,6},{5,7},{6,4},{7,5},{8,10},{9,11},{10,... | collective-permute-start | bytes 1671176 | tf_op jit(solution)/shard_map/ppermute | solution.py:140
  555.2 22.9 %collective-permute-start.65 = (bf16[64,2816]{1,0:T(8,128)(2,1)S(1)}, bf16[64,2816]{1,0:T(8,128)(2,1)S(1)}, u32[]{:S(2)}, u32[]{:S(2)}) collective-permute-start(bf16[64,2816]{1,0:T(8,128)(2,1)S(1)} %get-tuple-element.423), channel_id=1, source_target_pairs={{0,16},{16,0},{1,17},{17,1},{2,18},{18,2},{3,19},{19,3},{4,20},{20... | collective-permute-start | bytes 1081352 | tf_op jit(solution)/shard_map/ppermute | solution.py:170
  570.3 9.5 %collective-permute-start.72 = (bf16[176,512]{1,0:T(8,128)(2,1)S(1)}, bf16[176,512]{1,0:T(8,128)(2,1)S(1)}, u32[]{:S(2)}, u32[]{:S(2)}) collective-permute-start(bf16[176,512]{1,0:T(8,128)(2,1)S(1)} %get-tuple-element.431), channel_id=1, source_target_pairs={{0,16},{16,0},{1,17},{17,1},{2,18},{18,2},{3,19},{19,3},{4,20},{20... | collective-permute-start | bytes 540680 | tf_op jit(solution)/shard_map/ppermute | solution.py:170
  (146 other events, 1003.8 us)
Sparse Core Ops, SparseCore 0:
  18.0 30.8 all-gather.5
  51.0 33.8 all-gather.7
  87.1 39.9 all-gather.9
  141.2 37.9 all-gather.11
  220.8 58.8 all-gather.13
  318.4 56.6 reduce-scatter.6
  379.1 34.7 reduce-scatter.8
  431.0 27.8 reduce-scatter.10
  461.3 54.7 reduce-scatter.16
  518.5 33.1 reduce-scatter.14
  554.0 27.0 reduce-scatter.12

commit v5 on v4

--- a/solution.py
+++ b/solution.py
@@ -454,28 +454,29 @@
         p.sum = v[n * R : (n + 1) * R]
 
 
-def finish_kernel(widths, at_ref, keep_ref, got_ref, *outs):
+def finish_kernel(widths, at_ref, first_ref, second_ref, got_ref, *outs):
     s = at_ref[3]
     to = 0
     for w, out in zip(widths, outs):
-        out[0, :, pl.ds(pl.multiple_of(s * w, w), w)] = keep_ref[:, to : to + w].astype(F32)
+        keep = jnp.where(s == 0, first_ref[:, to : to + w].astype(F32), second_ref[:, to : to + w].astype(F32))
+        out[0, :, pl.ds(pl.multiple_of(s * w, w), w)] = keep
         out[0, :, pl.ds(pl.multiple_of((1 - s) * w, w), w)] = got_ref[:, to : to + w].astype(F32)
         to += w
 
 
-def finish(keep, got, widths, at):
-    R = keep.shape[0]
+def finish(a, b, got, widths, at):
+    R = got.shape[0]
     return pl.pallas_call(
         partial(finish_kernel, widths),
         grid_spec=pltpu.PrefetchScalarGridSpec(
             num_scalar_prefetch=1,
             grid=(1,),
-            in_specs=[pl.BlockSpec(keep.shape, lambda i, a: (0, 0))] * 2,
+            in_specs=[pl.BlockSpec(v.shape, lambda i, a: (0, 0)) for v in (a, b, got)],
             out_specs=[pl.BlockSpec((1, R, 2 * w), lambda i, a: (0, 0, 0)) for w in widths],
         ),
         out_shape=[jax.ShapeDtypeStruct((1, R, 2 * w), F32) for w in widths],
         compiler_params=PARAMS,
-    )(at, keep, got)
+    )(at, a, b, got)
 
 
 def causal(length):
@@ -988,13 +989,11 @@
     layer_out = jnp.where(first, x1, y1.astype(BF)).reshape((1,) + shape)
 
     def join(a, b, widths):
-        keep = jnp.where(first, a, b)
-        got = over_core(jnp.where(first, b, a))
-        return finish(keep, got, widths, at)
+        return finish(a, b, over_core(jnp.where(first, b, a[:, : b.shape[1]])), widths, at)
 
     dD = join(rD0.sum, rD1.sum, (W,))[0]
     dFg, dFu = join(rF0.sum, rF1.sum, (F, F))
-    dq, dk, dv, dg, dO = join(rA0.sum[:, : A + W], rA1.sum, (K, K, V, V, W))
+    dq, dk, dv, dg, dO = join(rA0.sum, rA1.sum, (K, K, V, V, W))
     t = rA0.sum[:, A + W :].astype(F32)
     return (
         layer_out,

time: 605 us -> 606 us (level)
    unnamed x260 -> x266, local copies, waits for them, and re-layouts: 31 us -> 33.2 us
  transfers between devices with their start and end apart: 84 -> 84, of which waited for: 36 -> 37; matrix products, arithmetic and copies ran while one was open for 31% -> 30% of each run, Pallas kernels for 13% -> 13%
where the time goes in v5:
time: 606 us; the launch traced here: 597 us
  waiting for transfers between devices  189 us (31%)
  other arithmetic  90.4 us (15%)
  Pallas kernels  89.7 us (15%)
  starting transfers between devices  79.7 us (13%)
  local copies, waits for them, and re-layouts  72.2 us (12%)
  matrix products  59.4 us (10%)
  between operations  16.1 us (3%)
    ppermute x46, waiting for transfers between devices, hop(): sent.append(lax.ppermute(v, 'dp', pairs(*step)))  154 us
    ppermute x46, starting transfers between devices, hop(): sent.append(lax.ppermute(v, 'dp', pairs(*step)))  43.3 us
    ppermute x27, starting transfers between devices, over_core(): return lax.ppermute(v, 'section', [(0, 1), (1, 0)])  34.7 us
    unnamed x266, local copies, waits for them, and re-layouts  33.2 us
    pallas_call x10, Pallas kernels, copy_call(): pl.pallas_call(kernel, grid_spec=pltpu.PrefetchScalarGridSpec(num_scalar_...  25.9 us
    all_gather x5, waiting for transfers between devices, gather(): v = lax.all_gather(v, 'dp', axis=0, tiled=True, axis_index_groups=LINES)  23.2 us
    dot_general x10, matrix products, mm(): lax.dot_general(a.astype(BF), b.astype(BF), (((1,), (0,)), ((), ())), pre...  23 us
    dot_general x10, matrix products, mm_nt(): lax.dot_general(a.astype(BF), b.astype(BF), (((1,), (1,)), ((), ())), pre...  22.4 us
  transfers between devices with their start and end apart: 84, of which 37 were waited for; matrix products, arithmetic and copies ran while one was open for 30% of the time, Pallas kernels for 13%

profile of v5, /device:TPU:1, one launch (start us, length us, event | category | flops | bytes accessed | tf_op | source)
XLA Modules:
  0.0 596.8 jit_solution(11861335157583583531)
XLA Ops:
  9.2 3.5 shard_map.288
  26.1 3.4 collective-permute-done.2
  34.1 14.8 %all-gather.6.cloned.1.call-done = bf16[256,2176]{1,0:T(8,128)(2,1)} async-done(((bf16[64,2176]{1,0:T(8,128)(2,1)}), bf16[256,2176]{1,0:T(8,128)(2,1)}) %all-gather.6.cloned.1.call-update) | async-done | bytes 1114128 | tf_op jit(solution)/shard_map/all_gather | solution.py:150
  52.8 21.7 %collective-permute-done.5.refs_1_ = bf16[4,64,2176]{2,1,0:T(8,128)(2,1)S(1)} collective-permute-done((bf16[4,64,2176]{2,1,0:T(8,128)(2,1)}, bf16[4,64,2176]{2,1,0:T(8,128)(2,1)S(1)}, u32[]{:S(2)}, u32[]{:S(2)}) %collective-permute-start.5) | collective-permute-done | bytes 1114144 | tf_op jit(solution)/shard_map/ppermute | solution.py:140
  82.2 5.5 collective-permute-done.8.refs_3_
  103.8 3.5 collective-permute-start.10
  107.3 2.5 multiply_convert_fusion.4
  110.4 4.0 convolution_convert_fusion.9.pre_ref
  114.4 3.0 shard_map.290
  118.6 2.5 shard_map.291
  122.9 5.6 collective-permute-done.13.refs_1_
  144.7 2.6 reshape.409.refs_0_
  152.0 9.3 %collective-permute-done.17.refs_1_ = bf16[4,176,512]{2,1,0:T(8,128)(2,1)S(1)} collective-permute-done((bf16[4,176,512]{2,1,0:T(8,128)(2,1)}, bf16[4,176,512]{2,1,0:T(8,128)(2,1)S(1)}, u32[]{:S(2)}, u32[]{:S(2)}) %collective-permute-start.17) | collective-permute-done | bytes 720928 | tf_op jit(solution)/shard_map/ppermute | solution.py:140
  163.8 3.7 shard_map.292
  173.3 7.0 %collective-permute-start.21 = (bf16[1408,512]{1,0:T(8,128)(2,1)}, bf16[1408,512]{1,0:T(8,128)(2,1)}, u32[]{:S(2)}, u32[]{:S(2)}) collective-permute-start(bf16[1408,512]{1,0:T(8,128)(2,1)} %bitcast.25), channel_id=1, source_target_pairs={{0,16},{16,0},{1,17},{17,1},{2,18},{18,2},{3,19},{19,3},{4,20},{20... | collective-permute-start | bytes 4325384 | tf_op jit(solution)/shard_map/ppermute | solution.py:170
  182.0 4.4 convolution_convert_fusion.1
  186.5 2.7 fusion.21
  189.2 16.5 %collective-permute-done.23.refs_1_ = bf16[4,64,2048]{2,1,0:T(8,128)(2,1)} collective-permute-done((bf16[4,64,2048]{2,1,0:T(8,128)(2,1)S(1)}, bf16[4,64,2048]{2,1,0:T(8,128)(2,1)}, u32[]{:S(2)}, u32[]{:S(2)}) %collective-permute-start.23) | collective-permute-done | bytes 1048608 | tf_op jit(solution)/shard_map/ppermute | solution.py:140
  210.7 2.8 shard_map.294
  213.5 2.8 convolution_convert_fusion.13
  222.3 3.4 shard_map.295
  237.4 3.1 shard_map.296
  246.9 14.3 %collective-permute-done.29.refs_1_ = bf16[4,64,2816]{2,1,0:T(8,128)(2,1)} collective-permute-done((bf16[4,64,2816]{2,1,0:T(8,128)(2,1)}, bf16[4,64,2816]{2,1,0:T(8,128)(2,1)}, u32[]{:S(2)}, u32[]{:S(2)}) %collective-permute-start.29) | collective-permute-done | bytes 1441824 | tf_op jit(solution)/shard_map/ppermute | solution.py:140
  267.9 3.4 add_add_fusion
  271.3 8.4 %all-gather.14.cloned.1.call-done = bf16[2816,512]{1,0:T(8,128)(2,1)} async-done(((bf16[704,512]{1,0:T(8,128)(2,1)}), bf16[2816,512]{1,0:T(8,128)(2,1)}) %all-gather.14.cloned.1.call-update) | async-done | bytes 2883600 | tf_op jit(solution)/shard_map/all_gather | solution.py:150
  283.4 4.4 shard_map.298
  287.9 3.4 convolution_convert_fusion
  292.6 3.2 fusion.6
  296.0 5.9 shard_map.300
  302.0 2.6 convolution_convert_fusion.4
  307.0 4.2 convolution_convert_fusion.11
  314.8 3.4 maximum_select_fusion
  318.3 3.1 fusion.44
  321.4 3.8 fusion.102
  329.6 8.1 %shard_map.301 = (bf16[512,1536]{1,0:T(8,128)(2,1)S(1)}, f32[512,256]{1,0:T(8,128)S(1)}, f32[1,256]{1,0:T(1,128)S(1)}) custom-call(bf16[512,1536]{1,0:T(8,128)(2,1)S(1)} %copy-done.3, f32[512,256]{1,0:T(8,128)S(1)} %convolution_add_fusion.logits_ref, f32[1,256]{1,0:T(1,128)S(1)} %reshape.402.gain_ref, bf16[512,512]{1,0:T(8,128)(2,1)S(1)} %convolution_convert_fusion.21.dg_ref), custom_call_target="tpu_custom_call" | custom-call | tf_op jit(solution)/shard_map/pallas_call | solution.py:629
  339.3 5.7 collective-permute-done.38.gy
  350.0 2.8 add_convert_fusion.4
  362.2 4.8 shard_map.303
  368.7 3.8 collective-permute-done.42.tx
  374.6 4.3 shard_map.304
  379.3 3.6 fusion.46
  385.5 3.0 copy-done.11
  388.4 2.7 fusion.9
  391.2 3.2 convolution_convert_fusion.10
  399.3 5.5 shard_map.302
  404.8 2.5 fusion.59
  414.2 4.8 fusion.35
  419.0 6.1 %collective-permute-done.49.tx = bf16[2,64,2048]{2,1,0:T(8,128)(2,1)S(1)} collective-permute-done((bf16[2,64,2048]{2,1,0:T(8,128)(2,1)}, bf16[2,64,2048]{2,1,0:T(8,128)(2,1)S(1)}, u32[]{:S(2)}, u32[]{:S(2)}) %collective-permute-start.49) | collective-permute-done | bytes 524320 | tf_op jit(solution)/shard_map/ppermute | solution.py:140
  427.3 3.6 shard_map.307
  440.7 8.0 %shard_map.305 = (bf16[512,1536]{1,0:T(8,128)(2,1)S(1)}, f32[512,256]{1,0:T(8,128)S(1)}, f32[1,256]{1,0:T(1,128)S(1)}) custom-call(bf16[512,1536]{1,0:T(8,128)(2,1)S(1)} %copy-done.1, f32[512,256]{1,0:T(8,128)S(1)} %convolution_add_fusion.1.logits_ref, f32[1,256]{1,0:T(1,128)S(1)} %reshape.399.gain_ref, bf16[512,512]{1,0:T(8,128)(2,1)S(1)} %convolution_convert_fusion.20.dg_ref), custom_call_target="tpu_custom_call" | custom-call | tf_op jit(solution)/shard_map/pallas_call | solution.py:629
  449.8 13.3 %collective-permute-done.51.gx = bf16[2,2,64,2816]{3,2,1,0:T(8,128)(2,1)} collective-permute-done((bf16[2,2,64,2816]{3,2,1,0:T(8,128)(2,1)}, bf16[2,2,64,2816]{3,2,1,0:T(8,128)(2,1)}, u32[]{:S(2)}, u32[]{:S(2)}) %collective-permute-start.51) | collective-permute-done | bytes 1441824 | tf_op jit(solution)/shard_map/ppermute | solution.py:140
  466.7 3.9 add_convert_fusion.1
  479.9 3.1 fusion.50
  485.5 4.7 shard_map.306
  496.5 4.3 shard_map.308
  505.8 14.0 %collective-permute-done.61.gy = bf16[2,2,64,2176]{3,2,1,0:T(8,128)(2,1)S(1)} collective-permute-done((bf16[2,2,64,2176]{3,2,1,0:T(8,128)(2,1)}, bf16[2,2,64,2176]{3,2,1,0:T(8,128)(2,1)S(1)}, u32[]{:S(2)}, u32[]{:S(2)}) %collective-permute-start.61) | collective-permute-done | bytes 1114144 | tf_op jit(solution)/shard_map/ppermute | solution.py:140
  520.8 4.9 collective-permute-done.59.gx
  531.1 6.2 %collective-permute-done.62.tx = bf16[2,64,2176]{2,1,0:T(8,128)(2,1)} collective-permute-done((bf16[2,64,2176]{2,1,0:T(8,128)(2,1)}, bf16[2,64,2176]{2,1,0:T(8,128)(2,1)}, u32[]{:S(2)}, u32[]{:S(2)}) %collective-permute-start.62) | collective-permute-done | bytes 557088 | tf_op jit(solution)/shard_map/ppermute | solution.py:140
  539.7 3.6 shard_map.309
  543.4 8.3 %reduce-scatter.15.cloned.1.call-done.first_ref = bf16[64,2816]{1,0:T(8,128)(2,1)} async-done(((bf16[256,2816]{1,0:T(8,128)(2,1)}), bf16[64,2816]{1,0:T(8,128)(2,1)}) %reduce-scatter.15.cloned.1.call-update) | async-done | bytes 360464 | tf_op jit(solution)/shard_map/reduce_scatter | solution.py:156
  559.6 3.5 collective-permute-done.67
  564.7 3.1 collective-permute-done.71
  569.3 3.9 collective-permute-start.72
  573.1 4.3 fusion.32
  (587 shorter events, 238.5 us)
Async XLA Ops:
  7.2 41.7 %all-gather.6.cloned.1.call-start = ((), (), s32[]{:S(2)}) async-start(), calls=%async_computation.6 | async-start | bytes 1392640 | tf_op jit(solution)/shard_map/all_gather | solution.py:150
  17.8 80.4 %all-gather.8.cloned.1.call-start = ((), (), s32[]{:S(2)}) async-start(), calls=%async_computation.7 | async-start | bytes 1802240 | tf_op jit(solution)/shard_map/all_gather | solution.py:150
  20.8 119.0 %all-gather.10.cloned.1.call-start = ((), (), s32[]{:S(2)}) async-start(), calls=%async_computation.8 | async-start | bytes 2211840 | tf_op jit(solution)/shard_map/all_gather | solution.py:150
  31.5 18.6 %collective-permute-start.6 = (bf16[176,256]{1,0:T(8,128)(2,1)S(1)}, bf16[176,256]{1,0:T(8,128)(2,1)}, u32[]{:S(2)}, u32[]{:S(2)}) collective-permute-start(bf16[176,256]{1,0:T(8,128)(2,1)S(1)} %slice.257), channel_id=1, source_target_pairs={{0,2},{1,3},{2,0},{3,1},{4,6},{5,7},{6,4},{7,5},{8,10},{9,11},{10,... | collective-permute-start | bytes 270344 | tf_op jit(solution)/shard_map/ppermute | solution.py:140
  48.9 25.5 %collective-permute-start.5 = (bf16[4,64,2176]{2,1,0:T(8,128)(2,1)}, bf16[4,64,2176]{2,1,0:T(8,128)(2,1)S(1)}, u32[]{:S(2)}, u32[]{:S(2)}) collective-permute-start(bf16[4,64,2176]{2,1,0:T(8,128)(2,1)} %bitcast.246), channel_id=1, source_target_pairs={{0,1},{1,0},{2,3},{3,2},{4,5},{5,4},{6,7},{7,6},{8,9},{9,8},{10,11... | collective-permute-start | bytes 3342344 | tf_op jit(solution)/shard_map/ppermute | solution.py:140
  50.1 25.2 %collective-permute-start.7 = (bf16[4,64,2176]{2,1,0:T(8,128)(2,1)}, bf16[4,64,2176]{2,1,0:T(8,128)(2,1)S(1)}, u32[]{:S(2)}, u32[]{:S(2)}) collective-permute-start(bf16[4,64,2176]{2,1,0:T(8,128)(2,1)} %bitcast.247), channel_id=1, source_target_pairs={{0,2},{1,3},{2,0},{3,1},{4,6},{5,7},{6,4},{7,5},{8,10},{9,11},{10,... | collective-permute-start | bytes 3342344 | tf_op jit(solution)/shard_map/ppermute | solution.py:140
  75.3 12.4 %collective-permute-start.8 = (bf16[2,64,2176]{2,1,0:T(8,128)(2,1)}, bf16[2,64,2176]{2,1,0:T(8,128)(2,1)S(1)}, u32[]{:S(2)}, u32[]{:S(2)}) collective-permute-start(bf16[2,64,2176]{2,1,0:T(8,128)(2,1)} %slice.258), channel_id=1, source_target_pairs={{0,2},{1,3},{2,0},{3,1},{4,6},{5,7},{6,4},{7,5},{8,10},{9,11},{10,... | collective-permute-start | bytes 1671176 | tf_op jit(solution)/shard_map/ppermute | solution.py:140
  77.4 12.1 %collective-permute-start.9 = (bf16[2,64,2176]{2,1,0:T(8,128)(2,1)}, bf16[2,64,2176]{2,1,0:T(8,128)(2,1)S(1)}, u32[]{:S(2)}, u32[]{:S(2)}) collective-permute-start(bf16[2,64,2176]{2,1,0:T(8,128)(2,1)} %slice.259), channel_id=1, source_target_pairs={{0,1},{1,0},{2,3},{3,2},{4,5},{5,4},{6,7},{7,6},{8,9},{9,8},{10,11... | collective-permute-start | bytes 1671176 | tf_op jit(solution)/shard_map/ppermute | solution.py:140
  82.1 104.3 %all-gather.12.cloned.1.call-start = ((), (), s32[]{:S(2)}) async-start(), calls=%async_computation.9 | async-start | bytes 1802240 | tf_op jit(solution)/shard_map/all_gather | solution.py:150
  98.3 30.2 %collective-permute-start.13 = (bf16[4,64,2816]{2,1,0:T(8,128)(2,1)}, bf16[4,64,2816]{2,1,0:T(8,128)(2,1)S(1)}, u32[]{:S(2)}, u32[]{:S(2)}) collective-permute-start(bf16[4,64,2816]{2,1,0:T(8,128)(2,1)} %bitcast.242), channel_id=1, source_target_pairs={{0,1},{1,0},{2,3},{3,2},{4,5},{5,4},{6,7},{7,6},{8,9},{9,8},{10,11... | collective-permute-start | bytes 4325384 | tf_op jit(solution)/shard_map/ppermute | solution.py:140
  99.8 30.2 %collective-permute-start.14 = (bf16[4,64,2816]{2,1,0:T(8,128)(2,1)}, bf16[4,64,2816]{2,1,0:T(8,128)(2,1)}, u32[]{:S(2)}, u32[]{:S(2)}) collective-permute-start(bf16[4,64,2816]{2,1,0:T(8,128)(2,1)} %bitcast.243), channel_id=1, source_target_pairs={{0,2},{1,3},{2,0},{3,1},{4,6},{5,7},{6,4},{7,5},{8,10},{9,11},{10,... | collective-permute-start | bytes 4325384 | tf_op jit(solution)/shard_map/ppermute | solution.py:140
  103.8 14.9 %collective-permute-start.10 = (bf16[512,512]{1,0:T(8,128)(2,1)}, bf16[512,512]{1,0:T(8,128)(2,1)}, u32[]{:S(2)}, u32[]{:S(2)}) collective-permute-start(bf16[512,512]{1,0:T(8,128)(2,1)} %bitcast.15), channel_id=1, source_target_pairs={{0,16},{16,0},{1,17},{17,1},{2,18},{18,2},{3,19},{19,3},{4,20},{20... | collective-permute-start | bytes 1572872 | tf_op jit(solution)/shard_map/ppermute | solution.py:170
  122.9 26.5 %collective-permute-start.11 = (bf16[512,1024]{1,0:T(8,128)(2,1)}, bf16[512,1024]{1,0:T(8,128)(2,1)}, u32[]{:S(2)}, u32[]{:S(2)}) collective-permute-start(bf16[512,1024]{1,0:T(8,128)(2,1)} %convolution_convert_fusion.15), channel_id=1, source_target_pairs={{0,16},{16,0},{1,17},{17,1},{2,18},{18,2},{3,19},{19,3},{4,20},{20... | collective-permute-start | bytes 3145736 | tf_op jit(solution)/shard_map/ppermute | solution.py:170
  130.0 17.6 %collective-permute-start.15 = (bf16[2,64,2816]{2,1,0:T(8,128)(2,1)}, bf16[2,64,2816]{2,1,0:T(8,128)(2,1)}, u32[]{:S(2)}, u32[]{:S(2)}) collective-permute-start(bf16[2,64,2816]{2,1,0:T(8,128)(2,1)} %slice.280), channel_id=1, source_target_pairs={{0,2},{1,3},{2,0},{3,1},{4,6},{5,7},{6,4},{7,5},{8,10},{9,11},{10,... | collective-permute-start | bytes 2162696 | tf_op jit(solution)/shard_map/ppermute | solution.py:140
  132.3 15.0 %collective-permute-start.16 = (bf16[2,64,2816]{2,1,0:T(8,128)(2,1)}, bf16[2,64,2816]{2,1,0:T(8,128)(2,1)}, u32[]{:S(2)}, u32[]{:S(2)}) collective-permute-start(bf16[2,64,2816]{2,1,0:T(8,128)(2,1)} %slice.281), channel_id=1, source_target_pairs={{0,1},{1,0},{2,3},{3,2},{4,5},{5,4},{6,7},{7,6},{8,9},{9,8},{10,11... | collective-permute-start | bytes 2162696 | tf_op jit(solution)/shard_map/ppermute | solution.py:140
  141.1 138.6 %all-gather.14.cloned.1.call-start = ((), (), s32[]{:S(2)}) async-start(), calls=%async_computation.10 | async-start | bytes 3604480 | tf_op jit(solution)/shard_map/all_gather | solution.py:150
  147.3 14.0 %collective-permute-start.17 = (bf16[4,176,512]{2,1,0:T(8,128)(2,1)}, bf16[4,176,512]{2,1,0:T(8,128)(2,1)S(1)}, u32[]{:S(2)}, u32[]{:S(2)}) collective-permute-start(bf16[4,176,512]{2,1,0:T(8,128)(2,1)} %reshape.409.refs_0_), channel_id=1, source_target_pairs={{0,1},{1,0},{2,3},{3,2},{4,5},{5,4},{6,7},{7,6},{8,9},{9,8},{10,11... | collective-permute-start | bytes 2162696 | tf_op jit(solution)/shard_map/ppermute | solution.py:140
  147.6 13.8 %collective-permute-start.18 = (bf16[4,176,512]{2,1,0:T(8,128)(2,1)}, bf16[4,176,512]{2,1,0:T(8,128)(2,1)S(1)}, u32[]{:S(2)}, u32[]{:S(2)}) collective-permute-start(bf16[4,176,512]{2,1,0:T(8,128)(2,1)} %reshape.409.refs_0_), channel_id=1, source_target_pairs={{0,2},{1,3},{2,0},{3,1},{4,6},{5,7},{6,4},{7,5},{8,10},{9,11},{10,... | collective-permute-start | bytes 2162696 | tf_op jit(solution)/shard_map/ppermute | solution.py:140
  161.4 8.6 %collective-permute-start.19 = (bf16[2,176,512]{2,1,0:T(8,128)(2,1)S(1)}, bf16[2,176,512]{2,1,0:T(8,128)(2,1)S(1)}, u32[]{:S(2)}, u32[]{:S(2)}) collective-permute-start(bf16[2,176,512]{2,1,0:T(8,128)(2,1)S(1)} %slice.284), channel_id=1, source_target_pairs={{0,2},{1,3},{2,0},{3,1},{4,6},{5,7},{6,4},{7,5},{8,10},{9,11},{10,... | collective-permute-start | bytes 1081352 | tf_op jit(solution)/shard_map/ppermute | solution.py:140
  173.3 37.4 %collective-permute-start.21 = (bf16[1408,512]{1,0:T(8,128)(2,1)}, bf16[1408,512]{1,0:T(8,128)(2,1)}, u32[]{:S(2)}, u32[]{:S(2)}) collective-permute-start(bf16[1408,512]{1,0:T(8,128)(2,1)} %bitcast.25), channel_id=1, source_target_pairs={{0,16},{16,0},{1,17},{17,1},{2,18},{18,2},{3,19},{19,3},{4,20},{20... | collective-permute-start | bytes 4325384 | tf_op jit(solution)/shard_map/ppermute | solution.py:170
  180.3 25.4 %collective-permute-start.23 = (bf16[4,64,2048]{2,1,0:T(8,128)(2,1)S(1)}, bf16[4,64,2048]{2,1,0:T(8,128)(2,1)}, u32[]{:S(2)}, u32[]{:S(2)}) collective-permute-start(bf16[4,64,2048]{2,1,0:T(8,128)(2,1)S(1)} %slice.283.refs_0_), channel_id=1, source_target_pairs={{0,1},{1,0},{2,3},{3,2},{4,5},{5,4},{6,7},{7,6},{8,9},{9,8},{10,11... | collective-permute-start | bytes 3145736 | tf_op jit(solution)/shard_map/ppermute | solution.py:140
  182.0 25.5 %collective-permute-start.24 = (bf16[4,64,2048]{2,1,0:T(8,128)(2,1)S(1)}, bf16[4,64,2048]{2,1,0:T(8,128)(2,1)}, u32[]{:S(2)}, u32[]{:S(2)}) collective-permute-start(bf16[4,64,2048]{2,1,0:T(8,128)(2,1)S(1)} %slice.283.refs_0_), channel_id=1, source_target_pairs={{0,2},{1,3},{2,0},{3,1},{4,6},{5,7},{6,4},{7,5},{8,10},{9,11},{10,... | collective-permute-start | bytes 3145736 | tf_op jit(solution)/shard_map/ppermute | solution.py:140
  207.5 13.5 %collective-permute-start.25 = (bf16[2,64,2048]{2,1,0:T(8,128)(2,1)}, bf16[2,64,2048]{2,1,0:T(8,128)(2,1)S(1)}, u32[]{:S(2)}, u32[]{:S(2)}) collective-permute-start(bf16[2,64,2048]{2,1,0:T(8,128)(2,1)} %slice.286), channel_id=1, source_target_pairs={{0,2},{1,3},{2,0},{3,1},{4,6},{5,7},{6,4},{7,5},{8,10},{9,11},{10,... | collective-permute-start | bytes 1572872 | tf_op jit(solution)/shard_map/ppermute | solution.py:140
  209.4 12.9 %collective-permute-start.26 = (bf16[2,64,2048]{2,1,0:T(8,128)(2,1)}, bf16[2,64,2048]{2,1,0:T(8,128)(2,1)}, u32[]{:S(2)}, u32[]{:S(2)}) collective-permute-start(bf16[2,64,2048]{2,1,0:T(8,128)(2,1)} %slice.287), channel_id=1, source_target_pairs={{0,1},{1,0},{2,3},{3,2},{4,5},{5,4},{6,7},{7,6},{8,9},{9,8},{10,11... | collective-permute-start | bytes 1572872 | tf_op jit(solution)/shard_map/ppermute | solution.py:140
  216.3 14.8 %collective-permute-start.22 = (bf16[512,1024]{1,0:T(8,128)(2,1)}, bf16[512,1024]{1,0:T(8,128)(2,1)}, u32[]{:S(2)}, u32[]{:S(2)}) collective-permute-start(bf16[512,1024]{1,0:T(8,128)(2,1)} %convolution_convert_fusion.13), channel_id=1, source_target_pairs={{0,16},{16,0},{1,17},{17,1},{2,18},{18,2},{3,19},{19,3},{4,20},{20... | collective-permute-start | bytes 3145736 | tf_op jit(solution)/shard_map/ppermute | solution.py:170
  220.7 198.3 %reduce-scatter.7.cloned.1.call-start = ((), (), s32[]{:S(2)}) async-start(), calls=%async_computation.11 | async-start | bytes 3604480 | tf_op jit(solution)/shard_map/reduce_scatter | solution.py:156
  227.6 33.5 %collective-permute-start.29 = (bf16[4,64,2816]{2,1,0:T(8,128)(2,1)}, bf16[4,64,2816]{2,1,0:T(8,128)(2,1)}, u32[]{:S(2)}, u32[]{:S(2)}) collective-permute-start(bf16[4,64,2816]{2,1,0:T(8,128)(2,1)} %bitcast.33.refs_0_), channel_id=1, source_target_pairs={{0,1},{1,0},{2,3},{3,2},{4,5},{5,4},{6,7},{7,6},{8,9},{9,8},{10,11... | collective-permute-start | bytes 4325384 | tf_op jit(solution)/shard_map/ppermute | solution.py:140
  228.9 34.3 %collective-permute-start.30 = (bf16[4,64,2816]{2,1,0:T(8,128)(2,1)}, bf16[4,64,2816]{2,1,0:T(8,128)(2,1)}, u32[]{:S(2)}, u32[]{:S(2)}) collective-permute-start(bf16[4,64,2816]{2,1,0:T(8,128)(2,1)} %bitcast.33.refs_0_), channel_id=1, source_target_pairs={{0,2},{1,3},{2,0},{3,1},{4,6},{5,7},{6,4},{7,5},{8,10},{9,11},{10,... | collective-permute-start | bytes 4325384 | tf_op jit(solution)/shard_map/ppermute | solution.py:140
  242.1 25.7 %collective-permute-start.28 = (bf16[512,1024]{1,0:T(8,128)(2,1)}, bf16[512,1024]{1,0:T(8,128)(2,1)}, u32[]{:S(2)}, u32[]{:S(2)}) collective-permute-start(bf16[512,1024]{1,0:T(8,128)(2,1)} %convolution_convert_fusion.14), channel_id=1, source_target_pairs={{0,16},{16,0},{1,17},{17,1},{2,18},{18,2},{3,19},{19,3},{4,20},{20... | collective-permute-start | bytes 3145736 | tf_op jit(solution)/shard_map/ppermute | solution.py:170
  263.1 20.0 %collective-permute-start.31 = (bf16[2,64,2816]{2,1,0:T(8,128)(2,1)}, bf16[2,64,2816]{2,1,0:T(8,128)(2,1)}, u32[]{:S(2)}, u32[]{:S(2)}) collective-permute-start(bf16[2,64,2816]{2,1,0:T(8,128)(2,1)} %slice.288), channel_id=1, source_target_pairs={{0,2},{1,3},{2,0},{3,1},{4,6},{5,7},{6,4},{7,5},{8,10},{9,11},{10,... | collective-permute-start | bytes 2162696 | tf_op jit(solution)/shard_map/ppermute | solution.py:140
  266.6 16.8 %collective-permute-start.32 = (bf16[2,64,2816]{2,1,0:T(8,128)(2,1)}, bf16[2,64,2816]{2,1,0:T(8,128)(2,1)}, u32[]{:S(2)}, u32[]{:S(2)}) collective-permute-start(bf16[2,64,2816]{2,1,0:T(8,128)(2,1)} %slice.289), channel_id=1, source_target_pairs={{0,1},{1,0},{2,3},{3,2},{4,5},{5,4},{6,7},{7,6},{8,9},{9,8},{10,11... | collective-permute-start | bytes 2162696 | tf_op jit(solution)/shard_map/ppermute | solution.py:140
  281.9 9.5 %collective-permute-start.33 = (bf16[1408,512]{1,0:T(8,128)(2,1)S(1)}, bf16[1408,512]{1,0:T(8,128)(2,1)S(1)}, u32[]{:S(2)}, u32[]{:S(2)}) collective-permute-start(bf16[1408,512]{1,0:T(8,128)(2,1)S(1)} %get-tuple-element.408), channel_id=1, source_target_pairs={{0,16},{16,0},{1,17},{17,1},{2,18},{18,2},{3,19},{19,3},{4,20},{20... | collective-permute-start | bytes 4325384 | tf_op jit(solution)/shard_map/ppermute | solution.py:170
  304.9 9.9 %collective-permute-start.41 = (bf16[1408,512]{1,0:T(8,128)(2,1)}, bf16[1408,512]{1,0:T(8,128)(2,1)}, u32[]{:S(2)}, u32[]{:S(2)}) collective-permute-start(bf16[1408,512]{1,0:T(8,128)(2,1)} %convolution_convert_fusion.4), channel_id=1, source_target_pairs={{0,16},{16,0},{1,17},{17,1},{2,18},{18,2},{3,19},{19,3},{4,20},{20... | collective-permute-start | bytes 4325384 | tf_op jit(solution)/shard_map/ppermute | solution.py:170
  311.1 37.5 %collective-permute-start.37 = (bf16[2,2,64,2816]{3,2,1,0:T(8,128)(2,1)}, bf16[2,2,64,2816]{3,2,1,0:T(8,128)(2,1)}, u32[]{:S(2)}, u32[]{:S(2)}) collective-permute-start(bf16[2,2,64,2816]{3,2,1,0:T(8,128)(2,1)} %copy-done.72), channel_id=1, source_target_pairs={{0,1},{1,0},{2,3},{3,2},{4,5},{5,4},{6,7},{7,6},{8,9},{9,8},{10,11... | collective-permute-start | bytes 4325384 | tf_op jit(solution)/shard_map/ppermute | solution.py:140
  312.4 32.6 %collective-permute-start.38 = (bf16[2,2,64,2816]{3,2,1,0:T(8,128)(2,1)}, bf16[2,2,64,2816]{3,2,1,0:T(8,128)(2,1)}, u32[]{:S(2)}, u32[]{:S(2)}) collective-permute-start(bf16[2,2,64,2816]{3,2,1,0:T(8,128)(2,1)} %copy-done.73), channel_id=1, source_target_pairs={{0,2},{1,3},{2,0},{3,1},{4,6},{5,7},{6,4},{7,5},{8,10},{9,11},{10,... | collective-permute-start | bytes 4325384 | tf_op jit(solution)/shard_map/ppermute | solution.py:140
  318.2 131.6 %reduce-scatter.9.cloned.1.call-start = ((), (), s32[]{:S(2)}) async-start(), calls=%async_computation.12 | async-start | bytes 1802240 | tf_op jit(solution)/shard_map/reduce_scatter | solution.py:156
  327.0 20.2 %collective-permute-start.35 = (bf16[512,1024]{1,0:T(8,128)(2,1)S(1)}, bf16[512,1024]{1,0:T(8,128)(2,1)S(1)}, u32[]{:S(2)}, u32[]{:S(2)}) collective-permute-start(bf16[512,1024]{1,0:T(8,128)(2,1)S(1)} %convolution_convert_fusion.12), channel_id=1, source_target_pairs={{0,16},{16,0},{1,17},{17,1},{2,18},{18,2},{3,19},{19,3},{4,20},{20... | collective-permute-start | bytes 3145736 | tf_op jit(solution)/shard_map/ppermute | solution.py:170
  329.4 19.2 %collective-permute-start.36 = (bf16[512,512]{1,0:T(8,128)(2,1)S(1)}, bf16[512,512]{1,0:T(8,128)(2,1)S(1)}, u32[]{:S(2)}, u32[]{:S(2)}) collective-permute-start(bf16[512,512]{1,0:T(8,128)(2,1)S(1)} %convolution_convert_fusion.18), channel_id=1, source_target_pairs={{0,16},{16,0},{1,17},{17,1},{2,18},{18,2},{3,19},{19,3},{4,20},{20... | collective-permute-start | bytes 1572872 | tf_op jit(solution)/shard_map/ppermute | solution.py:170
  352.8 26.4 %collective-permute-start.39 = (bf16[512,1024]{1,0:T(8,128)(2,1)}, bf16[512,1024]{1,0:T(8,128)(2,1)}, u32[]{:S(2)}, u32[]{:S(2)}) collective-permute-start(bf16[512,1024]{1,0:T(8,128)(2,1)} %add_convert_fusion.4), channel_id=1, source_target_pairs={{0,16},{16,0},{1,17},{17,1},{2,18},{18,2},{3,19},{19,3},{4,20},{20... | collective-permute-start | bytes 3145736 | tf_op jit(solution)/shard_map/ppermute | solution.py:170
  354.5 18.1 %collective-permute-start.42 = (bf16[2,64,2816]{2,1,0:T(8,128)(2,1)}, bf16[2,64,2816]{2,1,0:T(8,128)(2,1)}, u32[]{:S(2)}, u32[]{:S(2)}) collective-permute-start(bf16[2,64,2816]{2,1,0:T(8,128)(2,1)} %fusion.54), channel_id=1, source_target_pairs={{0,1},{1,0},{2,3},{3,2},{4,5},{5,4},{6,7},{7,6},{8,9},{9,8},{10,11... | collective-permute-start | bytes 2162696 | tf_op jit(solution)/shard_map/ppermute | solution.py:140
  356.8 17.8 %collective-permute-start.43 = (bf16[2,64,2816]{2,1,0:T(8,128)(2,1)}, bf16[2,64,2816]{2,1,0:T(8,128)(2,1)}, u32[]{:S(2)}, u32[]{:S(2)}) collective-permute-start(bf16[2,64,2816]{2,1,0:T(8,128)(2,1)} %fusion.53), channel_id=1, source_target_pairs={{0,2},{1,3},{2,0},{3,1},{4,6},{5,7},{6,4},{7,5},{8,10},{9,11},{10,... | collective-permute-start | bytes 2162696 | tf_op jit(solution)/shard_map/ppermute | solution.py:140
  356.8 10.9 %collective-permute-start.40 = (bf16[512,16]{0,1:T(8,128)(2,1)S(1)}, bf16[512,16]{0,1:T(8,128)(2,1)S(1)}, u32[]{:S(2)}, u32[]{:S(2)}) collective-permute-start(bf16[512,16]{0,1:T(8,128)(2,1)S(1)} %convolution_convert_fusion.22), channel_id=1, source_target_pairs={{0,16},{16,0},{1,17},{17,1},{2,18},{18,2},{3,19},{19,3},{4,20},{20... | collective-permute-start | bytes 49160 | tf_op jit(solution)/shard_map/ppermute | solution.py:170
  372.6 34.8 %collective-permute-start.45 = (bf16[2,2,64,2048]{3,2,1,0:T(8,128)(2,1)}, bf16[2,2,64,2048]{3,2,1,0:T(8,128)(2,1)S(1)}, u32[]{:S(2)}, u32[]{:S(2)}) collective-permute-start(bf16[2,2,64,2048]{3,2,1,0:T(8,128)(2,1)} %get-tuple-element.268), channel_id=1, source_target_pairs={{0,1},{1,0},{2,3},{3,2},{4,5},{5,4},{6,7},{7,6},{8,9},{9,8},{10,11... | collective-permute-start | bytes 3145736 | tf_op jit(solution)/shard_map/ppermute | solution.py:140
  374.6 30.2 %collective-permute-start.46 = (bf16[2,2,64,2048]{3,2,1,0:T(8,128)(2,1)}, bf16[2,2,64,2048]{3,2,1,0:T(8,128)(2,1)}, u32[]{:S(2)}, u32[]{:S(2)}) collective-permute-start(bf16[2,2,64,2048]{3,2,1,0:T(8,128)(2,1)} %get-tuple-element.270), channel_id=1, source_target_pairs={{0,2},{1,3},{2,0},{3,1},{4,6},{5,7},{6,4},{7,5},{8,10},{9,11},{10,... | collective-permute-start | bytes 3145736 | tf_op jit(solution)/shard_map/ppermute | solution.py:140
  379.0 141.8 %reduce-scatter.11.cloned.1.call-start = ((), (), s32[]{:S(2)}) async-start(), calls=%async_computation.13 | async-start | bytes 1310720 | tf_op jit(solution)/shard_map/reduce_scatter | solution.py:156
  394.4 13.9 %collective-permute-start.44 = (bf16[512,1024]{1,0:T(8,128)(2,1)S(1)}, bf16[512,1024]{1,0:T(8,128)(2,1)S(1)}, u32[]{:S(2)}, u32[]{:S(2)}) collective-permute-start(bf16[512,1024]{1,0:T(8,128)(2,1)S(1)} %convolution_convert_fusion.10), channel_id=1, source_target_pairs={{0,16},{16,0},{1,17},{17,1},{2,18},{18,2},{3,19},{19,3},{4,20},{20... | collective-permute-start | bytes 3145736 | tf_op jit(solution)/shard_map/ppermute | solution.py:170
  398.0 11.3 %collective-permute-start.48 = (bf16[1408,512]{1,0:T(8,128)(2,1)S(1)}, bf16[1408,512]{1,0:T(8,128)(2,1)S(1)}, u32[]{:S(2)}, u32[]{:S(2)}) collective-permute-start(bf16[1408,512]{1,0:T(8,128)(2,1)S(1)} %convolution_convert_fusion.2), channel_id=1, source_target_pairs={{0,16},{16,0},{1,17},{17,1},{2,18},{18,2},{3,19},{19,3},{4,20},{20... | collective-permute-start | bytes 4325384 | tf_op jit(solution)/shard_map/ppermute | solution.py:170
  411.5 13.7 %collective-permute-start.49 = (bf16[2,64,2048]{2,1,0:T(8,128)(2,1)}, bf16[2,64,2048]{2,1,0:T(8,128)(2,1)S(1)}, u32[]{:S(2)}, u32[]{:S(2)}) collective-permute-start(bf16[2,64,2048]{2,1,0:T(8,128)(2,1)} %fusion.59), channel_id=1, source_target_pairs={{0,1},{1,0},{2,3},{3,2},{4,5},{5,4},{6,7},{7,6},{8,9},{9,8},{10,11... | collective-permute-start | bytes 1572872 | tf_op jit(solution)/shard_map/ppermute | solution.py:140
  412.7 13.3 %collective-permute-start.50 = (bf16[2,64,2048]{2,1,0:T(8,128)(2,1)}, bf16[2,64,2048]{2,1,0:T(8,128)(2,1)}, u32[]{:S(2)}, u32[]{:S(2)}) collective-permute-start(bf16[2,64,2048]{2,1,0:T(8,128)(2,1)} %fusion.58), channel_id=1, source_target_pairs={{0,2},{1,3},{2,0},{3,1},{4,6},{5,7},{6,4},{7,5},{8,10},{9,11},{10,... | collective-permute-start | bytes 1572872 | tf_op jit(solution)/shard_map/ppermute | solution.py:140
  430.9 96.2 %reduce-scatter.17.cloned.1.call-start = ((), (), s32[]{:S(2)}) async-start(), calls=%async_computation.16 | async-start | bytes 3604480 | tf_op jit(solution)/shard_map/reduce_scatter | solution.py:156
  431.0 32.1 %collective-permute-start.51 = (bf16[2,2,64,2816]{3,2,1,0:T(8,128)(2,1)}, bf16[2,2,64,2816]{3,2,1,0:T(8,128)(2,1)}, u32[]{:S(2)}, u32[]{:S(2)}) collective-permute-start(bf16[2,2,64,2816]{3,2,1,0:T(8,128)(2,1)} %copy-done.71), channel_id=1, source_target_pairs={{0,1},{1,0},{2,3},{3,2},{4,5},{5,4},{6,7},{7,6},{8,9},{9,8},{10,11... | collective-permute-start | bytes 4325384 | tf_op jit(solution)/shard_map/ppermute | solution.py:140
  431.4 31.9 %collective-permute-start.52 = (bf16[2,2,64,2816]{3,2,1,0:T(8,128)(2,1)}, bf16[2,2,64,2816]{3,2,1,0:T(8,128)(2,1)}, u32[]{:S(2)}, u32[]{:S(2)}) collective-permute-start(bf16[2,2,64,2816]{3,2,1,0:T(8,128)(2,1)} %copy-done.70), channel_id=1, source_target_pairs={{0,2},{1,3},{2,0},{3,1},{4,6},{5,7},{6,4},{7,5},{8,10},{9,11},{10,... | collective-permute-start | bytes 4325384 | tf_op jit(solution)/shard_map/ppermute | solution.py:140
  432.8 118.8 %reduce-scatter.15.cloned.1.call-start = ((), (), s32[]{:S(2)}) async-start(), calls=%async_computation.15 | async-start | bytes 1802240 | tf_op jit(solution)/shard_map/reduce_scatter | solution.py:156
  463.7 15.9 %collective-permute-start.54 = (bf16[512,16]{0,1:T(8,128)(2,1)S(1)}, bf16[512,16]{0,1:T(8,128)(2,1)S(1)}, u32[]{:S(2)}, u32[]{:S(2)}) collective-permute-start(bf16[512,16]{0,1:T(8,128)(2,1)S(1)} %convolution_convert_fusion.23), channel_id=1, source_target_pairs={{0,16},{16,0},{1,17},{17,1},{2,18},{18,2},{3,19},{19,3},{4,20},{20... | collective-permute-start | bytes 49160 | tf_op jit(solution)/shard_map/ppermute | solution.py:170
  470.6 9.3 %collective-permute-start.53 = (bf16[512,1024]{1,0:T(8,128)(2,1)S(1)}, bf16[512,1024]{1,0:T(8,128)(2,1)}, u32[]{:S(2)}, u32[]{:S(2)}) collective-permute-start(bf16[512,1024]{1,0:T(8,128)(2,1)S(1)} %add_convert_fusion.1), channel_id=1, source_target_pairs={{0,16},{16,0},{1,17},{17,1},{2,18},{18,2},{3,19},{19,3},{4,20},{20... | collective-permute-start | bytes 3145736 | tf_op jit(solution)/shard_map/ppermute | solution.py:170
  476.5 20.0 %collective-permute-start.58 = (bf16[2,64,2816]{2,1,0:T(8,128)(2,1)}, bf16[2,64,2816]{2,1,0:T(8,128)(2,1)}, u32[]{:S(2)}, u32[]{:S(2)}) collective-permute-start(bf16[2,64,2816]{2,1,0:T(8,128)(2,1)} %fusion.52), channel_id=1, source_target_pairs={{0,1},{1,0},{2,3},{3,2},{4,5},{5,4},{6,7},{7,6},{8,9},{9,8},{10,11... | collective-permute-start | bytes 2162696 | tf_op jit(solution)/shard_map/ppermute | solution.py:140
  477.7 17.4 %collective-permute-start.60 = (bf16[2,64,2816]{2,1,0:T(8,128)(2,1)}, bf16[2,64,2816]{2,1,0:T(8,128)(2,1)}, u32[]{:S(2)}, u32[]{:S(2)}) collective-permute-start(bf16[2,64,2816]{2,1,0:T(8,128)(2,1)} %fusion.51), channel_id=1, source_target_pairs={{0,2},{1,3},{2,0},{3,1},{4,6},{5,7},{6,4},{7,5},{8,10},{9,11},{10,... | collective-permute-start | bytes 2162696 | tf_op jit(solution)/shard_map/ppermute | solution.py:140
  495.1 24.8 %collective-permute-start.61 = (bf16[2,2,64,2176]{3,2,1,0:T(8,128)(2,1)}, bf16[2,2,64,2176]{3,2,1,0:T(8,128)(2,1)S(1)}, u32[]{:S(2)}, u32[]{:S(2)}) collective-permute-start(bf16[2,2,64,2176]{3,2,1,0:T(8,128)(2,1)} %get-tuple-element.316), channel_id=1, source_target_pairs={{0,2},{1,3},{2,0},{3,1},{4,6},{5,7},{6,4},{7,5},{8,10},{9,11},{10,... | collective-permute-start | bytes 3342344 | tf_op jit(solution)/shard_map/ppermute | solution.py:140
  500.8 80.3 %reduce-scatter.13.cloned.1.call-start = ((), (), s32[]{:S(2)}) async-start(), calls=%async_computation.14 | async-start | bytes 1392640 | tf_op jit(solution)/shard_map/reduce_scatter | solution.py:156
  501.2 24.5 %collective-permute-start.59 = (bf16[2,2,64,2176]{3,2,1,0:T(8,128)(2,1)}, bf16[2,2,64,2176]{3,2,1,0:T(8,128)(2,1)S(1)}, u32[]{:S(2)}, u32[]{:S(2)}) collective-permute-start(bf16[2,2,64,2176]{3,2,1,0:T(8,128)(2,1)} %copy-done.74), channel_id=1, source_target_pairs={{0,1},{1,0},{2,3},{3,2},{4,5},{5,4},{6,7},{7,6},{8,9},{9,8},{10,11... | collective-permute-start | bytes 3342344 | tf_op jit(solution)/shard_map/ppermute | solution.py:140
  525.7 11.6 %collective-permute-start.62 = (bf16[2,64,2176]{2,1,0:T(8,128)(2,1)}, bf16[2,64,2176]{2,1,0:T(8,128)(2,1)}, u32[]{:S(2)}, u32[]{:S(2)}) collective-permute-start(bf16[2,64,2176]{2,1,0:T(8,128)(2,1)} %fusion.57), channel_id=1, source_target_pairs={{0,1},{1,0},{2,3},{3,2},{4,5},{5,4},{6,7},{7,6},{8,9},{9,8},{10,11... | collective-permute-start | bytes 1671176 | tf_op jit(solution)/shard_map/ppermute | solution.py:140
  527.0 11.4 %collective-permute-start.63 = (bf16[2,64,2176]{2,1,0:T(8,128)(2,1)}, bf16[2,64,2176]{2,1,0:T(8,128)(2,1)S(1)}, u32[]{:S(2)}, u32[]{:S(2)}) collective-permute-start(bf16[2,64,2176]{2,1,0:T(8,128)(2,1)} %fusion.56), channel_id=1, source_target_pairs={{0,2},{1,3},{2,0},{3,1},{4,6},{5,7},{6,4},{7,5},{8,10},{9,11},{10,... | collective-permute-start | bytes 1671176 | tf_op jit(solution)/shard_map/ppermute | solution.py:140
  555.2 22.3 %collective-permute-start.65 = (bf16[64,2816]{1,0:T(8,128)(2,1)S(1)}, bf16[64,2816]{1,0:T(8,128)(2,1)S(1)}, u32[]{:S(2)}, u32[]{:S(2)}) collective-permute-start(bf16[64,2816]{1,0:T(8,128)(2,1)S(1)} %broadcast_select_fusion), channel_id=1, source_target_pairs={{0,16},{16,0},{1,17},{17,1},{2,18},{18,2},{3,19},{19,3},{4,20},{20... | collective-permute-start | bytes 1081352 | tf_op jit(solution)/shard_map/ppermute | solution.py:170
  569.3 9.9 %collective-permute-start.72 = (bf16[176,512]{1,0:T(8,128)(2,1)S(1)}, bf16[176,512]{1,0:T(8,128)(2,1)S(1)}, u32[]{:S(2)}, u32[]{:S(2)}) collective-permute-start(bf16[176,512]{1,0:T(8,128)(2,1)S(1)} %get-tuple-element.396), channel_id=1, source_target_pairs={{0,16},{16,0},{1,17},{17,1},{2,18},{18,2},{3,19},{19,3},{4,20},{20... | collective-permute-start | bytes 540680 | tf_op jit(solution)/shard_map/ppermute | solution.py:170
  (149 other events, 962.1 us)
Sparse Core Ops, SparseCore 0:
  18.0 30.8 all-gather.5
  51.0 33.8 all-gather.7
  87.1 39.9 all-gather.9
  141.2 37.9 all-gather.11
  220.8 58.8 all-gather.13
  318.3 56.6 reduce-scatter.6
  379.1 34.7 reduce-scatter.8
  431.0 27.8 reduce-scatter.10
  461.4 54.8 reduce-scatter.16
  518.5 33.1 reduce-scatter.14
  554.1 27.0 reduce-scatter.12
